TPU v7x, 32 devices: a whole 2x2x4 slice. The times are simulated.
32 devices in a mesh: seg: 4 (over y, x), exp: 8 (over z, core).
Axes of the slice: x: 2, y: 2, z: 4, core: 2. Of those that a mesh axis runs over, the one named last changes fastest.
Arguments:
- images: float32 [8, 2048, 4096], P('exp', 'seg'), may hold values from -6 to 6
- psf_coef: float32 [8, 2, 3], P('exp'), may hold values from 0.2 to 1
- phases: int32 [8, 2], P('exp'), may hold values from 0 to 15
- col_shift: int32 [8], P('exp'), may hold values from -40 to 40
- band_offset: int32 [8], P('exp'), may hold values from 0 to 16
- exposure_weight: bfloat16 [8], P('exp'), may hold values from 0.5 to 4
- patch_site: int32 [160], replicated, may hold values from 0 to 159, each once
Outputs:
- coadded: float32 [160, 32, 2048], P('exp', 'seg')
Inputs may be any that keep to these rules, and one draw needn't show every extreme that they name: `phases`: a phase index p moves the sampling point by p / 16 of a pixel, the first entry along rows, the second along columns. An exposure's pixel column j lands on sky column j + col_shift. An exposure covers the sky bands band_offset to band_offset + 2048 / 32 - 1. `patch_site`: every sky position 2 * band + half is the site of exactly one stored patch.
All inputs are finite; a program needn't handle non-finite values.
Results may differ from a plain program's by a relative error of at most 0.0029.
Values may be sent and summed in bfloat16 or wider, within the bound.
No kernel may reach another device: no remote copies, remote signals or barrier semaphores. Data moves between devices by JAX's collectives and lax.ppermute only.
A program may use at most 128 MiB of HBM per device.

v0:
```python
import jax
import jax.numpy as jnp
from jax import lax
from jax.sharding import PartitionSpec as P

BAND_ROWS = 32
TAPS = 21
PHASES = 16


sigmas = (1.0, 2.0, 3.5)
block_cols = 128


def extended_2(block, sides, width):
    for axis, dim in sides:
        count = lax.axis_size(axis)
        forward = [(i, i + 1) for i in range(count - 1)]
        backward = [(target, source) for source, target in forward]
        low = lax.ppermute(
            lax.slice_in_dim(block, block.shape[dim] - width, None, axis=dim), axis, forward
        )
        high = lax.ppermute(lax.slice_in_dim(block, 0, width, axis=dim), axis, backward)
        block = jnp.concatenate([low, block, high], axis=dim)
    return block


def basis_table():
    offsets = jnp.arange(TAPS).astype(jnp.float32) - TAPS // 2
    table_rows = []
    for spread in sigmas:
        curve = jnp.exp(-offsets * offsets / (2.0 * spread * spread))
        table_rows.append(curve / jnp.sum(curve))
    return jnp.stack(table_rows)


def lanczos_weights(phase):
    fraction = phase.astype(jnp.float32) / PHASES
    offsets = jnp.arange(6).astype(jnp.float32) - 2.0
    shifted = offsets - fraction
    values = jnp.sinc(shifted) * jnp.sinc(shifted / 3.0)
    return values / jnp.sum(values)


def band_matrix(weights, count_out, count_in, lead):
    distance = (
        lax.broadcasted_iota(jnp.int32, (count_out, count_in), 1)
        - lax.broadcasted_iota(jnp.int32, (count_out, count_in), 0)
        - lead
    )
    matrix = jnp.zeros((count_out, count_in), jnp.float32)
    for position in range(weights.shape[0]):
        matrix = matrix + jnp.where(distance == position, weights[position], 0.0)
    return matrix


def across_columns(source, matrix):
    count_rows, count_cols = source.shape
    padded = jnp.pad(source, ((0, 0), (block_cols, block_cols)))
    padded = padded.reshape(count_rows, count_cols // block_cols + 2, block_cols)
    windows = jnp.concatenate([padded[:, :-2], padded[:, 1:-1], padded[:, 2:]], axis=2)
    result = jnp.einsum(
        "rbk,ck->rbc",
        windows,
        matrix,
        precision=lax.Precision.HIGHEST,
        preferred_element_type=jnp.float32,
    )
    return result.reshape(count_rows, count_cols)


def combine_slots(received):
    pieces, covers = received
    totals = jnp.sum(pieces, axis=0, dtype=jnp.float32)
    weights = jnp.sum(covers, axis=0, dtype=jnp.float32)
    return totals / jnp.maximum(weights, 1.0)[:, None, :]


def per_device(images, psf_coef, phases, col_shift, band_offset, exposure_weight, patch_site):
    exposure = images[0]
    count_rows, count_cols = exposure.shape
    half_cols = count_cols // 2
    segment_count = lax.axis_size("seg")
    owner_count = lax.axis_size("exp")
    quarter = BAND_ROWS // segment_count
    kernel_reach = TAPS // 2
    basis_rows = basis_table()
    kernel_rows = jnp.sum(psf_coef[0, 0][:, None] * basis_rows, axis=0)
    kernel_cols = jnp.sum(psf_coef[0, 1][:, None] * basis_rows, axis=0)
    shift_rows = lanczos_weights(phases[0, 0])
    shift_cols = lanczos_weights(phases[0, 1])
    offset_cols = col_shift[0]
    kernel_matrix = band_matrix(kernel_cols, block_cols, 3 * block_cols, block_cols - kernel_reach)
    lanczos_matrix = band_matrix(
        shift_cols, block_cols, 3 * block_cols, block_cols - 2 - offset_cols
    )
    across = across_columns(across_columns(exposure, kernel_matrix), lanczos_matrix)
    extended = extended_2(across, (("seg", 0),), kernel_reach)
    inner = band_matrix(kernel_rows, count_rows, count_rows + 2 * kernel_reach, 0)
    matched = jnp.dot(
        inner, extended, precision=lax.Precision.HIGHEST, preferred_element_type=jnp.float32
    )
    widened = extended_2(matched, (("seg", 0),), 3)
    outer = band_matrix(shift_rows, count_rows, count_rows + 6, 1)
    warped = jnp.dot(
        outer, widened, precision=lax.Precision.HIGHEST, preferred_element_type=jnp.float32
    )
    scale_weight = exposure_weight[0]
    sent_rows = (scale_weight.astype(jnp.float32) * warped).astype(jnp.bfloat16)
    columns = jnp.arange(count_cols, dtype=jnp.int32)
    inside_cols = (columns - offset_cols >= 0) & (columns - offset_cols < count_cols)
    coverage = jnp.where(inside_cols, scale_weight, jnp.zeros((), jnp.bfloat16)).reshape(
        2, half_cols
    )
    site_band = patch_site // 2
    site_half = patch_site % 2
    patch_count = patch_site.shape[0]
    own_slots = patch_count // owner_count
    bands_here = count_rows // BAND_ROWS
    nothing = jnp.zeros((), jnp.bfloat16)
    chosen_cover = jnp.where(site_half[:, None] == 1, coverage[1][None, :], coverage[0][None, :])
    band_grid = sent_rows.reshape(bands_here, segment_count, quarter, count_cols)
    swapped = lax.all_to_all(band_grid, "seg", split_axis=1, concat_axis=1, tiled=True)
    swapped = swapped.reshape(bands_here, segment_count, quarter, 2, half_cols)
    relative = site_band - band_offset[0]
    present = (relative >= 0) & (relative < segment_count * bands_here)
    safe_band = jnp.clip(relative, 0, segment_count * bands_here - 1)
    pieces = swapped[safe_band % bands_here, safe_band // bands_here, :, site_half, :]
    pieces = jnp.where(present[:, None, None], pieces, nothing)
    pieces = pieces.reshape(owner_count, own_slots, quarter, half_cols)
    covers = jnp.where(present[:, None], chosen_cover, nothing)
    covers = covers.reshape(owner_count, own_slots, half_cols)
    coadded = combine_slots(
        (
            lax.all_to_all(pieces, "exp", split_axis=0, concat_axis=0, tiled=True),
            lax.all_to_all(covers, "exp", split_axis=0, concat_axis=0, tiled=True),
        )
    )
    return coadded


def solution(mesh):
    placed = (
        P("exp", "seg", None),
        P("exp", None, None),
        P("exp", None),
        P("exp"),
        P("exp"),
        P("exp"),
        P(),
    )
    return jax.shard_map(
        per_device, mesh=mesh, in_specs=placed, out_specs=P("exp", "seg", None), check_vma=False
    )
```

profile of v0, /device:TPU:0, one launch (start us, length us, event | category | flops | bytes accessed | tf_op | source)
XLA Modules:
  0.0 501.6 jit_solution(3490975994644793937)
XLA Ops:
  0.6 0.6 exponential_reduce_fusion.1
  1.2 0.7 exponential_reduce_fusion.2
  1.9 9.0 %copy.76 = f32[1,512,4096]{1,2,0:T(8,128)} copy(f32[1,512,4096]{2,1,0:T(8,128)} %param.8) | data formatting | bytes 16777216 | tf_op args[0]
  10.9 7.9 %pad.7 = f32[512,4352]{0,1:T(8,128)} pad(f32[512,4096]{0,1:T(8,128)} %bitcast.90, f32[]{:T(128)} %constant.66.clone.1), padding=0_0x128_128 | pad | bytes 17301508 | tf_op jit(solution)/shard_map/jit(_pad)/pad | solution.py:59
  18.8 17.9 %fusion.454 = (f32[512,32,128]{0,2,1:T(8,128)}, f32[512,32,128]{0,2,1:T(8,128)}, f32[512,32,128]{0,2,1:T(8,128)}) fusion(f32[512,34,128]{0,2,1:T(8,128)} %bitcast.88), kind=kLoop, calls=%fused_computation.478 | loop fusion | bytes 50331648 | tf_op jit(solution)/shard_map/slice | solution.py:61
  36.7 9.0 %copy.92 = f32[512,32,128]{2,0,1:T(8,128)} copy(f32[512,32,128]{0,2,1:T(8,128)} %get-tuple-element.17) | data formatting | bytes 16777216
  45.7 9.0 %copy.91 = f32[512,32,128]{2,0,1:T(8,128)} copy(f32[512,32,128]{0,2,1:T(8,128)} %get-tuple-element.16) | data formatting | bytes 16777216
  54.7 9.0 %copy.90 = f32[512,32,128]{2,0,1:T(8,128)} copy(f32[512,32,128]{0,2,1:T(8,128)} %get-tuple-element.15) | data formatting | bytes 16777216
  63.6 0.7 exponential_divide_fusion
  64.9 0.6 exponential_divide_fusion.2
  65.7 0.7 fusion.463
  66.4 0.6 fusion.461
  67.0 42.8 %fusion = f32[512,32,128]{0,2,1:T(8,128)S(1)} fusion(f32[512,32,128]{2,0,1:T(8,128)} %copy.92, f32[512,32,128]{2,0,1:T(8,128)} %copy.91, f32[512,32,128]{2,0,1:T(8,128)} %copy.90, f32[]{:T(128)} %bitcast.54, f32[]{:T(128)} %bitcast.53, f32[]{:T(128)} %bitcast.52, f32[]{:T(128)} %bitcast.51, f32[]{:T(128)} %bitcast.50, f32[]{:T(128)} %bitcast.49, ...), kind=kOutput, calls=%fused_computation.1 | convolution fusion | flops 9679405056 | bytes 33554516 | tf_op jit(solution)/shard_map/rbk,ck->rbc/dot_general | solution.py:62
  109.9 4.5 pad.8
  114.3 18.1 %fusion.453 = (f32[512,32,128]{0,2,1:T(8,128)}, f32[512,32,128]{0,2,1:T(8,128)}, f32[512,32,128]{0,2,1:T(8,128)}) fusion(f32[512,34,128]{0,2,1:T(8,128)} %bitcast.89), kind=kLoop, calls=%fused_computation.477 | loop fusion | bytes 50331648 | tf_op jit(solution)/shard_map/slice | solution.py:61
  132.4 9.0 %copy.95 = f32[512,32,128]{2,0,1:T(8,128)} copy(f32[512,32,128]{0,2,1:T(8,128)} %get-tuple-element.14) | data formatting | bytes 16777216
  141.4 9.0 %copy.94 = f32[512,32,128]{2,0,1:T(8,128)} copy(f32[512,32,128]{0,2,1:T(8,128)} %get-tuple-element.13) | data formatting | bytes 16777216
  150.4 9.0 %copy.93 = f32[512,32,128]{2,0,1:T(8,128)} copy(f32[512,32,128]{0,2,1:T(8,128)} %get-tuple-element.12) | data formatting | bytes 16777216
  160.5 0.7 fusion.386
  161.2 0.7 broadcast_divide_fusion.1
  161.9 0.7 fusion.462
  163.2 30.3 %fusion.6 = f32[512,32,128]{2,0,1:T(8,128)S(1)} fusion(f32[512,32,128]{2,0,1:T(8,128)} %copy.95, f32[512,32,128]{2,0,1:T(8,128)} %copy.94, f32[512,32,128]{2,0,1:T(8,128)} %copy.93, f32[]{:T(128)} %bitcast.65, f32[]{:T(128)} %bitcast.64, f32[]{:T(128)} %bitcast.63, f32[]{:T(128)} %bitcast.62, f32[]{:T(128)} %bitcast.61, f32[]{:T(128)} %bitcast.60, s32[]{:T(128)S(6)} %sub.242), kind=kOutput, calls=%fused_computation.7 | convolution fusion | flops 9677193216 | bytes 33554460 | tf_op jit(solution)/shard_map/rbk,ck->rbc/dot_general | solution.py:62
  193.6 3.2 copy-done
  197.1 1.3 collective-permute-start.1
  198.6 5.5 %collective-permute-start = (f32[10,4096]{1,0:T(8,128)S(1)}, f32[10,4096]{1,0:T(8,128)S(1)}, u32[]{:S(2)}, u32[]{:S(2)}) collective-permute-start(f32[10,4096]{1,0:T(8,128)S(1)} %bitcast.98), channel_id=1, source_target_pairs={{0,8},{8,16},{16,24},{1,9},{9,17},{17,25},{2,10},{10,18},{18,26},{... | collective-permute-start | bytes 491528 | tf_op jit(solution)/shard_map/ppermute | solution.py:20
  204.8 0.7 fusion.387
  205.5 0.7 broadcast_divide_fusion.2
  206.1 9.3 %copy.84 = f32[512,32,128]{0,2,1:T(8,128)} copy(f32[512,32,128]{2,0,1:T(8,128)} %copy-done) | data formatting | bytes 16777216 | tf_op jit(solution)/shard_map/rbk,ck->rbc/dot_general | solution.py:62
  215.4 0.7 fusion.460
  216.1 0.6 copy.87
  216.8 2.0 copy.86
  218.8 38.6 %fusion.12 = f32[512,4096]{1,0:T(8,128)S(1)} fusion(f32[10,4096]{0,1:T(8,128)S(1)} %copy.87, f32[512,4096]{0,1:T(8,128)} %bitcast.93, f32[10,4096]{0,1:T(8,128)} %copy.86, f32[]{:T(128)} %bitcast.30, f32[]{:T(128)} %bitcast.29, f32[]{:T(128)} %bitcast.28, f32[]{:T(128)} %bitcast.27, f32[]{:T(128)} %bitcast.26, f32[]{:T(128)} %bitcast.25, f32[]{:T(128)} %bitcast.24, ...), kind=kOutput, calls=%fused_computation.13 | convolution fusion | flops 13409736704 | bytes 17104980 | tf_op jit(solution)/shard_map/dot_general | solution.py:100
  257.4 1.3 collective-permute-start.3
  258.7 5.4 %collective-permute-start.2 = (f32[3,4096]{1,0:T(4,128)S(1)}, f32[3,4096]{1,0:T(4,128)S(1)}, u32[]{:S(2)}, u32[]{:S(2)}) collective-permute-start(f32[3,4096]{1,0:T(4,128)S(1)} %get-tuple-element.18), channel_id=1, source_target_pairs={{0,8},{8,16},{16,24},{1,9},{9,17},{17,25},{2,10},{10,18},{18,26},{... | collective-permute-start | bytes 147464 | tf_op jit(solution)/shard_map/ppermute | solution.py:20
  264.2 0.7 fusion.458
  266.0 26.2 %multiply_convert_fusion = bf16[512,4096]{1,0:T(8,128)(2,1)S(1)} fusion(f32[3,4096]{1,0:T(4,128)S(1)} %collective-permute-done.3, f32[512,4096]{1,0:T(8,128)} %copy-done.1, f32[3,4096]{1,0:T(4,128)S(1)} %collective-permute-done.2, f32[]{:T(128)S(6)} %convert_element_type.60, f32[]{:T(128)} %bitcast.8, f32[]{:T(128)} %bitcast.7, f32[]{:T(128)} %bitcast.6, ...), kind=kOutput, calls=%fused_computation.26 | convolution fusion | flops 13049373696 | bytes 12681244 | tf_op jit(solution)/shard_map/dot_general | solution.py:105
  292.3 2.2 copy.88
  294.5 6.4 %all-to-all-start = ((bf16[16,4,8,4096]{3,2,0,1:T(8,128)(2,1)}), bf16[16,4,8,4096]{3,2,0,1:T(8,128)(2,1)}, u32[]{:S(2)}, u32[]{:S(2)}) async-start(bf16[16,4,8,4096]{3,2,0,1:T(8,128)(2,1)} %copy.88), calls=%async_computation | async-start | bytes 8388608 | tf_op jit(solution)/shard_map/all_to_all | solution.py:123
  301.8 1.0 select_select_fusion
  302.8 44.9 %all-to-all-done = bf16[16,4,8,4096]{3,2,0,1:T(8,128)(2,1)} async-done(((bf16[16,4,8,4096]{3,2,0,1:T(8,128)(2,1)}), bf16[16,4,8,4096]{3,2,0,1:T(8,128)(2,1)}, u32[]{:S(2)}, u32[]{:S(2)}) %all-to-all-start) | async-done | bytes 4194336 | tf_op jit(solution)/shard_map/all_to_all | solution.py:123
  347.7 4.9 all-to-all-start.2
  352.6 16.7 %gather_fusion = bf16[160,8,2048]{2,1,0:T(8,128)(2,1)} fusion(bf16[16,4,8,2,2048]{4,2,3,0,1:T(8,128)(2,1)} %bitcast.69, s32[160]{0:T(256)S(1)} %fusion.364), kind=kCustom, calls=%fused_computation | custom fusion | bytes 10487680 | tf_op jit(solution)/shard_map/gather | solution.py:128
  369.3 5.3 %broadcast_select_fusion = bf16[8,20,8,2048]{3,2,1,0:T(8,128)(2,1)} fusion(bf16[8,20,8,2048]{3,2,1,0:T(8,128)(2,1)} %bitcast.91, pred[8,20]{1,0:T(8,128)(4,1)S(1)} %broadcast_in_dim.304), kind=kLoop, calls=%fused_computation.27 | loop fusion | flops 2621440 | bytes 10485920 | tf_op jit(solution)/shard_map/jit(_where)/select_n | solution.py:129
  374.5 5.2 %all-to-all-start.1 = ((bf16[8,20,8,2048]{3,2,1,0:T(8,128)(2,1)}), bf16[8,20,8,2048]{3,2,1,0:T(8,128)(2,1)}, u32[]{:S(2)}, u32[]{:S(2)}) async-start(bf16[8,20,8,2048]{3,2,1,0:T(8,128)(2,1)} %broadcast_select_fusion), calls=%async_computation.1 | async-start | bytes 10485760 | tf_op jit(solution)/shard_map/all_to_all | solution.py:135
  379.7 0.7 convert_reduce_fusion.1
  380.5 115.8 %all-to-all-done.1 = bf16[8,20,8,2048]{3,2,1,0:T(8,128)(2,1)} async-done(((bf16[8,20,8,2048]{3,2,1,0:T(8,128)(2,1)}), bf16[8,20,8,2048]{3,2,1,0:T(8,128)(2,1)}, u32[]{:S(2)}, u32[]{:S(2)}) %all-to-all-start.1) | async-done | bytes 5242912 | tf_op jit(solution)/shard_map/all_to_all | solution.py:135
  496.3 3.6 convert_reduce_fusion
  499.9 1.2 broadcast_divide_fusion
  (34 shorter events, 3.3 us)
Async XLA Ops:
  54.7 10.9 %copy-start.3 = (f32[1,2,3]{2,1,0:T(2,128)S(1)}, f32[1,2,3]{2,1,0:T(2,128)}, u32[]{:S(2)}) copy-start(f32[1,2,3]{2,1,0:T(2,128)} %param.9) | copy-start | bytes 76
  150.4 9.0 %copy-start.2 = (s32[1,2]{1,0:T(1,128)S(1)}, s32[1,2]{1,0:T(1,128)}, u32[]{:S(2)}) copy-start(s32[1,2]{1,0:T(1,128)} %param.10) | copy-start | bytes 28
  193.6 3.2 copy-start
  197.1 19.0 %collective-permute-start.1 = (f32[10,4096]{1,0:T(8,128)S(1)}, f32[10,4096]{1,0:T(8,128)S(1)}, u32[]{:S(2)}, u32[]{:S(2)}) collective-permute-start(f32[10,4096]{1,0:T(8,128)S(1)} %bitcast.97), channel_id=1, source_target_pairs={{8,0},{16,8},{24,16},{9,1},{17,9},{25,17},{10,2},{18,10},{26,18},{... | collective-permute-start | bytes 491528 | tf_op jit(solution)/shard_map/ppermute | solution.py:23
  198.6 18.1 %collective-permute-start = (f32[10,4096]{1,0:T(8,128)S(1)}, f32[10,4096]{1,0:T(8,128)S(1)}, u32[]{:S(2)}, u32[]{:S(2)}) collective-permute-start(f32[10,4096]{1,0:T(8,128)S(1)} %bitcast.98), channel_id=1, source_target_pairs={{0,8},{8,16},{16,24},{1,9},{9,17},{17,25},{2,10},{10,18},{18,26},{... | collective-permute-start | bytes 491528 | tf_op jit(solution)/shard_map/ppermute | solution.py:20
  257.4 7.4 %copy-start.1 = (f32[512,4096]{1,0:T(8,128)}, f32[512,4096]{1,0:T(8,128)S(1)}, u32[]{:S(2)}) copy-start(f32[512,4096]{1,0:T(8,128)S(1)} %fusion.12) | copy-start | bytes 25165828
  257.4 8.1 %collective-permute-start.3 = (f32[3,4096]{1,0:T(4,128)S(1)}, f32[3,4096]{1,0:T(4,128)S(1)}, u32[]{:S(2)}, u32[]{:S(2)}) collective-permute-start(f32[3,4096]{1,0:T(4,128)S(1)} %get-tuple-element.19), channel_id=1, source_target_pairs={{8,0},{16,8},{24,16},{9,1},{17,9},{25,17},{10,2},{18,10},{26,18},{... | collective-permute-start | bytes 147464 | tf_op jit(solution)/shard_map/ppermute | solution.py:23
  258.7 7.3 %collective-permute-start.2 = (f32[3,4096]{1,0:T(4,128)S(1)}, f32[3,4096]{1,0:T(4,128)S(1)}, u32[]{:S(2)}, u32[]{:S(2)}) collective-permute-start(f32[3,4096]{1,0:T(4,128)S(1)} %get-tuple-element.18), channel_id=1, source_target_pairs={{0,8},{8,16},{16,24},{1,9},{9,17},{17,25},{2,10},{10,18},{18,26},{... | collective-permute-start | bytes 147464 | tf_op jit(solution)/shard_map/ppermute | solution.py:20
  294.5 7.0 %copy-start.4 = (s32[160]{0:T(256)S(1)}, s32[160]{0:T(256)}, u32[]{:S(2)}) copy-start(s32[160]{0:T(256)} %param.14) | copy-start | bytes 1924
  294.5 53.2 %all-to-all-start = ((bf16[16,4,8,4096]{3,2,0,1:T(8,128)(2,1)}), bf16[16,4,8,4096]{3,2,0,1:T(8,128)(2,1)}, u32[]{:S(2)}, u32[]{:S(2)}) async-start(bf16[16,4,8,4096]{3,2,0,1:T(8,128)(2,1)} %copy.88), calls=%async_computation | async-start | bytes 8388608 | tf_op jit(solution)/shard_map/all_to_all | solution.py:123
  347.7 26.8 %all-to-all-start.2 = ((bf16[8,20,2048]{2,1,0:T(8,128)(2,1)}), bf16[8,20,2048]{2,1,0:T(8,128)(2,1)S(1)}, u32[]{:S(2)}, u32[]{:S(2)}) async-start(bf16[8,20,2048]{2,1,0:T(8,128)(2,1)} %select_select_fusion), calls=%async_computation.2 | async-start | bytes 1572864 | tf_op jit(solution)/shard_map/all_to_all | solution.py:136
  374.5 121.8 %all-to-all-start.1 = ((bf16[8,20,8,2048]{3,2,1,0:T(8,128)(2,1)}), bf16[8,20,8,2048]{3,2,1,0:T(8,128)(2,1)}, u32[]{:S(2)}, u32[]{:S(2)}) async-start(bf16[8,20,8,2048]{3,2,1,0:T(8,128)(2,1)} %broadcast_select_fusion), calls=%async_computation.1 | async-start | bytes 10485760 | tf_op jit(solution)/shard_map/all_to_all | solution.py:135
where the time goes:
time: 512 us; the launch traced here: 502 us
  waiting for transfers between devices  161 us (31%)
  local copies, waits for them, and re-layouts  150 us (29%)
  matrix products  138 us (27%)
  starting transfers between devices  29.9 us (6%)
  other arithmetic  18.6 us (4%)
    all_to_all x1, waiting for transfers between devices, per_device(): lax.all_to_all(pieces, 'exp', split_axis=0, concat_axis=0, tiled=True)  116 us
    dot_general x2, matrix products, across_columns(): jnp.einsum('rbk,ck->rbc', windows, matrix, precision=lax.Precision.HIGHES...  73.1 us
    unnamed x21, local copies, waits for them, and re-layouts  66.4 us
    all_to_all x1, waiting for transfers between devices, per_device(): lax.all_to_all(band_grid, 'seg', split_axis=1, concat_axis=1, tiled=True)  44.9 us
    dot_general x1, matrix products, per_device(): jnp.dot(inner, extended, precision=lax.Precision.HIGHEST, preferred_eleme...  38.6 us
    slice x2, local copies, waits for them, and re-layouts, across_columns(): padded[:, :-2]  36 us
    dot_general x1, matrix products, per_device(): jnp.dot(outer, widened, precision=lax.Precision.HIGHEST, preferred_elemen...  26.2 us
    gather x1, local copies, waits for them, and re-layouts, per_device(): swapped[safe_band % bands_here, safe_band // bands_here, :, site_half, :]  16.7 us
  transfers between devices with their start and end apart: 7, of which 3 were waited for; matrix products, arithmetic and copies ran while one was open for 7% of the time, Pallas kernels for 0%

commit v1 on v0

v1 whole, which is shorter than its diff:
```python
import functools

import jax
import jax.numpy as jnp
import numpy as np
from jax import lax
from jax.experimental import pallas as pl
from jax.experimental.pallas import tpu as pltpu
from jax.sharding import Mesh, PartitionSpec as P

BAND_ROWS = 32
TAPS = 21
PHASES = 16
LANCZOS = 6
SPAN = TAPS + LANCZOS - 1
LEAD = TAPS // 2 + 2
HALO = 16
SIDE = 128
TILE = 256
STRIP = 128
CHUNKS = 2
VMEM = 48 * 1024 * 1024

sigmas = (1.0, 2.0, 3.5)


def basis_table():
    offsets = np.arange(TAPS) - TAPS // 2
    curves = [np.exp(-offsets * offsets / (2.0 * spread * spread)) for spread in sigmas]
    return [[float(value) for value in curve / curve.sum()] for curve in curves]


def lanczos_table():
    shifted = np.arange(LANCZOS)[None, :] - 2.0 - np.arange(PHASES)[:, None] / PHASES
    values = np.sinc(shifted) * np.sinc(shifted / 3.0)
    return (values / values.sum(axis=1, keepdims=True)).astype(np.float32)


def split(value):
    high = value.astype(jnp.bfloat16)
    return high, (value - high.astype(jnp.float32)).astype(jnp.bfloat16)


def banded(taps, masks, distance):
    matrix = jnp.zeros(distance.shape, jnp.float32)
    kernel, lanczos = taps
    weighted = [jnp.where(mask, lanczos[n], 0.0) for n, mask in enumerate(masks)]
    for t in range(SPAN):
        row = jnp.zeros_like(weighted[0])
        for n in range(LANCZOS):
            if 0 <= t - n < TAPS:
                row = row + kernel[t - n] * weighted[n]
        matrix = matrix + jnp.where(distance == t, row, 0.0)
    return matrix


def matrices_kernel(place, coef, phases, shift, table, rows_out, cols_out, *, rows, width, segments):
    basis = basis_table()

    def taps_of(axis):
        kernel = [sum(coef[axis, k] * basis[k][t] for k in range(len(sigmas))) for t in range(TAPS)]
        return kernel, [table[phases[axis], n] for n in range(LANCZOS)]

    taps = taps_of(1)
    offset = shift[0]
    zero = jnp.zeros((SIDE, SIDE), jnp.bfloat16)
    for variant, first in enumerate((0, None, width - TILE)):
        for part in range(2):
            for block in range(4):
                if not part <= block <= part + 2:
                    for term in range(2):
                        cols_out[variant, term, pl.ds(block * SIDE, SIDE), pl.ds(part * SIDE, SIDE)] = zero
                    continue
                output = part * SIDE + lax.broadcasted_iota(jnp.int32, (1, SIDE), 1)
                if first is None:
                    masks = [jnp.full((1, SIDE), True)] * LANCZOS
                else:
                    matched = first + output - offset
                    masks = [
                        (matched + (n - 2) >= 0) & (matched + (n - 2) < width) for n in range(LANCZOS)
                    ]
                distance = (
                    lax.broadcasted_iota(jnp.int32, (SIDE, SIDE), 0)
                    - lax.broadcasted_iota(jnp.int32, (SIDE, SIDE), 1)
                    + (offset + LEAD - SIDE + (block - part) * SIDE)
                )
                high, low = split(banded(taps, masks, distance))
                cols_out[variant, 0, pl.ds(block * SIDE, SIDE), pl.ds(part * SIDE, SIDE)] = high
                cols_out[variant, 1, pl.ds(block * SIDE, SIDE), pl.ds(part * SIDE, SIDE)] = low

    taps = taps_of(0)
    span = STRIP + 2 * HALO
    quarter = BAND_ROWS // segments
    bands = STRIP // BAND_ROWS
    order = lax.broadcasted_iota(jnp.int32, (1, STRIP), 1)
    within = lax.rem(order, bands * quarter)
    output = (
        lax.div(within, quarter) * BAND_ROWS + lax.div(order, bands * quarter) * quarter + lax.rem(within, quarter)
    )
    depth = cols_pad(3 * span)
    stacked = lax.broadcasted_iota(jnp.int32, (depth, STRIP), 0)
    term = jnp.where(stacked >= 2 * span, 2, jnp.where(stacked >= span, 1, 0))
    distance = stacked - term * span - output + (LEAD - HALO)
    for variant, first in enumerate((0, STRIP, rows - STRIP)):
        matched = place[0] * rows + first + output
        masks = [
            (matched + (n - 2) >= 0) & (matched + (n - 2) < rows * segments) for n in range(LANCZOS)
        ]
        matrix = banded(taps, masks, distance).T
        high, low = split(matrix)
        column = lax.broadcasted_iota(jnp.int32, matrix.shape, 1)
        both = jnp.where(column >= 2 * span, low.astype(jnp.float32), high.astype(jnp.float32))
        rows_out[variant] = both.astype(jnp.bfloat16)[:, : 3 * span]


def cols_pad(count):
    return -(-count // 128) * 128


def build_matrices(place, coef, phases, shift, rows, width, segments):
    span = 3 * (STRIP + 2 * HALO)
    smem = pl.BlockSpec(memory_space=pltpu.SMEM)
    vmem = pl.BlockSpec(memory_space=pltpu.VMEM)
    return pl.pallas_call(
        functools.partial(matrices_kernel, rows=rows, width=width, segments=segments),
        out_shape=(
            jax.ShapeDtypeStruct((3, STRIP, span), jnp.bfloat16),
            jax.ShapeDtypeStruct((3, 2, TILE + 2 * SIDE, TILE), jnp.bfloat16),
        ),
        in_specs=[smem] * 5,
        out_specs=(vmem, vmem),
        compiler_params=pltpu.CompilerParams(vmem_limit_bytes=VMEM),
        cost_estimate=pl.CostEstimate(flops=4_000_000, bytes_accessed=4_000_000, transcendentals=0),
        name="band_matrices",
    )(place, coef, phases, shift, jnp.asarray(lanczos_table()))


def filter_kernel(
    weight, low_l, low_c, low_r, mid_l, mid_c, mid_r, high_l, high_c, high_r, rows_m, cols_m, out,
    ext_high, ext_low, mat_high, mat_low, *, first_chunk, last_chunk, segments,
):
    half = pl.program_id(0)
    halves = pl.num_programs(0)
    rows, chunk = mid_c.shape
    at_left = first_chunk & (half == 0)
    at_right = last_chunk & (half == halves - 1)
    span = STRIP + 2 * HALO

    for row, parts in (
        (0, (low_l, low_c, low_r)),
        (HALO, (mid_l, mid_c, mid_r)),
        (HALO + rows, (high_l, high_c, high_r)),
    ):
        count = parts[0].shape[0]
        for part, column, outside in zip(parts, (0, SIDE, SIDE + chunk), (at_left, False, at_right)):
            value = part[...]
            if outside is not False:
                value = jnp.where(outside, 0.0, value)
            high, low = split(value)
            place = (pl.ds(row, count), pl.ds(column, value.shape[1]))
            ext_high[place] = high
            ext_low[place] = low

    strips = rows // STRIP
    quarters = rows // segments
    piece = STRIP // segments
    for tile in range((chunk + 2 * SIDE) // TILE):
        columns = pl.ds(tile * TILE, TILE)
        for strip in range(strips):
            window = pl.ds(strip * STRIP, span)
            variant = 0 if strip == 0 else (2 if strip == strips - 1 else 1)
            high = ext_high[window, columns]
            stack = jnp.concatenate([high, ext_low[window, columns], high], axis=0)
            matched = jnp.dot(rows_m[variant], stack, preferred_element_type=jnp.float32)
            high, low = split(matched)
            for quarter in range(segments):
                target = (pl.ds(quarter * quarters + strip * piece, piece), columns)
                mat_high[target] = high[quarter * piece : (quarter + 1) * piece]
                mat_low[target] = low[quarter * piece : (quarter + 1) * piece]

    tiles = chunk // TILE
    for tile in range(tiles):
        variant = jnp.int32(1)
        if tile == 0:
            variant = jnp.where(at_left, 0, variant)
        if tile == tiles - 1:
            variant = jnp.where(at_right, 2, variant)
        taps_high = cols_m[variant, 0]
        taps_low = cols_m[variant, 1]
        window = pl.ds(tile * TILE, TILE + 2 * SIDE)
        for strip in range(strips):
            place = pl.ds(strip * STRIP, STRIP)
            high = mat_high[place, window]
            warped = jnp.dot(high, taps_high, preferred_element_type=jnp.float32)
            warped += jnp.dot(mat_low[place, window], taps_high, preferred_element_type=jnp.float32)
            warped += jnp.dot(high, taps_low, preferred_element_type=jnp.float32)
            out[place, pl.ds(tile * TILE, TILE)] = (weight[0] * warped).astype(jnp.bfloat16)


def filter_chunk(weight, low, image, high, rows_m, cols_m, index, chunk, segments):
    rows, width = image.shape
    halves = 2
    half_blocks = width // halves // SIDE
    start = index * chunk // SIDE
    blocks = chunk // SIDE
    last = width // SIDE - 1

    def left(h):
        return 0, jnp.maximum(h * half_blocks + start - 1, 0)

    def centre(h):
        return 0, h * (half_blocks // blocks) + index

    def right(h):
        return 0, jnp.minimum(h * half_blocks + start + blocks, last)

    def whole(array):
        return pl.BlockSpec(array.shape, lambda h: (0,) * array.ndim)

    specs = [pl.BlockSpec(memory_space=pltpu.SMEM)]
    for source in (low, image, high):
        specs += [
            pl.BlockSpec((source.shape[0], SIDE), left),
            pl.BlockSpec((source.shape[0], chunk), centre),
            pl.BlockSpec((source.shape[0], SIDE), right),
        ]
    wide = chunk + 2 * SIDE
    return pl.pallas_call(
        functools.partial(
            filter_kernel,
            first_chunk=index == 0,
            last_chunk=(index + 1) * chunk == width // halves,
            segments=segments,
        ),
        out_shape=jax.ShapeDtypeStruct((rows, halves * chunk), jnp.bfloat16),
        grid=(halves,),
        in_specs=specs + [whole(rows_m), whole(cols_m)],
        out_specs=pl.BlockSpec((rows, chunk), lambda h: (0, h)),
        scratch_shapes=[
            pltpu.VMEM((rows + 2 * HALO, wide), jnp.bfloat16),
            pltpu.VMEM((rows + 2 * HALO, wide), jnp.bfloat16),
            pltpu.VMEM((rows, wide), jnp.bfloat16),
            pltpu.VMEM((rows, wide), jnp.bfloat16),
        ],
        compiler_params=pltpu.CompilerParams(vmem_limit_bytes=VMEM),
        cost_estimate=pl.CostEstimate(
            flops=halves * 2 * rows * chunk * 2048, bytes_accessed=halves * rows * chunk * 6, transcendentals=0
        ),
        name="warp_filter",
    )(weight, *([low] * 3), *([image] * 3), *([high] * 3), rows_m, cols_m)


def pair_kernel(info, sites, mine, other, out, *, quarter):
    chunk = out.shape[1]
    rows_two = 2 * quarter
    bands = mine.shape[0] // quarter

    def rows_of(source, offset, site):
        relative = lax.shift_right_logical(site, 1) - offset
        present = (relative >= 0) & (relative < bands)
        safe = jnp.clip(relative, 0, bands - 1)
        tile = source[
            pl.ds(pl.multiple_of(lax.shift_right_logical(safe, 1) * rows_two, rows_two), rows_two),
            pl.ds(pl.multiple_of((site & 1) * chunk, 128), chunk),
        ].astype(jnp.float32)
        rows = jnp.where((safe & 1) == 1, tile[quarter:], tile[:quarter])
        return jnp.where(present, rows, 0.0)

    def two_slots(step, carry):
        parts = []
        for slot in range(2):
            site = sites[step * 2 + slot]
            parts.append(rows_of(mine, info[0], site) + rows_of(other, info[1], site))
        out[pl.ds(pl.multiple_of(step * rows_two, rows_two), rows_two), :] = jnp.concatenate(parts, axis=0).astype(jnp.bfloat16)
        return carry

    lax.fori_loop(0, out.shape[0] // rows_two, two_slots, 0)


def pair_sum(info, sites, mine, other, slots, quarter):
    rows, double = mine.shape
    chunk = double // 2
    smem = pl.BlockSpec(memory_space=pltpu.SMEM)
    vmem = pl.BlockSpec(memory_space=pltpu.VMEM)
    return pl.pallas_call(
        functools.partial(pair_kernel, quarter=quarter),
        out_shape=jax.ShapeDtypeStruct((slots * quarter, chunk), jnp.bfloat16),
        in_specs=[smem, smem, vmem, vmem],
        out_specs=vmem,
        compiler_params=pltpu.CompilerParams(vmem_limit_bytes=VMEM),
        cost_estimate=pl.CostEstimate(
            flops=8 * slots * quarter * chunk,
            bytes_accessed=4 * rows * double + 2 * slots * quarter * chunk,
            transcendentals=0,
        ),
        name="pair_sum",
    )(info, sites, mine, other)


def finish_kernel(pieces, scale, *rest):
    out = rest[-1]
    total = pieces[0].astype(jnp.float32)
    for index in range(1, pieces.shape[0]):
        total += pieces[index].astype(jnp.float32)
    out[...] = total / scale[...]


def finish_chunk(pieces, scale, result, index):
    count, rows, chunk = pieces.shape
    column = pl.BlockSpec((rows, chunk), lambda i: (0, index))
    specs = [pl.BlockSpec(pieces.shape, lambda i: (0, 0, 0)), column]
    operands = [pieces, scale]
    aliases = {}
    if result is not None:
        specs.append(pl.BlockSpec(memory_space=pl.ANY))
        operands.append(result)
        aliases = {2: 0}
    return pl.pallas_call(
        finish_kernel,
        out_shape=jax.ShapeDtypeStruct(scale.shape, jnp.float32),
        grid=(1,),
        in_specs=specs,
        out_specs=column,
        input_output_aliases=aliases,
        compiler_params=pltpu.CompilerParams(vmem_limit_bytes=VMEM),
        cost_estimate=pl.CostEstimate(
            flops=count * rows * chunk, bytes_accessed=rows * chunk * (2 * count + 8), transcendentals=0
        ),
        name="patch_mean",
    )(*operands)


def per_device(images, psf_coef, phases, col_shift, band_offset, exposure_weight, patch_site):
    image = images[0]
    rows, width = image.shape
    segments = lax.axis_size("seg")
    lines = lax.axis_size("line")
    cores = lax.axis_size("core")
    quarter = BAND_ROWS // segments
    half_cols = width // 2
    chunk = half_cols // CHUNKS
    patches = patch_site.shape[0]
    own_slots = patches // (lines * cores)
    core = lax.axis_index("core")
    line = lax.axis_index("line")

    forward = [(i, i + 1) for i in range(segments - 1)]
    backward = [(i + 1, i) for i in range(segments - 1)]
    low = lax.ppermute(image[rows - HALO :], "seg", forward)
    high = lax.ppermute(image[:HALO], "seg", backward)
    weight = exposure_weight.astype(jnp.float32)
    facts = jnp.stack([col_shift[0].astype(jnp.float32), band_offset[0].astype(jnp.float32), weight[0]])
    facts = lax.all_gather(facts, ("line", "core"), axis=0, tiled=False)

    place = lax.axis_index("seg").astype(jnp.int32).reshape(1)
    rows_m, cols_m = build_matrices(place, psf_coef[0], phases[0], col_shift, rows, width, segments)

    sites = patch_site.reshape(lines, cores, own_slots)
    own_sites = lax.dynamic_index_in_dim(
        lax.dynamic_index_in_dim(sites, line, 0, keepdims=False), core, 0, keepdims=False
    )
    bands = segments * rows // BAND_ROWS
    site = jnp.repeat(own_sites, quarter)[:, None]
    column = (site % 2) * half_cols + jnp.arange(half_cols, dtype=jnp.int32)[None, :]
    total = jnp.zeros((own_slots * quarter, half_cols), jnp.float32)
    for exposure in range(lines * cores):
        moved = column - facts[exposure, 0].astype(jnp.int32)
        relative = site // 2 - facts[exposure, 1].astype(jnp.int32)
        inside = (moved >= 0) & (moved < width) & (relative >= 0) & (relative < bands)
        total = total + jnp.where(inside, facts[exposure, 2], 0.0)
    scale = jnp.maximum(total, 1.0)

    offsets = facts[:, 1].astype(jnp.int32).reshape(lines, cores)
    pair = lax.dynamic_index_in_dim(offsets, line, 0, keepdims=False)
    info = jnp.stack([pair[core], pair[1 - core]])
    pair_sites = lax.dynamic_index_in_dim(sites, core, 1, keepdims=False).reshape(-1)

    result = None
    swap = [(i, i ^ 1) for i in range(cores)]
    for index in range(CHUNKS):
        sent = filter_chunk(weight, low, image, high, rows_m, cols_m, index, chunk, segments)
        mine = lax.all_to_all(
            sent.reshape(segments, rows // segments, 2 * chunk), "seg", split_axis=0, concat_axis=0, tiled=True
        ).reshape(rows, 2 * chunk)
        other = lax.ppermute(mine, "core", swap)
        pieces = pair_sum(info, pair_sites, mine, other, lines * own_slots, quarter)
        pieces = lax.all_to_all(
            pieces.reshape(lines, own_slots * quarter, chunk), "line", split_axis=0, concat_axis=0, tiled=True
        )
        result = finish_chunk(pieces, scale, result, index)
    return result.reshape(own_slots, quarter, half_cols)


def solution(mesh):
    segments, exposures = mesh.shape["seg"], mesh.shape["exp"]
    parted = Mesh(mesh.devices.reshape(segments, exposures // 2, 2), ("seg", "line", "core"))
    spread = ("line", "core")
    placed = (
        P(spread, "seg", None),
        P(spread, None, None),
        P(spread, None),
        P(spread),
        P(spread),
        P(spread),
        P(),
    )
    return jax.shard_map(
        per_device, mesh=parted, in_specs=placed, out_specs=P(spread, "seg", None), check_vma=False
    )
```

time: 512 us -> 173 us (0.34); the launches traced: 502 us -> 172 us
  local copies, waits for them, and re-layouts: 150 us -> 9.4 us
  matrix products: 138 us -> 0 us
  waiting for transfers between devices: 161 us -> 45.9 us
  blocking collectives: 0 us -> 44.7 us
  Pallas kernels: 0 us -> 29.7 us
  starting transfers between devices: 29.9 us -> 19.1 us
  between operations: 3.92 us -> 12.8 us
  other arithmetic: 18.6 us -> 10.4 us
    dot_general x4 -> x0, matrix products: 138 us -> none  [the longest x2 73.1 us: across_columns(): jnp.einsum('rbk,ck->rbc', windows, matrix, precision=lax.Precision.HIGHES...]
    all_to_all x3, waiting for transfers between devices: 161 us -> 43.2 us  [the longest x2 37 us: per_device(): lax.all_to_all(pieces.reshape(lines, own_slots * quarter, chunk), 'line',...]
    unnamed x21 -> x20, local copies, waits for them, and re-layouts: 66.4 us -> 5.81 us
    slice x13 -> x3, local copies, waits for them, and re-layouts: 40.2 us -> 2.47 us  [the longest x2 1.41 us: per_device(): relative = site // 2 - facts[exposure, 1].astype(jnp.int32)]
    pallas_call x0 -> x7, Pallas kernels: none -> 29.7 us  [the longest x2 15.1 us: filter_chunk(): pl.pallas_call(functools.partial(filter_kernel, first_chunk=index == 0, l...]
    all_to_all x0 -> x1, blocking collectives: none -> 27.3 us  [per_device(): lax.all_to_all(sent.reshape(segments, rows // segments, 2 * chunk), 'seg'...]
    unnamed x0 -> x1, blocking collectives: none -> 17.4 us
    gather x1 -> x0, local copies, waits for them, and re-layouts: 16.7 us -> none  [per_device(): swapped[safe_band % bands_here, safe_band // bands_here, :, site_half, :]]
  transfers between devices with their start and end apart: 7 -> 7, of which waited for: 3 -> 4; matrix products, arithmetic and copies ran while one was open for 7% -> 8% of each run, Pallas kernels for 0% -> 13%
where the time goes in v1:
time: 173 us; the launch traced here: 172 us
  waiting for transfers between devices  45.9 us (27%)
  blocking collectives  44.7 us (26%)
  Pallas kernels  29.7 us (17%)
  starting transfers between devices  19.1 us (11%)
  between operations  12.8 us (7%)
  other arithmetic  10.4 us (6%)
  local copies, waits for them, and re-layouts  9.4 us (5%)
    all_to_all x2, waiting for transfers between devices, per_device(): lax.all_to_all(pieces.reshape(lines, own_slots * quarter, chunk), 'line',...  37 us
    all_to_all x1, blocking collectives, per_device(): lax.all_to_all(sent.reshape(segments, rows // segments, 2 * chunk), 'seg'...  27.3 us
    unnamed x1, blocking collectives  17.4 us
    pallas_call x2, Pallas kernels, filter_chunk(): pl.pallas_call(functools.partial(filter_kernel, first_chunk=index == 0, l...  15.1 us
    max x1, other arithmetic, per_device(): scale = jnp.maximum(total, 1.0)  8.69 us
    all_to_all x2, starting transfers between devices, per_device(): lax.all_to_all(pieces.reshape(lines, own_slots * quarter, chunk), 'line',...  8.4 us
    pallas_call x2, Pallas kernels, pair_sum(): pl.pallas_call(functools.partial(pair_kernel, quarter=quarter), out_shape...  6.83 us
    all_to_all x1, waiting for transfers between devices, per_device(): lax.all_to_all(sent.reshape(segments, rows // segments, 2 * chunk), 'seg'...  6.27 us
  transfers between devices with their start and end apart: 7, of which 4 were waited for; matrix products, arithmetic and copies ran while one was open for 8% of the time, Pallas kernels for 13%

profile of v1, /device:TPU:0, one launch (start us, length us, event | category | flops | bytes accessed | tf_op | source)
XLA Modules:
  0.0 172.1 jit_solution(13751769902307883143)
XLA Ops:
  0.0 1.1 slice_bitcast_fusion
  1.1 4.9 %collective-permute-start = (f32[16,4096]{1,0:T(8,128)S(1)}, f32[16,4096]{1,0:T(8,128)S(1)}, u32[]{:S(2)}, u32[]{:S(2)}) collective-permute-start(f32[16,4096]{1,0:T(8,128)S(1)} %get-tuple-element.12), channel_id=1, source_target_pairs={{0,8},{8,16},{16,24},{1,9},{9,17},{17,25},{2,10},{10,18},{18,26},{... | collective-permute-start | bytes 786440 | tf_op jit(solution)/shard_map/ppermute | solution.py:349
  5.9 1.3 collective-permute-start.1
  8.6 0.0 copy-start.4
  8.6 0.7 copy-done.4
  9.2 0.7 copy-done.5
  9.9 0.7 copy-done.6
  10.6 5.8 %band_matrices.1 = (bf16[3,128,480]{2,1,0:T(8,128)(2,1)S(1)}, bf16[3,2,512,256]{3,2,1,0:T(8,128)(2,1)S(1)}) custom-call(s32[1]{0:T(128)} %bitcast.6.place, f32[2,3]{1,0:T(2,128)S(1)} %bitcast.49, s32[2]{0:T(128)S(1)} %bitcast.50, s32[1]{0:T(128)S(6)} %copy.12.shift, f32[16,6]{1,0:T(8,128)S(1)} %copy-done.6), custom_call_target="tpu_custom_call" | custom-call | flops 4000000 | bytes 4000000 | tf_op jit(solution)/shard_map/band_matrices/pallas_call | solution.py:124
  16.4 0.0 collective-permute-done.low_l.low_c.low_r
  16.4 2.7 %collective-permute-done.1.high_l.high_c.high_r = f32[16,4096]{1,0:T(8,128)S(1)} collective-permute-done((f32[16,4096]{1,0:T(8,128)S(1)}, f32[16,4096]{1,0:T(8,128)S(1)}, u32[]{:S(2)}, u32[]{:S(2)}) %collective-permute-start.1) | collective-permute-done | bytes 262176 | tf_op jit(solution)/shard_map/ppermute | solution.py:350
  19.0 7.1 %warp_filter.3 = bf16[512,2048]{1,0:T(8,128)(2,1)S(1)} custom-call(f32[1]{0:T(128)S(6)} %convert_element_type.116.weight, f32[16,4096]{1,0:T(8,128)S(1)} %collective-permute-done.low_l.low_c.low_r, f32[16,4096]{1,0:T(8,128)S(1)} %collective-permute-done.low_l.low_c.low_r, f32[16,4096]{1,0:T(8,128)S(1)} %collective-permute-done.low_l.low_c.low_r, ...), custom_call_target="tpu_custom_call" | custom-call | flops 4294967296 | bytes 6291456 | tf_op jit(solution)/shard_map/warp_filter/pallas_call | solution.py:228
  26.2 27.3 %all_to_all.20 = bf16[4,128,2048]{2,1,0:T(8,128)(2,1)S(1)} all-to-all(bf16[4,128,2048]{2,1,0:T(8,128)(2,1)S(1)} %bitcast.44), channel_id=1, replica_groups=mesh['seg'=4,'line'=4,'core'=2] {'seg'}, dimensions={0} | all-to-all | bytes 4194304 | tf_op jit(solution)/shard_map/all_to_all | solution.py:382
  53.4 0.0 collective-permute-start.3
  53.4 8.0 %warp_filter.2 = bf16[512,2048]{1,0:T(8,128)(2,1)} custom-call(f32[1]{0:T(128)S(6)} %convert_element_type.116.weight, f32[16,4096]{1,0:T(8,128)S(1)} %collective-permute-done.low_l.low_c.low_r, f32[16,4096]{1,0:T(8,128)S(1)} %collective-permute-done.low_l.low_c.low_r, f32[16,4096]{1,0:T(8,128)S(1)} %collective-permute-done.low_l.low_c.low_r, ...), custom_call_target="tpu_custom_call" | custom-call | flops 4294967296 | bytes 6291456 | tf_op jit(solution)/shard_map/warp_filter/pallas_call | solution.py:228
  61.4 4.6 %all-to-all-start = ((bf16[4,128,2048]{2,1,0:T(8,128)(2,1)}), bf16[4,128,2048]{2,1,0:T(8,128)(2,1)}, u32[]{:S(2)}, u32[]{:S(2)}) async-start(bf16[4,128,2048]{2,1,0:T(8,128)(2,1)} %bitcast.9), calls=%async_computation | async-start | bytes 4194304 | tf_op jit(solution)/shard_map/all_to_all | solution.py:382
  66.6 0.6 dynamic-slice.4
  67.9 0.2 maximum_dynamic-update-slice_fusion
  68.1 17.4 %all-reduce = f32[24]{0:T(128)S(1)} all-reduce(f32[24]{0:T(128)S(1)} %maximum_dynamic-update-slice_fusion), channel_id=2, replica_groups=mesh['seg'=4,'line'=4,'core'=2] {'line','core'}, use_global_device_ids=true, to_apply=%add | all-reduce | flops 24 | bytes 192
  85.5 0.1 reshape.432
  85.6 6.3 %all-to-all-done = bf16[4,128,2048]{2,1,0:T(8,128)(2,1)} async-done(((bf16[4,128,2048]{2,1,0:T(8,128)(2,1)}), bf16[4,128,2048]{2,1,0:T(8,128)(2,1)}, u32[]{:S(2)}, u32[]{:S(2)}) %all-to-all-start) | async-done | bytes 2097184 | tf_op jit(solution)/shard_map/all_to_all | solution.py:382
  91.8 0.0 collective-permute-start.2
  91.9 0.2 convert_reduce_fusion
  92.0 0.1 convert_element_type.118
  92.1 0.1 reshape.422
  92.2 0.1 reshape.423.sites
  92.3 0.6 fusion.51
  92.9 1.3 pad_add_fusion.info
  94.2 0.0 collective-permute-done.3.other
  94.2 3.1 %pair_sum.3 = bf16[640,1024]{1,0:T(8,128)(2,1)S(1)} custom-call(s32[2]{0:T(128)S(1)} %pad_add_fusion.info, s32[80]{0:T(128)S(1)} %reshape.423.sites, bf16[512,2048]{1,0:T(8,128)(2,1)S(1)} %bitcast.46, bf16[512,2048]{1,0:T(8,128)(2,1)} %collective-permute-done.3.other), custom_call_target="tpu_custom_call" | custom-call | flops 5242880 | bytes 5505024 | tf_op jit(solution)/shard_map/pair_sum/pallas_call | solution.py:285
  97.3 0.0 copy-start.3
  97.3 1.0 copy-done.3
  98.4 4.9 %all-to-all-start.3 = ((bf16[4,160,1024]{2,1,0:T(8,128)(2,1)}), bf16[4,160,1024]{2,1,0:T(8,128)(2,1)S(1)}, u32[]{:S(2)}, u32[]{:S(2)}) async-start(bf16[4,160,1024]{2,1,0:T(8,128)(2,1)} %bitcast.48), calls=%async_computation.3 | async-start | bytes 2621440 | tf_op jit(solution)/shard_map/all_to_all | solution.py:387
  103.2 0.0 collective-permute-done.2.other
  103.3 3.7 %pair_sum.2 = bf16[640,1024]{1,0:T(8,128)(2,1)S(1)} custom-call(s32[2]{0:T(128)S(1)} %pad_add_fusion.info, s32[80]{0:T(128)S(1)} %reshape.423.sites, bf16[512,2048]{1,0:T(8,128)(2,1)} %bitcast.10.mine, bf16[512,2048]{1,0:T(8,128)(2,1)} %collective-permute-done.2.other), custom_call_target="tpu_custom_call" | custom-call | flops 5242880 | bytes 5505024 | tf_op jit(solution)/shard_map/pair_sum/pallas_call | solution.py:285
  107.0 0.0 copy-start.2
  107.0 1.1 copy-done.2
  108.1 27.2 %all-to-all-done.3.pieces = bf16[4,160,1024]{2,1,0:T(8,128)(2,1)S(1)} async-done(((bf16[4,160,1024]{2,1,0:T(8,128)(2,1)}), bf16[4,160,1024]{2,1,0:T(8,128)(2,1)S(1)}, u32[]{:S(2)}, u32[]{:S(2)}) %all-to-all-start.3) | async-done | bytes 1310752 | tf_op jit(solution)/shard_map/all_to_all | solution.py:387
  135.3 1.1 copy-done
  136.3 3.5 %all-to-all-start.1 = ((bf16[4,160,1024]{2,1,0:T(8,128)(2,1)}), bf16[4,160,1024]{2,1,0:T(8,128)(2,1)S(1)}, u32[]{:S(2)}, u32[]{:S(2)}) async-start(bf16[4,160,1024]{2,1,0:T(8,128)(2,1)} %bitcast.47), calls=%async_computation.1 | async-start | bytes 2621440 | tf_op jit(solution)/shard_map/all_to_all | solution.py:387
  139.9 0.1 broadcast_in_dim.40
  140.0 0.1 broadcast_in_dim_reshape.3
  140.0 0.0 copy-start.1
  140.1 0.7 fusion.50
  141.4 0.7 fusion.49
  151.5 8.7 %add_maximum_fusion.scale = f32[160,2048]{1,0:T(8,128)S(1)} fusion(f32[]{:T(128)} %bitcast.36, s32[]{:T(128)} %bitcast.34, f32[]{:T(128)} %bitcast.33, s32[]{:T(128)} %bitcast.31, f32[]{:T(128)} %bitcast.30, s32[]{:T(128)} %bitcast.28, f32[]{:T(128)} %bitcast.27, s32[]{:T(128)} %bitcast.25, f32[]{:T(128)} %bitcast.24, s32[]{:T(128)} %bitcast.22, f32[]{:T(128)} %bitcast.21, ...), kind=kLoop, calls=%fused_computation | loop fusion | flops 21299200 | bytes 1313984 | tf_op jit(solution)/shard_map/max | solution.py:371
  160.2 1.0 patch_mean.2.rest_0_
  161.3 9.8 %all-to-all-done.1.pieces = bf16[4,160,1024]{2,1,0:T(8,128)(2,1)S(1)} async-done(((bf16[4,160,1024]{2,1,0:T(8,128)(2,1)}), bf16[4,160,1024]{2,1,0:T(8,128)(2,1)S(1)}, u32[]{:S(2)}, u32[]{:S(2)}) %all-to-all-start.1) | async-done | bytes 1310752 | tf_op jit(solution)/shard_map/all_to_all | solution.py:387
  171.0 1.0 patch_mean.3
  (14 shorter events, 0.1 us)
Async XLA Ops:
  1.1 15.3 %collective-permute-start = (f32[16,4096]{1,0:T(8,128)S(1)}, f32[16,4096]{1,0:T(8,128)S(1)}, u32[]{:S(2)}, u32[]{:S(2)}) collective-permute-start(f32[16,4096]{1,0:T(8,128)S(1)} %get-tuple-element.12), channel_id=1, source_target_pairs={{0,8},{8,16},{16,24},{1,9},{9,17},{17,25},{2,10},{10,18},{18,26},{... | collective-permute-start | bytes 786440 | tf_op jit(solution)/shard_map/ppermute | solution.py:349
  5.9 13.1 %collective-permute-start.1 = (f32[16,4096]{1,0:T(8,128)S(1)}, f32[16,4096]{1,0:T(8,128)S(1)}, u32[]{:S(2)}, u32[]{:S(2)}) collective-permute-start(f32[16,4096]{1,0:T(8,128)S(1)} %get-tuple-element.11), channel_id=1, source_target_pairs={{8,0},{16,8},{24,16},{9,1},{17,9},{25,17},{10,2},{18,10},{26,18},{... | collective-permute-start | bytes 786440 | tf_op jit(solution)/shard_map/ppermute | solution.py:350
  8.6 0.7 copy-start.4
  9.2 0.7 copy-start.5
  9.9 0.7 copy-start.6
  53.4 40.8 %collective-permute-start.3 = (bf16[512,2048]{1,0:T(8,128)(2,1)S(1)}, bf16[512,2048]{1,0:T(8,128)(2,1)}, u32[]{:S(2)}, u32[]{:S(2)}) collective-permute-start(bf16[512,2048]{1,0:T(8,128)(2,1)S(1)} %bitcast.45), channel_id=1, source_target_pairs={{0,1},{1,0},{2,3},{3,2},{4,5},{5,4},{6,7},{7,6},{8,9},{9,8},{10,11... | collective-permute-start | bytes 6291464 | tf_op jit(solution)/shard_map/ppermute | solution.py:385
  61.4 5.3 %copy-start.8 = (u32[32]{0:T(128)S(1)}, u32[32]{0:T(128)}, u32[]{:S(2)}) copy-start(u32[32]{0:T(128)} %constant.133) | copy-start | bytes 388
  61.4 30.8 %copy-start.7 = (s32[160]{0:T(256)S(1)}, s32[160]{0:T(256)}, u32[]{:S(2)}) copy-start(s32[160]{0:T(256)} %param.14) | copy-start | bytes 1924
  61.4 30.5 %all-to-all-start = ((bf16[4,128,2048]{2,1,0:T(8,128)(2,1)}), bf16[4,128,2048]{2,1,0:T(8,128)(2,1)}, u32[]{:S(2)}, u32[]{:S(2)}) async-start(bf16[4,128,2048]{2,1,0:T(8,128)(2,1)} %bitcast.9), calls=%async_computation | async-start | bytes 4194304 | tf_op jit(solution)/shard_map/all_to_all | solution.py:382
  91.8 11.4 %collective-permute-start.2 = (bf16[512,2048]{1,0:T(8,128)(2,1)}, bf16[512,2048]{1,0:T(8,128)(2,1)}, u32[]{:S(2)}, u32[]{:S(2)}) collective-permute-start(bf16[512,2048]{1,0:T(8,128)(2,1)} %bitcast.10.mine), channel_id=1, source_target_pairs={{0,1},{1,0},{2,3},{3,2},{4,5},{5,4},{6,7},{7,6},{8,9},{9,8},{10,11... | collective-permute-start | bytes 6291464 | tf_op jit(solution)/shard_map/ppermute | solution.py:385
  97.3 1.1 copy-start.3
  98.4 36.9 %all-to-all-start.3 = ((bf16[4,160,1024]{2,1,0:T(8,128)(2,1)}), bf16[4,160,1024]{2,1,0:T(8,128)(2,1)S(1)}, u32[]{:S(2)}, u32[]{:S(2)}) async-start(bf16[4,160,1024]{2,1,0:T(8,128)(2,1)} %bitcast.48), calls=%async_computation.3 | async-start | bytes 2621440 | tf_op jit(solution)/shard_map/all_to_all | solution.py:387
  107.0 1.1 copy-start.2
  135.3 1.1 copy-start
  136.3 34.7 %all-to-all-start.1 = ((bf16[4,160,1024]{2,1,0:T(8,128)(2,1)}), bf16[4,160,1024]{2,1,0:T(8,128)(2,1)S(1)}, u32[]{:S(2)}, u32[]{:S(2)}) async-start(bf16[4,160,1024]{2,1,0:T(8,128)(2,1)} %bitcast.47), calls=%async_computation.1 | async-start | bytes 2621440 | tf_op jit(solution)/shard_map/all_to_all | solution.py:387
  140.0 20.2 %copy-start.1 = (bf16[4,160,1024]{2,1,0:T(8,128)(2,1)S(1)}, bf16[4,160,1024]{2,1,0:T(8,128)(2,1)}, u32[]{:S(2)}) copy-start(bf16[4,160,1024]{2,1,0:T(8,128)(2,1)} %copy-done) | copy-start | bytes 3932164

commit v2 on v1

v2 whole, which is shorter than its diff:
```python
import functools

import jax
import jax.numpy as jnp
import numpy as np
from jax import lax
from jax.experimental import pallas as pl
from jax.experimental.pallas import tpu as pltpu
from jax.sharding import Mesh, PartitionSpec as P

BAND_ROWS = 32
TAPS = 21
PHASES = 16
LANCZOS = 6
SPAN = TAPS + LANCZOS - 1
LEAD = TAPS // 2 + 2
HALO = 16
SIDE = 128
TILE = 256
STRIP = 128
PARTS = (4, 4, 4, 4)
VMEM = 48 * 1024 * 1024

sigmas = (1.0, 2.0, 3.5)


def basis_table():
    offsets = np.arange(TAPS) - TAPS // 2
    curves = [np.exp(-offsets * offsets / (2.0 * spread * spread)) for spread in sigmas]
    return [[float(value) for value in curve / curve.sum()] for curve in curves]


def lanczos_table():
    shifted = np.arange(LANCZOS)[None, :] - 2.0 - np.arange(PHASES)[:, None] / PHASES
    values = np.sinc(shifted) * np.sinc(shifted / 3.0)
    return (values / values.sum(axis=1, keepdims=True)).astype(np.float32)


def lanczos_taps(phase):
    table = lanczos_table()
    taps = []
    for n in range(LANCZOS):
        tap = jnp.float32(table[0, n])
        for index in range(1, PHASES):
            tap = jnp.where(phase == index, jnp.float32(table[index, n]), tap)
        taps.append(tap)
    return taps


def split(value):
    high = value.astype(jnp.bfloat16)
    return high, (value - high.astype(jnp.float32)).astype(jnp.bfloat16)


def banded(taps, masks, distance):
    matrix = jnp.zeros(distance.shape, jnp.float32)
    kernel, lanczos = taps
    weighted = [jnp.where(mask, lanczos[n], 0.0) for n, mask in enumerate(masks)]
    for t in range(SPAN):
        row = jnp.zeros_like(weighted[0])
        for n in range(LANCZOS):
            if 0 <= t - n < TAPS:
                row = row + kernel[t - n] * weighted[n]
        matrix = matrix + jnp.where(distance == t, row, 0.0)
    return matrix


def matrices_kernel(place, coef, phases, shift, rows_out, cols_out, *, rows, width, segments):
    basis = basis_table()

    def taps_of(axis):
        kernel = [sum(coef[axis, k] * basis[k][t] for k in range(len(sigmas))) for t in range(TAPS)]
        return kernel, lanczos_taps(phases[axis])

    taps = taps_of(1)
    offset = shift[0]
    zero = jnp.zeros((SIDE, SIDE), jnp.bfloat16)
    for variant, first in enumerate((0, None, width - TILE)):
        for part in range(2):
            for block in range(4):
                if not part <= block <= part + 2:
                    for term in range(2):
                        cols_out[variant, term, pl.ds(block * SIDE, SIDE), pl.ds(part * SIDE, SIDE)] = zero
                    continue
                output = part * SIDE + lax.broadcasted_iota(jnp.int32, (1, SIDE), 1)
                if first is None:
                    masks = [jnp.full((1, SIDE), True)] * LANCZOS
                else:
                    matched = first + output - offset
                    masks = [
                        (matched + (n - 2) >= 0) & (matched + (n - 2) < width) for n in range(LANCZOS)
                    ]
                distance = (
                    lax.broadcasted_iota(jnp.int32, (SIDE, SIDE), 0)
                    - lax.broadcasted_iota(jnp.int32, (SIDE, SIDE), 1)
                    + (offset + LEAD - SIDE + (block - part) * SIDE)
                )
                high, low = split(banded(taps, masks, distance))
                cols_out[variant, 0, pl.ds(block * SIDE, SIDE), pl.ds(part * SIDE, SIDE)] = high
                cols_out[variant, 1, pl.ds(block * SIDE, SIDE), pl.ds(part * SIDE, SIDE)] = low

    taps = taps_of(0)
    span = STRIP + 2 * HALO
    quarter = BAND_ROWS // segments
    bands = STRIP // BAND_ROWS
    order = lax.broadcasted_iota(jnp.int32, (1, STRIP), 1)
    within = lax.rem(order, bands * quarter)
    owner = lax.div(order, bands * quarter) ^ place[0]
    output = lax.div(within, quarter) * BAND_ROWS + owner * quarter + lax.rem(within, quarter)
    depth = cols_pad(3 * span)
    stacked = lax.broadcasted_iota(jnp.int32, (depth, STRIP), 0)
    term = jnp.where(stacked >= 2 * span, 2, jnp.where(stacked >= span, 1, 0))
    distance = stacked - term * span - output + (LEAD - HALO)
    for variant, first in enumerate((0, STRIP, rows - STRIP)):
        matched = place[0] * rows + first + output
        masks = [
            (matched + (n - 2) >= 0) & (matched + (n - 2) < rows * segments) for n in range(LANCZOS)
        ]
        matrix = banded(taps, masks, distance).T
        high, low = split(matrix)
        column = lax.broadcasted_iota(jnp.int32, matrix.shape, 1)
        both = jnp.where(column >= 2 * span, low.astype(jnp.float32), high.astype(jnp.float32))
        rows_out[variant] = both.astype(jnp.bfloat16)[:, : 3 * span]


def cols_pad(count):
    return -(-count // 128) * 128


def build_matrices(place, coef, phases, shift, rows, width, segments):
    span = 3 * (STRIP + 2 * HALO)
    smem = pl.BlockSpec(memory_space=pltpu.SMEM)
    vmem = pl.BlockSpec(memory_space=pltpu.VMEM)
    return pl.pallas_call(
        functools.partial(matrices_kernel, rows=rows, width=width, segments=segments),
        out_shape=(
            jax.ShapeDtypeStruct((3, STRIP, span), jnp.bfloat16),
            jax.ShapeDtypeStruct((3, 2, TILE + 2 * SIDE, TILE), jnp.bfloat16),
        ),
        in_specs=[smem] * 4,
        out_specs=(vmem, vmem),
        compiler_params=pltpu.CompilerParams(vmem_limit_bytes=VMEM),
        cost_estimate=pl.CostEstimate(flops=4_000_000, bytes_accessed=4_000_000, transcendentals=0),
        name="band_matrices",
    )(place, coef, phases, shift)


def filter_kernel(
    weight, low_l, low_c, low_r, mid_l, mid_c, mid_r, high_l, high_c, high_r, rows_m, cols_m, *rest,
    first_chunk, last_chunk, segments,
):
    outs, (ext_high, ext_low, mat_high, mat_low) = rest[:segments], rest[segments:]
    half = pl.program_id(0)
    halves = pl.num_programs(0)
    rows, chunk = mid_c.shape
    at_left = first_chunk & (half == 0)
    at_right = last_chunk & (half == halves - 1)
    span = STRIP + 2 * HALO

    for row, parts in (
        (0, (low_l, low_c, low_r)),
        (HALO, (mid_l, mid_c, mid_r)),
        (HALO + rows, (high_l, high_c, high_r)),
    ):
        count = parts[0].shape[0]
        for part, column, outside in zip(parts, (0, SIDE, SIDE + chunk), (at_left, False, at_right)):
            value = part[...]
            if outside is not False:
                value = jnp.where(outside, 0.0, value)
            high, low = split(value)
            place = (pl.ds(row, count), pl.ds(column, value.shape[1]))
            ext_high[place] = high
            ext_low[place] = low

    strips = rows // STRIP
    for tile in range((chunk + 2 * SIDE) // TILE):
        columns = pl.ds(tile * TILE, TILE)
        for strip in range(strips):
            window = pl.ds(strip * STRIP, span)
            variant = 0 if strip == 0 else (2 if strip == strips - 1 else 1)
            high = ext_high[window, columns]
            stack = jnp.concatenate([high, ext_low[window, columns], high], axis=0)
            matched = jnp.dot(rows_m[variant], stack, preferred_element_type=jnp.float32)
            high, low = split(matched)
            mat_high[pl.ds(strip * STRIP, STRIP), columns] = high
            mat_low[pl.ds(strip * STRIP, STRIP), columns] = low

    tiles = chunk // TILE
    piece = STRIP // segments
    for tile in range(tiles):
        variant = jnp.int32(1)
        if tile == 0:
            variant = jnp.where(at_left, 0, variant)
        if tile == tiles - 1:
            variant = jnp.where(at_right, 2, variant)
        taps_high = cols_m[variant, 0]
        taps_low = cols_m[variant, 1]
        window = pl.ds(tile * TILE, TILE + 2 * SIDE)
        for strip in range(strips):
            place = pl.ds(strip * STRIP, STRIP)
            high = mat_high[place, window]
            warped = jnp.dot(high, taps_high, preferred_element_type=jnp.float32)
            warped += jnp.dot(mat_low[place, window], taps_high, preferred_element_type=jnp.float32)
            warped += jnp.dot(high, taps_low, preferred_element_type=jnp.float32)
            sent = (weight[0] * warped).astype(jnp.bfloat16)
            for owner, out in enumerate(outs):
                out[pl.ds(strip * piece, piece), pl.ds(tile * TILE, TILE)] = sent[owner * piece : (owner + 1) * piece]


def filter_chunk(weight, low, image, high, rows_m, cols_m, start, chunk, segments):
    rows, width = image.shape
    halves = 2
    half_blocks = width // halves // SIDE
    first = start // SIDE
    blocks = chunk // SIDE
    last = width // SIDE - 1

    def left(h):
        return 0, jnp.maximum(h * half_blocks + first - 1, 0)

    def centre(h):
        return 0, h * (half_blocks // blocks) + start // chunk

    def right(h):
        return 0, jnp.minimum(h * half_blocks + first + blocks, last)

    def whole(array):
        return pl.BlockSpec(array.shape, lambda h: (0,) * array.ndim)

    specs = [pl.BlockSpec(memory_space=pltpu.SMEM)]
    for source in (low, image, high):
        specs += [
            pl.BlockSpec((source.shape[0], SIDE), left),
            pl.BlockSpec((source.shape[0], chunk), centre),
            pl.BlockSpec((source.shape[0], SIDE), right),
        ]
    wide = chunk + 2 * SIDE
    return pl.pallas_call(
        functools.partial(
            filter_kernel,
            first_chunk=start == 0,
            last_chunk=start + chunk == width // halves,
            segments=segments,
        ),
        out_shape=[jax.ShapeDtypeStruct((rows // segments, halves * chunk), jnp.bfloat16)] * segments,
        grid=(halves,),
        in_specs=specs + [whole(rows_m), whole(cols_m)],
        out_specs=[pl.BlockSpec((rows // segments, chunk), lambda h: (0, h))] * segments,
        scratch_shapes=[
            pltpu.VMEM((rows + 2 * HALO, wide), jnp.bfloat16),
            pltpu.VMEM((rows + 2 * HALO, wide), jnp.bfloat16),
            pltpu.VMEM((rows, wide), jnp.bfloat16),
            pltpu.VMEM((rows, wide), jnp.bfloat16),
        ],
        compiler_params=pltpu.CompilerParams(vmem_limit_bytes=VMEM),
        cost_estimate=pl.CostEstimate(
            flops=halves * 2 * rows * chunk * 2048, bytes_accessed=halves * rows * chunk * 6, transcendentals=0
        ),
        name="warp_filter",
    )(weight, *([low] * 3), *([image] * 3), *([high] * 3), rows_m, cols_m)


def pair_kernel(place, offset, other_offset, sites, *rest, segments, lines, cores, quarter):
    mine, other = rest[:segments], rest[segments : 2 * segments]
    outs, (mine_all, other_all) = rest[2 * segments : 2 * segments + lines], rest[2 * segments + lines :]
    block = mine[0].shape[0]
    chunk = outs[0].shape[1]
    block_bands = block // quarter
    bands = block_bands * segments
    slots = outs[0].shape[0] // quarter
    two = 2 * quarter
    for step in range(segments):
        mine_all[pl.ds(step * block, block), :] = mine[step][...]
        other_all[pl.ds(step * block, block), :] = other[step][...]
    segment, line, core = place[0], place[1], place[2]

    def rows_of(source, from_offset, site):
        relative = lax.shift_right_logical(site, 1) - from_offset
        present = (relative >= 0) & (relative < bands)
        safe = jnp.clip(relative, 0, bands - 1)
        held = (lax.div(safe, block_bands) ^ segment) * block + lax.rem(safe, block_bands) // 2 * two
        tile = source[
            pl.ds(pl.multiple_of(held, two), two), pl.ds(pl.multiple_of((site & 1) * chunk, 128), chunk)
        ].astype(jnp.float32)
        rows = jnp.where((safe & 1) == 1, tile[quarter:], tile[:quarter])
        return jnp.where(present, rows, 0.0)

    for target, out in reversed(list(enumerate(outs))):
        owner = (line ^ target) * cores + core

        def summed(slot, owner=owner):
            site = sites[owner * slots + slot]
            return rows_of(mine_all, offset[0], site) + rows_of(other_all, other_offset[0], site)

        def two_slots(step, carry, summed=summed, out=out):
            rows = jnp.concatenate([summed(2 * step), summed(2 * step + 1)], axis=0)
            out[pl.ds(pl.multiple_of(step * two, two), two), :] = rows.astype(jnp.bfloat16)
            return carry

        lax.fori_loop(0, slots // 2, two_slots, 0)
        if slots % 2:
            out[pl.ds((slots - 1) * quarter, quarter), :] = summed(slots - 1).astype(jnp.bfloat16)


def pair_sum(place, offset, other_offset, sites, mine, other, slots, lines, cores, quarter):
    block, double = mine[0].shape
    chunk = double // 2
    segments = len(mine)
    smem = pl.BlockSpec(memory_space=pltpu.SMEM)
    vmem = pl.BlockSpec(memory_space=pltpu.VMEM)
    return pl.pallas_call(
        functools.partial(pair_kernel, segments=segments, lines=lines, cores=cores, quarter=quarter),
        out_shape=[jax.ShapeDtypeStruct((slots * quarter, chunk), jnp.bfloat16)] * lines,
        in_specs=[smem] * 4 + [vmem] * (2 * segments),
        out_specs=[vmem] * lines,
        scratch_shapes=[pltpu.VMEM((segments * block, double), jnp.bfloat16)] * 2,
        compiler_params=pltpu.CompilerParams(vmem_limit_bytes=VMEM),
        cost_estimate=pl.CostEstimate(
            flops=8 * lines * slots * quarter * chunk,
            bytes_accessed=4 * segments * block * double + 2 * lines * slots * quarter * chunk,
            transcendentals=0,
        ),
        name="pair_sum",
    )(place, offset, other_offset, sites, *mine, *other)


def weight_kernel(place, sites, facts, out, *, cores, quarter, width, bands):
    slots = out.shape[0] // quarter
    half_cols = out.shape[1]
    owner = place[1] * cores + place[2]
    column = lax.broadcasted_iota(jnp.int32, (quarter, half_cols), 1)

    def one_slot(slot, carry):
        site = sites[owner * slots + slot]
        band = lax.shift_right_logical(site, 1)
        total = jnp.zeros((quarter, half_cols), jnp.float32)
        for exposure in range(facts.shape[0]):
            first = facts[exposure, 0].astype(jnp.int32) - (site & 1) * half_cols
            relative = band - facts[exposure, 1].astype(jnp.int32)
            weight = jnp.where((relative >= 0) & (relative < bands), facts[exposure, 2], 0.0)
            total = total + jnp.where((column >= first) & (column < first + width), weight, 0.0)
        out[pl.ds(pl.multiple_of(slot * quarter, quarter), quarter), :] = jnp.maximum(total, 1.0)
        return carry

    lax.fori_loop(0, slots, one_slot, 0)


def patch_weights(place, sites, facts, slots, quarter, cores, width, bands):
    smem = pl.BlockSpec(memory_space=pltpu.SMEM)
    return pl.pallas_call(
        functools.partial(weight_kernel, cores=cores, quarter=quarter, width=width, bands=bands),
        out_shape=jax.ShapeDtypeStruct((slots * quarter, width // 2), jnp.float32),
        in_specs=[smem] * 3,
        out_specs=pl.BlockSpec(memory_space=pltpu.VMEM),
        cost_estimate=pl.CostEstimate(
            flops=40 * slots * quarter * width // 2, bytes_accessed=2 * slots * quarter * width, transcendentals=0
        ),
        name="patch_weights",
    )(place, sites, facts)


def finish_kernel(*refs, count):
    pieces, scale, out = refs[:count], refs[count], refs[-1]
    total = pieces[0][...].astype(jnp.float32)
    for piece in pieces[1:]:
        total += piece[...].astype(jnp.float32)
    out[...] = total / scale[...]


def finish_chunk(pieces, scale, result, start):
    rows, chunk = pieces[0].shape
    column = pl.BlockSpec((rows, chunk), lambda i: (0, start // chunk))
    specs = [pl.BlockSpec((rows, chunk), lambda i: (0, 0))] * len(pieces) + [column]
    operands = [*pieces, scale]
    aliases = {}
    if result is not None:
        specs.append(pl.BlockSpec(memory_space=pl.ANY))
        aliases = {len(operands): 0}
        operands.append(result)
    return pl.pallas_call(
        functools.partial(finish_kernel, count=len(pieces)),
        out_shape=jax.ShapeDtypeStruct(scale.shape, jnp.float32),
        grid=(1,),
        in_specs=specs,
        out_specs=column,
        input_output_aliases=aliases,
        compiler_params=pltpu.CompilerParams(vmem_limit_bytes=VMEM),
        cost_estimate=pl.CostEstimate(
            flops=len(pieces) * rows * chunk, bytes_accessed=rows * chunk * (2 * len(pieces) + 8), transcendentals=0
        ),
        name="patch_mean",
    )(*operands)


def swapped(value, axis, distance):
    count = lax.axis_size(axis)
    return lax.ppermute(value, axis, [(i, i ^ distance) for i in range(count)])


def scatter_sum(pieces):
    lines = len(pieces)
    pieces = list(pieces)
    kept = [pieces[0]]
    step = 1
    while step < lines:
        for distance in reversed(range(step, lines, 2 * step)):
            received = swapped(pieces[distance], "line", step)
            target = distance ^ step
            if target == 0:
                kept.append(received)
            else:
                both = pieces[target].astype(jnp.float32) + received.astype(jnp.float32)
                pieces[target] = both.astype(jnp.bfloat16)
        step *= 2
    return kept


def per_device(images, psf_coef, phases, col_shift, band_offset, exposure_weight, patch_site):
    image = images[0]
    rows, width = image.shape
    segments = lax.axis_size("seg")
    lines = lax.axis_size("line")
    cores = lax.axis_size("core")
    quarter = BAND_ROWS // segments
    half_cols = width // 2
    slots = patch_site.shape[0] // (lines * cores)
    bands = segments * rows // BAND_ROWS
    place = jnp.stack([lax.axis_index(axis) for axis in ("seg", "line", "core")]).astype(jnp.int32)

    forward = [(i, i + 1) for i in range(segments - 1)]
    backward = [(i + 1, i) for i in range(segments - 1)]
    low = lax.ppermute(image[rows - HALO :], "seg", forward)
    high = lax.ppermute(image[:HALO], "seg", backward)
    rows_m, cols_m = build_matrices(place, psf_coef[0], phases[0], col_shift, rows, width, segments)
    weight = exposure_weight.astype(jnp.float32)

    chunks = []
    start = 0
    for part in PARTS:
        chunks.append((start, half_cols // part))
        start += half_cols // part
    sent = [
        filter_chunk(weight, low, image, high, rows_m, cols_m, start, chunk, segments) for start, chunk in chunks
    ]

    other_offset = swapped(band_offset, "core", 1)
    facts = jnp.stack([col_shift.astype(jnp.float32), band_offset.astype(jnp.float32), weight], axis=1)
    facts = jnp.concatenate([facts, swapped(facts, "core", 1)], axis=0)
    step = 1
    while step < lines:
        facts = jnp.concatenate([facts, swapped(facts, "line", step)], axis=0)
        step *= 2
    scale = patch_weights(place, patch_site, facts, slots, quarter, cores, width, bands)

    result = None
    for (start, chunk), outgoing in zip(chunks, sent):
        mine = [outgoing[0]] + [swapped(outgoing[d], "seg", d) for d in range(1, segments)]
        other = [swapped(block, "core", 1) for block in mine]
        pieces = pair_sum(
            place, band_offset, other_offset, patch_site, mine, other, slots, lines, cores, quarter
        )
        result = finish_chunk(scatter_sum(pieces), scale, result, start)
    return result.reshape(slots, quarter, half_cols)


def solution(mesh):
    segments, exposures = mesh.shape["seg"], mesh.shape["exp"]
    parted = Mesh(mesh.devices.reshape(segments, exposures // 2, 2), ("seg", "line", "core"))
    spread = ("line", "core")
    placed = (
        P(spread, "seg", None),
        P(spread, None, None),
        P(spread, None),
        P(spread),
        P(spread),
        P(spread),
        P(),
    )
    return jax.shard_map(
        per_device, mesh=parted, in_specs=placed, out_specs=P(spread, "seg", None), check_vma=False
    )
```

time: 173 us -> 142 us (0.82)
  blocking collectives: 44.7 us -> 0 us
  starting transfers between devices: 19.1 us -> 40.1 us
  Pallas kernels: 29.7 us -> 45.7 us
  between operations: 12.8 us -> 2.22 us
  other arithmetic: 10.4 us -> 1.14 us
  local copies, waits for them, and re-layouts: 9.4 us -> 3.73 us
  waiting for transfers between devices: 45.9 us -> 49.3 us
    ppermute x2 -> x44, waiting for transfers between devices: 0.01 us -> 47.2 us  [swapped(): return lax.ppermute(value, axis, [(i, i ^ distance) for i in range(count)])]
    all_to_all x3 -> x0, waiting for transfers between devices: 43.2 us -> none  [the longest x2 37 us: per_device(): lax.all_to_all(pieces.reshape(lines, own_slots * quarter, chunk), 'line',...]
    ppermute x2 -> x44, starting transfers between devices: 0.01 us -> 33.9 us  [swapped(): return lax.ppermute(value, axis, [(i, i ^ distance) for i in range(count)])]
    all_to_all x1 -> x0, blocking collectives: 27.3 us -> none  [per_device(): lax.all_to_all(sent.reshape(segments, rows // segments, 2 * chunk), 'seg'...]
    unnamed x1 -> x0, blocking collectives: 17.4 us -> none
    pallas_call x6 -> x13, Pallas kernels: 24 us -> 40 us  [the longest x4 18.1 us: filter_chunk(): pl.pallas_call(functools.partial(filter_kernel, first_chunk=start == 0, l...]
    all_to_all x3 -> x0, starting transfers between devices: 13 us -> none  [the longest x2 8.4 us: per_device(): lax.all_to_all(pieces.reshape(lines, own_slots * quarter, chunk), 'line',...]
    max x1 -> x0, other arithmetic: 8.69 us -> none  [per_device(): scale = jnp.maximum(total, 1.0)]
  transfers between devices with their start and end apart: 7 -> 46, of which waited for: 4 -> 14; matrix products, arithmetic and copies ran while one was open for 8% -> 1% of each run, Pallas kernels for 13% -> 32%
where the time goes in v2:
time: 142 us
  waiting for transfers between devices  49.3 us (35%)
  Pallas kernels  45.7 us (32%)
  starting transfers between devices  40.1 us (28%)
  local copies, waits for them, and re-layouts  3.73 us (3%)
  between operations  2.22 us (2%)
    ppermute x44, waiting for transfers between devices, swapped(): return lax.ppermute(value, axis, [(i, i ^ distance) for i in range(count)])  47.2 us
    ppermute x44, starting transfers between devices, swapped(): return lax.ppermute(value, axis, [(i, i ^ distance) for i in range(count)])  33.9 us
    pallas_call x4, Pallas kernels, filter_chunk(): pl.pallas_call(functools.partial(filter_kernel, first_chunk=start == 0, l...  18.1 us
    pallas_call x4, Pallas kernels, pair_sum(): pl.pallas_call(functools.partial(pair_kernel, segments=segments, lines=li...  14.4 us
    pallas_call x1, Pallas kernels, build_matrices(): pl.pallas_call(functools.partial(matrices_kernel, rows=rows, width=width,...  5.67 us
    ppermute x1, starting transfers between devices, per_device(): low = lax.ppermute(image[rows - HALO:], 'seg', forward)  4.86 us
    pallas_call x1, Pallas kernels, patch_weights(): pl.pallas_call(functools.partial(weight_kernel, cores=cores, quarter=quar...  4.27 us
    pallas_call x4, Pallas kernels, finish_chunk(): pl.pallas_call(functools.partial(finish_kernel, count=len(pieces)), out_s...  3.22 us
  transfers between devices with their start and end apart: 46, of which 14 were waited for; matrix products, arithmetic and copies ran while one was open for 1% of the time, Pallas kernels for 32%

profile of v2, /device:TPU:0, one launch (start us, length us, event | category | flops | bytes accessed | tf_op | source)
XLA Modules:
  0.0 142.1 jit_solution(15365634412416830041)
XLA Ops:
  0.0 1.1 slice_bitcast_fusion
  1.1 4.9 %collective-permute-start.1 = (f32[16,4096]{1,0:T(8,128)S(1)}, f32[16,4096]{1,0:T(8,128)S(1)}, u32[]{:S(2)}, u32[]{:S(2)}) collective-permute-start(f32[16,4096]{1,0:T(8,128)S(1)} %get-tuple-element.74), channel_id=1, source_target_pairs={{0,8},{8,16},{16,24},{1,9},{9,17},{17,25},{2,10},{10,18},{18,26},{... | collective-permute-start | bytes 786440 | tf_op jit(solution)/shard_map/ppermute | solution.py:432
  5.9 1.3 collective-permute-start.2
  9.9 0.7 copy-done.4
  10.6 0.7 copy-done.5
  11.3 5.7 %band_matrices.1 = (bf16[3,128,480]{2,1,0:T(8,128)(2,1)S(1)}, bf16[3,2,512,256]{3,2,1,0:T(8,128)(2,1)S(1)}) custom-call(s32[3]{0:T(128)S(1)} %pad_add_fusion.place, f32[2,3]{1,0:T(2,128)S(1)} %bitcast.14, s32[2]{0:T(128)S(1)} %bitcast.15, s32[1]{0:T(128)S(6)} %copy.14.shift), custom_call_target="tpu_custom_call" | custom-call | flops 4000000 | bytes 4000000 | tf_op jit(solution)/shard_map/band_matrices/pallas_call | solution.py:134
  17.0 2.1 %collective-permute-done.2.high_l.high_c.high_r = f32[16,4096]{1,0:T(8,128)S(1)} collective-permute-done((f32[16,4096]{1,0:T(8,128)S(1)}, f32[16,4096]{1,0:T(8,128)S(1)}, u32[]{:S(2)}, u32[]{:S(2)}) %collective-permute-start.2) | collective-permute-done | bytes 262176 | tf_op jit(solution)/shard_map/ppermute | solution.py:433
  19.0 4.5 %warp_filter.4 = (bf16[128,1024]{1,0:T(8,128)(2,1)S(1)}, bf16[128,1024]{1,0:T(8,128)(2,1)S(1)}, bf16[128,1024]{1,0:T(8,128)(2,1)S(1)}, bf16[128,1024]{1,0:T(8,128)(2,1)S(1)}) custom-call(f32[1]{0:T(128)} %convert_element_type.45.weight, f32[16,4096]{1,0:T(8,128)S(1)} %collective-permute-done.1.low_l.low_c.low_r, ...), custom_call_target="tpu_custom_call" | custom-call | flops 2147483648 | bytes 3145728 | tf_op jit(solution)/shard_map/warp_filter/pallas_call | solution.py:238
  23.5 1.6 %collective-permute-start.3 = (bf16[128,1024]{1,0:T(8,128)(2,1)S(1)}, bf16[128,1024]{1,0:T(8,128)(2,1)S(1)}, u32[]{:S(2)}, u32[]{:S(2)}) collective-permute-start(bf16[128,1024]{1,0:T(8,128)(2,1)S(1)} %get-tuple-element.42), channel_id=1, source_target_pairs={{0,8},{8,0},{16,24},{24,16},{1,9},{9,1},{17,25},{25,17},{2,10},{10... | collective-permute-start | bytes 786440 | tf_op jit(solution)/shard_map/ppermute | solution.py:397
  25.2 0.8 collective-permute-start.4
  26.0 1.6 %collective-permute-start.14 = (f32[2,3]{1,0:T(2,128)S(1)}, f32[2,3]{1,0:T(2,128)S(1)}, u32[]{:S(2)}, u32[]{:S(2)}) collective-permute-start(f32[2,3]{1,0:T(2,128)S(1)} %pad_maximum_fusion.2), channel_id=1, source_target_pairs={{0,2},{2,0},{4,6},{6,4},{1,3},{3,1},{5,7},{7,5},{8,10},{10,8},{12,... | collective-permute-start | bytes 80 | tf_op jit(solution)/shard_map/ppermute | solution.py:397
  27.6 1.1 collective-permute-start.5
  28.7 4.5 %warp_filter.5 = (bf16[128,1024]{1,0:T(8,128)(2,1)S(1)}, bf16[128,1024]{1,0:T(8,128)(2,1)S(1)}, bf16[128,1024]{1,0:T(8,128)(2,1)S(1)}, bf16[128,1024]{1,0:T(8,128)(2,1)S(1)}) custom-call(f32[1]{0:T(128)} %convert_element_type.45.weight, f32[16,4096]{1,0:T(8,128)S(1)} %collective-permute-done.1.low_l.low_c.low_r, ...), custom_call_target="tpu_custom_call" | custom-call | flops 2147483648 | bytes 3145728 | tf_op jit(solution)/shard_map/warp_filter/pallas_call | solution.py:238
  33.3 1.6 %collective-permute-start.16 = (bf16[128,1024]{1,0:T(8,128)(2,1)S(1)}, bf16[128,1024]{1,0:T(8,128)(2,1)S(1)}, u32[]{:S(2)}, u32[]{:S(2)}) collective-permute-start(bf16[128,1024]{1,0:T(8,128)(2,1)S(1)} %get-tuple-element.50), channel_id=1, source_target_pairs={{0,8},{8,0},{16,24},{24,16},{1,9},{9,1},{17,25},{25,17},{2,10},{10... | collective-permute-start | bytes 786440 | tf_op jit(solution)/shard_map/ppermute | solution.py:397
  34.9 0.8 collective-permute-start.17
  35.8 2.4 %collective-permute-done.4.rest_2_ = bf16[128,1024]{1,0:T(8,128)(2,1)S(1)} collective-permute-done((bf16[128,1024]{1,0:T(8,128)(2,1)S(1)}, bf16[128,1024]{1,0:T(8,128)(2,1)S(1)}, u32[]{:S(2)}, u32[]{:S(2)}) %collective-permute-start.4) | collective-permute-done | bytes 262176 | tf_op jit(solution)/shard_map/ppermute | solution.py:397
  38.1 3.3 %collective-permute-start.18 = (bf16[128,1024]{1,0:T(8,128)(2,1)S(1)}, bf16[128,1024]{1,0:T(8,128)(2,1)S(1)}, u32[]{:S(2)}, u32[]{:S(2)}) collective-permute-start(bf16[128,1024]{1,0:T(8,128)(2,1)S(1)} %get-tuple-element.52), channel_id=1, source_target_pairs={{0,24},{8,16},{16,8},{24,0},{1,25},{9,17},{17,9},{25,1},{2,26},{10... | collective-permute-start | bytes 786440 | tf_op jit(solution)/shard_map/ppermute | solution.py:397
  41.4 4.5 %warp_filter.6 = (bf16[128,1024]{1,0:T(8,128)(2,1)S(1)}, bf16[128,1024]{1,0:T(8,128)(2,1)S(1)}, bf16[128,1024]{1,0:T(8,128)(2,1)S(1)}, bf16[128,1024]{1,0:T(8,128)(2,1)S(1)}) custom-call(f32[1]{0:T(128)} %convert_element_type.45.weight, f32[16,4096]{1,0:T(8,128)S(1)} %collective-permute-done.1.low_l.low_c.low_r, ...), custom_call_target="tpu_custom_call" | custom-call | flops 2147483648 | bytes 3145728 | tf_op jit(solution)/shard_map/warp_filter/pallas_call | solution.py:238
  45.9 0.8 collective-permute-start.26
  46.7 4.6 %warp_filter.7 = (bf16[128,1024]{1,0:T(8,128)(2,1)S(1)}, bf16[128,1024]{1,0:T(8,128)(2,1)S(1)}, bf16[128,1024]{1,0:T(8,128)(2,1)S(1)}, bf16[128,1024]{1,0:T(8,128)(2,1)S(1)}) custom-call(f32[1]{0:T(128)} %convert_element_type.45.weight, f32[16,4096]{1,0:T(8,128)S(1)} %collective-permute-done.1.low_l.low_c.low_r, ...), custom_call_target="tpu_custom_call" | custom-call | flops 2147483648 | bytes 3145728 | tf_op jit(solution)/shard_map/warp_filter/pallas_call | solution.py:238
  51.3 2.8 %collective-permute-start.28 = (bf16[128,1024]{1,0:T(8,128)(2,1)S(1)}, bf16[128,1024]{1,0:T(8,128)(2,1)S(1)}, u32[]{:S(2)}, u32[]{:S(2)}) collective-permute-start(bf16[128,1024]{1,0:T(8,128)(2,1)S(1)} %get-tuple-element.60), channel_id=1, source_target_pairs={{0,24},{8,16},{16,8},{24,0},{1,25},{9,17},{17,9},{25,1},{2,26},{10... | collective-permute-start | bytes 786440 | tf_op jit(solution)/shard_map/ppermute | solution.py:397
  54.1 0.8 collective-permute-start.36
  54.9 1.5 %collective-permute-start.37 = (bf16[128,1024]{1,0:T(8,128)(2,1)S(1)}, bf16[128,1024]{1,0:T(8,128)(2,1)S(1)}, u32[]{:S(2)}, u32[]{:S(2)}) collective-permute-start(bf16[128,1024]{1,0:T(8,128)(2,1)S(1)} %get-tuple-element.67), channel_id=1, source_target_pairs={{0,16},{8,24},{16,0},{24,8},{1,17},{9,25},{17,1},{25,9},{2,18},{10... | collective-permute-start | bytes 786440 | tf_op jit(solution)/shard_map/ppermute | solution.py:397
  56.4 5.1 %collective-permute-done.27.rest_2_ = bf16[128,1024]{1,0:T(8,128)(2,1)S(1)} collective-permute-done((bf16[128,1024]{1,0:T(8,128)(2,1)S(1)}, bf16[128,1024]{1,0:T(8,128)(2,1)S(1)}, u32[]{:S(2)}, u32[]{:S(2)}) %collective-permute-start.27) | collective-permute-done | bytes 262176 | tf_op jit(solution)/shard_map/ppermute | solution.py:397
  61.5 0.5 collective-permute-start.8
  62.0 5.6 %collective-permute-done.36.rest_1_ = bf16[128,1024]{1,0:T(8,128)(2,1)S(1)} collective-permute-done((bf16[128,1024]{1,0:T(8,128)(2,1)S(1)}, bf16[128,1024]{1,0:T(8,128)(2,1)S(1)}, u32[]{:S(2)}, u32[]{:S(2)}) %collective-permute-start.36) | collective-permute-done | bytes 262176 | tf_op jit(solution)/shard_map/ppermute | solution.py:397
  67.6 5.0 %collective-permute-done.37.rest_2_ = bf16[128,1024]{1,0:T(8,128)(2,1)S(1)} collective-permute-done((bf16[128,1024]{1,0:T(8,128)(2,1)S(1)}, bf16[128,1024]{1,0:T(8,128)(2,1)S(1)}, u32[]{:S(2)}, u32[]{:S(2)}) %collective-permute-start.37) | collective-permute-done | bytes 262176 | tf_op jit(solution)/shard_map/ppermute | solution.py:397
  75.8 3.6 %pair_sum.4 = (bf16[160,512]{1,0:T(8,128)(2,1)S(1)}, bf16[160,512]{1,0:T(8,128)(2,1)S(1)}, bf16[160,512]{1,0:T(8,128)(2,1)S(1)}, bf16[160,512]{1,0:T(8,128)(2,1)S(1)}) custom-call(s32[3]{0:T(128)S(1)} %pad_add_fusion.place, s32[1]{0:T(128)S(6)} %copy.15.offset, s32[1]{0:T(128)} %collective-permute-done.other_offset, s32[160]{0:T(256)S(1)} %copy-done.2, ...), custom_call_target="tpu_custom_call" | custom-call | flops 2621440 | bytes 2752512 | tf_op jit(solution)/shard_map/pair_sum/pallas_call | solution.py:311
  79.4 1.8 %collective-permute-start.11 = (bf16[160,512]{1,0:T(8,128)(2,1)S(1)}, bf16[160,512]{1,0:T(8,128)(2,1)S(1)}, u32[]{:S(2)}, u32[]{:S(2)}) collective-permute-start(bf16[160,512]{1,0:T(8,128)(2,1)S(1)} %get-tuple-element.48), channel_id=1, source_target_pairs={{0,2},{2,0},{4,6},{6,4},{1,3},{3,1},{5,7},{7,5},{8,10},{10,8},{12,... | collective-permute-start | bytes 491528 | tf_op jit(solution)/shard_map/ppermute | solution.py:397
  81.3 3.6 %pair_sum.5 = (bf16[160,512]{1,0:T(8,128)(2,1)S(1)}, bf16[160,512]{1,0:T(8,128)(2,1)S(1)}, bf16[160,512]{1,0:T(8,128)(2,1)S(1)}, bf16[160,512]{1,0:T(8,128)(2,1)S(1)}) custom-call(s32[3]{0:T(128)S(1)} %pad_add_fusion.place, s32[1]{0:T(128)S(6)} %copy.15.offset, s32[1]{0:T(128)} %collective-permute-done.other_offset, s32[160]{0:T(256)S(1)} %copy-done.2, ...), custom_call_target="tpu_custom_call" | custom-call | flops 2621440 | bytes 2752512 | tf_op jit(solution)/shard_map/pair_sum/pallas_call | solution.py:311
  84.9 3.6 %pair_sum.6 = (bf16[160,512]{1,0:T(8,128)(2,1)S(1)}, bf16[160,512]{1,0:T(8,128)(2,1)S(1)}, bf16[160,512]{1,0:T(8,128)(2,1)S(1)}, bf16[160,512]{1,0:T(8,128)(2,1)S(1)}) custom-call(s32[3]{0:T(128)S(1)} %pad_add_fusion.place, s32[1]{0:T(128)S(6)} %copy.15.offset, s32[1]{0:T(128)} %collective-permute-done.other_offset, s32[160]{0:T(256)S(1)} %copy-done.2, ...), custom_call_target="tpu_custom_call" | custom-call | flops 2621440 | bytes 2752512 | tf_op jit(solution)/shard_map/pair_sum/pallas_call | solution.py:311
  88.5 2.6 %collective-permute-start.15 = (f32[4,3]{1,0:T(4,128)S(1)}, f32[4,3]{1,0:T(4,128)S(1)}, u32[]{:S(2)}, u32[]{:S(2)}) collective-permute-start(f32[4,3]{1,0:T(4,128)S(1)} %pad_maximum_fusion.1), channel_id=1, source_target_pairs={{0,4},{2,6},{4,0},{6,2},{1,5},{3,7},{5,1},{7,3},{8,12},{10,14},{12... | collective-permute-start | bytes 152 | tf_op jit(solution)/shard_map/ppermute | solution.py:397
  91.5 1.7 %collective-permute-start.33 = (bf16[160,512]{1,0:T(8,128)(2,1)S(1)}, bf16[160,512]{1,0:T(8,128)(2,1)S(1)}, u32[]{:S(2)}, u32[]{:S(2)}) collective-permute-start(bf16[160,512]{1,0:T(8,128)(2,1)S(1)} %get-tuple-element.62), channel_id=1, source_target_pairs={{0,2},{2,0},{4,6},{6,4},{1,3},{3,1},{5,7},{7,5},{8,10},{10,8},{12,... | collective-permute-start | bytes 491528 | tf_op jit(solution)/shard_map/ppermute | solution.py:397
  93.5 3.6 %pair_sum.7 = (bf16[160,512]{1,0:T(8,128)(2,1)S(1)}, bf16[160,512]{1,0:T(8,128)(2,1)S(1)}, bf16[160,512]{1,0:T(8,128)(2,1)S(1)}, bf16[160,512]{1,0:T(8,128)(2,1)S(1)}) custom-call(s32[3]{0:T(128)S(1)} %pad_add_fusion.place, s32[1]{0:T(128)S(6)} %copy.15.offset, s32[1]{0:T(128)} %collective-permute-done.other_offset, s32[160]{0:T(256)S(1)} %copy-done.2, ...), custom_call_target="tpu_custom_call" | custom-call | flops 2621440 | bytes 2752512 | tf_op jit(solution)/shard_map/pair_sum/pallas_call | solution.py:311
  97.2 1.8 %collective-permute-start.43 = (bf16[160,512]{1,0:T(8,128)(2,1)S(1)}, bf16[160,512]{1,0:T(8,128)(2,1)S(1)}, u32[]{:S(2)}, u32[]{:S(2)}) collective-permute-start(bf16[160,512]{1,0:T(8,128)(2,1)S(1)} %get-tuple-element.70), channel_id=1, source_target_pairs={{0,2},{2,0},{4,6},{6,4},{1,3},{3,1},{5,7},{7,5},{8,10},{10,8},{12,... | collective-permute-start | bytes 491528 | tf_op jit(solution)/shard_map/ppermute | solution.py:397
  99.0 6.3 %collective-permute-done.34 = bf16[160,512]{1,0:T(8,128)(2,1)S(1)} collective-permute-done((bf16[160,512]{1,0:T(8,128)(2,1)S(1)}, bf16[160,512]{1,0:T(8,128)(2,1)S(1)}, u32[]{:S(2)}, u32[]{:S(2)}) %collective-permute-start.34) | collective-permute-done | bytes 163872 | tf_op jit(solution)/shard_map/ppermute | solution.py:397
  105.7 5.5 %collective-permute-done.44 = bf16[160,512]{1,0:T(8,128)(2,1)S(1)} collective-permute-done((bf16[160,512]{1,0:T(8,128)(2,1)S(1)}, bf16[160,512]{1,0:T(8,128)(2,1)S(1)}, u32[]{:S(2)}, u32[]{:S(2)}) %collective-permute-start.44) | collective-permute-done | bytes 163872 | tf_op jit(solution)/shard_map/ppermute | solution.py:397
  111.5 2.6 %collective-permute-start.45 = (bf16[160,512]{1,0:T(8,128)(2,1)S(1)}, bf16[160,512]{1,0:T(8,128)(2,1)S(1)}, u32[]{:S(2)}, u32[]{:S(2)}) collective-permute-start(bf16[160,512]{1,0:T(8,128)(2,1)S(1)} %add_convert_fusion), channel_id=1, source_target_pairs={{0,4},{2,6},{4,0},{6,2},{1,5},{3,7},{5,1},{7,3},{8,12},{10,14},{12... | collective-permute-start | bytes 491528 | tf_op jit(solution)/shard_map/ppermute | solution.py:397
  115.0 1.7 %collective-permute-start.10 = (bf16[160,512]{1,0:T(8,128)(2,1)S(1)}, bf16[160,512]{1,0:T(8,128)(2,1)S(1)}, u32[]{:S(2)}, u32[]{:S(2)}) collective-permute-start(bf16[160,512]{1,0:T(8,128)(2,1)S(1)} %get-tuple-element.46), channel_id=1, source_target_pairs={{0,2},{2,0},{4,6},{6,4},{1,3},{3,1},{5,7},{7,5},{8,10},{10,8},{12,... | collective-permute-start | bytes 491528 | tf_op jit(solution)/shard_map/ppermute | solution.py:397
  116.7 14.7 %collective-permute-done.45.refs_2_ = bf16[160,512]{1,0:T(8,128)(2,1)S(1)} collective-permute-done((bf16[160,512]{1,0:T(8,128)(2,1)S(1)}, bf16[160,512]{1,0:T(8,128)(2,1)S(1)}, u32[]{:S(2)}, u32[]{:S(2)}) %collective-permute-start.45) | collective-permute-done | bytes 163872 | tf_op jit(solution)/shard_map/ppermute | solution.py:397
  131.4 0.7 pad_maximum_fusion.facts
  132.1 4.3 %patch_weights.1.refs_3_ = f32[160,2048]{1,0:T(8,128)} custom-call(s32[3]{0:T(128)} %copy-done.3, s32[160]{0:T(256)} %sites.9, f32[8,3]{1,0:T(8,128)} %pad_maximum_fusion.facts), custom_call_target="tpu_custom_call" | custom-call | flops 13107200 | bytes 1310720 | tf_op jit(solution)/shard_map/patch_weights/pallas_call | solution.py:350
  136.3 1.3 copy-done
  137.7 0.8 patch_mean.4.refs_4_
  138.5 0.8 patch_mean.5.refs_4_
  139.3 0.8 patch_mean.6.refs_4_
  140.1 1.2 collective-permute-done.12.refs_2_
  141.3 0.8 patch_mean.7
  (80 shorter events, 6.6 us)
Async XLA Ops:
  1.1 15.9 %collective-permute-start.1 = (f32[16,4096]{1,0:T(8,128)S(1)}, f32[16,4096]{1,0:T(8,128)S(1)}, u32[]{:S(2)}, u32[]{:S(2)}) collective-permute-start(f32[16,4096]{1,0:T(8,128)S(1)} %get-tuple-element.74), channel_id=1, source_target_pairs={{0,8},{8,16},{16,24},{1,9},{9,17},{17,25},{2,10},{10,18},{18,26},{... | collective-permute-start | bytes 786440 | tf_op jit(solution)/shard_map/ppermute | solution.py:432
  5.9 13.1 %collective-permute-start.2 = (f32[16,4096]{1,0:T(8,128)S(1)}, f32[16,4096]{1,0:T(8,128)S(1)}, u32[]{:S(2)}, u32[]{:S(2)}) collective-permute-start(f32[16,4096]{1,0:T(8,128)S(1)} %get-tuple-element.73), channel_id=1, source_target_pairs={{8,0},{16,8},{24,16},{9,1},{17,9},{25,17},{10,2},{18,10},{26,18},{... | collective-permute-start | bytes 786440 | tf_op jit(solution)/shard_map/ppermute | solution.py:433
  7.2 26.0 %collective-permute-start = (s32[1]{0:T(128)}, s32[1]{0:T(128)}, u32[]{:S(2)}, u32[]{:S(2)}) collective-permute-start(s32[1]{0:T(128)} %param.11), channel_id=1, source_target_pairs={{0,1},{1,0},{2,3},{3,2},{4,5},{5,4},{6,7},{7,6},{8,9},{9,8},{10,11... | collective-permute-start | bytes 20 | tf_op jit(solution)/shard_map/ppermute | solution.py:397
  9.4 15.7 %collective-permute-start.13 = (f32[1,3]{1,0:T(1,128)S(1)}, f32[1,3]{1,0:T(1,128)S(1)}, u32[]{:S(2)}, u32[]{:S(2)}) collective-permute-start(f32[1,3]{1,0:T(1,128)S(1)} %pad_maximum_fusion.3), channel_id=1, source_target_pairs={{0,1},{1,0},{2,3},{3,2},{4,5},{5,4},{6,7},{7,6},{8,9},{9,8},{10,11... | collective-permute-start | bytes 44 | tf_op jit(solution)/shard_map/ppermute | solution.py:397
  9.9 83.6 %copy-start.3 = (s32[3]{0:T(128)}, s32[3]{0:T(128)S(1)}, u32[]{:S(2)}) copy-start(s32[3]{0:T(128)S(1)} %pad_add_fusion.place) | copy-start | bytes 40
  23.5 11.4 %collective-permute-start.3 = (bf16[128,1024]{1,0:T(8,128)(2,1)S(1)}, bf16[128,1024]{1,0:T(8,128)(2,1)S(1)}, u32[]{:S(2)}, u32[]{:S(2)}) collective-permute-start(bf16[128,1024]{1,0:T(8,128)(2,1)S(1)} %get-tuple-element.42), channel_id=1, source_target_pairs={{0,8},{8,0},{16,24},{24,16},{1,9},{9,1},{17,25},{25,17},{2,10},{10... | collective-permute-start | bytes 786440 | tf_op jit(solution)/shard_map/ppermute | solution.py:397
  25.2 13.0 %collective-permute-start.4 = (bf16[128,1024]{1,0:T(8,128)(2,1)S(1)}, bf16[128,1024]{1,0:T(8,128)(2,1)S(1)}, u32[]{:S(2)}, u32[]{:S(2)}) collective-permute-start(bf16[128,1024]{1,0:T(8,128)(2,1)S(1)} %get-tuple-element.43), channel_id=1, source_target_pairs={{0,16},{8,24},{16,0},{24,8},{1,17},{9,25},{17,1},{25,9},{2,18},{10... | collective-permute-start | bytes 786440 | tf_op jit(solution)/shard_map/ppermute | solution.py:397
  26.0 7.3 %collective-permute-start.14 = (f32[2,3]{1,0:T(2,128)S(1)}, f32[2,3]{1,0:T(2,128)S(1)}, u32[]{:S(2)}, u32[]{:S(2)}) collective-permute-start(f32[2,3]{1,0:T(2,128)S(1)} %pad_maximum_fusion.2), channel_id=1, source_target_pairs={{0,2},{2,0},{4,6},{6,4},{1,3},{3,1},{5,7},{7,5},{8,10},{10,8},{12,... | collective-permute-start | bytes 80 | tf_op jit(solution)/shard_map/ppermute | solution.py:397
  27.6 13.8 %collective-permute-start.5 = (bf16[128,1024]{1,0:T(8,128)(2,1)S(1)}, bf16[128,1024]{1,0:T(8,128)(2,1)S(1)}, u32[]{:S(2)}, u32[]{:S(2)}) collective-permute-start(bf16[128,1024]{1,0:T(8,128)(2,1)S(1)} %get-tuple-element.44), channel_id=1, source_target_pairs={{0,24},{8,16},{16,8},{24,0},{1,25},{9,17},{17,9},{25,1},{2,26},{10... | collective-permute-start | bytes 786440 | tf_op jit(solution)/shard_map/ppermute | solution.py:397
  33.3 12.7 %collective-permute-start.6 = (bf16[128,1024]{1,0:T(8,128)(2,1)S(1)}, bf16[128,1024]{1,0:T(8,128)(2,1)S(1)}, u32[]{:S(2)}, u32[]{:S(2)}) collective-permute-start(bf16[128,1024]{1,0:T(8,128)(2,1)S(1)} %get-tuple-element.41.rest_0_), channel_id=1, source_target_pairs={{0,1},{1,0},{2,3},{3,2},{4,5},{5,4},{6,7},{7,6},{8,9},{9,8},{10,11... | collective-permute-start | bytes 786440 | tf_op jit(solution)/shard_map/ppermute | solution.py:397
  33.3 13.3 %collective-permute-start.16 = (bf16[128,1024]{1,0:T(8,128)(2,1)S(1)}, bf16[128,1024]{1,0:T(8,128)(2,1)S(1)}, u32[]{:S(2)}, u32[]{:S(2)}) collective-permute-start(bf16[128,1024]{1,0:T(8,128)(2,1)S(1)} %get-tuple-element.50), channel_id=1, source_target_pairs={{0,8},{8,0},{16,24},{24,16},{1,9},{9,1},{17,25},{25,17},{2,10},{10... | collective-permute-start | bytes 786440 | tf_op jit(solution)/shard_map/ppermute | solution.py:397
  34.9 16.4 %collective-permute-start.17 = (bf16[128,1024]{1,0:T(8,128)(2,1)S(1)}, bf16[128,1024]{1,0:T(8,128)(2,1)S(1)}, u32[]{:S(2)}, u32[]{:S(2)}) collective-permute-start(bf16[128,1024]{1,0:T(8,128)(2,1)S(1)} %get-tuple-element.51), channel_id=1, source_target_pairs={{0,16},{8,24},{16,0},{24,8},{1,17},{9,25},{17,1},{25,9},{2,18},{10... | collective-permute-start | bytes 786440 | tf_op jit(solution)/shard_map/ppermute | solution.py:397
  38.1 16.0 %collective-permute-start.18 = (bf16[128,1024]{1,0:T(8,128)(2,1)S(1)}, bf16[128,1024]{1,0:T(8,128)(2,1)S(1)}, u32[]{:S(2)}, u32[]{:S(2)}) collective-permute-start(bf16[128,1024]{1,0:T(8,128)(2,1)S(1)} %get-tuple-element.52), channel_id=1, source_target_pairs={{0,24},{8,16},{16,8},{24,0},{1,25},{9,17},{17,9},{25,1},{2,26},{10... | collective-permute-start | bytes 786440 | tf_op jit(solution)/shard_map/ppermute | solution.py:397
  41.4 12.7 %collective-permute-start.19 = (bf16[128,1024]{1,0:T(8,128)(2,1)S(1)}, bf16[128,1024]{1,0:T(8,128)(2,1)S(1)}, u32[]{:S(2)}, u32[]{:S(2)}) collective-permute-start(bf16[128,1024]{1,0:T(8,128)(2,1)S(1)} %get-tuple-element.49.rest_0_), channel_id=1, source_target_pairs={{0,1},{1,0},{2,3},{3,2},{4,5},{5,4},{6,7},{7,6},{8,9},{9,8},{10,11... | collective-permute-start | bytes 786440 | tf_op jit(solution)/shard_map/ppermute | solution.py:397
  45.9 8.9 %collective-permute-start.26 = (bf16[128,1024]{1,0:T(8,128)(2,1)S(1)}, bf16[128,1024]{1,0:T(8,128)(2,1)S(1)}, u32[]{:S(2)}, u32[]{:S(2)}) collective-permute-start(bf16[128,1024]{1,0:T(8,128)(2,1)S(1)} %get-tuple-element.58), channel_id=1, source_target_pairs={{0,8},{8,0},{16,24},{24,16},{1,9},{9,1},{17,25},{25,17},{2,10},{10... | collective-permute-start | bytes 786440 | tf_op jit(solution)/shard_map/ppermute | solution.py:397
  46.7 29.1 %copy-start.2 = (s32[160]{0:T(256)S(1)}, s32[160]{0:T(256)}, u32[]{:S(2)}) copy-start(s32[160]{0:T(256)} %sites.9) | copy-start | bytes 1924
  46.7 14.8 %collective-permute-start.27 = (bf16[128,1024]{1,0:T(8,128)(2,1)S(1)}, bf16[128,1024]{1,0:T(8,128)(2,1)S(1)}, u32[]{:S(2)}, u32[]{:S(2)}) collective-permute-start(bf16[128,1024]{1,0:T(8,128)(2,1)S(1)} %get-tuple-element.59), channel_id=1, source_target_pairs={{0,16},{8,24},{16,0},{24,8},{1,17},{9,25},{17,1},{25,9},{2,18},{10... | collective-permute-start | bytes 786440 | tf_op jit(solution)/shard_map/ppermute | solution.py:397
  51.3 10.2 %collective-permute-start.28 = (bf16[128,1024]{1,0:T(8,128)(2,1)S(1)}, bf16[128,1024]{1,0:T(8,128)(2,1)S(1)}, u32[]{:S(2)}, u32[]{:S(2)}) collective-permute-start(bf16[128,1024]{1,0:T(8,128)(2,1)S(1)} %get-tuple-element.60), channel_id=1, source_target_pairs={{0,24},{8,16},{16,8},{24,0},{1,25},{9,17},{17,9},{25,1},{2,26},{10... | collective-permute-start | bytes 786440 | tf_op jit(solution)/shard_map/ppermute | solution.py:397
  54.1 7.4 %collective-permute-start.29 = (bf16[128,1024]{1,0:T(8,128)(2,1)S(1)}, bf16[128,1024]{1,0:T(8,128)(2,1)S(1)}, u32[]{:S(2)}, u32[]{:S(2)}) collective-permute-start(bf16[128,1024]{1,0:T(8,128)(2,1)S(1)} %get-tuple-element.57.rest_0_), channel_id=1, source_target_pairs={{0,1},{1,0},{2,3},{3,2},{4,5},{5,4},{6,7},{7,6},{8,9},{9,8},{10,11... | collective-permute-start | bytes 786440 | tf_op jit(solution)/shard_map/ppermute | solution.py:397
  54.1 13.5 %collective-permute-start.36 = (bf16[128,1024]{1,0:T(8,128)(2,1)S(1)}, bf16[128,1024]{1,0:T(8,128)(2,1)S(1)}, u32[]{:S(2)}, u32[]{:S(2)}) collective-permute-start(bf16[128,1024]{1,0:T(8,128)(2,1)S(1)} %get-tuple-element.66), channel_id=1, source_target_pairs={{0,8},{8,0},{16,24},{24,16},{1,9},{9,1},{17,25},{25,17},{2,10},{10... | collective-permute-start | bytes 786440 | tf_op jit(solution)/shard_map/ppermute | solution.py:397
  54.9 17.7 %collective-permute-start.37 = (bf16[128,1024]{1,0:T(8,128)(2,1)S(1)}, bf16[128,1024]{1,0:T(8,128)(2,1)S(1)}, u32[]{:S(2)}, u32[]{:S(2)}) collective-permute-start(bf16[128,1024]{1,0:T(8,128)(2,1)S(1)} %get-tuple-element.67), channel_id=1, source_target_pairs={{0,16},{8,24},{16,0},{24,8},{1,17},{9,25},{17,1},{25,9},{2,18},{10... | collective-permute-start | bytes 786440 | tf_op jit(solution)/shard_map/ppermute | solution.py:397
  61.5 11.1 %collective-permute-start.38 = (bf16[128,1024]{1,0:T(8,128)(2,1)S(1)}, bf16[128,1024]{1,0:T(8,128)(2,1)S(1)}, u32[]{:S(2)}, u32[]{:S(2)}) collective-permute-start(bf16[128,1024]{1,0:T(8,128)(2,1)S(1)} %get-tuple-element.68), channel_id=1, source_target_pairs={{0,24},{8,16},{16,8},{24,0},{1,25},{9,17},{17,9},{25,1},{2,26},{10... | collective-permute-start | bytes 786440 | tf_op jit(solution)/shard_map/ppermute | solution.py:397
  61.5 11.6 %collective-permute-start.7 = (bf16[128,1024]{1,0:T(8,128)(2,1)S(1)}, bf16[128,1024]{1,0:T(8,128)(2,1)S(1)}, u32[]{:S(2)}, u32[]{:S(2)}) collective-permute-start(bf16[128,1024]{1,0:T(8,128)(2,1)S(1)} %collective-permute-done.3.rest_1_), channel_id=1, source_target_pairs={{0,1},{1,0},{2,3},{3,2},{4,5},{5,4},{6,7},{7,6},{8,9},{9,8},{10,11... | collective-permute-start | bytes 786440 | tf_op jit(solution)/shard_map/ppermute | solution.py:397
  61.5 11.7 %collective-permute-start.8 = (bf16[128,1024]{1,0:T(8,128)(2,1)S(1)}, bf16[128,1024]{1,0:T(8,128)(2,1)S(1)}, u32[]{:S(2)}, u32[]{:S(2)}) collective-permute-start(bf16[128,1024]{1,0:T(8,128)(2,1)S(1)} %collective-permute-done.4.rest_2_), channel_id=1, source_target_pairs={{0,1},{1,0},{2,3},{3,2},{4,5},{5,4},{6,7},{7,6},{8,9},{9,8},{10,11... | collective-permute-start | bytes 786440 | tf_op jit(solution)/shard_map/ppermute | solution.py:397
  67.6 6.0 %collective-permute-start.9 = (bf16[128,1024]{1,0:T(8,128)(2,1)S(1)}, bf16[128,1024]{1,0:T(8,128)(2,1)S(1)}, u32[]{:S(2)}, u32[]{:S(2)}) collective-permute-start(bf16[128,1024]{1,0:T(8,128)(2,1)S(1)} %collective-permute-done.5.rest_3_), channel_id=1, source_target_pairs={{0,1},{1,0},{2,3},{3,2},{4,5},{5,4},{6,7},{7,6},{8,9},{9,8},{10,11... | collective-permute-start | bytes 786440 | tf_op jit(solution)/shard_map/ppermute | solution.py:397
  72.6 1.5 %collective-permute-start.20 = (bf16[128,1024]{1,0:T(8,128)(2,1)S(1)}, bf16[128,1024]{1,0:T(8,128)(2,1)S(1)}, u32[]{:S(2)}, u32[]{:S(2)}) collective-permute-start(bf16[128,1024]{1,0:T(8,128)(2,1)S(1)} %collective-permute-done.16.rest_1_), channel_id=1, source_target_pairs={{0,1},{1,0},{2,3},{3,2},{4,5},{5,4},{6,7},{7,6},{8,9},{9,8},{10,11... | collective-permute-start | bytes 786440 | tf_op jit(solution)/shard_map/ppermute | solution.py:397
  72.6 1.9 %collective-permute-start.21 = (bf16[128,1024]{1,0:T(8,128)(2,1)S(1)}, bf16[128,1024]{1,0:T(8,128)(2,1)S(1)}, u32[]{:S(2)}, u32[]{:S(2)}) collective-permute-start(bf16[128,1024]{1,0:T(8,128)(2,1)S(1)} %collective-permute-done.17.rest_2_), channel_id=1, source_target_pairs={{0,1},{1,0},{2,3},{3,2},{4,5},{5,4},{6,7},{7,6},{8,9},{9,8},{10,11... | collective-permute-start | bytes 786440 | tf_op jit(solution)/shard_map/ppermute | solution.py:397
  73.1 1.8 %collective-permute-start.22 = (bf16[128,1024]{1,0:T(8,128)(2,1)S(1)}, bf16[128,1024]{1,0:T(8,128)(2,1)S(1)}, u32[]{:S(2)}, u32[]{:S(2)}) collective-permute-start(bf16[128,1024]{1,0:T(8,128)(2,1)S(1)} %collective-permute-done.18.rest_3_), channel_id=1, source_target_pairs={{0,1},{1,0},{2,3},{3,2},{4,5},{5,4},{6,7},{7,6},{8,9},{9,8},{10,11... | collective-permute-start | bytes 786440 | tf_op jit(solution)/shard_map/ppermute | solution.py:397
  73.2 2.1 %collective-permute-start.30 = (bf16[128,1024]{1,0:T(8,128)(2,1)S(1)}, bf16[128,1024]{1,0:T(8,128)(2,1)S(1)}, u32[]{:S(2)}, u32[]{:S(2)}) collective-permute-start(bf16[128,1024]{1,0:T(8,128)(2,1)S(1)} %collective-permute-done.26.rest_1_), channel_id=1, source_target_pairs={{0,1},{1,0},{2,3},{3,2},{4,5},{5,4},{6,7},{7,6},{8,9},{9,8},{10,11... | collective-permute-start | bytes 786440 | tf_op jit(solution)/shard_map/ppermute | solution.py:397
  73.6 2.0 %collective-permute-start.31 = (bf16[128,1024]{1,0:T(8,128)(2,1)S(1)}, bf16[128,1024]{1,0:T(8,128)(2,1)S(1)}, u32[]{:S(2)}, u32[]{:S(2)}) collective-permute-start(bf16[128,1024]{1,0:T(8,128)(2,1)S(1)} %collective-permute-done.27.rest_2_), channel_id=1, source_target_pairs={{0,1},{1,0},{2,3},{3,2},{4,5},{5,4},{6,7},{7,6},{8,9},{9,8},{10,11... | collective-permute-start | bytes 786440 | tf_op jit(solution)/shard_map/ppermute | solution.py:397
  74.1 5.3 %collective-permute-start.32 = (bf16[128,1024]{1,0:T(8,128)(2,1)S(1)}, bf16[128,1024]{1,0:T(8,128)(2,1)S(1)}, u32[]{:S(2)}, u32[]{:S(2)}) collective-permute-start(bf16[128,1024]{1,0:T(8,128)(2,1)S(1)} %collective-permute-done.28.rest_3_), channel_id=1, source_target_pairs={{0,1},{1,0},{2,3},{3,2},{4,5},{5,4},{6,7},{7,6},{8,9},{9,8},{10,11... | collective-permute-start | bytes 786440 | tf_op jit(solution)/shard_map/ppermute | solution.py:397
  74.5 14.0 %collective-permute-start.39 = (bf16[128,1024]{1,0:T(8,128)(2,1)S(1)}, bf16[128,1024]{1,0:T(8,128)(2,1)S(1)}, u32[]{:S(2)}, u32[]{:S(2)}) collective-permute-start(bf16[128,1024]{1,0:T(8,128)(2,1)S(1)} %get-tuple-element.65.rest_0_), channel_id=1, source_target_pairs={{0,1},{1,0},{2,3},{3,2},{4,5},{5,4},{6,7},{7,6},{8,9},{9,8},{10,11... | collective-permute-start | bytes 786440 | tf_op jit(solution)/shard_map/ppermute | solution.py:397
  74.9 16.3 %collective-permute-start.40 = (bf16[128,1024]{1,0:T(8,128)(2,1)S(1)}, bf16[128,1024]{1,0:T(8,128)(2,1)S(1)}, u32[]{:S(2)}, u32[]{:S(2)}) collective-permute-start(bf16[128,1024]{1,0:T(8,128)(2,1)S(1)} %collective-permute-done.36.rest_1_), channel_id=1, source_target_pairs={{0,1},{1,0},{2,3},{3,2},{4,5},{5,4},{6,7},{7,6},{8,9},{9,8},{10,11... | collective-permute-start | bytes 786440 | tf_op jit(solution)/shard_map/ppermute | solution.py:397
  75.3 16.2 %collective-permute-start.41 = (bf16[128,1024]{1,0:T(8,128)(2,1)S(1)}, bf16[128,1024]{1,0:T(8,128)(2,1)S(1)}, u32[]{:S(2)}, u32[]{:S(2)}) collective-permute-start(bf16[128,1024]{1,0:T(8,128)(2,1)S(1)} %collective-permute-done.37.rest_2_), channel_id=1, source_target_pairs={{0,1},{1,0},{2,3},{3,2},{4,5},{5,4},{6,7},{7,6},{8,9},{9,8},{10,11... | collective-permute-start | bytes 786440 | tf_op jit(solution)/shard_map/ppermute | solution.py:397
  75.6 17.6 %collective-permute-start.42 = (bf16[128,1024]{1,0:T(8,128)(2,1)S(1)}, bf16[128,1024]{1,0:T(8,128)(2,1)S(1)}, u32[]{:S(2)}, u32[]{:S(2)}) collective-permute-start(bf16[128,1024]{1,0:T(8,128)(2,1)S(1)} %collective-permute-done.38.rest_3_), channel_id=1, source_target_pairs={{0,1},{1,0},{2,3},{3,2},{4,5},{5,4},{6,7},{7,6},{8,9},{9,8},{10,11... | collective-permute-start | bytes 786440 | tf_op jit(solution)/shard_map/ppermute | solution.py:397
  79.4 17.7 %collective-permute-start.11 = (bf16[160,512]{1,0:T(8,128)(2,1)S(1)}, bf16[160,512]{1,0:T(8,128)(2,1)S(1)}, u32[]{:S(2)}, u32[]{:S(2)}) collective-permute-start(bf16[160,512]{1,0:T(8,128)(2,1)S(1)} %get-tuple-element.48), channel_id=1, source_target_pairs={{0,2},{2,0},{4,6},{6,4},{1,3},{3,1},{5,7},{7,5},{8,10},{10,8},{12,... | collective-permute-start | bytes 491528 | tf_op jit(solution)/shard_map/ppermute | solution.py:397
  88.5 25.7 %collective-permute-start.15 = (f32[4,3]{1,0:T(4,128)S(1)}, f32[4,3]{1,0:T(4,128)S(1)}, u32[]{:S(2)}, u32[]{:S(2)}) collective-permute-start(f32[4,3]{1,0:T(4,128)S(1)} %pad_maximum_fusion.1), channel_id=1, source_target_pairs={{0,4},{2,6},{4,0},{6,2},{1,5},{3,7},{5,1},{7,3},{8,12},{10,14},{12... | collective-permute-start | bytes 152 | tf_op jit(solution)/shard_map/ppermute | solution.py:397
  91.2 20.4 %collective-permute-start.24 = (bf16[160,512]{1,0:T(8,128)(2,1)S(1)}, bf16[160,512]{1,0:T(8,128)(2,1)S(1)}, u32[]{:S(2)}, u32[]{:S(2)}) collective-permute-start(bf16[160,512]{1,0:T(8,128)(2,1)S(1)} %get-tuple-element.56), channel_id=1, source_target_pairs={{0,2},{2,0},{4,6},{6,4},{1,3},{3,1},{5,7},{7,5},{8,10},{10,8},{12,... | collective-permute-start | bytes 491528 | tf_op jit(solution)/shard_map/ppermute | solution.py:397
  91.5 23.1 %collective-permute-start.33 = (bf16[160,512]{1,0:T(8,128)(2,1)S(1)}, bf16[160,512]{1,0:T(8,128)(2,1)S(1)}, u32[]{:S(2)}, u32[]{:S(2)}) collective-permute-start(bf16[160,512]{1,0:T(8,128)(2,1)S(1)} %get-tuple-element.62), channel_id=1, source_target_pairs={{0,2},{2,0},{4,6},{6,4},{1,3},{3,1},{5,7},{7,5},{8,10},{10,8},{12,... | collective-permute-start | bytes 491528 | tf_op jit(solution)/shard_map/ppermute | solution.py:397
  93.2 12.1 %collective-permute-start.34 = (bf16[160,512]{1,0:T(8,128)(2,1)S(1)}, bf16[160,512]{1,0:T(8,128)(2,1)S(1)}, u32[]{:S(2)}, u32[]{:S(2)}) collective-permute-start(bf16[160,512]{1,0:T(8,128)(2,1)S(1)} %get-tuple-element.64), channel_id=1, source_target_pairs={{0,2},{2,0},{4,6},{6,4},{1,3},{3,1},{5,7},{7,5},{8,10},{10,8},{12,... | collective-permute-start | bytes 491528 | tf_op jit(solution)/shard_map/ppermute | solution.py:397
  97.2 17.9 %collective-permute-start.43 = (bf16[160,512]{1,0:T(8,128)(2,1)S(1)}, bf16[160,512]{1,0:T(8,128)(2,1)S(1)}, u32[]{:S(2)}, u32[]{:S(2)}) collective-permute-start(bf16[160,512]{1,0:T(8,128)(2,1)S(1)} %get-tuple-element.70), channel_id=1, source_target_pairs={{0,2},{2,0},{4,6},{6,4},{1,3},{3,1},{5,7},{7,5},{8,10},{10,8},{12,... | collective-permute-start | bytes 491528 | tf_op jit(solution)/shard_map/ppermute | solution.py:397
  105.3 5.8 %collective-permute-start.44 = (bf16[160,512]{1,0:T(8,128)(2,1)S(1)}, bf16[160,512]{1,0:T(8,128)(2,1)S(1)}, u32[]{:S(2)}, u32[]{:S(2)}) collective-permute-start(bf16[160,512]{1,0:T(8,128)(2,1)S(1)} %get-tuple-element.72), channel_id=1, source_target_pairs={{0,2},{2,0},{4,6},{6,4},{1,3},{3,1},{5,7},{7,5},{8,10},{10,8},{12,... | collective-permute-start | bytes 491528 | tf_op jit(solution)/shard_map/ppermute | solution.py:397
  111.1 27.3 %collective-permute-start.35 = (bf16[160,512]{1,0:T(8,128)(2,1)S(1)}, bf16[160,512]{1,0:T(8,128)(2,1)S(1)}, u32[]{:S(2)}, u32[]{:S(2)}) collective-permute-start(bf16[160,512]{1,0:T(8,128)(2,1)S(1)} %add_convert_fusion.1), channel_id=1, source_target_pairs={{0,4},{2,6},{4,0},{6,2},{1,5},{3,7},{5,1},{7,3},{8,12},{10,14},{12... | collective-permute-start | bytes 491528 | tf_op jit(solution)/shard_map/ppermute | solution.py:397
  111.5 19.9 %collective-permute-start.45 = (bf16[160,512]{1,0:T(8,128)(2,1)S(1)}, bf16[160,512]{1,0:T(8,128)(2,1)S(1)}, u32[]{:S(2)}, u32[]{:S(2)}) collective-permute-start(bf16[160,512]{1,0:T(8,128)(2,1)S(1)} %add_convert_fusion), channel_id=1, source_target_pairs={{0,4},{2,6},{4,0},{6,2},{1,5},{3,7},{5,1},{7,3},{8,12},{10,14},{12... | collective-permute-start | bytes 491528 | tf_op jit(solution)/shard_map/ppermute | solution.py:397
  114.2 25.1 %collective-permute-start.23 = (bf16[160,512]{1,0:T(8,128)(2,1)S(1)}, bf16[160,512]{1,0:T(8,128)(2,1)S(1)}, u32[]{:S(2)}, u32[]{:S(2)}) collective-permute-start(bf16[160,512]{1,0:T(8,128)(2,1)S(1)} %get-tuple-element.54), channel_id=1, source_target_pairs={{0,2},{2,0},{4,6},{6,4},{1,3},{3,1},{5,7},{7,5},{8,10},{10,8},{12,... | collective-permute-start | bytes 491528 | tf_op jit(solution)/shard_map/ppermute | solution.py:397
  114.6 24.6 %collective-permute-start.25 = (bf16[160,512]{1,0:T(8,128)(2,1)S(1)}, bf16[160,512]{1,0:T(8,128)(2,1)S(1)}, u32[]{:S(2)}, u32[]{:S(2)}) collective-permute-start(bf16[160,512]{1,0:T(8,128)(2,1)S(1)} %add_convert_fusion.2), channel_id=1, source_target_pairs={{0,4},{2,6},{4,0},{6,2},{1,5},{3,7},{5,1},{7,3},{8,12},{10,14},{12... | collective-permute-start | bytes 491528 | tf_op jit(solution)/shard_map/ppermute | solution.py:397
  115.0 25.1 %collective-permute-start.10 = (bf16[160,512]{1,0:T(8,128)(2,1)S(1)}, bf16[160,512]{1,0:T(8,128)(2,1)S(1)}, u32[]{:S(2)}, u32[]{:S(2)}) collective-permute-start(bf16[160,512]{1,0:T(8,128)(2,1)S(1)} %get-tuple-element.46), channel_id=1, source_target_pairs={{0,2},{2,0},{4,6},{6,4},{1,3},{3,1},{5,7},{7,5},{8,10},{10,8},{12,... | collective-permute-start | bytes 491528 | tf_op jit(solution)/shard_map/ppermute | solution.py:397
  131.4 9.9 %collective-permute-start.12 = (bf16[160,512]{1,0:T(8,128)(2,1)S(1)}, bf16[160,512]{1,0:T(8,128)(2,1)S(1)}, u32[]{:S(2)}, u32[]{:S(2)}) collective-permute-start(bf16[160,512]{1,0:T(8,128)(2,1)S(1)} %add_convert_fusion.3), channel_id=1, source_target_pairs={{0,4},{2,6},{4,0},{6,2},{1,5},{3,7},{5,1},{7,3},{8,12},{10,14},{12... | collective-permute-start | bytes 491528 | tf_op jit(solution)/shard_map/ppermute | solution.py:397
  (4 other events, 4.7 us)

commit v3 on v2

v3 whole, which is shorter than its diff:
```python
import functools

import jax
import jax.numpy as jnp
import numpy as np
from jax import lax
from jax.experimental import pallas as pl
from jax.experimental.pallas import tpu as pltpu
from jax.sharding import Mesh, PartitionSpec as P

BAND_ROWS = 32
TAPS = 21
PHASES = 16
LANCZOS = 6
SPAN = TAPS + LANCZOS - 1
LEAD = TAPS // 2 + 2
HALO = 16
SIDE = 128
TILE = 256
STRIP = 128
PARTS = (4, 4, 4, 4)
VMEM = 48 * 1024 * 1024
COST = pl.CostEstimate(flops=1, bytes_accessed=1, transcendentals=0)

sigmas = (1.0, 2.0, 3.5)


def basis_table():
    offsets = np.arange(TAPS) - TAPS // 2
    curves = [np.exp(-offsets * offsets / (2.0 * spread * spread)) for spread in sigmas]
    return [[float(value) for value in curve / curve.sum()] for curve in curves]


def lanczos_table():
    shifted = np.arange(LANCZOS)[None, :] - 2.0 - np.arange(PHASES)[:, None] / PHASES
    values = np.sinc(shifted) * np.sinc(shifted / 3.0)
    return (values / values.sum(axis=1, keepdims=True)).astype(np.float32)


def lanczos_taps(phase):
    table = lanczos_table()
    taps = []
    for n in range(LANCZOS):
        tap = jnp.float32(table[0, n])
        for index in range(1, PHASES):
            tap = jnp.where(phase == index, jnp.float32(table[index, n]), tap)
        taps.append(tap)
    return taps


def split(value):
    high = value.astype(jnp.bfloat16)
    return high, (value - high.astype(jnp.float32)).astype(jnp.bfloat16)


def banded(taps, mask_sets, distance):
    kernel, lanczos = taps
    sets = [[jnp.where(mask, lanczos[n], 0.0) for n, mask in enumerate(masks)] for masks in mask_sets]
    matrices = [jnp.zeros(distance.shape, jnp.float32) for _ in sets]
    for t in range(SPAN):
        here = distance == t
        for index, weighted in enumerate(sets):
            row = jnp.zeros_like(weighted[0])
            for n in range(LANCZOS):
                if 0 <= t - n < TAPS:
                    row = row + kernel[t - n] * weighted[n]
            matrices[index] = jnp.where(here, row, matrices[index])
    return matrices


def matrices_kernel(place, coef, phases, shift, rows_out, cols_out, *, rows, width, segments):
    basis = basis_table()

    def taps_of(axis):
        kernel = [sum(coef[0, axis, k] * basis[k][t] for k in range(len(sigmas))) for t in range(TAPS)]
        return kernel, lanczos_taps(phases[0, axis])

    def kept(matched, extent):
        return [(matched + (n - 2) >= 0) & (matched + (n - 2) < extent) for n in range(LANCZOS)]

    taps = taps_of(1)
    offset = shift[0]
    column = lax.broadcasted_iota(jnp.int32, (1, SIDE), 1)
    everything = [jnp.full((1, SIDE), True)] * LANCZOS
    mask_sets = [kept(column - offset, width), everything, kept(column + (width - SIDE) - offset, width)]
    for part, block in ((0, 3), (1, 0)):
        for variant in range(3):
            for term in range(2):
                place_out = (pl.ds(block * SIDE, SIDE), pl.ds(part * SIDE, SIDE))
                cols_out[(variant, term, *place_out)] = jnp.zeros((SIDE, SIDE), jnp.bfloat16)
    for step in range(3):
        distance = (
            lax.broadcasted_iota(jnp.int32, (SIDE, SIDE), 0)
            - lax.broadcasted_iota(jnp.int32, (SIDE, SIDE), 1)
            + (offset + LEAD - SIDE + step * SIDE)
        )
        pairs = [split(matrix) for matrix in banded(taps, mask_sets, distance)]
        for part in range(2):
            for variant in range(3):
                chosen = variant if variant == 2 * part else 1
                for term in range(2):
                    place_out = (pl.ds((part + step) * SIDE, SIDE), pl.ds(part * SIDE, SIDE))
                    cols_out[(variant, term, *place_out)] = pairs[chosen][term]

    taps = taps_of(0)
    span = STRIP + 2 * HALO
    quarter = BAND_ROWS // segments
    bands = STRIP // BAND_ROWS
    order = lax.broadcasted_iota(jnp.int32, (1, STRIP), 1)
    within = lax.rem(order, bands * quarter)
    owner = lax.div(order, bands * quarter) ^ place[0]
    output = lax.div(within, quarter) * BAND_ROWS + owner * quarter + lax.rem(within, quarter)
    distance = lax.broadcasted_iota(jnp.int32, (span, STRIP), 0) - output + (LEAD - HALO)
    mask_sets = [
        kept(place[0] * rows + first + output, rows * segments) for first in (0, STRIP, rows - STRIP)
    ]
    rest = jnp.zeros((cols_pad(3 * span) - 3 * span, STRIP), jnp.float32)
    for variant, matrix in enumerate(banded(taps, mask_sets, distance)):
        high = matrix.astype(jnp.bfloat16).astype(jnp.float32)
        stacked = jnp.concatenate([high, high, matrix - high, rest], axis=0).T
        rows_out[variant] = stacked.astype(jnp.bfloat16)[:, : 3 * span]


def cols_pad(count):
    return -(-count // 128) * 128


def build_matrices(place, coef, phases, shift, rows, width, segments):
    span = 3 * (STRIP + 2 * HALO)
    smem = pl.BlockSpec(memory_space=pltpu.SMEM)
    vmem = pl.BlockSpec(memory_space=pltpu.VMEM)
    return pl.pallas_call(
        functools.partial(matrices_kernel, rows=rows, width=width, segments=segments),
        out_shape=(
            jax.ShapeDtypeStruct((3, STRIP, span), jnp.bfloat16),
            jax.ShapeDtypeStruct((3, 2, TILE + 2 * SIDE, TILE), jnp.bfloat16),
        ),
        in_specs=[smem] * 4,
        out_specs=(vmem, vmem),
        compiler_params=pltpu.CompilerParams(vmem_limit_bytes=VMEM),
        cost_estimate=COST,
        name="band_matrices",
    )(place, coef, phases, shift)


def filter_kernel(
    weight, low_l, low_c, low_r, mid_l, mid_c, mid_r, high_l, high_c, high_r, rows_m, cols_m, *rest,
    first_chunk, last_chunk, segments,
):
    *outs, ext_high, ext_low, mat_high, mat_low = rest[-segments - 4 :]
    half = pl.program_id(0)
    halves = pl.num_programs(0)
    rows, chunk = mid_c.shape
    at_left = first_chunk & (half == 0)
    at_right = last_chunk & (half == halves - 1)
    span = STRIP + 2 * HALO

    for row, parts in (
        (0, (low_l, low_c, low_r)),
        (HALO, (mid_l, mid_c, mid_r)),
        (HALO + rows, (high_l, high_c, high_r)),
    ):
        count = parts[0].shape[0]
        for part, column, outside in zip(parts, (0, SIDE, SIDE + chunk), (at_left, False, at_right)):
            value = part[...]
            if outside is not False:
                value = jnp.where(outside, 0.0, value)
            high, low = split(value)
            place = (pl.ds(row, count), pl.ds(column, value.shape[1]))
            ext_high[place] = high
            ext_low[place] = low

    strips = rows // STRIP
    for tile in range((chunk + 2 * SIDE) // TILE):
        columns = pl.ds(tile * TILE, TILE)
        for strip in range(strips):
            window = pl.ds(strip * STRIP, span)
            variant = 0 if strip == 0 else (2 if strip == strips - 1 else 1)
            high = ext_high[window, columns]
            stack = jnp.concatenate([high, ext_low[window, columns], high], axis=0)
            matched = jnp.dot(rows_m[variant], stack, preferred_element_type=jnp.float32)
            high, low = split(matched)
            mat_high[pl.ds(strip * STRIP, STRIP), columns] = high
            mat_low[pl.ds(strip * STRIP, STRIP), columns] = low

    tiles = chunk // TILE
    piece = STRIP // segments
    for tile in range(tiles):
        variant = jnp.int32(1)
        if tile == 0:
            variant = jnp.where(at_left, 0, variant)
        if tile == tiles - 1:
            variant = jnp.where(at_right, 2, variant)
        taps_high = cols_m[variant, 0]
        taps_low = cols_m[variant, 1]
        window = pl.ds(tile * TILE, TILE + 2 * SIDE)
        for strip in range(strips):
            place = pl.ds(strip * STRIP, STRIP)
            high = mat_high[place, window]
            warped = jnp.dot(high, taps_high, preferred_element_type=jnp.float32)
            warped += jnp.dot(mat_low[place, window], taps_high, preferred_element_type=jnp.float32)
            warped += jnp.dot(high, taps_low, preferred_element_type=jnp.float32)
            sent = (weight[0] * warped).astype(jnp.bfloat16)
            for owner, out in enumerate(outs):
                out[pl.ds(strip * piece, piece), pl.ds(tile * TILE, TILE)] = sent[owner * piece : (owner + 1) * piece]


def filter_chunk(weight, low, image, high, rows_m, cols_m, after, start, chunk, segments):
    rows, width = image.shape
    halves = 2
    half_blocks = width // halves // SIDE
    first = start // SIDE
    blocks = chunk // SIDE
    last = width // SIDE - 1

    def left(h):
        return 0, jnp.maximum(h * half_blocks + first - 1, 0)

    def centre(h):
        return 0, h * (half_blocks // blocks) + start // chunk

    def right(h):
        return 0, jnp.minimum(h * half_blocks + first + blocks, last)

    def whole(array):
        return pl.BlockSpec(array.shape, lambda h: (0,) * array.ndim)

    specs = [pl.BlockSpec(memory_space=pltpu.SMEM)]
    for source in (low, image, high):
        specs += [
            pl.BlockSpec((source.shape[0], SIDE), left),
            pl.BlockSpec((source.shape[0], chunk), centre),
            pl.BlockSpec((source.shape[0], SIDE), right),
        ]
    wide = chunk + 2 * SIDE
    return pl.pallas_call(
        functools.partial(
            filter_kernel,
            first_chunk=start == 0,
            last_chunk=start + chunk == width // halves,
            segments=segments,
        ),
        out_shape=[jax.ShapeDtypeStruct((rows // segments, halves * chunk), jnp.bfloat16)] * segments,
        grid=(halves,),
        in_specs=specs + [whole(rows_m), whole(cols_m)] + [pl.BlockSpec(memory_space=pl.ANY)] * len(after),
        out_specs=[pl.BlockSpec((rows // segments, chunk), lambda h: (0, h))] * segments,
        scratch_shapes=[
            pltpu.VMEM((rows + 2 * HALO, wide), jnp.bfloat16),
            pltpu.VMEM((rows + 2 * HALO, wide), jnp.bfloat16),
            pltpu.VMEM((rows, wide), jnp.bfloat16),
            pltpu.VMEM((rows, wide), jnp.bfloat16),
        ],
        compiler_params=pltpu.CompilerParams(vmem_limit_bytes=VMEM),
        cost_estimate=COST,
        name="warp_filter",
    )(weight, *([low] * 3), *([image] * 3), *([high] * 3), rows_m, cols_m, *after)


def join_kernel(*refs):
    block = refs[0].shape[0]
    for step, ref in enumerate(refs[:-1]):
        refs[-1][pl.ds(step * block, block), :] = ref[...]


def joined(blocks):
    block, columns = blocks[0].shape
    vmem = pl.BlockSpec(memory_space=pltpu.VMEM)
    return pl.pallas_call(
        join_kernel,
        out_shape=jax.ShapeDtypeStruct((len(blocks) * block, columns), blocks[0].dtype),
        in_specs=[vmem] * len(blocks),
        out_specs=vmem,
        compiler_params=pltpu.CompilerParams(vmem_limit_bytes=VMEM),
        cost_estimate=COST,
        name="join_blocks",
    )(*blocks)


def groups_of(lines):
    groups = []
    step = 1
    while step < lines:
        groups.append(list(range(step, lines, 2 * step)))
        step *= 2
    return groups + [[0]]


def pair_kernel(place, table, mine, other, *rest, slots, groups, quarter):
    outs, (mine_all, other_all) = rest[: len(groups)], rest[len(groups) :]
    rows = mine.shape[0]
    chunk = outs[0].shape[2]
    count = table.shape[0] // 3
    for source, held in ((mine, mine_all), (other, other_all)):
        held[pl.ds(0, rows), :] = source[...].astype(jnp.float32)
        held[pl.ds(rows, quarter), :] = jnp.zeros((quarter, source.shape[1]), jnp.float32)
    line = place[1]

    for group, out in zip(groups, outs):
        for index, distance in enumerate(group):
            first = (line ^ distance) * slots

            def summed(slot, first=first):
                column = pl.ds(pl.multiple_of(table[first + slot] * chunk, 128), chunk)
                from_mine = pl.ds(pl.multiple_of(table[count + first + slot], quarter), quarter)
                from_other = pl.ds(pl.multiple_of(table[2 * count + first + slot], quarter), quarter)
                return mine_all[from_mine, column] + other_all[from_other, column]

            for slot in range(0, slots - 1, 2):
                rows_two = jnp.concatenate([summed(slot), summed(slot + 1)], axis=0)
                out[index, pl.ds(slot * quarter, 2 * quarter), :] = rows_two.astype(jnp.bfloat16)
            if slots % 2:
                out[index, pl.ds((slots - 1) * quarter, quarter), :] = summed(slots - 1).astype(jnp.bfloat16)


def pair_sum(place, table, mine, other, after, slots, lines, quarter):
    rows, double = mine.shape
    chunk = double // 2
    groups = groups_of(lines)
    smem = pl.BlockSpec(memory_space=pltpu.SMEM)
    vmem = pl.BlockSpec(memory_space=pltpu.VMEM)

    def kernel(*refs):
        pair_kernel(*refs[:4], *refs[4 + len(after) :], slots=slots, groups=groups, quarter=quarter)

    return pl.pallas_call(
        kernel,
        out_shape=[jax.ShapeDtypeStruct((len(group), slots * quarter, chunk), jnp.bfloat16) for group in groups],
        in_specs=[smem, smem, vmem, vmem] + [pl.BlockSpec(memory_space=pl.ANY)] * len(after),
        out_specs=[vmem] * len(groups),
        scratch_shapes=[pltpu.VMEM((rows + quarter, double), jnp.float32)] * 2,
        compiler_params=pltpu.CompilerParams(vmem_limit_bytes=VMEM),
        cost_estimate=COST,
        name="pair_sum",
    )(place, table, mine, other, *after)


def weight_kernel(place, sites, facts, out, covers, *, cores, quarter, width, bands):
    slots = out.shape[0] // quarter
    half_cols = out.shape[1]
    exposures = facts.shape[0]
    owner = place[1] * cores + place[2]
    column = lax.broadcasted_iota(jnp.int32, (quarter, half_cols), 1)
    for half in range(2):
        for exposure in range(exposures):
            first = facts[exposure, 0].astype(jnp.int32) - half * half_cols
            inside = (column >= first) & (column < first + width)
            covers[half * exposures + exposure] = jnp.where(inside, facts[exposure, 2], 0.0)

    def one_slot(slot, carry):
        site = sites[owner * slots + slot]
        total = jnp.zeros((quarter, half_cols), jnp.float32)
        for exposure in range(exposures):
            relative = lax.shift_right_logical(site, 1) - facts[exposure, 1].astype(jnp.int32)
            present = jnp.where((relative >= 0) & (relative < bands), jnp.float32(1.0), jnp.float32(0.0))
            total = total + present * covers[(site & 1) * exposures + exposure]
        out[pl.ds(pl.multiple_of(slot * quarter, quarter), quarter), :] = jnp.maximum(total, 1.0)
        return carry

    lax.fori_loop(0, slots, one_slot, 0)


def patch_weights(place, sites, facts, slots, quarter, cores, width, bands):
    smem = pl.BlockSpec(memory_space=pltpu.SMEM)
    return pl.pallas_call(
        functools.partial(weight_kernel, cores=cores, quarter=quarter, width=width, bands=bands),
        out_shape=jax.ShapeDtypeStruct((slots * quarter, width // 2), jnp.float32),
        in_specs=[smem] * 3,
        out_specs=pl.BlockSpec(memory_space=pltpu.VMEM),
        scratch_shapes=[pltpu.VMEM((2 * facts.shape[0], quarter, width // 2), jnp.float32)],
        compiler_params=pltpu.CompilerParams(vmem_limit_bytes=VMEM),
        cost_estimate=COST,
        name="patch_weights",
    )(place, sites, facts)


def finish_kernel(*refs, count):
    pieces, scale, out = refs[:count], refs[count], refs[-1]
    total = pieces[0][...].astype(jnp.float32)
    for piece in pieces[1:]:
        total += piece[...].astype(jnp.float32)
    out[...] = total / scale[...]


def finish_chunk(pieces, scale, result, start):
    _, rows, chunk = pieces[0].shape
    column = pl.BlockSpec((rows, chunk), lambda i: (0, start // chunk))
    specs = [pl.BlockSpec((None, rows, chunk), lambda i: (0, 0, 0))] * len(pieces) + [column]
    operands = [*pieces, scale]
    aliases = {}
    if result is not None:
        specs.append(pl.BlockSpec(memory_space=pl.ANY))
        aliases = {len(operands): 0}
        operands.append(result)
    return pl.pallas_call(
        functools.partial(finish_kernel, count=len(pieces)),
        out_shape=jax.ShapeDtypeStruct(scale.shape, jnp.float32),
        grid=(1,),
        in_specs=specs,
        out_specs=column,
        input_output_aliases=aliases,
        compiler_params=pltpu.CompilerParams(vmem_limit_bytes=VMEM),
        cost_estimate=pl.CostEstimate(
            flops=len(pieces) * rows * chunk, bytes_accessed=rows * chunk * (2 * len(pieces) + 8), transcendentals=0
        ),
        name="patch_mean",
    )(*operands)


def swapped(value, axis, distance):
    count = lax.axis_size(axis)
    return lax.ppermute(value, axis, [(i, i ^ distance) for i in range(count)])


def scatter_sum(pieces):
    pieces = list(pieces)
    kept = [pieces[-1]]
    for stage in range(len(pieces) - 1):
        received = swapped(pieces[stage], "line", 1 << stage)
        kept.append(received)
        for later in range(stage + 1, len(pieces) - 1):
            step = 1 << (later - stage - 1)
            part = received[step :: 2 * step].astype(jnp.float32)
            pieces[later] = (pieces[later].astype(jnp.float32) + part).astype(jnp.bfloat16)
    return kept, pieces[-2]


def per_device(images, psf_coef, phases, col_shift, band_offset, exposure_weight, patch_site):
    image = images[0]
    rows, width = image.shape
    segments = lax.axis_size("seg")
    lines = lax.axis_size("line")
    cores = lax.axis_size("core")
    quarter = BAND_ROWS // segments
    half_cols = width // 2
    slots = patch_site.shape[0] // (lines * cores)
    bands = segments * rows // BAND_ROWS
    place = jnp.stack([lax.axis_index(axis) for axis in ("seg", "line", "core")]).astype(jnp.int32)

    forward = [(i, i + 1) for i in range(segments - 1)]
    backward = [(i + 1, i) for i in range(segments - 1)]
    low = lax.ppermute(image[rows - HALO :], "seg", forward)
    high = lax.ppermute(image[:HALO], "seg", backward)
    rows_m, cols_m = build_matrices(place, psf_coef, phases, col_shift, rows, width, segments)
    weight = exposure_weight.astype(jnp.float32)

    chunks = []
    start = 0
    for part in PARTS:
        chunks.append((start, half_cols // part))
        start += half_cols // part
    other_offset = swapped(band_offset, "core", 1)
    sites = lax.dynamic_index_in_dim(patch_site.reshape(lines, cores, slots), place[2], 1, keepdims=False).reshape(-1)
    here = rows // BAND_ROWS

    def rows_from(offset):
        relative = sites // 2 - offset
        held = ((relative // here) ^ place[0]) * here + relative % here
        return jnp.where((relative >= 0) & (relative < bands), held, bands) * quarter

    table = jnp.concatenate([sites % 2, rows_from(band_offset), rows_from(other_offset)])
    facts = jnp.stack([col_shift.astype(jnp.float32), band_offset.astype(jnp.float32), weight], axis=1)
    facts = jnp.concatenate([facts, swapped(facts, "core", 1)], axis=0)
    early = facts
    step = 1
    while step < lines:
        early = facts
        facts = jnp.concatenate([facts, swapped(facts, "line", step)], axis=0)
        step *= 2
    scale = patch_weights(place, patch_site, facts, slots, quarter, cores, width, bands)

    def tied(values, others):
        return lax.optimization_barrier((values, others))[0]

    result = None
    count = len(chunks)
    sent, sums, partial, kept = [None] * count, [None] * count, [None] * count, [None] * count

    def filtered(index):
        start, chunk = chunks[index]
        sent[index] = filter_chunk(weight, low, image, high, rows_m, cols_m, [], start, chunk, segments)

    filtered(0)
    for index, (start, chunk) in enumerate(chunks):
        outgoing = sent[index]
        received = [swapped(outgoing[d], "seg", d) for d in range(1, segments)]
        if index + 1 < count:
            filtered(index + 1)
            received = tied(received, sent[index + 1])
        if index == 0:
            received = tied(received, early)
        if index == 1:
            received = tied(received, scale)
        if index >= 1:
            received = tied(received, partial[index - 1])
        if index >= 2:
            received = tied(received, kept[index - 2])
        mine = joined([outgoing[0]] + received)
        other = swapped(mine, "core", 1)
        sums[index] = pair_sum(place, table, mine, other, [], slots, lines, quarter)
        kept[index], partial[index] = scatter_sum(sums[index])
        result = finish_chunk(kept[index], scale, result, start)
    return result.reshape(slots, quarter, half_cols)


def solution(mesh):
    segments, exposures = mesh.shape["seg"], mesh.shape["exp"]
    parted = Mesh(mesh.devices.reshape(segments, exposures // 2, 2), ("seg", "line", "core"))
    spread = ("line", "core")
    placed = (
        P(spread, "seg", None),
        P(spread, None, None),
        P(spread, None),
        P(spread),
        P(spread),
        P(spread),
        P(),
    )
    return jax.shard_map(
        per_device, mesh=parted, in_specs=placed, out_specs=P(spread, "seg", None), check_vma=False
    )
```

time: 142 us -> 139 us (0.979)
  Pallas kernels: 45.7 us -> 31.1 us
  waiting for transfers between devices: 49.3 us -> 58.9 us
  local copies, waits for them, and re-layouts: 3.73 us -> 5.92 us
  starting transfers between devices: 40.1 us -> 38.3 us
    ppermute x44 -> x28, waiting for transfers between devices: 47.2 us -> 58.9 us  [swapped(): return lax.ppermute(value, axis, [(i, i ^ distance) for i in range(count)])]
    pallas_call x4 -> x8, Pallas kernels: 14.4 us -> 5.53 us  [the longest x4 5.26 us: pair_sum(): pl.pallas_call(kernel, out_shape=[jax.ShapeDtypeStruct((len(group), slots...]
    pallas_call x1, Pallas kernels: 5.67 us -> 2.15 us  [build_matrices(): pl.pallas_call(functools.partial(matrices_kernel, rows=rows, width=width,...]
    pallas_call x1, Pallas kernels: 4.27 us -> 1.84 us  [patch_weights(): pl.pallas_call(functools.partial(weight_kernel, cores=cores, quarter=quar...]
    ppermute x44 -> x28, starting transfers between devices: 33.9 us -> 31.5 us  [swapped(): return lax.ppermute(value, axis, [(i, i ^ distance) for i in range(count)])]
    ppermute x1, waiting for transfers between devices: 2.07 us -> 0.01 us  [per_device(): high = lax.ppermute(image[:HALO], 'seg', backward)]
    unnamed x12 -> x26, local copies, waits for them, and re-layouts: 2.66 us -> 4.67 us
  transfers between devices with their start and end apart: 46 -> 30, of which waited for: 14 -> 15; matrix products, arithmetic and copies ran while one was open for 1% -> 2% of each run, Pallas kernels for 32% -> 15%
where the time goes in v3:
time: 139 us
  waiting for transfers between devices  58.9 us (42%)
  starting transfers between devices  38.3 us (28%)
  Pallas kernels  31.1 us (22%)
  local copies, waits for them, and re-layouts  5.92 us (4%)
  other arithmetic  2.5 us (2%)
  between operations  2.29 us (2%)
    ppermute x28, waiting for transfers between devices, swapped(): return lax.ppermute(value, axis, [(i, i ^ distance) for i in range(count)])  58.9 us
    ppermute x28, starting transfers between devices, swapped(): return lax.ppermute(value, axis, [(i, i ^ distance) for i in range(count)])  31.5 us
    pallas_call x4, Pallas kernels, filter_chunk(): pl.pallas_call(functools.partial(filter_kernel, first_chunk=start == 0, l...  18.3 us
    ppermute x1, starting transfers between devices, per_device(): low = lax.ppermute(image[rows - HALO:], 'seg', forward)  5.49 us
    pallas_call x4, Pallas kernels, pair_sum(): pl.pallas_call(kernel, out_shape=[jax.ShapeDtypeStruct((len(group), slots...  5.26 us
    unnamed x26, local copies, waits for them, and re-layouts  4.67 us
    pallas_call x4, Pallas kernels, finish_chunk(): pl.pallas_call(functools.partial(finish_kernel, count=len(pieces)), out_s...  3.23 us
  transfers between devices with their start and end apart: 30, of which 15 were waited for; matrix products, arithmetic and copies ran while one was open for 2% of the time, Pallas kernels for 15%

profile of v3, /device:TPU:0, one launch (start us, length us, event | category | flops | bytes accessed | tf_op | source)
XLA Modules:
  0.0 139.0 jit_solution(7684531566648539401)
XLA Ops:
  0.0 1.1 slice_bitcast_fusion
  1.1 1.3 collective-permute-start.2
  2.4 5.5 %collective-permute-start.1 = (f32[16,4096]{1,0:T(8,128)S(1)}, f32[16,4096]{1,0:T(8,128)S(1)}, u32[]{:S(2)}, u32[]{:S(2)}) collective-permute-start(f32[16,4096]{1,0:T(8,128)S(1)} %get-tuple-element.128), channel_id=1, source_target_pairs={{0,8},{8,16},{16,24},{1,9},{9,17},{17,25},{2,10},{10,18},{18,26},{... | collective-permute-start | bytes 786440 | tf_op jit(solution)/shard_map/ppermute | solution.py:441
  9.9 2.1 %band_matrices.1 = (bf16[3,128,480]{2,1,0:T(8,128)(2,1)S(1)}, bf16[3,2,512,256]{3,2,1,0:T(8,128)(2,1)S(1)}) custom-call(s32[3]{0:T(128)S(1)} %pad_add_fusion.1.place.refs_0_, f32[1,2,3]{2,1,0:T(2,128)S(1)} %copy-done.3, s32[1,2]{1,0:T(1,128)S(1)} %copy-done.4, s32[1]{0:T(128)S(6)} %copy.14.shift), custom_call_target="tpu_custom_call" | custom-call | flops 1 | bytes 1 | tf_op jit(solution)/shard_map/band_matrices/pallas_call | solution.py:132
  13.4 4.6 %warp_filter.7 = (bf16[128,1024]{1,0:T(8,128)(2,1)S(1)}, bf16[128,1024]{1,0:T(8,128)(2,1)S(1)}, bf16[128,1024]{1,0:T(8,128)(2,1)S(1)}, bf16[128,1024]{1,0:T(8,128)(2,1)S(1)}) custom-call(f32[1]{0:T(128)} %convert_element_type.45.weight, f32[16,4096]{1,0:T(8,128)S(1)} %collective-permute-done.1.low_l.low_c.low_r, ...), custom_call_target="tpu_custom_call" | custom-call | flops 1 | bytes 1 | tf_op jit(solution)/shard_map/warp_filter/pallas_call | solution.py:236
  18.0 4.0 %collective-permute-start.15 = (bf16[128,1024]{1,0:T(8,128)(2,1)S(1)}, bf16[128,1024]{1,0:T(8,128)(2,1)S(1)}, u32[]{:S(2)}, u32[]{:S(2)}) collective-permute-start(bf16[128,1024]{1,0:T(8,128)(2,1)S(1)} %get-tuple-element.89), channel_id=1, source_target_pairs={{0,8},{8,0},{16,24},{24,16},{1,9},{9,1},{17,25},{25,17},{2,10},{10... | collective-permute-start | bytes 786440 | tf_op jit(solution)/shard_map/ppermute | solution.py:411
  21.9 3.7 %collective-permute-start.16 = (bf16[128,1024]{1,0:T(8,128)(2,1)S(1)}, bf16[128,1024]{1,0:T(8,128)(2,1)S(1)}, u32[]{:S(2)}, u32[]{:S(2)}) collective-permute-start(bf16[128,1024]{1,0:T(8,128)(2,1)S(1)} %get-tuple-element.90), channel_id=1, source_target_pairs={{0,16},{8,24},{16,0},{24,8},{1,17},{9,25},{17,1},{25,9},{2,18},{10... | collective-permute-start | bytes 786440 | tf_op jit(solution)/shard_map/ppermute | solution.py:411
  25.7 1.1 collective-permute-done.12
  26.9 1.6 %collective-permute-start.13 = (f32[2,3]{1,0:T(2,128)S(1)}, f32[2,3]{1,0:T(2,128)S(1)}, u32[]{:S(2)}, u32[]{:S(2)}) collective-permute-start(f32[2,3]{1,0:T(2,128)S(1)} %pad_maximum_fusion.2), channel_id=1, source_target_pairs={{0,2},{2,0},{4,6},{6,4},{1,3},{3,1},{5,7},{7,5},{8,10},{10,8},{12,... | collective-permute-start | bytes 80 | tf_op jit(solution)/shard_map/ppermute | solution.py:411
  28.5 2.0 %collective-permute-done.13 = f32[2,3]{1,0:T(2,128)S(1)} collective-permute-done((f32[2,3]{1,0:T(2,128)S(1)}, f32[2,3]{1,0:T(2,128)S(1)}, u32[]{:S(2)}, u32[]{:S(2)}) %collective-permute-start.13) | collective-permute-done | bytes 56 | tf_op jit(solution)/shard_map/ppermute | solution.py:411
  31.7 4.5 %warp_filter.6 = (bf16[128,1024]{1,0:T(8,128)(2,1)S(1)}, bf16[128,1024]{1,0:T(8,128)(2,1)S(1)}, bf16[128,1024]{1,0:T(8,128)(2,1)S(1)}, bf16[128,1024]{1,0:T(8,128)(2,1)S(1)}) custom-call(f32[1]{0:T(128)} %convert_element_type.45.weight, f32[16,4096]{1,0:T(8,128)S(1)} %collective-permute-done.1.low_l.low_c.low_r, ...), custom_call_target="tpu_custom_call" | custom-call | flops 1 | bytes 1 | tf_op jit(solution)/shard_map/warp_filter/pallas_call | solution.py:236
  36.9 0.7 copy-done.7
  39.8 1.8 %collective-permute-done = s32[1]{0:T(128)} collective-permute-done((s32[1]{0:T(128)}, s32[1]{0:T(128)}, u32[]{:S(2)}, u32[]{:S(2)}) %collective-permute-start) | collective-permute-done | bytes 36 | tf_op jit(solution)/shard_map/ppermute | solution.py:411
  42.3 1.8 %pair_sum.4 = (bf16[2,160,512]{2,1,0:T(8,128)(2,1)S(1)}, bf16[1,160,512]{2,1,0:T(8,128)(2,1)S(1)}, bf16[1,160,512]{2,1,0:T(8,128)(2,1)S(1)}) custom-call(s32[3]{0:T(128)S(1)} %pad_add_fusion.1.place.refs_0_, s32[240]{0:T(256)S(1)} %pad_add_fusion.refs_1_, bf16[512,1024]{1,0:T(8,128)(2,1)S(1)} %join_blocks.4.refs_2_, ...), custom_call_target="tpu_custom_call" | custom-call | flops 1 | bytes 1 | tf_op jit(solution)/shard_map/pair_sum/pallas_call | solution.py:325
  44.1 1.6 %collective-permute-start.19 = (bf16[2,160,512]{2,1,0:T(8,128)(2,1)S(1)}, bf16[2,160,512]{2,1,0:T(8,128)(2,1)S(1)}, u32[]{:S(2)}, u32[]{:S(2)}) collective-permute-start(bf16[2,160,512]{2,1,0:T(8,128)(2,1)S(1)} %get-tuple-element.99), channel_id=1, source_target_pairs={{0,2},{2,0},{4,6},{6,4},{1,3},{3,1},{5,7},{7,5},{8,10},{10,8},{12,... | collective-permute-start | bytes 983048 | tf_op jit(solution)/shard_map/ppermute | solution.py:411
  45.8 1.5 %collective-permute-start.9 = (bf16[128,1024]{1,0:T(8,128)(2,1)S(1)}, bf16[128,1024]{1,0:T(8,128)(2,1)S(1)}, u32[]{:S(2)}, u32[]{:S(2)}) collective-permute-start(bf16[128,1024]{1,0:T(8,128)(2,1)S(1)} %copy-done.10), channel_id=1, source_target_pairs={{0,8},{8,0},{16,24},{24,16},{1,9},{9,1},{17,25},{25,17},{2,10},{10... | collective-permute-start | bytes 786440 | tf_op jit(solution)/shard_map/ppermute | solution.py:411
  47.2 2.0 %collective-permute-start.10 = (bf16[128,1024]{1,0:T(8,128)(2,1)S(1)}, bf16[128,1024]{1,0:T(8,128)(2,1)S(1)}, u32[]{:S(2)}, u32[]{:S(2)}) collective-permute-start(bf16[128,1024]{1,0:T(8,128)(2,1)S(1)} %copy-done.8), channel_id=1, source_target_pairs={{0,16},{8,24},{16,0},{24,8},{1,17},{9,25},{17,1},{25,9},{2,18},{10... | collective-permute-start | bytes 786440 | tf_op jit(solution)/shard_map/ppermute | solution.py:411
  49.3 2.6 %collective-permute-start.14 = (f32[4,3]{1,0:T(4,128)}, f32[4,3]{1,0:T(4,128)S(1)}, u32[]{:S(2)}, u32[]{:S(2)}) collective-permute-start(f32[4,3]{1,0:T(4,128)} %pad_maximum_fusion.1), channel_id=1, source_target_pairs={{0,4},{2,6},{4,0},{6,2},{1,5},{3,7},{5,1},{7,3},{8,12},{10,14},{12... | collective-permute-start | bytes 152 | tf_op jit(solution)/shard_map/ppermute | solution.py:411
  51.9 2.2 %collective-permute-done.14 = f32[4,3]{1,0:T(4,128)S(1)} collective-permute-done((f32[4,3]{1,0:T(4,128)}, f32[4,3]{1,0:T(4,128)S(1)}, u32[]{:S(2)}, u32[]{:S(2)}) %collective-permute-start.14) | collective-permute-done | bytes 80 | tf_op jit(solution)/shard_map/ppermute | solution.py:411
  54.1 0.8 pad_maximum_fusion.facts
  54.9 1.8 %patch_weights.1.refs_3_ = f32[160,2048]{1,0:T(8,128)S(1)} custom-call(s32[3]{0:T(128)S(1)} %pad_add_fusion.1.place.refs_0_, s32[160]{0:T(256)S(1)} %copy-done.2, f32[8,3]{1,0:T(8,128)S(1)} %pad_maximum_fusion.facts), custom_call_target="tpu_custom_call" | custom-call | flops 1 | bytes 1 | tf_op jit(solution)/shard_map/patch_weights/pallas_call | solution.py:364
  56.7 4.6 %warp_filter.5 = (bf16[128,1024]{1,0:T(8,128)(2,1)S(1)}, bf16[128,1024]{1,0:T(8,128)(2,1)S(1)}, bf16[128,1024]{1,0:T(8,128)(2,1)S(1)}, bf16[128,1024]{1,0:T(8,128)(2,1)S(1)}) custom-call(f32[1]{0:T(128)} %convert_element_type.45.weight, f32[16,4096]{1,0:T(8,128)S(1)} %collective-permute-done.1.low_l.low_c.low_r, ...), custom_call_target="tpu_custom_call" | custom-call | flops 1 | bytes 1 | tf_op jit(solution)/shard_map/warp_filter/pallas_call | solution.py:236
  61.6 2.6 %collective-permute-done.20.refs_3_ = bf16[512,1024]{1,0:T(8,128)(2,1)S(1)} collective-permute-done((bf16[512,1024]{1,0:T(8,128)(2,1)S(1)}, bf16[512,1024]{1,0:T(8,128)(2,1)S(1)}, u32[]{:S(2)}, u32[]{:S(2)}) %collective-permute-start.20) | collective-permute-done | bytes 1048608 | tf_op jit(solution)/shard_map/ppermute | solution.py:411
  64.2 1.1 pair_sum.5
  65.4 2.7 %collective-permute-start.21 = (bf16[2,160,512]{2,1,0:T(8,128)(2,1)S(1)}, bf16[2,160,512]{2,1,0:T(8,128)(2,1)S(1)}, u32[]{:S(2)}, u32[]{:S(2)}) collective-permute-start(bf16[2,160,512]{2,1,0:T(8,128)(2,1)S(1)} %get-tuple-element.104), channel_id=1, source_target_pairs={{0,2},{2,0},{4,6},{6,4},{1,3},{3,1},{5,7},{7,5},{8,10},{10,8},{12,... | collective-permute-start | bytes 983048 | tf_op jit(solution)/shard_map/ppermute | solution.py:411
  68.1 1.5 %collective-permute-start.6 = (bf16[128,1024]{1,0:T(8,128)(2,1)S(1)}, bf16[128,1024]{1,0:T(8,128)(2,1)S(1)}, u32[]{:S(2)}, u32[]{:S(2)}) collective-permute-start(bf16[128,1024]{1,0:T(8,128)(2,1)S(1)} %get-tuple-element.72), channel_id=1, source_target_pairs={{0,8},{8,0},{16,24},{24,16},{1,9},{9,1},{17,25},{25,17},{2,10},{10... | collective-permute-start | bytes 786440 | tf_op jit(solution)/shard_map/ppermute | solution.py:411
  69.6 2.0 %collective-permute-start.7 = (bf16[128,1024]{1,0:T(8,128)(2,1)S(1)}, bf16[128,1024]{1,0:T(8,128)(2,1)S(1)}, u32[]{:S(2)}, u32[]{:S(2)}) collective-permute-start(bf16[128,1024]{1,0:T(8,128)(2,1)S(1)} %get-tuple-element.73), channel_id=1, source_target_pairs={{0,16},{8,24},{16,0},{24,8},{1,17},{9,25},{17,1},{25,9},{2,18},{10... | collective-permute-start | bytes 786440 | tf_op jit(solution)/shard_map/ppermute | solution.py:411
  71.6 4.7 %warp_filter.4 = (bf16[128,1024]{1,0:T(8,128)(2,1)S(1)}, bf16[128,1024]{1,0:T(8,128)(2,1)S(1)}, bf16[128,1024]{1,0:T(8,128)(2,1)S(1)}, bf16[128,1024]{1,0:T(8,128)(2,1)S(1)}) custom-call(f32[1]{0:T(128)} %convert_element_type.45.weight, f32[16,4096]{1,0:T(8,128)S(1)} %collective-permute-done.1.low_l.low_c.low_r, ...), custom_call_target="tpu_custom_call" | custom-call | flops 1 | bytes 1 | tf_op jit(solution)/shard_map/warp_filter/pallas_call | solution.py:236
  76.3 1.0 collective-permute-done.6.refs_1_
  77.3 5.2 %collective-permute-done.7.refs_2_ = bf16[128,1024]{1,0:T(8,128)(2,1)S(1)} collective-permute-done((bf16[128,1024]{1,0:T(8,128)(2,1)S(1)}, bf16[128,1024]{1,0:T(8,128)(2,1)S(1)}, u32[]{:S(2)}, u32[]{:S(2)}) %collective-permute-start.7) | collective-permute-done | bytes 262176 | tf_op jit(solution)/shard_map/ppermute | solution.py:411
  82.5 0.7 collective-permute-done.8.refs_3_
  83.6 9.1 %collective-permute-done.22.refs_2_ = bf16[1,160,512]{2,1,0:T(8,128)(2,1)S(1)} collective-permute-done((bf16[1,160,512]{2,1,0:T(8,128)(2,1)S(1)}, bf16[1,160,512]{2,1,0:T(8,128)(2,1)S(1)}, u32[]{:S(2)}, u32[]{:S(2)}) %collective-permute-start.22) | collective-permute-done | bytes 163872 | tf_op jit(solution)/shard_map/ppermute | solution.py:411
  92.9 2.6 %collective-permute-done.23.refs_3_ = bf16[512,1024]{1,0:T(8,128)(2,1)S(1)} collective-permute-done((bf16[512,1024]{1,0:T(8,128)(2,1)S(1)}, bf16[512,1024]{1,0:T(8,128)(2,1)S(1)}, u32[]{:S(2)}, u32[]{:S(2)}) %collective-permute-start.23) | collective-permute-done | bytes 1048608 | tf_op jit(solution)/shard_map/ppermute | solution.py:411
  95.5 1.1 pair_sum.6
  96.8 1.5 %collective-permute-start.3 = (bf16[128,1024]{1,0:T(8,128)(2,1)S(1)}, bf16[128,1024]{1,0:T(8,128)(2,1)S(1)}, u32[]{:S(2)}, u32[]{:S(2)}) collective-permute-start(bf16[128,1024]{1,0:T(8,128)(2,1)S(1)} %get-tuple-element.68), channel_id=1, source_target_pairs={{0,8},{8,0},{16,24},{24,16},{1,9},{9,1},{17,25},{25,17},{2,10},{10... | collective-permute-start | bytes 786440 | tf_op jit(solution)/shard_map/ppermute | solution.py:411
  98.4 2.0 %collective-permute-start.5 = (bf16[128,1024]{1,0:T(8,128)(2,1)S(1)}, bf16[128,1024]{1,0:T(8,128)(2,1)S(1)}, u32[]{:S(2)}, u32[]{:S(2)}) collective-permute-start(bf16[128,1024]{1,0:T(8,128)(2,1)S(1)} %get-tuple-element.70), channel_id=1, source_target_pairs={{0,24},{8,16},{16,8},{24,0},{1,25},{9,17},{17,9},{25,1},{2,26},{10... | collective-permute-start | bytes 786440 | tf_op jit(solution)/shard_map/ppermute | solution.py:411
  100.3 1.7 %collective-permute-start.25 = (bf16[1,160,512]{2,1,0:T(8,128)(2,1)S(1)}, bf16[1,160,512]{2,1,0:T(8,128)(2,1)S(1)}, u32[]{:S(2)}, u32[]{:S(2)}) collective-permute-start(bf16[1,160,512]{2,1,0:T(8,128)(2,1)S(1)} %add_convert_fusion.2), channel_id=1, source_target_pairs={{0,4},{2,6},{4,0},{6,2},{1,5},{3,7},{5,1},{7,3},{8,12},{10,14},{12... | collective-permute-start | bytes 491528 | tf_op jit(solution)/shard_map/ppermute | solution.py:411
  102.0 7.4 %collective-permute-done.24.refs_1_ = bf16[2,160,512]{2,1,0:T(8,128)(2,1)S(1)} collective-permute-done((bf16[2,160,512]{2,1,0:T(8,128)(2,1)S(1)}, bf16[2,160,512]{2,1,0:T(8,128)(2,1)S(1)}, u32[]{:S(2)}, u32[]{:S(2)}) %collective-permute-start.24) | collective-permute-done | bytes 327712 | tf_op jit(solution)/shard_map/ppermute | solution.py:411
  109.5 2.5 %collective-permute-done.4.refs_2_ = bf16[128,1024]{1,0:T(8,128)(2,1)S(1)} collective-permute-done((bf16[128,1024]{1,0:T(8,128)(2,1)S(1)}, bf16[128,1024]{1,0:T(8,128)(2,1)S(1)}, u32[]{:S(2)}, u32[]{:S(2)}) %collective-permute-start.4) | collective-permute-done | bytes 262176 | tf_op jit(solution)/shard_map/ppermute | solution.py:411
  112.2 2.6 %collective-permute-done.26.refs_3_ = bf16[512,1024]{1,0:T(8,128)(2,1)S(1)} collective-permute-done((bf16[512,1024]{1,0:T(8,128)(2,1)S(1)}, bf16[512,1024]{1,0:T(8,128)(2,1)S(1)}, u32[]{:S(2)}, u32[]{:S(2)}) %collective-permute-start.26) | collective-permute-done | bytes 1048608 | tf_op jit(solution)/shard_map/ppermute | solution.py:411
  114.8 1.1 pair_sum.7
  116.0 1.7 %collective-permute-start.27 = (bf16[2,160,512]{2,1,0:T(8,128)(2,1)S(1)}, bf16[2,160,512]{2,1,0:T(8,128)(2,1)S(1)}, u32[]{:S(2)}, u32[]{:S(2)}) collective-permute-start(bf16[2,160,512]{2,1,0:T(8,128)(2,1)S(1)} %get-tuple-element.122), channel_id=1, source_target_pairs={{0,2},{2,0},{4,6},{6,4},{1,3},{3,1},{5,7},{7,5},{8,10},{10,8},{12,... | collective-permute-start | bytes 983048 | tf_op jit(solution)/shard_map/ppermute | solution.py:411
  117.8 11.5 %collective-permute-done.27.refs_1_ = bf16[2,160,512]{2,1,0:T(8,128)(2,1)S(1)} collective-permute-done((bf16[2,160,512]{2,1,0:T(8,128)(2,1)S(1)}, bf16[2,160,512]{2,1,0:T(8,128)(2,1)S(1)}, u32[]{:S(2)}, u32[]{:S(2)}) %collective-permute-start.27) | collective-permute-done | bytes 327712 | tf_op jit(solution)/shard_map/ppermute | solution.py:411
  129.4 0.8 patch_mean.4.refs_4_
  130.2 0.8 patch_mean.5.refs_4_
  131.0 0.8 patch_mean.6.refs_4_
  131.8 6.4 %collective-permute-done.28.refs_2_ = bf16[1,160,512]{2,1,0:T(8,128)(2,1)S(1)} collective-permute-done((bf16[1,160,512]{2,1,0:T(8,128)(2,1)S(1)}, bf16[1,160,512]{2,1,0:T(8,128)(2,1)S(1)}, u32[]{:S(2)}, u32[]{:S(2)}) %collective-permute-start.28) | collective-permute-done | bytes 163872 | tf_op jit(solution)/shard_map/ppermute | solution.py:411
  138.2 0.8 patch_mean.7
  (72 shorter events, 7.7 us)
Async XLA Ops:
  1.1 12.3 %collective-permute-start.2 = (f32[16,4096]{1,0:T(8,128)S(1)}, f32[16,4096]{1,0:T(8,128)S(1)}, u32[]{:S(2)}, u32[]{:S(2)}) collective-permute-start(f32[16,4096]{1,0:T(8,128)S(1)} %get-tuple-element.127), channel_id=1, source_target_pairs={{8,0},{16,8},{24,16},{9,1},{17,9},{25,17},{10,2},{18,10},{26,18},{... | collective-permute-start | bytes 786440 | tf_op jit(solution)/shard_map/ppermute | solution.py:442
  2.4 11.0 %collective-permute-start.1 = (f32[16,4096]{1,0:T(8,128)S(1)}, f32[16,4096]{1,0:T(8,128)S(1)}, u32[]{:S(2)}, u32[]{:S(2)}) collective-permute-start(f32[16,4096]{1,0:T(8,128)S(1)} %get-tuple-element.128), channel_id=1, source_target_pairs={{0,8},{8,16},{16,24},{1,9},{9,17},{17,25},{2,10},{10,18},{18,26},{... | collective-permute-start | bytes 786440 | tf_op jit(solution)/shard_map/ppermute | solution.py:441
  8.6 0.7 copy-start.3
  9.3 0.7 copy-start.4
  18.0 20.4 %collective-permute-start.15 = (bf16[128,1024]{1,0:T(8,128)(2,1)S(1)}, bf16[128,1024]{1,0:T(8,128)(2,1)S(1)}, u32[]{:S(2)}, u32[]{:S(2)}) collective-permute-start(bf16[128,1024]{1,0:T(8,128)(2,1)S(1)} %get-tuple-element.89), channel_id=1, source_target_pairs={{0,8},{8,0},{16,24},{24,16},{1,9},{9,1},{17,25},{25,17},{2,10},{10... | collective-permute-start | bytes 786440 | tf_op jit(solution)/shard_map/ppermute | solution.py:411
  21.9 16.4 %collective-permute-start.16 = (bf16[128,1024]{1,0:T(8,128)(2,1)S(1)}, bf16[128,1024]{1,0:T(8,128)(2,1)S(1)}, u32[]{:S(2)}, u32[]{:S(2)}) collective-permute-start(bf16[128,1024]{1,0:T(8,128)(2,1)S(1)} %get-tuple-element.90), channel_id=1, source_target_pairs={{0,16},{8,24},{16,0},{24,8},{1,17},{9,25},{17,1},{25,9},{2,18},{10... | collective-permute-start | bytes 786440 | tf_op jit(solution)/shard_map/ppermute | solution.py:411
  25.6 12.8 %collective-permute-start.17 = (bf16[128,1024]{1,0:T(8,128)(2,1)S(1)}, bf16[128,1024]{1,0:T(8,128)(2,1)S(1)}, u32[]{:S(2)}, u32[]{:S(2)}) collective-permute-start(bf16[128,1024]{1,0:T(8,128)(2,1)S(1)} %get-tuple-element.91), channel_id=1, source_target_pairs={{0,24},{8,16},{16,8},{24,0},{1,25},{9,17},{17,9},{25,1},{2,26},{10... | collective-permute-start | bytes 786440 | tf_op jit(solution)/shard_map/ppermute | solution.py:411
  25.7 1.1 collective-permute-start.12
  26.8 3.7 %copy-start.11 = (f32[1,3]{1,0:T(1,128)}, f32[1,3]{1,0:T(1,128)S(1)}, u32[]{:S(2)}) copy-start(f32[1,3]{1,0:T(1,128)S(1)} %collective-permute-done.12) | copy-start | bytes 40
  26.9 3.6 %collective-permute-start.13 = (f32[2,3]{1,0:T(2,128)S(1)}, f32[2,3]{1,0:T(2,128)S(1)}, u32[]{:S(2)}, u32[]{:S(2)}) collective-permute-start(f32[2,3]{1,0:T(2,128)S(1)} %pad_maximum_fusion.2), channel_id=1, source_target_pairs={{0,2},{2,0},{4,6},{6,4},{1,3},{3,1},{5,7},{7,5},{8,10},{10,8},{12,... | collective-permute-start | bytes 80 | tf_op jit(solution)/shard_map/ppermute | solution.py:411
  30.5 0.6 copy-start.12
  36.2 0.7 copy-start
  36.9 0.7 copy-start.7
  37.6 0.7 copy-start.9
  38.3 0.7 copy-start.5
  38.3 1.2 copy-start.2
  39.1 3.2 %collective-permute-start.18 = (bf16[512,1024]{1,0:T(8,128)(2,1)S(1)}, bf16[512,1024]{1,0:T(8,128)(2,1)}, u32[]{:S(2)}, u32[]{:S(2)}) collective-permute-start(bf16[512,1024]{1,0:T(8,128)(2,1)S(1)} %join_blocks.4.refs_2_), channel_id=1, source_target_pairs={{0,1},{1,0},{2,3},{3,2},{4,5},{5,4},{6,7},{7,6},{8,9},{9,8},{10,11... | collective-permute-start | bytes 3145736 | tf_op jit(solution)/shard_map/ppermute | solution.py:411
  39.1 2.6 %collective-permute-start = (s32[1]{0:T(128)}, s32[1]{0:T(128)}, u32[]{:S(2)}, u32[]{:S(2)}) collective-permute-start(s32[1]{0:T(128)} %param.11), channel_id=1, source_target_pairs={{0,1},{1,0},{2,3},{3,2},{4,5},{5,4},{6,7},{7,6},{8,9},{9,8},{10,11... | collective-permute-start | bytes 20 | tf_op jit(solution)/shard_map/ppermute | solution.py:411
  39.8 6.0 %copy-start.10 = (bf16[128,1024]{1,0:T(8,128)(2,1)S(1)}, bf16[128,1024]{1,0:T(8,128)(2,1)}, u32[]{:S(2)}) copy-start(bf16[128,1024]{1,0:T(8,128)(2,1)} %copy-done.9) | copy-start | bytes 786436
  39.8 7.5 %copy-start.8 = (bf16[128,1024]{1,0:T(8,128)(2,1)S(1)}, bf16[128,1024]{1,0:T(8,128)(2,1)}, u32[]{:S(2)}) copy-start(bf16[128,1024]{1,0:T(8,128)(2,1)} %copy-done.7) | copy-start | bytes 786436
  39.8 9.5 %copy-start.6 = (bf16[128,1024]{1,0:T(8,128)(2,1)S(1)}, bf16[128,1024]{1,0:T(8,128)(2,1)}, u32[]{:S(2)}) copy-start(bf16[128,1024]{1,0:T(8,128)(2,1)} %copy-done.5) | copy-start | bytes 786436
  44.1 17.2 %collective-permute-start.19 = (bf16[2,160,512]{2,1,0:T(8,128)(2,1)S(1)}, bf16[2,160,512]{2,1,0:T(8,128)(2,1)S(1)}, u32[]{:S(2)}, u32[]{:S(2)}) collective-permute-start(bf16[2,160,512]{2,1,0:T(8,128)(2,1)S(1)} %get-tuple-element.99), channel_id=1, source_target_pairs={{0,2},{2,0},{4,6},{6,4},{1,3},{3,1},{5,7},{7,5},{8,10},{10,8},{12,... | collective-permute-start | bytes 983048 | tf_op jit(solution)/shard_map/ppermute | solution.py:411
  45.8 15.6 %collective-permute-start.9 = (bf16[128,1024]{1,0:T(8,128)(2,1)S(1)}, bf16[128,1024]{1,0:T(8,128)(2,1)S(1)}, u32[]{:S(2)}, u32[]{:S(2)}) collective-permute-start(bf16[128,1024]{1,0:T(8,128)(2,1)S(1)} %copy-done.10), channel_id=1, source_target_pairs={{0,8},{8,0},{16,24},{24,16},{1,9},{9,1},{17,25},{25,17},{2,10},{10... | collective-permute-start | bytes 786440 | tf_op jit(solution)/shard_map/ppermute | solution.py:411
  47.2 14.1 %collective-permute-start.10 = (bf16[128,1024]{1,0:T(8,128)(2,1)S(1)}, bf16[128,1024]{1,0:T(8,128)(2,1)S(1)}, u32[]{:S(2)}, u32[]{:S(2)}) collective-permute-start(bf16[128,1024]{1,0:T(8,128)(2,1)S(1)} %copy-done.8), channel_id=1, source_target_pairs={{0,16},{8,24},{16,0},{24,8},{1,17},{9,25},{17,1},{25,9},{2,18},{10... | collective-permute-start | bytes 786440 | tf_op jit(solution)/shard_map/ppermute | solution.py:411
  49.3 12.1 %collective-permute-start.11 = (bf16[128,1024]{1,0:T(8,128)(2,1)S(1)}, bf16[128,1024]{1,0:T(8,128)(2,1)S(1)}, u32[]{:S(2)}, u32[]{:S(2)}) collective-permute-start(bf16[128,1024]{1,0:T(8,128)(2,1)S(1)} %copy-done.6), channel_id=1, source_target_pairs={{0,24},{8,16},{16,8},{24,0},{1,25},{9,17},{17,9},{25,1},{2,26},{10... | collective-permute-start | bytes 786440 | tf_op jit(solution)/shard_map/ppermute | solution.py:411
  49.3 4.8 %collective-permute-start.14 = (f32[4,3]{1,0:T(4,128)}, f32[4,3]{1,0:T(4,128)S(1)}, u32[]{:S(2)}, u32[]{:S(2)}) collective-permute-start(f32[4,3]{1,0:T(4,128)} %pad_maximum_fusion.1), channel_id=1, source_target_pairs={{0,4},{2,6},{4,0},{6,2},{1,5},{3,7},{5,1},{7,3},{8,12},{10,14},{12... | collective-permute-start | bytes 152 | tf_op jit(solution)/shard_map/ppermute | solution.py:411
  56.7 4.7 %copy-start.1 = (bf16[128,1024]{1,0:T(8,128)(2,1)S(1)}, bf16[128,1024]{1,0:T(8,128)(2,1)}, u32[]{:S(2)}) copy-start(bf16[128,1024]{1,0:T(8,128)(2,1)} %copy-done) | copy-start | bytes 786436
  61.5 2.7 %collective-permute-start.20 = (bf16[512,1024]{1,0:T(8,128)(2,1)S(1)}, bf16[512,1024]{1,0:T(8,128)(2,1)S(1)}, u32[]{:S(2)}, u32[]{:S(2)}) collective-permute-start(bf16[512,1024]{1,0:T(8,128)(2,1)S(1)} %join_blocks.5.refs_2_), channel_id=1, source_target_pairs={{0,1},{1,0},{2,3},{3,2},{4,5},{5,4},{6,7},{7,6},{8,9},{9,8},{10,11... | collective-permute-start | bytes 3145736 | tf_op jit(solution)/shard_map/ppermute | solution.py:411
  65.4 18.2 %collective-permute-start.21 = (bf16[2,160,512]{2,1,0:T(8,128)(2,1)S(1)}, bf16[2,160,512]{2,1,0:T(8,128)(2,1)S(1)}, u32[]{:S(2)}, u32[]{:S(2)}) collective-permute-start(bf16[2,160,512]{2,1,0:T(8,128)(2,1)S(1)} %get-tuple-element.104), channel_id=1, source_target_pairs={{0,2},{2,0},{4,6},{6,4},{1,3},{3,1},{5,7},{7,5},{8,10},{10,8},{12,... | collective-permute-start | bytes 983048 | tf_op jit(solution)/shard_map/ppermute | solution.py:411
  68.1 9.2 %collective-permute-start.6 = (bf16[128,1024]{1,0:T(8,128)(2,1)S(1)}, bf16[128,1024]{1,0:T(8,128)(2,1)S(1)}, u32[]{:S(2)}, u32[]{:S(2)}) collective-permute-start(bf16[128,1024]{1,0:T(8,128)(2,1)S(1)} %get-tuple-element.72), channel_id=1, source_target_pairs={{0,8},{8,0},{16,24},{24,16},{1,9},{9,1},{17,25},{25,17},{2,10},{10... | collective-permute-start | bytes 786440 | tf_op jit(solution)/shard_map/ppermute | solution.py:411
  69.6 12.9 %collective-permute-start.7 = (bf16[128,1024]{1,0:T(8,128)(2,1)S(1)}, bf16[128,1024]{1,0:T(8,128)(2,1)S(1)}, u32[]{:S(2)}, u32[]{:S(2)}) collective-permute-start(bf16[128,1024]{1,0:T(8,128)(2,1)S(1)} %get-tuple-element.73), channel_id=1, source_target_pairs={{0,16},{8,24},{16,0},{24,8},{1,17},{9,25},{17,1},{25,9},{2,18},{10... | collective-permute-start | bytes 786440 | tf_op jit(solution)/shard_map/ppermute | solution.py:411
  71.6 11.7 %collective-permute-start.8 = (bf16[128,1024]{1,0:T(8,128)(2,1)S(1)}, bf16[128,1024]{1,0:T(8,128)(2,1)S(1)}, u32[]{:S(2)}, u32[]{:S(2)}) collective-permute-start(bf16[128,1024]{1,0:T(8,128)(2,1)S(1)} %get-tuple-element.74), channel_id=1, source_target_pairs={{0,24},{8,16},{16,8},{24,0},{1,25},{9,17},{17,9},{25,1},{2,26},{10... | collective-permute-start | bytes 786440 | tf_op jit(solution)/shard_map/ppermute | solution.py:411
  83.3 9.5 %collective-permute-start.22 = (bf16[1,160,512]{2,1,0:T(8,128)(2,1)S(1)}, bf16[1,160,512]{2,1,0:T(8,128)(2,1)S(1)}, u32[]{:S(2)}, u32[]{:S(2)}) collective-permute-start(bf16[1,160,512]{2,1,0:T(8,128)(2,1)S(1)} %add_convert_fusion.3), channel_id=1, source_target_pairs={{0,4},{2,6},{4,0},{6,2},{1,5},{3,7},{5,1},{7,3},{8,12},{10,14},{12... | collective-permute-start | bytes 491528 | tf_op jit(solution)/shard_map/ppermute | solution.py:411
  92.8 2.7 %collective-permute-start.23 = (bf16[512,1024]{1,0:T(8,128)(2,1)S(1)}, bf16[512,1024]{1,0:T(8,128)(2,1)S(1)}, u32[]{:S(2)}, u32[]{:S(2)}) collective-permute-start(bf16[512,1024]{1,0:T(8,128)(2,1)S(1)} %join_blocks.6.refs_2_), channel_id=1, source_target_pairs={{0,1},{1,0},{2,3},{3,2},{4,5},{5,4},{6,7},{7,6},{8,9},{9,8},{10,11... | collective-permute-start | bytes 3145736 | tf_op jit(solution)/shard_map/ppermute | solution.py:411
  96.7 12.8 %collective-permute-start.24 = (bf16[2,160,512]{2,1,0:T(8,128)(2,1)S(1)}, bf16[2,160,512]{2,1,0:T(8,128)(2,1)S(1)}, u32[]{:S(2)}, u32[]{:S(2)}) collective-permute-start(bf16[2,160,512]{2,1,0:T(8,128)(2,1)S(1)} %get-tuple-element.113), channel_id=1, source_target_pairs={{0,2},{2,0},{4,6},{6,4},{1,3},{3,1},{5,7},{7,5},{8,10},{10,8},{12,... | collective-permute-start | bytes 983048 | tf_op jit(solution)/shard_map/ppermute | solution.py:411
  96.8 12.7 %collective-permute-start.3 = (bf16[128,1024]{1,0:T(8,128)(2,1)S(1)}, bf16[128,1024]{1,0:T(8,128)(2,1)S(1)}, u32[]{:S(2)}, u32[]{:S(2)}) collective-permute-start(bf16[128,1024]{1,0:T(8,128)(2,1)S(1)} %get-tuple-element.68), channel_id=1, source_target_pairs={{0,8},{8,0},{16,24},{24,16},{1,9},{9,1},{17,25},{25,17},{2,10},{10... | collective-permute-start | bytes 786440 | tf_op jit(solution)/shard_map/ppermute | solution.py:411
  98.3 13.7 %collective-permute-start.4 = (bf16[128,1024]{1,0:T(8,128)(2,1)S(1)}, bf16[128,1024]{1,0:T(8,128)(2,1)S(1)}, u32[]{:S(2)}, u32[]{:S(2)}) collective-permute-start(bf16[128,1024]{1,0:T(8,128)(2,1)S(1)} %get-tuple-element.69), channel_id=1, source_target_pairs={{0,16},{8,24},{16,0},{24,8},{1,17},{9,25},{17,1},{25,9},{2,18},{10... | collective-permute-start | bytes 786440 | tf_op jit(solution)/shard_map/ppermute | solution.py:411
  98.4 13.6 %collective-permute-start.5 = (bf16[128,1024]{1,0:T(8,128)(2,1)S(1)}, bf16[128,1024]{1,0:T(8,128)(2,1)S(1)}, u32[]{:S(2)}, u32[]{:S(2)}) collective-permute-start(bf16[128,1024]{1,0:T(8,128)(2,1)S(1)} %get-tuple-element.70), channel_id=1, source_target_pairs={{0,24},{8,16},{16,8},{24,0},{1,25},{9,17},{17,9},{25,1},{2,26},{10... | collective-permute-start | bytes 786440 | tf_op jit(solution)/shard_map/ppermute | solution.py:411
  100.3 11.7 %collective-permute-start.25 = (bf16[1,160,512]{2,1,0:T(8,128)(2,1)S(1)}, bf16[1,160,512]{2,1,0:T(8,128)(2,1)S(1)}, u32[]{:S(2)}, u32[]{:S(2)}) collective-permute-start(bf16[1,160,512]{2,1,0:T(8,128)(2,1)S(1)} %add_convert_fusion.2), channel_id=1, source_target_pairs={{0,4},{2,6},{4,0},{6,2},{1,5},{3,7},{5,1},{7,3},{8,12},{10,14},{12... | collective-permute-start | bytes 491528 | tf_op jit(solution)/shard_map/ppermute | solution.py:411
  112.1 2.7 %collective-permute-start.26 = (bf16[512,1024]{1,0:T(8,128)(2,1)S(1)}, bf16[512,1024]{1,0:T(8,128)(2,1)S(1)}, u32[]{:S(2)}, u32[]{:S(2)}) collective-permute-start(bf16[512,1024]{1,0:T(8,128)(2,1)S(1)} %join_blocks.7.refs_2_), channel_id=1, source_target_pairs={{0,1},{1,0},{2,3},{3,2},{4,5},{5,4},{6,7},{7,6},{8,9},{9,8},{10,11... | collective-permute-start | bytes 3145736 | tf_op jit(solution)/shard_map/ppermute | solution.py:411
  116.0 13.3 %collective-permute-start.27 = (bf16[2,160,512]{2,1,0:T(8,128)(2,1)S(1)}, bf16[2,160,512]{2,1,0:T(8,128)(2,1)S(1)}, u32[]{:S(2)}, u32[]{:S(2)}) collective-permute-start(bf16[2,160,512]{2,1,0:T(8,128)(2,1)S(1)} %get-tuple-element.122), channel_id=1, source_target_pairs={{0,2},{2,0},{4,6},{6,4},{1,3},{3,1},{5,7},{7,5},{8,10},{10,8},{12,... | collective-permute-start | bytes 983048 | tf_op jit(solution)/shard_map/ppermute | solution.py:411
  117.7 13.3 %collective-permute-start.29 = (bf16[1,160,512]{2,1,0:T(8,128)(2,1)S(1)}, bf16[1,160,512]{2,1,0:T(8,128)(2,1)S(1)}, u32[]{:S(2)}, u32[]{:S(2)}) collective-permute-start(bf16[1,160,512]{2,1,0:T(8,128)(2,1)S(1)} %add_convert_fusion.1), channel_id=1, source_target_pairs={{0,4},{2,6},{4,0},{6,2},{1,5},{3,7},{5,1},{7,3},{8,12},{10,14},{12... | collective-permute-start | bytes 491528 | tf_op jit(solution)/shard_map/ppermute | solution.py:411
  129.3 8.9 %collective-permute-start.28 = (bf16[1,160,512]{2,1,0:T(8,128)(2,1)S(1)}, bf16[1,160,512]{2,1,0:T(8,128)(2,1)S(1)}, u32[]{:S(2)}, u32[]{:S(2)}) collective-permute-start(bf16[1,160,512]{2,1,0:T(8,128)(2,1)S(1)} %add_convert_fusion), channel_id=1, source_target_pairs={{0,4},{2,6},{4,0},{6,2},{1,5},{3,7},{5,1},{7,3},{8,12},{10,14},{12... | collective-permute-start | bytes 491528 | tf_op jit(solution)/shard_map/ppermute | solution.py:411

commit v4 on v3

--- a/solution.py
+++ b/solution.py
@@ -277,12 +277,7 @@
 
 
 def groups_of(lines):
-    groups = []
-    step = 1
-    while step < lines:
-        groups.append(list(range(step, lines, 2 * step)))
-        step *= 2
-    return groups + [[0]]
+    return [list(range(lines))]
 
 
 def pair_kernel(place, table, mine, other, *rest, slots, groups, quarter):
@@ -297,7 +292,7 @@
 
     for group, out in zip(groups, outs):
         for index, distance in enumerate(group):
-            first = (line ^ distance) * slots
+            first = distance * slots
 
             def summed(slot, first=first):
                 column = pl.ds(pl.multiple_of(table[first + slot] * chunk, 128), chunk)
@@ -412,16 +407,7 @@
 
 
 def scatter_sum(pieces):
-    pieces = list(pieces)
-    kept = [pieces[-1]]
-    for stage in range(len(pieces) - 1):
-        received = swapped(pieces[stage], "line", 1 << stage)
-        kept.append(received)
-        for later in range(stage + 1, len(pieces) - 1):
-            step = 1 << (later - stage - 1)
-            part = received[step :: 2 * step].astype(jnp.float32)
-            pieces[later] = (pieces[later].astype(jnp.float32) + part).astype(jnp.bfloat16)
-    return kept, pieces[-2]
+    return lax.psum_scatter(pieces, "line", scatter_dimension=0, tiled=True)
 
 
 def per_device(images, psf_coef, phases, col_shift, band_offset, exposure_weight, patch_site):
@@ -473,11 +459,12 @@
 
     result = None
     count = len(chunks)
-    sent, sums, partial, kept = [None] * count, [None] * count, [None] * count, [None] * count
+    sent, sums, kept = [None] * count, [None] * count, [None] * count
 
     def filtered(index):
         start, chunk = chunks[index]
-        sent[index] = filter_chunk(weight, low, image, high, rows_m, cols_m, [], start, chunk, segments)
+        held = tied(weight, sums[index - 2]) if index >= 2 else weight
+        sent[index] = filter_chunk(held, low, image, high, rows_m, cols_m, [], start, chunk, segments)
 
     filtered(0)
     for index, (start, chunk) in enumerate(chunks):
@@ -491,14 +478,14 @@
         if index == 1:
             received = tied(received, scale)
         if index >= 1:
-            received = tied(received, partial[index - 1])
+            received = tied(received, sums[index - 1])
         if index >= 2:
             received = tied(received, kept[index - 2])
         mine = joined([outgoing[0]] + received)
         other = swapped(mine, "core", 1)
-        sums[index] = pair_sum(place, table, mine, other, [], slots, lines, quarter)
-        kept[index], partial[index] = scatter_sum(sums[index])
-        result = finish_chunk(kept[index], scale, result, start)
+        sums[index] = pair_sum(place, table, mine, other, [], slots, lines, quarter)[0]
+        kept[index] = scatter_sum(sums[index])
+        result = finish_chunk([kept[index]], scale, result, start)
     return result.reshape(slots, quarter, half_cols)
 
 

time: 139 us -> 155 us (1.12)
  between operations: 2.29 us -> 15.4 us
  starting transfers between devices: 38.3 us -> 30.4 us
  local copies, waits for them, and re-layouts: 5.92 us -> 13 us
  Pallas kernels: 31.1 us -> 34.8 us
    reduce_scatter x0 -> x4, waiting for transfers between devices: none -> 37 us  [scatter_sum(): return lax.psum_scatter(pieces, 'line', scatter_dimension=0, tiled=True)]
    ppermute x28 -> x20, waiting for transfers between devices: 58.9 us -> 23.1 us  [swapped(): return lax.ppermute(value, axis, [(i, i ^ distance) for i in range(count)])]
    ppermute x28 -> x20, starting transfers between devices: 31.5 us -> 23.3 us  [swapped(): return lax.ppermute(value, axis, [(i, i ^ distance) for i in range(count)])]
    unnamed x26 -> x40, local copies, waits for them, and re-layouts: 4.67 us -> 11.7 us
    pallas_call x4, Pallas kernels: 0.28 us -> 2.5 us  [joined(): pl.pallas_call(join_kernel, out_shape=jax.ShapeDtypeStruct((len(blocks) *...]
    pallas_call x4, Pallas kernels: 18.3 us -> 20.2 us  [filter_chunk(): pl.pallas_call(functools.partial(filter_kernel, first_chunk=start == 0, l...]
  transfers between devices with their start and end apart: 30 -> 26, of which waited for: 15 -> 11; matrix products, arithmetic and copies ran while one was open for 2% -> 1% of each run, Pallas kernels for 15% -> 19%
where the time goes in v4:
time: 155 us
  waiting for transfers between devices  60.2 us (39%)
  Pallas kernels  34.8 us (22%)
  starting transfers between devices  30.4 us (20%)
  between operations  15.4 us (10%)
  local copies, waits for them, and re-layouts  13 us (8%)
    reduce_scatter x4, waiting for transfers between devices, scatter_sum(): return lax.psum_scatter(pieces, 'line', scatter_dimension=0, tiled=True)  37 us
    ppermute x20, starting transfers between devices, swapped(): return lax.ppermute(value, axis, [(i, i ^ distance) for i in range(count)])  23.3 us
    ppermute x20, waiting for transfers between devices, swapped(): return lax.ppermute(value, axis, [(i, i ^ distance) for i in range(count)])  23.1 us
    pallas_call x4, Pallas kernels, filter_chunk(): pl.pallas_call(functools.partial(filter_kernel, first_chunk=start == 0, l...  20.2 us
    unnamed x40, local copies, waits for them, and re-layouts  11.7 us
    ppermute x1, starting transfers between devices, per_device(): low = lax.ppermute(image[rows - HALO:], 'seg', forward)  5.49 us
    pallas_call x4, Pallas kernels, pair_sum(): pl.pallas_call(kernel, out_shape=[jax.ShapeDtypeStruct((len(group), slots...  5.02 us
    pallas_call x4, Pallas kernels, finish_chunk(): pl.pallas_call(functools.partial(finish_kernel, count=len(pieces)), out_s...  3.13 us
  transfers between devices with their start and end apart: 26, of which 11 were waited for; matrix products, arithmetic and copies ran while one was open for 1% of the time, Pallas kernels for 19%

profile of v4, /device:TPU:0, one launch (start us, length us, event | category | flops | bytes accessed | tf_op | source)
XLA Modules:
  0.0 154.9 jit_solution(17409616250094697590)
XLA Ops:
  6.5 1.1 slice_bitcast_fusion
  7.6 1.3 collective-permute-start.2
  8.9 5.5 %collective-permute-start.1 = (f32[16,4096]{1,0:T(8,128)S(1)}, f32[16,4096]{1,0:T(8,128)S(1)}, u32[]{:S(2)}, u32[]{:S(2)}) collective-permute-start(f32[16,4096]{1,0:T(8,128)S(1)} %get-tuple-element.108), channel_id=1, source_target_pairs={{0,8},{8,16},{16,24},{1,9},{9,17},{17,25},{2,10},{10,18},{18,26},{... | collective-permute-start | bytes 786440 | tf_op jit(solution)/shard_map/ppermute | solution.py:427
  16.5 2.1 %band_matrices.1 = (bf16[3,128,480]{2,1,0:T(8,128)(2,1)S(1)}, bf16[3,2,512,256]{3,2,1,0:T(8,128)(2,1)S(1)}) custom-call(s32[3]{0:T(128)S(1)} %pad_add_fusion.1.place.refs_0_, f32[1,2,3]{2,1,0:T(2,128)S(1)} %copy-done.18, s32[1,2]{1,0:T(1,128)S(1)} %copy-done.19, s32[1]{0:T(128)S(6)} %copy.14.shift), custom_call_target="tpu_custom_call" | custom-call | flops 1 | bytes 1 | tf_op jit(solution)/shard_map/band_matrices/pallas_call | solution.py:132
  20.0 4.6 %warp_filter.5 = (bf16[128,1024]{1,0:T(8,128)(2,1)S(1)}, bf16[128,1024]{1,0:T(8,128)(2,1)S(1)}, bf16[128,1024]{1,0:T(8,128)(2,1)S(1)}, bf16[128,1024]{1,0:T(8,128)(2,1)S(1)}) custom-call(f32[1]{0:T(128)} %convert_element_type.9.weight, f32[16,4096]{1,0:T(8,128)S(1)} %collective-permute-done.1.low_l.low_c.low_r, ...), custom_call_target="tpu_custom_call" | custom-call | flops 1 | bytes 1 | tf_op jit(solution)/shard_map/warp_filter/pallas_call | solution.py:236
  24.5 3.9 %collective-permute-start.6 = (bf16[128,1024]{1,0:T(8,128)(2,1)S(1)}, bf16[128,1024]{1,0:T(8,128)(2,1)S(1)}, u32[]{:S(2)}, u32[]{:S(2)}) collective-permute-start(bf16[128,1024]{1,0:T(8,128)(2,1)S(1)} %get-tuple-element.62), channel_id=1, source_target_pairs={{0,8},{8,0},{16,24},{24,16},{1,9},{9,1},{17,25},{25,17},{2,10},{10... | collective-permute-start | bytes 786440 | tf_op jit(solution)/shard_map/ppermute | solution.py:406
  28.5 3.7 %collective-permute-start.7 = (bf16[128,1024]{1,0:T(8,128)(2,1)S(1)}, bf16[128,1024]{1,0:T(8,128)(2,1)S(1)}, u32[]{:S(2)}, u32[]{:S(2)}) collective-permute-start(bf16[128,1024]{1,0:T(8,128)(2,1)S(1)} %get-tuple-element.63), channel_id=1, source_target_pairs={{0,16},{8,24},{16,0},{24,8},{1,17},{9,25},{17,1},{25,9},{2,18},{10... | collective-permute-start | bytes 786440 | tf_op jit(solution)/shard_map/ppermute | solution.py:406
  32.2 1.1 collective-permute-done.9
  33.4 1.6 %collective-permute-start.10 = (f32[2,3]{1,0:T(2,128)S(1)}, f32[2,3]{1,0:T(2,128)S(1)}, u32[]{:S(2)}, u32[]{:S(2)}) collective-permute-start(f32[2,3]{1,0:T(2,128)S(1)} %pad_maximum_fusion.2), channel_id=1, source_target_pairs={{0,2},{2,0},{4,6},{6,4},{1,3},{3,1},{5,7},{7,5},{8,10},{10,8},{12,... | collective-permute-start | bytes 80 | tf_op jit(solution)/shard_map/ppermute | solution.py:406
  35.0 2.0 %collective-permute-done.10 = f32[2,3]{1,0:T(2,128)S(1)} collective-permute-done((f32[2,3]{1,0:T(2,128)S(1)}, f32[2,3]{1,0:T(2,128)S(1)}, u32[]{:S(2)}, u32[]{:S(2)}) %collective-permute-start.10) | collective-permute-done | bytes 56 | tf_op jit(solution)/shard_map/ppermute | solution.py:406
  37.1 5.2 %warp_filter.4 = (bf16[128,1024]{1,0:T(8,128)(2,1)S(1)}, bf16[128,1024]{1,0:T(8,128)(2,1)}, bf16[128,1024]{1,0:T(8,128)(2,1)}, bf16[128,1024]{1,0:T(8,128)(2,1)}) custom-call(f32[1]{0:T(128)} %convert_element_type.9.weight, f32[16,4096]{1,0:T(8,128)S(1)} %collective-permute-done.1.low_l.low_c.low_r, f32[16,4096]{1,0:T(8,128)S(1)} %collective-permute-done.1.low_l.low_c.low_r, ...), custom_call_target="tpu_custom_call" | custom-call | flops 1 | bytes 1 | tf_op jit(solution)/shard_map/warp_filter/pallas_call | solution.py:236
  43.9 1.8 %collective-permute-done = s32[1]{0:T(128)} collective-permute-done((s32[1]{0:T(128)}, s32[1]{0:T(128)}, u32[]{:S(2)}, u32[]{:S(2)}) %collective-permute-start) | collective-permute-done | bytes 36 | tf_op jit(solution)/shard_map/ppermute | solution.py:406
  46.3 1.5 collective-permute-start.3
  47.8 2.0 %collective-permute-start.4 = (bf16[128,1024]{1,0:T(8,128)(2,1)}, bf16[128,1024]{1,0:T(8,128)(2,1)}, u32[]{:S(2)}, u32[]{:S(2)}) collective-permute-start(bf16[128,1024]{1,0:T(8,128)(2,1)} %get-tuple-element.59), channel_id=1, source_target_pairs={{0,16},{8,24},{16,0},{24,8},{1,17},{9,25},{17,1},{25,9},{2,18},{10... | collective-permute-start | bytes 786440 | tf_op jit(solution)/shard_map/ppermute | solution.py:406
  49.9 1.8 %pair_sum.4 = bf16[4,160,512]{2,1,0:T(8,128)(2,1)S(1)} custom-call(s32[3]{0:T(128)S(1)} %pad_add_fusion.1.place.refs_0_, s32[240]{0:T(256)S(1)} %pad_add_fusion.refs_1_, bf16[512,1024]{1,0:T(8,128)(2,1)S(1)} %join_blocks.4.refs_2_, bf16[512,1024]{1,0:T(8,128)(2,1)} %collective-permute-done.11.refs_3_), custom_call_target="tpu_custom_call" | custom-call | flops 1 | bytes 1 | tf_op jit(solution)/shard_map/pair_sum/pallas_call | solution.py:320
  51.7 0.8 copy-done.3
  52.6 2.7 %collective-permute-start.12 = (f32[4,3]{1,0:T(4,128)S(1)}, f32[4,3]{1,0:T(4,128)S(1)}, u32[]{:S(2)}, u32[]{:S(2)}) collective-permute-start(f32[4,3]{1,0:T(4,128)S(1)} %pad_maximum_fusion.1), channel_id=1, source_target_pairs={{0,4},{2,6},{4,0},{6,2},{1,5},{3,7},{5,1},{7,3},{8,12},{10,14},{12... | collective-permute-start | bytes 152 | tf_op jit(solution)/shard_map/ppermute | solution.py:406
  55.3 1.9 %collective-permute-done.12 = f32[4,3]{1,0:T(4,128)S(1)} collective-permute-done((f32[4,3]{1,0:T(4,128)S(1)}, f32[4,3]{1,0:T(4,128)S(1)}, u32[]{:S(2)}, u32[]{:S(2)}) %collective-permute-start.12) | collective-permute-done | bytes 80 | tf_op jit(solution)/shard_map/ppermute | solution.py:406
  57.3 1.8 %patch_weights.1.refs_1_ = f32[160,2048]{1,0:T(8,128)S(1)} custom-call(s32[3]{0:T(128)S(1)} %pad_add_fusion.1.place.refs_0_, s32[160]{0:T(256)S(1)} %copy-done.17, f32[8,3]{1,0:T(8,128)S(1)} %pad_maximum_fusion.facts), custom_call_target="tpu_custom_call" | custom-call | flops 1 | bytes 1 | tf_op jit(solution)/shard_map/patch_weights/pallas_call | solution.py:359
  59.1 1.0 copy-done.1
  60.1 5.2 %warp_filter.6 = (bf16[128,1024]{1,0:T(8,128)(2,1)S(1)}, bf16[128,1024]{1,0:T(8,128)(2,1)}, bf16[128,1024]{1,0:T(8,128)(2,1)}, bf16[128,1024]{1,0:T(8,128)(2,1)}) custom-call(f32[1]{0:T(128)} %convert_element_type.9.weight, f32[16,4096]{1,0:T(8,128)S(1)} %collective-permute-done.1.low_l.low_c.low_r, f32[16,4096]{1,0:T(8,128)S(1)} %collective-permute-done.1.low_l.low_c.low_r, ...), custom_call_target="tpu_custom_call" | custom-call | flops 1 | bytes 1 | tf_op jit(solution)/shard_map/warp_filter/pallas_call | solution.py:236
  66.1 1.2 join_blocks.5.refs_2_
  67.3 1.5 collective-permute-start.17
  68.9 2.0 %collective-permute-start.18 = (bf16[128,1024]{1,0:T(8,128)(2,1)}, bf16[128,1024]{1,0:T(8,128)(2,1)}, u32[]{:S(2)}, u32[]{:S(2)}) collective-permute-start(bf16[128,1024]{1,0:T(8,128)(2,1)} %get-tuple-element.74), channel_id=1, source_target_pairs={{0,16},{8,24},{16,0},{24,8},{1,17},{9,25},{17,1},{25,9},{2,18},{10... | collective-permute-start | bytes 786440 | tf_op jit(solution)/shard_map/ppermute | solution.py:406
  70.9 1.1 pair_sum.5
  72.0 0.8 copy-done.4
  73.1 1.0 copy-done.2
  74.1 5.2 %warp_filter.7 = (bf16[128,1024]{1,0:T(8,128)(2,1)S(1)}, bf16[128,1024]{1,0:T(8,128)(2,1)}, bf16[128,1024]{1,0:T(8,128)(2,1)}, bf16[128,1024]{1,0:T(8,128)(2,1)}) custom-call(f32[1]{0:T(128)} %convert_element_type.9.weight, f32[16,4096]{1,0:T(8,128)S(1)} %collective-permute-done.1.low_l.low_c.low_r, f32[16,4096]{1,0:T(8,128)S(1)} %collective-permute-done.1.low_l.low_c.low_r, ...), custom_call_target="tpu_custom_call" | custom-call | flops 1 | bytes 1 | tf_op jit(solution)/shard_map/warp_filter/pallas_call | solution.py:236
  80.0 3.5 %collective-permute-done.18.refs_2_ = bf16[128,1024]{1,0:T(8,128)(2,1)} collective-permute-done((bf16[128,1024]{1,0:T(8,128)(2,1)}, bf16[128,1024]{1,0:T(8,128)(2,1)}, u32[]{:S(2)}, u32[]{:S(2)}) %collective-permute-start.18) | collective-permute-done | bytes 262176 | tf_op jit(solution)/shard_map/ppermute | solution.py:406
  83.4 1.0 copy-done.10
  84.4 1.2 join_blocks.6.refs_2_
  85.7 1.6 %collective-permute-start.14 = (bf16[128,1024]{1,0:T(8,128)(2,1)}, bf16[128,1024]{1,0:T(8,128)(2,1)S(1)}, u32[]{:S(2)}, u32[]{:S(2)}) collective-permute-start(bf16[128,1024]{1,0:T(8,128)(2,1)} %get-tuple-element.87), channel_id=1, source_target_pairs={{0,8},{8,0},{16,24},{24,16},{1,9},{9,1},{17,25},{25,17},{2,10},{10... | collective-permute-start | bytes 786440 | tf_op jit(solution)/shard_map/ppermute | solution.py:406
  87.8 1.4 collective-permute-start.16
  89.2 1.1 pair_sum.6
  90.3 0.8 copy-done.5
  91.2 3.8 %collective-permute-done.14.refs_1_ = bf16[128,1024]{1,0:T(8,128)(2,1)S(1)} collective-permute-done((bf16[128,1024]{1,0:T(8,128)(2,1)}, bf16[128,1024]{1,0:T(8,128)(2,1)S(1)}, u32[]{:S(2)}, u32[]{:S(2)}) %collective-permute-start.14) | collective-permute-done | bytes 262176 | tf_op jit(solution)/shard_map/ppermute | solution.py:406
  95.0 4.6 %collective-permute-done.15.refs_2_ = bf16[128,1024]{1,0:T(8,128)(2,1)S(1)} collective-permute-done((bf16[128,1024]{1,0:T(8,128)(2,1)}, bf16[128,1024]{1,0:T(8,128)(2,1)S(1)}, u32[]{:S(2)}, u32[]{:S(2)}) %collective-permute-start.15) | collective-permute-done | bytes 262176 | tf_op jit(solution)/shard_map/ppermute | solution.py:406
  99.7 1.7 %collective-permute-done.16.refs_3_ = bf16[128,1024]{1,0:T(8,128)(2,1)S(1)} collective-permute-done((bf16[128,1024]{1,0:T(8,128)(2,1)}, bf16[128,1024]{1,0:T(8,128)(2,1)S(1)}, u32[]{:S(2)}, u32[]{:S(2)}) %collective-permute-start.16) | collective-permute-done | bytes 262176 | tf_op jit(solution)/shard_map/ppermute | solution.py:406
  101.6 2.6 %collective-permute-done.21.refs_3_ = bf16[512,1024]{1,0:T(8,128)(2,1)S(1)} collective-permute-done((bf16[512,1024]{1,0:T(8,128)(2,1)S(1)}, bf16[512,1024]{1,0:T(8,128)(2,1)S(1)}, u32[]{:S(2)}, u32[]{:S(2)}) %collective-permute-start.21) | collective-permute-done | bytes 1048608 | tf_op jit(solution)/shard_map/ppermute | solution.py:406
  104.2 1.1 pair_sum.7
  105.3 0.9 copy-done.6
  106.2 0.8 patch_mean.4.refs_2_
  107.2 0.8 patch_mean.5.refs_2_
  107.9 15.5 %reduce-scatter.11.cloned.1.call-done.refs_0_ = bf16[1,160,512]{2,1,0:T(8,128)(2,1)} async-done(((bf16[4,160,512]{2,1,0:T(8,128)(2,1)}), bf16[1,160,512]{2,1,0:T(8,128)(2,1)}) %reduce-scatter.11.cloned.1.call-update) | async-done | bytes 163856 | tf_op jit(solution)/shard_map/reduce_scatter | solution.py:410
  123.4 0.9 copy-done.14
  124.3 0.8 patch_mean.6.refs_2_
  125.1 21.5 %reduce-scatter.9.cloned.1.call-done.refs_0_ = bf16[1,160,512]{2,1,0:T(8,128)(2,1)} async-done(((bf16[4,160,512]{2,1,0:T(8,128)(2,1)}), bf16[1,160,512]{2,1,0:T(8,128)(2,1)}) %reduce-scatter.9.cloned.1.call-update) | async-done | bytes 163856 | tf_op jit(solution)/shard_map/reduce_scatter | solution.py:410
  146.7 0.9 copy-done.15
  (78 shorter events, 7.6 us)
Async XLA Ops:
  6.5 76.9 %reduce-scatter.5.cloned.1.call-start = ((), (), s32[]{:S(2)}) async-start(), calls=%async_computation.4 | async-start | bytes 819200 | tf_op jit(solution)/shard_map/reduce_scatter | solution.py:410
  7.6 12.4 %collective-permute-start.2 = (f32[16,4096]{1,0:T(8,128)S(1)}, f32[16,4096]{1,0:T(8,128)S(1)}, u32[]{:S(2)}, u32[]{:S(2)}) collective-permute-start(f32[16,4096]{1,0:T(8,128)S(1)} %get-tuple-element.107), channel_id=1, source_target_pairs={{8,0},{16,8},{24,16},{9,1},{17,9},{25,17},{10,2},{18,10},{26,18},{... | collective-permute-start | bytes 786440 | tf_op jit(solution)/shard_map/ppermute | solution.py:428
  8.9 11.1 %collective-permute-start.1 = (f32[16,4096]{1,0:T(8,128)S(1)}, f32[16,4096]{1,0:T(8,128)S(1)}, u32[]{:S(2)}, u32[]{:S(2)}) collective-permute-start(f32[16,4096]{1,0:T(8,128)S(1)} %get-tuple-element.108), channel_id=1, source_target_pairs={{0,8},{8,16},{16,24},{1,9},{9,17},{17,25},{2,10},{10,18},{18,26},{... | collective-permute-start | bytes 786440 | tf_op jit(solution)/shard_map/ppermute | solution.py:427
  15.1 0.7 copy-start.18
  15.8 0.7 copy-start.19
  18.6 18.4 %copy-start = (bf16[3,128,480]{2,1,0:T(8,128)(2,1)}, bf16[3,128,480]{2,1,0:T(8,128)(2,1)S(1)}, u32[]{:S(2)}) copy-start(bf16[3,128,480]{2,1,0:T(8,128)(2,1)S(1)} %get-tuple-element.55.rows_m) | copy-start | bytes 1105924
  24.5 18.4 %collective-permute-start.6 = (bf16[128,1024]{1,0:T(8,128)(2,1)S(1)}, bf16[128,1024]{1,0:T(8,128)(2,1)S(1)}, u32[]{:S(2)}, u32[]{:S(2)}) collective-permute-start(bf16[128,1024]{1,0:T(8,128)(2,1)S(1)} %get-tuple-element.62), channel_id=1, source_target_pairs={{0,8},{8,0},{16,24},{24,16},{1,9},{9,1},{17,25},{25,17},{2,10},{10... | collective-permute-start | bytes 786440 | tf_op jit(solution)/shard_map/ppermute | solution.py:406
  28.5 14.5 %collective-permute-start.7 = (bf16[128,1024]{1,0:T(8,128)(2,1)S(1)}, bf16[128,1024]{1,0:T(8,128)(2,1)S(1)}, u32[]{:S(2)}, u32[]{:S(2)}) collective-permute-start(bf16[128,1024]{1,0:T(8,128)(2,1)S(1)} %get-tuple-element.63), channel_id=1, source_target_pairs={{0,16},{8,24},{16,0},{24,8},{1,17},{9,25},{17,1},{25,9},{2,18},{10... | collective-permute-start | bytes 786440 | tf_op jit(solution)/shard_map/ppermute | solution.py:406
  32.1 10.9 %collective-permute-start.8 = (bf16[128,1024]{1,0:T(8,128)(2,1)S(1)}, bf16[128,1024]{1,0:T(8,128)(2,1)S(1)}, u32[]{:S(2)}, u32[]{:S(2)}) collective-permute-start(bf16[128,1024]{1,0:T(8,128)(2,1)S(1)} %get-tuple-element.64), channel_id=1, source_target_pairs={{0,24},{8,16},{16,8},{24,0},{1,25},{9,17},{17,9},{25,1},{2,26},{10... | collective-permute-start | bytes 786440 | tf_op jit(solution)/shard_map/ppermute | solution.py:406
  32.2 1.1 collective-permute-start.9
  33.4 3.6 %collective-permute-start.10 = (f32[2,3]{1,0:T(2,128)S(1)}, f32[2,3]{1,0:T(2,128)S(1)}, u32[]{:S(2)}, u32[]{:S(2)}) collective-permute-start(f32[2,3]{1,0:T(2,128)S(1)} %pad_maximum_fusion.2), channel_id=1, source_target_pairs={{0,2},{2,0},{4,6},{6,4},{1,3},{3,1},{5,7},{7,5},{8,10},{10,8},{12,... | collective-permute-start | bytes 80 | tf_op jit(solution)/shard_map/ppermute | solution.py:406
  42.3 0.7 copy-start.7
  43.0 0.7 copy-start.17
  43.1 6.8 %collective-permute-start.11 = (bf16[512,1024]{1,0:T(8,128)(2,1)S(1)}, bf16[512,1024]{1,0:T(8,128)(2,1)}, u32[]{:S(2)}, u32[]{:S(2)}) collective-permute-start(bf16[512,1024]{1,0:T(8,128)(2,1)S(1)} %join_blocks.4.refs_2_), channel_id=1, source_target_pairs={{0,1},{1,0},{2,3},{3,2},{4,5},{5,4},{6,7},{7,6},{8,9},{9,8},{10,11... | collective-permute-start | bytes 3145736 | tf_op jit(solution)/shard_map/ppermute | solution.py:406
  43.2 2.5 %collective-permute-start = (s32[1]{0:T(128)}, s32[1]{0:T(128)}, u32[]{:S(2)}, u32[]{:S(2)}) collective-permute-start(s32[1]{0:T(128)} %param.11), channel_id=1, source_target_pairs={{0,1},{1,0},{2,3},{3,2},{4,5},{5,4},{6,7},{7,6},{8,9},{9,8},{10,11... | collective-permute-start | bytes 20 | tf_op jit(solution)/shard_map/ppermute | solution.py:406
  46.3 19.7 %collective-permute-start.3 = (bf16[128,1024]{1,0:T(8,128)(2,1)}, bf16[128,1024]{1,0:T(8,128)(2,1)}, u32[]{:S(2)}, u32[]{:S(2)}) collective-permute-start(bf16[128,1024]{1,0:T(8,128)(2,1)} %get-tuple-element.58), channel_id=1, source_target_pairs={{0,8},{8,0},{16,24},{24,16},{1,9},{9,1},{17,25},{25,17},{2,10},{10... | collective-permute-start | bytes 786440 | tf_op jit(solution)/shard_map/ppermute | solution.py:406
  47.8 18.2 %collective-permute-start.4 = (bf16[128,1024]{1,0:T(8,128)(2,1)}, bf16[128,1024]{1,0:T(8,128)(2,1)}, u32[]{:S(2)}, u32[]{:S(2)}) collective-permute-start(bf16[128,1024]{1,0:T(8,128)(2,1)} %get-tuple-element.59), channel_id=1, source_target_pairs={{0,16},{8,24},{16,0},{24,8},{1,17},{9,25},{17,1},{25,9},{2,18},{10... | collective-permute-start | bytes 786440 | tf_op jit(solution)/shard_map/ppermute | solution.py:406
  49.8 16.2 %collective-permute-start.5 = (bf16[128,1024]{1,0:T(8,128)(2,1)}, bf16[128,1024]{1,0:T(8,128)(2,1)}, u32[]{:S(2)}, u32[]{:S(2)}) collective-permute-start(bf16[128,1024]{1,0:T(8,128)(2,1)} %get-tuple-element.60), channel_id=1, source_target_pairs={{0,24},{8,16},{16,8},{24,0},{1,25},{9,17},{17,9},{25,1},{2,26},{10... | collective-permute-start | bytes 786440 | tf_op jit(solution)/shard_map/ppermute | solution.py:406
  51.7 0.8 copy-start.3
  52.6 48.9 %reduce-scatter.7.cloned.1.call-start = ((), (), s32[]{:S(2)}) async-start(), calls=%async_computation.5 | async-start | bytes 819200 | tf_op jit(solution)/shard_map/reduce_scatter | solution.py:410
  52.6 4.5 %collective-permute-start.12 = (f32[4,3]{1,0:T(4,128)S(1)}, f32[4,3]{1,0:T(4,128)S(1)}, u32[]{:S(2)}, u32[]{:S(2)}) collective-permute-start(f32[4,3]{1,0:T(4,128)S(1)} %pad_maximum_fusion.1), channel_id=1, source_target_pairs={{0,4},{2,6},{4,0},{6,2},{1,5},{3,7},{5,1},{7,3},{8,12},{10,14},{12... | collective-permute-start | bytes 152 | tf_op jit(solution)/shard_map/ppermute | solution.py:406
  59.1 1.0 copy-start.1
  60.1 5.9 %copy-start.8 = (bf16[128,1024]{1,0:T(8,128)(2,1)S(1)}, bf16[128,1024]{1,0:T(8,128)(2,1)}, u32[]{:S(2)}) copy-start(bf16[128,1024]{1,0:T(8,128)(2,1)} %copy-done.7) | copy-start | bytes 786436
  65.3 0.7 copy-start.9
  67.2 3.6 %collective-permute-start.13 = (bf16[512,1024]{1,0:T(8,128)(2,1)S(1)}, bf16[512,1024]{1,0:T(8,128)(2,1)S(1)}, u32[]{:S(2)}, u32[]{:S(2)}) collective-permute-start(bf16[512,1024]{1,0:T(8,128)(2,1)S(1)} %join_blocks.5.refs_2_), channel_id=1, source_target_pairs={{0,1},{1,0},{2,3},{3,2},{4,5},{5,4},{6,7},{7,6},{8,9},{9,8},{10,11... | collective-permute-start | bytes 3145736 | tf_op jit(solution)/shard_map/ppermute | solution.py:406
  67.3 12.6 %collective-permute-start.17 = (bf16[128,1024]{1,0:T(8,128)(2,1)}, bf16[128,1024]{1,0:T(8,128)(2,1)}, u32[]{:S(2)}, u32[]{:S(2)}) collective-permute-start(bf16[128,1024]{1,0:T(8,128)(2,1)} %get-tuple-element.73), channel_id=1, source_target_pairs={{0,8},{8,0},{16,24},{24,16},{1,9},{9,1},{17,25},{25,17},{2,10},{10... | collective-permute-start | bytes 786440 | tf_op jit(solution)/shard_map/ppermute | solution.py:406
  68.9 14.6 %collective-permute-start.18 = (bf16[128,1024]{1,0:T(8,128)(2,1)}, bf16[128,1024]{1,0:T(8,128)(2,1)}, u32[]{:S(2)}, u32[]{:S(2)}) collective-permute-start(bf16[128,1024]{1,0:T(8,128)(2,1)} %get-tuple-element.74), channel_id=1, source_target_pairs={{0,16},{8,24},{16,0},{24,8},{1,17},{9,25},{17,1},{25,9},{2,18},{10... | collective-permute-start | bytes 786440 | tf_op jit(solution)/shard_map/ppermute | solution.py:406
  70.9 12.6 %collective-permute-start.19 = (bf16[128,1024]{1,0:T(8,128)(2,1)}, bf16[128,1024]{1,0:T(8,128)(2,1)}, u32[]{:S(2)}, u32[]{:S(2)}) collective-permute-start(bf16[128,1024]{1,0:T(8,128)(2,1)} %get-tuple-element.75), channel_id=1, source_target_pairs={{0,24},{8,16},{16,8},{24,0},{1,25},{9,17},{17,9},{25,1},{2,26},{10... | collective-permute-start | bytes 786440 | tf_op jit(solution)/shard_map/ppermute | solution.py:406
  72.0 0.8 copy-start.4
  72.8 50.6 %reduce-scatter.11.cloned.1.call-start = ((), (), s32[]{:S(2)}) async-start(), calls=%async_computation.7 | async-start | bytes 819200 | tf_op jit(solution)/shard_map/reduce_scatter | solution.py:410
  73.1 1.0 copy-start.2
  79.3 0.7 copy-start.11
  83.4 1.0 copy-start.10
  85.6 15.9 %copy-start.12 = (bf16[128,1024]{1,0:T(8,128)(2,1)S(1)}, bf16[128,1024]{1,0:T(8,128)(2,1)}, u32[]{:S(2)}) copy-start(bf16[128,1024]{1,0:T(8,128)(2,1)} %copy-done.11) | copy-start | bytes 786436
  85.6 3.6 %collective-permute-start.20 = (bf16[512,1024]{1,0:T(8,128)(2,1)S(1)}, bf16[512,1024]{1,0:T(8,128)(2,1)S(1)}, u32[]{:S(2)}, u32[]{:S(2)}) collective-permute-start(bf16[512,1024]{1,0:T(8,128)(2,1)S(1)} %join_blocks.6.refs_2_), channel_id=1, source_target_pairs={{0,1},{1,0},{2,3},{3,2},{4,5},{5,4},{6,7},{7,6},{8,9},{9,8},{10,11... | collective-permute-start | bytes 3145736 | tf_op jit(solution)/shard_map/ppermute | solution.py:406
  85.7 9.4 %collective-permute-start.14 = (bf16[128,1024]{1,0:T(8,128)(2,1)}, bf16[128,1024]{1,0:T(8,128)(2,1)S(1)}, u32[]{:S(2)}, u32[]{:S(2)}) collective-permute-start(bf16[128,1024]{1,0:T(8,128)(2,1)} %get-tuple-element.87), channel_id=1, source_target_pairs={{0,8},{8,0},{16,24},{24,16},{1,9},{9,1},{17,25},{25,17},{2,10},{10... | collective-permute-start | bytes 786440 | tf_op jit(solution)/shard_map/ppermute | solution.py:406
  87.2 12.5 %collective-permute-start.15 = (bf16[128,1024]{1,0:T(8,128)(2,1)}, bf16[128,1024]{1,0:T(8,128)(2,1)S(1)}, u32[]{:S(2)}, u32[]{:S(2)}) collective-permute-start(bf16[128,1024]{1,0:T(8,128)(2,1)} %get-tuple-element.88), channel_id=1, source_target_pairs={{0,16},{8,24},{16,0},{24,8},{1,17},{9,25},{17,1},{25,9},{2,18},{10... | collective-permute-start | bytes 786440 | tf_op jit(solution)/shard_map/ppermute | solution.py:406
  87.8 13.6 %collective-permute-start.16 = (bf16[128,1024]{1,0:T(8,128)(2,1)}, bf16[128,1024]{1,0:T(8,128)(2,1)S(1)}, u32[]{:S(2)}, u32[]{:S(2)}) collective-permute-start(bf16[128,1024]{1,0:T(8,128)(2,1)} %get-tuple-element.89), channel_id=1, source_target_pairs={{0,24},{8,16},{16,8},{24,0},{1,25},{9,17},{17,9},{25,1},{2,26},{10... | collective-permute-start | bytes 786440 | tf_op jit(solution)/shard_map/ppermute | solution.py:406
  90.3 0.8 copy-start.5
  91.2 55.5 %reduce-scatter.9.cloned.1.call-start = ((), (), s32[]{:S(2)}) async-start(), calls=%async_computation.6 | async-start | bytes 819200 | tf_op jit(solution)/shard_map/reduce_scatter | solution.py:410
  101.5 4.7 %copy-start.16 = (bf16[1,160,512]{2,1,0:T(8,128)(2,1)S(1)}, bf16[1,160,512]{2,1,0:T(8,128)(2,1)}, u32[]{:S(2)}) copy-start(bf16[1,160,512]{2,1,0:T(8,128)(2,1)} %reduce-scatter.5.cloned.1.call-done.refs_0_) | copy-start | bytes 491524
  101.5 2.7 %collective-permute-start.21 = (bf16[512,1024]{1,0:T(8,128)(2,1)S(1)}, bf16[512,1024]{1,0:T(8,128)(2,1)S(1)}, u32[]{:S(2)}, u32[]{:S(2)}) collective-permute-start(bf16[512,1024]{1,0:T(8,128)(2,1)S(1)} %join_blocks.7.refs_2_), channel_id=1, source_target_pairs={{0,1},{1,0},{2,3},{3,2},{4,5},{5,4},{6,7},{7,6},{8,9},{9,8},{10,11... | collective-permute-start | bytes 3145736 | tf_op jit(solution)/shard_map/ppermute | solution.py:406
  105.3 0.9 copy-start.6
  106.2 0.9 copy-start.13
  123.4 0.9 copy-start.14
  146.7 0.9 copy-start.15
Sparse Core Ops, SparseCore 0:
  52.7 23.8 reduce-scatter.4
  78.9 21.1 reduce-scatter.6
  102.4 21.0 reduce-scatter.10
  125.6 21.0 reduce-scatter.8

commit v5 on v4

--- a/solution.py
+++ b/solution.py
@@ -18,7 +18,7 @@
 SIDE = 128
 TILE = 256
 STRIP = 128
-PARTS = (4, 4, 4, 4)
+PARTS = (2, 2)
 VMEM = 48 * 1024 * 1024
 COST = pl.CostEstimate(flops=1, bytes_accessed=1, transcendentals=0)
 
@@ -147,7 +147,7 @@
     weight, low_l, low_c, low_r, mid_l, mid_c, mid_r, high_l, high_c, high_r, rows_m, cols_m, *rest,
     first_chunk, last_chunk, segments,
 ):
-    *outs, ext_high, ext_low, mat_high, mat_low = rest[-segments - 4 :]
+    *outs, ext_high, ext_low, mat_high, mat_low = rest
     half = pl.program_id(0)
     halves = pl.num_programs(0)
     rows, chunk = mid_c.shape
@@ -205,7 +205,7 @@
                 out[pl.ds(strip * piece, piece), pl.ds(tile * TILE, TILE)] = sent[owner * piece : (owner + 1) * piece]
 
 
-def filter_chunk(weight, low, image, high, rows_m, cols_m, after, start, chunk, segments):
+def filter_chunk(weight, low, image, high, rows_m, cols_m, start, chunk, segments):
     rows, width = image.shape
     halves = 2
     half_blocks = width // halves // SIDE
@@ -242,7 +242,7 @@
         ),
         out_shape=[jax.ShapeDtypeStruct((rows // segments, halves * chunk), jnp.bfloat16)] * segments,
         grid=(halves,),
-        in_specs=specs + [whole(rows_m), whole(cols_m)] + [pl.BlockSpec(memory_space=pl.ANY)] * len(after),
+        in_specs=specs + [whole(rows_m), whole(cols_m)],
         out_specs=[pl.BlockSpec((rows // segments, chunk), lambda h: (0, h))] * segments,
         scratch_shapes=[
             pltpu.VMEM((rows + 2 * HALO, wide), jnp.bfloat16),
@@ -253,7 +253,7 @@
         compiler_params=pltpu.CompilerParams(vmem_limit_bytes=VMEM),
         cost_estimate=COST,
         name="warp_filter",
-    )(weight, *([low] * 3), *([image] * 3), *([high] * 3), rows_m, cols_m, *after)
+    )(weight, *([low] * 3), *([image] * 3), *([high] * 3), rows_m, cols_m)
 
 
 def join_kernel(*refs):
@@ -276,57 +276,58 @@
     )(*blocks)
 
 
-def groups_of(lines):
-    return [list(range(lines))]
-
-
-def pair_kernel(place, table, mine, other, *rest, slots, groups, quarter):
-    outs, (mine_all, other_all) = rest[: len(groups)], rest[len(groups) :]
+def stage_distances(lines):
+    stages = []
+    step = 1
+    while step < lines:
+        stages.append(list(reversed(range(step, lines, 2 * step))))
+        step *= 2
+    return stages
+
+
+def pair_kernel(place, table, mine, other, *rest, slots, distances, quarter):
+    *outs, mine_all, other_all = rest
     rows = mine.shape[0]
-    chunk = outs[0].shape[2]
+    chunk = outs[0].shape[1]
     count = table.shape[0] // 3
     for source, held in ((mine, mine_all), (other, other_all)):
         held[pl.ds(0, rows), :] = source[...].astype(jnp.float32)
         held[pl.ds(rows, quarter), :] = jnp.zeros((quarter, source.shape[1]), jnp.float32)
     line = place[1]
 
-    for group, out in zip(groups, outs):
-        for index, distance in enumerate(group):
-            first = distance * slots
-
-            def summed(slot, first=first):
-                column = pl.ds(pl.multiple_of(table[first + slot] * chunk, 128), chunk)
-                from_mine = pl.ds(pl.multiple_of(table[count + first + slot], quarter), quarter)
-                from_other = pl.ds(pl.multiple_of(table[2 * count + first + slot], quarter), quarter)
-                return mine_all[from_mine, column] + other_all[from_other, column]
-
-            for slot in range(0, slots - 1, 2):
-                rows_two = jnp.concatenate([summed(slot), summed(slot + 1)], axis=0)
-                out[index, pl.ds(slot * quarter, 2 * quarter), :] = rows_two.astype(jnp.bfloat16)
-            if slots % 2:
-                out[index, pl.ds((slots - 1) * quarter, quarter), :] = summed(slots - 1).astype(jnp.bfloat16)
-
-
-def pair_sum(place, table, mine, other, after, slots, lines, quarter):
+    for distance, out in zip(distances, outs):
+        first = (line ^ distance) * slots
+
+        def summed(slot, first=first):
+            column = pl.ds(pl.multiple_of(table[first + slot] * chunk, 128), chunk)
+            from_mine = pl.ds(pl.multiple_of(table[count + first + slot], quarter), quarter)
+            from_other = pl.ds(pl.multiple_of(table[2 * count + first + slot], quarter), quarter)
+            return mine_all[from_mine, column] + other_all[from_other, column]
+
+        for slot in range(0, slots - 1, 2):
+            rows_two = jnp.concatenate([summed(slot), summed(slot + 1)], axis=0)
+            out[pl.ds(slot * quarter, 2 * quarter), :] = rows_two.astype(jnp.bfloat16)
+        if slots % 2:
+            out[pl.ds((slots - 1) * quarter, quarter), :] = summed(slots - 1).astype(jnp.bfloat16)
+
+
+def pair_sum(place, table, mine, other, slots, lines, quarter):
     rows, double = mine.shape
     chunk = double // 2
-    groups = groups_of(lines)
+    distances = sum(stage_distances(lines), []) + [0]
     smem = pl.BlockSpec(memory_space=pltpu.SMEM)
     vmem = pl.BlockSpec(memory_space=pltpu.VMEM)
-
-    def kernel(*refs):
-        pair_kernel(*refs[:4], *refs[4 + len(after) :], slots=slots, groups=groups, quarter=quarter)
-
-    return pl.pallas_call(
-        kernel,
-        out_shape=[jax.ShapeDtypeStruct((len(group), slots * quarter, chunk), jnp.bfloat16) for group in groups],
-        in_specs=[smem, smem, vmem, vmem] + [pl.BlockSpec(memory_space=pl.ANY)] * len(after),
-        out_specs=[vmem] * len(groups),
+    outs = pl.pallas_call(
+        functools.partial(pair_kernel, slots=slots, distances=distances, quarter=quarter),
+        out_shape=[jax.ShapeDtypeStruct((slots * quarter, chunk), jnp.bfloat16)] * lines,
+        in_specs=[smem, smem, vmem, vmem],
+        out_specs=[vmem] * lines,
         scratch_shapes=[pltpu.VMEM((rows + quarter, double), jnp.float32)] * 2,
         compiler_params=pltpu.CompilerParams(vmem_limit_bytes=VMEM),
         cost_estimate=COST,
         name="pair_sum",
-    )(place, table, mine, other, *after)
+    )(place, table, mine, other)
+    return dict(zip(distances, outs))
 
 
 def weight_kernel(place, sites, facts, out, covers, *, cores, quarter, width, bands):
@@ -377,9 +378,9 @@
 
 
 def finish_chunk(pieces, scale, result, start):
-    _, rows, chunk = pieces[0].shape
+    rows, chunk = pieces[0].shape
     column = pl.BlockSpec((rows, chunk), lambda i: (0, start // chunk))
-    specs = [pl.BlockSpec((None, rows, chunk), lambda i: (0, 0, 0))] * len(pieces) + [column]
+    specs = [pl.BlockSpec((rows, chunk), lambda i: (0, 0))] * len(pieces) + [column]
     operands = [*pieces, scale]
     aliases = {}
     if result is not None:
@@ -407,7 +408,19 @@
 
 
 def scatter_sum(pieces):
-    return lax.psum_scatter(pieces, "line", scatter_dimension=0, tiled=True)
+    pieces = dict(pieces)
+    kept, added = [pieces[0]], []
+    for stage, distances in enumerate(stage_distances(len(pieces))):
+        for distance in distances:
+            received = swapped(pieces[distance], "line", 1 << stage)
+            target = distance ^ (1 << stage)
+            if target:
+                both = pieces[target].astype(jnp.float32) + received.astype(jnp.float32)
+                pieces[target] = both.astype(jnp.bfloat16)
+                added = [pieces[target]]
+            else:
+                kept.append(received)
+    return kept, added
 
 
 def per_device(images, psf_coef, phases, col_shift, band_offset, exposure_weight, patch_site):
@@ -459,12 +472,12 @@
 
     result = None
     count = len(chunks)
-    sent, sums, kept = [None] * count, [None] * count, [None] * count
+    sent, sums, kept, added = [None] * count, [None] * count, [None] * count, [None] * count
 
     def filtered(index):
         start, chunk = chunks[index]
         held = tied(weight, sums[index - 2]) if index >= 2 else weight
-        sent[index] = filter_chunk(held, low, image, high, rows_m, cols_m, [], start, chunk, segments)
+        sent[index] = filter_chunk(held, low, image, high, rows_m, cols_m, start, chunk, segments)
 
     filtered(0)
     for index, (start, chunk) in enumerate(chunks):
@@ -478,14 +491,12 @@
         if index == 1:
             received = tied(received, scale)
         if index >= 1:
-            received = tied(received, sums[index - 1])
-        if index >= 2:
-            received = tied(received, kept[index - 2])
+            received = tied(received, (added[index - 1], kept[index - 1][:-1]))
         mine = joined([outgoing[0]] + received)
         other = swapped(mine, "core", 1)
-        sums[index] = pair_sum(place, table, mine, other, [], slots, lines, quarter)[0]
-        kept[index] = scatter_sum(sums[index])
-        result = finish_chunk([kept[index]], scale, result, start)
+        sums[index] = pair_sum(place, table, mine, other, slots, lines, quarter)
+        kept[index], added[index] = scatter_sum(sums[index])
+        result = finish_chunk(kept[index], scale, result, start)
     return result.reshape(slots, quarter, half_cols)
 
 

time: 155 us -> 120 us (0.77)
  between operations: 15.4 us -> 2.18 us
  local copies, waits for them, and re-layouts: 13 us -> 2.61 us
  Pallas kernels: 34.8 us -> 24.5 us
  starting transfers between devices: 30.4 us -> 28.5 us
    reduce_scatter x4 -> x0, waiting for transfers between devices: 37 us -> none  [scatter_sum(): return lax.psum_scatter(pieces, 'line', scatter_dimension=0, tiled=True)]
    ppermute x20 -> x18, waiting for transfers between devices: 23.1 us -> 53.9 us  [swapped(): return lax.ppermute(value, axis, [(i, i ^ distance) for i in range(count)])]
    unnamed x40 -> x10, local copies, waits for them, and re-layouts: 11.7 us -> 1.35 us
    ppermute x1, waiting for transfers between devices: 0.01 us -> 6.9 us  [per_device(): high = lax.ppermute(image[:HALO], 'seg', backward)]
    pallas_call x4 -> x2, Pallas kernels: 20.2 us -> 14.3 us  [filter_chunk(): pl.pallas_call(functools.partial(filter_kernel, first_chunk=start == 0, l...]
    pallas_call x4 -> x2, Pallas kernels: 2.5 us -> 0.27 us  [joined(): pl.pallas_call(join_kernel, out_shape=jax.ShapeDtypeStruct((len(blocks) *...]
    pallas_call x4 -> x2, Pallas kernels: 3.13 us -> 1.99 us  [finish_chunk(): pl.pallas_call(functools.partial(finish_kernel, count=len(pieces)), out_s...]
    pallas_call x4 -> x2, Pallas kernels: 5.02 us -> 3.91 us  [pair_sum(): pl.pallas_call(functools.partial(pair_kernel, slots=slots, distances=dist...]
  transfers between devices with their start and end apart: 26 -> 20, of which waited for: 11 -> 12; matrix products, arithmetic and copies ran while one was open for 1% -> 1% of each run, Pallas kernels for 19% -> 12%
where the time goes in v5:
time: 120 us
  waiting for transfers between devices  60.8 us (51%)
  starting transfers between devices  28.5 us (24%)
  Pallas kernels  24.5 us (20%)
  local copies, waits for them, and re-layouts  2.61 us (2%)
  between operations  2.18 us (2%)
  other arithmetic  1.25 us (1%)
    ppermute x18, waiting for transfers between devices, swapped(): return lax.ppermute(value, axis, [(i, i ^ distance) for i in range(count)])  53.9 us
    ppermute x18, starting transfers between devices, swapped(): return lax.ppermute(value, axis, [(i, i ^ distance) for i in range(count)])  22.3 us
    pallas_call x2, Pallas kernels, filter_chunk(): pl.pallas_call(functools.partial(filter_kernel, first_chunk=start == 0, l...  14.3 us
    ppermute x1, waiting for transfers between devices, per_device(): high = lax.ppermute(image[:HALO], 'seg', backward)  6.9 us
    ppermute x1, starting transfers between devices, per_device(): low = lax.ppermute(image[rows - HALO:], 'seg', forward)  4.86 us
    pallas_call x2, Pallas kernels, pair_sum(): pl.pallas_call(functools.partial(pair_kernel, slots=slots, distances=dist...  3.91 us
  transfers between devices with their start and end apart: 20, of which 12 were waited for; matrix products, arithmetic and copies ran while one was open for 1% of the time, Pallas kernels for 12%

profile of v5, /device:TPU:0, one launch (start us, length us, event | category | flops | bytes accessed | tf_op | source)
XLA Modules:
  0.0 119.9 jit_solution(12184602240141694501)
XLA Ops:
  0.0 1.1 slice_bitcast_fusion
  1.1 4.9 %collective-permute-start.1 = (f32[16,4096]{1,0:T(8,128)S(1)}, f32[16,4096]{1,0:T(8,128)S(1)}, u32[]{:S(2)}, u32[]{:S(2)}) collective-permute-start(f32[16,4096]{1,0:T(8,128)S(1)} %get-tuple-element.68), channel_id=1, source_target_pairs={{0,8},{8,16},{16,24},{1,9},{9,17},{17,25},{2,10},{10,18},{18,26},{... | collective-permute-start | bytes 786440 | tf_op jit(solution)/shard_map/ppermute | solution.py:440
  5.9 1.3 %collective-permute-start.2 = (f32[16,4096]{1,0:T(8,128)S(1)}, f32[16,4096]{1,0:T(8,128)S(1)}, u32[]{:S(2)}, u32[]{:S(2)}) collective-permute-start(f32[16,4096]{1,0:T(8,128)S(1)} %get-tuple-element.67), channel_id=1, source_target_pairs={{8,0},{16,8},{24,16},{9,1},{17,9},{25,17},{10,2},{18,10},{26,18},{... | collective-permute-start | bytes 786440 | tf_op jit(solution)/shard_map/ppermute | solution.py:441
  7.9 0.1 pad_add_fusion.1.place
  8.0 0.7 copy-done.1
  8.7 0.7 copy-done.2
  9.3 2.1 %band_matrices.1 = (bf16[3,128,480]{2,1,0:T(8,128)(2,1)S(1)}, bf16[3,2,512,256]{3,2,1,0:T(8,128)(2,1)S(1)}) custom-call(s32[3]{0:T(128)S(1)} %pad_add_fusion.1.place, f32[1,2,3]{2,1,0:T(2,128)S(1)} %copy-done.1, s32[1,2]{1,0:T(1,128)S(1)} %copy-done.2, s32[1]{0:T(128)S(6)} %copy.10.shift), custom_call_target="tpu_custom_call" | custom-call | flops 1 | bytes 1 | tf_op jit(solution)/shard_map/band_matrices/pallas_call | solution.py:132
  12.1 6.9 %collective-permute-done.2.high_l.high_c.high_r = f32[16,4096]{1,0:T(8,128)S(1)} collective-permute-done((f32[16,4096]{1,0:T(8,128)S(1)}, f32[16,4096]{1,0:T(8,128)S(1)}, u32[]{:S(2)}, u32[]{:S(2)}) %collective-permute-start.2) | collective-permute-done | bytes 262176 | tf_op jit(solution)/shard_map/ppermute | solution.py:441
  19.0 7.2 %warp_filter.3 = (bf16[128,2048]{1,0:T(8,128)(2,1)S(1)}, bf16[128,2048]{1,0:T(8,128)(2,1)S(1)}, bf16[128,2048]{1,0:T(8,128)(2,1)S(1)}, bf16[128,2048]{1,0:T(8,128)(2,1)S(1)}) custom-call(f32[1]{0:T(128)} %convert_element_type.27.weight, f32[16,4096]{1,0:T(8,128)S(1)} %collective-permute-done.1.low_l.low_c.low_r, ...), custom_call_target="tpu_custom_call" | custom-call | flops 1 | bytes 1 | tf_op jit(solution)/shard_map/warp_filter/pallas_call | solution.py:236
  26.3 2.9 %collective-permute-start.11 = (bf16[128,2048]{1,0:T(8,128)(2,1)S(1)}, bf16[128,2048]{1,0:T(8,128)(2,1)S(1)}, u32[]{:S(2)}, u32[]{:S(2)}) collective-permute-start(bf16[128,2048]{1,0:T(8,128)(2,1)S(1)} %get-tuple-element.47), channel_id=1, source_target_pairs={{0,24},{8,16},{16,8},{24,0},{1,25},{9,17},{17,9},{25,1},{2,26},{10... | collective-permute-start | bytes 1572872 | tf_op jit(solution)/shard_map/ppermute | solution.py:407
  29.2 0.5 collective-permute-start.9
  30.5 1.1 collective-permute-done.6
  31.7 1.6 %collective-permute-start.7 = (f32[2,3]{1,0:T(2,128)S(1)}, f32[2,3]{1,0:T(2,128)S(1)}, u32[]{:S(2)}, u32[]{:S(2)}) collective-permute-start(f32[2,3]{1,0:T(2,128)S(1)} %pad_maximum_fusion.2), channel_id=1, source_target_pairs={{0,2},{2,0},{4,6},{6,4},{1,3},{3,1},{5,7},{7,5},{8,10},{10,8},{12,... | collective-permute-start | bytes 80 | tf_op jit(solution)/shard_map/ppermute | solution.py:407
  33.3 2.0 %collective-permute-done.7 = f32[2,3]{1,0:T(2,128)S(1)} collective-permute-done((f32[2,3]{1,0:T(2,128)S(1)}, f32[2,3]{1,0:T(2,128)S(1)}, u32[]{:S(2)}, u32[]{:S(2)}) %collective-permute-start.7) | collective-permute-done | bytes 56 | tf_op jit(solution)/shard_map/ppermute | solution.py:407
  35.4 7.2 %warp_filter.2 = (bf16[128,2048]{1,0:T(8,128)(2,1)S(1)}, bf16[128,2048]{1,0:T(8,128)(2,1)S(1)}, bf16[128,2048]{1,0:T(8,128)(2,1)S(1)}, bf16[128,2048]{1,0:T(8,128)(2,1)S(1)}) custom-call(f32[1]{0:T(128)} %convert_element_type.27.weight, f32[16,4096]{1,0:T(8,128)S(1)} %collective-permute-done.1.low_l.low_c.low_r, ...), custom_call_target="tpu_custom_call" | custom-call | flops 1 | bytes 1 | tf_op jit(solution)/shard_map/warp_filter/pallas_call | solution.py:236
  42.6 7.7 %collective-permute-done.10.refs_2_ = bf16[128,2048]{1,0:T(8,128)(2,1)S(1)} collective-permute-done((bf16[128,2048]{1,0:T(8,128)(2,1)S(1)}, bf16[128,2048]{1,0:T(8,128)(2,1)S(1)}, u32[]{:S(2)}, u32[]{:S(2)}) %collective-permute-start.10) | collective-permute-done | bytes 524320 | tf_op jit(solution)/shard_map/ppermute | solution.py:407
  50.3 1.2 %collective-permute-done.9.refs_1_ = bf16[128,2048]{1,0:T(8,128)(2,1)S(1)} collective-permute-done((bf16[128,2048]{1,0:T(8,128)(2,1)S(1)}, bf16[128,2048]{1,0:T(8,128)(2,1)S(1)}, u32[]{:S(2)}, u32[]{:S(2)}) %collective-permute-start.9) | collective-permute-done | bytes 524320 | tf_op jit(solution)/shard_map/ppermute | solution.py:407
  51.5 0.1 join_blocks.2.mine
  51.8 0.5 collective-permute-start
  52.3 0.1 reshape.12
  52.4 0.1 reshape.13
  52.5 1.6 %collective-permute-start.3 = (bf16[128,2048]{1,0:T(8,128)(2,1)}, bf16[128,2048]{1,0:T(8,128)(2,1)S(1)}, u32[]{:S(2)}, u32[]{:S(2)}) collective-permute-start(bf16[128,2048]{1,0:T(8,128)(2,1)} %copy-done.4), channel_id=1, source_target_pairs={{0,8},{8,0},{16,24},{24,16},{1,9},{9,1},{17,25},{25,17},{2,10},{10... | collective-permute-start | bytes 1572872 | tf_op jit(solution)/shard_map/ppermute | solution.py:407
  54.1 0.4 collective-permute-start.4
  54.4 1.6 %collective-permute-start.5 = (bf16[128,2048]{1,0:T(8,128)(2,1)S(1)}, bf16[128,2048]{1,0:T(8,128)(2,1)S(1)}, u32[]{:S(2)}, u32[]{:S(2)}) collective-permute-start(bf16[128,2048]{1,0:T(8,128)(2,1)S(1)} %get-tuple-element.40), channel_id=1, source_target_pairs={{0,24},{8,16},{16,8},{24,0},{1,25},{9,17},{17,9},{25,1},{2,26},{10... | collective-permute-start | bytes 1572872 | tf_op jit(solution)/shard_map/ppermute | solution.py:407
  56.1 0.6 fusion.2
  56.7 2.5 %pair_sum.2 = (bf16[160,1024]{1,0:T(8,128)(2,1)S(1)}, bf16[160,1024]{1,0:T(8,128)(2,1)S(1)}, bf16[160,1024]{1,0:T(8,128)(2,1)S(1)}, bf16[160,1024]{1,0:T(8,128)(2,1)S(1)}) custom-call(s32[3]{0:T(128)S(1)} %pad_add_fusion.1.place, s32[240]{0:T(256)S(1)} %pad_add_fusion.table, bf16[512,2048]{1,0:T(8,128)(2,1)S(1)} %join_blocks.2.mine, ...), custom_call_target="tpu_custom_call" | custom-call | flops 1 | bytes 1 | tf_op jit(solution)/shard_map/pair_sum/pallas_call | solution.py:320
  59.2 1.6 %collective-permute-start.13 = (bf16[160,1024]{1,0:T(8,128)(2,1)S(1)}, bf16[160,1024]{1,0:T(8,128)(2,1)S(1)}, u32[]{:S(2)}, u32[]{:S(2)}) collective-permute-start(bf16[160,1024]{1,0:T(8,128)(2,1)S(1)} %get-tuple-element.55), channel_id=1, source_target_pairs={{0,2},{2,0},{4,6},{6,4},{1,3},{3,1},{5,7},{7,5},{8,10},{10,8},{12,... | collective-permute-start | bytes 983048 | tf_op jit(solution)/shard_map/ppermute | solution.py:407
  60.8 2.6 %collective-permute-start.8 = (f32[4,3]{1,0:T(4,128)S(1)}, f32[4,3]{1,0:T(4,128)S(1)}, u32[]{:S(2)}, u32[]{:S(2)}) collective-permute-start(f32[4,3]{1,0:T(4,128)S(1)} %pad_maximum_fusion.1), channel_id=1, source_target_pairs={{0,4},{2,6},{4,0},{6,2},{1,5},{3,7},{5,1},{7,3},{8,12},{10,14},{12... | collective-permute-start | bytes 152 | tf_op jit(solution)/shard_map/ppermute | solution.py:407
  63.4 4.7 %collective-permute-done.8 = f32[4,3]{1,0:T(4,128)S(1)} collective-permute-done((f32[4,3]{1,0:T(4,128)S(1)}, f32[4,3]{1,0:T(4,128)S(1)}, u32[]{:S(2)}, u32[]{:S(2)}) %collective-permute-start.8) | collective-permute-done | bytes 80 | tf_op jit(solution)/shard_map/ppermute | solution.py:407
  68.1 3.5 %collective-permute-start.14 = (bf16[160,1024]{1,0:T(8,128)(2,1)S(1)}, bf16[160,1024]{1,0:T(8,128)(2,1)S(1)}, u32[]{:S(2)}, u32[]{:S(2)}) collective-permute-start(bf16[160,1024]{1,0:T(8,128)(2,1)S(1)} %get-tuple-element.57), channel_id=1, source_target_pairs={{0,2},{2,0},{4,6},{6,4},{1,3},{3,1},{5,7},{7,5},{8,10},{10,8},{12,... | collective-permute-start | bytes 983048 | tf_op jit(solution)/shard_map/ppermute | solution.py:407
  71.6 0.1 pad_maximum_fusion.facts
  71.7 1.8 %patch_weights.1.refs_3_ = f32[160,2048]{1,0:T(8,128)S(1)} custom-call(s32[3]{0:T(128)S(1)} %pad_add_fusion.1.place, s32[160]{0:T(256)S(1)} %copy-done, f32[8,3]{1,0:T(8,128)S(1)} %pad_maximum_fusion.facts), custom_call_target="tpu_custom_call" | custom-call | flops 1 | bytes 1 | tf_op jit(solution)/shard_map/patch_weights/pallas_call | solution.py:360
  73.5 5.6 %collective-permute-done.4.refs_2_ = bf16[128,2048]{1,0:T(8,128)(2,1)S(1)} collective-permute-done((bf16[128,2048]{1,0:T(8,128)(2,1)}, bf16[128,2048]{1,0:T(8,128)(2,1)S(1)}, u32[]{:S(2)}, u32[]{:S(2)}) %collective-permute-start.4) | collective-permute-done | bytes 524320 | tf_op jit(solution)/shard_map/ppermute | solution.py:407
  79.1 0.1 add_convert_fusion.1
  79.3 0.1 join_blocks.3.mine
  79.5 4.1 %collective-permute-done.15.other = bf16[512,2048]{1,0:T(8,128)(2,1)S(1)} collective-permute-done((bf16[512,2048]{1,0:T(8,128)(2,1)S(1)}, bf16[512,2048]{1,0:T(8,128)(2,1)S(1)}, u32[]{:S(2)}, u32[]{:S(2)}) %collective-permute-start.15) | collective-permute-done | bytes 2097184 | tf_op jit(solution)/shard_map/ppermute | solution.py:407
  83.6 1.4 %pair_sum.3 = (bf16[160,1024]{1,0:T(8,128)(2,1)S(1)}, bf16[160,1024]{1,0:T(8,128)(2,1)S(1)}, bf16[160,1024]{1,0:T(8,128)(2,1)S(1)}, bf16[160,1024]{1,0:T(8,128)(2,1)S(1)}) custom-call(s32[3]{0:T(128)S(1)} %pad_add_fusion.1.place, s32[240]{0:T(256)S(1)} %pad_add_fusion.table, bf16[512,2048]{1,0:T(8,128)(2,1)S(1)} %join_blocks.3.mine, ...), custom_call_target="tpu_custom_call" | custom-call | flops 1 | bytes 1 | tf_op jit(solution)/shard_map/pair_sum/pallas_call | solution.py:320
  85.1 1.6 %collective-permute-start.17 = (bf16[160,1024]{1,0:T(8,128)(2,1)S(1)}, bf16[160,1024]{1,0:T(8,128)(2,1)S(1)}, u32[]{:S(2)}, u32[]{:S(2)}) collective-permute-start(bf16[160,1024]{1,0:T(8,128)(2,1)S(1)} %get-tuple-element.64), channel_id=1, source_target_pairs={{0,2},{2,0},{4,6},{6,4},{1,3},{3,1},{5,7},{7,5},{8,10},{10,8},{12,... | collective-permute-start | bytes 983048 | tf_op jit(solution)/shard_map/ppermute | solution.py:407
  86.7 2.6 %collective-permute-start.19 = (bf16[160,1024]{1,0:T(8,128)(2,1)S(1)}, bf16[160,1024]{1,0:T(8,128)(2,1)S(1)}, u32[]{:S(2)}, u32[]{:S(2)}) collective-permute-start(bf16[160,1024]{1,0:T(8,128)(2,1)S(1)} %add_convert_fusion.1), channel_id=1, source_target_pairs={{0,4},{2,6},{4,0},{6,2},{1,5},{3,7},{5,1},{7,3},{8,12},{10,14},{12... | collective-permute-start | bytes 983048 | tf_op jit(solution)/shard_map/ppermute | solution.py:407
  89.3 0.4 collective-permute-start.16
  89.7 12.8 %collective-permute-done.17 = bf16[160,1024]{1,0:T(8,128)(2,1)S(1)} collective-permute-done((bf16[160,1024]{1,0:T(8,128)(2,1)S(1)}, bf16[160,1024]{1,0:T(8,128)(2,1)S(1)}, u32[]{:S(2)}, u32[]{:S(2)}) %collective-permute-start.17) | collective-permute-done | bytes 327712 | tf_op jit(solution)/shard_map/ppermute | solution.py:407
  102.6 0.1 add_convert_fusion
  102.7 0.6 collective-permute-start.18
  103.3 0.2 collective-permute-done.19.refs_2_
  103.5 1.0 patch_mean.2.refs_4_
  104.5 10.7 %collective-permute-done.16.refs_1_ = bf16[160,1024]{1,0:T(8,128)(2,1)S(1)} collective-permute-done((bf16[160,1024]{1,0:T(8,128)(2,1)S(1)}, bf16[160,1024]{1,0:T(8,128)(2,1)S(1)}, u32[]{:S(2)}, u32[]{:S(2)}) %collective-permute-start.16) | collective-permute-done | bytes 327712 | tf_op jit(solution)/shard_map/ppermute | solution.py:407
  115.2 3.7 %collective-permute-done.18.refs_2_ = bf16[160,1024]{1,0:T(8,128)(2,1)S(1)} collective-permute-done((bf16[160,1024]{1,0:T(8,128)(2,1)S(1)}, bf16[160,1024]{1,0:T(8,128)(2,1)S(1)}, u32[]{:S(2)}, u32[]{:S(2)}) %collective-permute-start.18) | collective-permute-done | bytes 327712 | tf_op jit(solution)/shard_map/ppermute | solution.py:407
  118.9 1.0 patch_mean.3
  (26 shorter events, 0.6 us)
Async XLA Ops:
  1.1 11.1 %collective-permute-start.1 = (f32[16,4096]{1,0:T(8,128)S(1)}, f32[16,4096]{1,0:T(8,128)S(1)}, u32[]{:S(2)}, u32[]{:S(2)}) collective-permute-start(f32[16,4096]{1,0:T(8,128)S(1)} %get-tuple-element.68), channel_id=1, source_target_pairs={{0,8},{8,16},{16,24},{1,9},{9,17},{17,25},{2,10},{10,18},{18,26},{... | collective-permute-start | bytes 786440 | tf_op jit(solution)/shard_map/ppermute | solution.py:440
  5.9 13.1 %collective-permute-start.2 = (f32[16,4096]{1,0:T(8,128)S(1)}, f32[16,4096]{1,0:T(8,128)S(1)}, u32[]{:S(2)}, u32[]{:S(2)}) collective-permute-start(f32[16,4096]{1,0:T(8,128)S(1)} %get-tuple-element.67), channel_id=1, source_target_pairs={{8,0},{16,8},{24,16},{9,1},{17,9},{25,17},{10,2},{18,10},{26,18},{... | collective-permute-start | bytes 786440 | tf_op jit(solution)/shard_map/ppermute | solution.py:441
  8.0 0.7 copy-start.1
  8.7 0.7 copy-start.2
  26.2 24.1 %collective-permute-start.10 = (bf16[128,2048]{1,0:T(8,128)(2,1)S(1)}, bf16[128,2048]{1,0:T(8,128)(2,1)S(1)}, u32[]{:S(2)}, u32[]{:S(2)}) collective-permute-start(bf16[128,2048]{1,0:T(8,128)(2,1)S(1)} %get-tuple-element.46), channel_id=1, source_target_pairs={{0,16},{8,24},{16,0},{24,8},{1,17},{9,25},{17,1},{25,9},{2,18},{10... | collective-permute-start | bytes 1572872 | tf_op jit(solution)/shard_map/ppermute | solution.py:407
  26.3 24.0 %collective-permute-start.11 = (bf16[128,2048]{1,0:T(8,128)(2,1)S(1)}, bf16[128,2048]{1,0:T(8,128)(2,1)S(1)}, u32[]{:S(2)}, u32[]{:S(2)}) collective-permute-start(bf16[128,2048]{1,0:T(8,128)(2,1)S(1)} %get-tuple-element.47), channel_id=1, source_target_pairs={{0,24},{8,16},{16,8},{24,0},{1,25},{9,17},{17,9},{25,1},{2,26},{10... | collective-permute-start | bytes 1572872 | tf_op jit(solution)/shard_map/ppermute | solution.py:407
  29.2 22.3 %collective-permute-start.9 = (bf16[128,2048]{1,0:T(8,128)(2,1)S(1)}, bf16[128,2048]{1,0:T(8,128)(2,1)S(1)}, u32[]{:S(2)}, u32[]{:S(2)}) collective-permute-start(bf16[128,2048]{1,0:T(8,128)(2,1)S(1)} %get-tuple-element.45), channel_id=1, source_target_pairs={{0,8},{8,0},{16,24},{24,16},{1,9},{9,1},{17,25},{25,17},{2,10},{10... | collective-permute-start | bytes 1572872 | tf_op jit(solution)/shard_map/ppermute | solution.py:407
  30.5 1.1 collective-permute-start.6
  31.7 3.6 %collective-permute-start.7 = (f32[2,3]{1,0:T(2,128)S(1)}, f32[2,3]{1,0:T(2,128)S(1)}, u32[]{:S(2)}, u32[]{:S(2)}) collective-permute-start(f32[2,3]{1,0:T(2,128)S(1)} %pad_maximum_fusion.2), channel_id=1, source_target_pairs={{0,2},{2,0},{4,6},{6,4},{1,3},{3,1},{5,7},{7,5},{8,10},{10,8},{12,... | collective-permute-start | bytes 80 | tf_op jit(solution)/shard_map/ppermute | solution.py:407
  42.5 9.0 %copy-start.4 = (bf16[128,2048]{1,0:T(8,128)(2,1)}, bf16[128,2048]{1,0:T(8,128)(2,1)S(1)}, u32[]{:S(2)}) copy-start(bf16[128,2048]{1,0:T(8,128)(2,1)S(1)} %get-tuple-element.38) | copy-start | bytes 1572868
  42.6 9.1 %copy-start.3 = (bf16[128,2048]{1,0:T(8,128)(2,1)}, bf16[128,2048]{1,0:T(8,128)(2,1)S(1)}, u32[]{:S(2)}) copy-start(bf16[128,2048]{1,0:T(8,128)(2,1)S(1)} %get-tuple-element.39) | copy-start | bytes 1572868
  51.5 0.7 copy-start
  51.7 5.0 %collective-permute-start.12 = (bf16[512,2048]{1,0:T(8,128)(2,1)S(1)}, bf16[512,2048]{1,0:T(8,128)(2,1)}, u32[]{:S(2)}, u32[]{:S(2)}) collective-permute-start(bf16[512,2048]{1,0:T(8,128)(2,1)S(1)} %join_blocks.2.mine), channel_id=1, source_target_pairs={{0,1},{1,0},{2,3},{3,2},{4,5},{5,4},{6,7},{7,6},{8,9},{9,8},{10,11... | collective-permute-start | bytes 6291464 | tf_op jit(solution)/shard_map/ppermute | solution.py:407
  51.8 4.3 %collective-permute-start = (s32[1]{0:T(128)}, s32[1]{0:T(128)}, u32[]{:S(2)}, u32[]{:S(2)}) collective-permute-start(s32[1]{0:T(128)} %param.11), channel_id=1, source_target_pairs={{0,1},{1,0},{2,3},{3,2},{4,5},{5,4},{6,7},{7,6},{8,9},{9,8},{10,11... | collective-permute-start | bytes 20 | tf_op jit(solution)/shard_map/ppermute | solution.py:407
  52.5 21.0 %collective-permute-start.3 = (bf16[128,2048]{1,0:T(8,128)(2,1)}, bf16[128,2048]{1,0:T(8,128)(2,1)S(1)}, u32[]{:S(2)}, u32[]{:S(2)}) collective-permute-start(bf16[128,2048]{1,0:T(8,128)(2,1)} %copy-done.4), channel_id=1, source_target_pairs={{0,8},{8,0},{16,24},{24,16},{1,9},{9,1},{17,25},{25,17},{2,10},{10... | collective-permute-start | bytes 1572872 | tf_op jit(solution)/shard_map/ppermute | solution.py:407
  54.1 25.1 %collective-permute-start.4 = (bf16[128,2048]{1,0:T(8,128)(2,1)}, bf16[128,2048]{1,0:T(8,128)(2,1)S(1)}, u32[]{:S(2)}, u32[]{:S(2)}) collective-permute-start(bf16[128,2048]{1,0:T(8,128)(2,1)} %copy-done.3), channel_id=1, source_target_pairs={{0,16},{8,24},{16,0},{24,8},{1,17},{9,25},{17,1},{25,9},{2,18},{10... | collective-permute-start | bytes 1572872 | tf_op jit(solution)/shard_map/ppermute | solution.py:407
  54.4 24.7 %collective-permute-start.5 = (bf16[128,2048]{1,0:T(8,128)(2,1)S(1)}, bf16[128,2048]{1,0:T(8,128)(2,1)S(1)}, u32[]{:S(2)}, u32[]{:S(2)}) collective-permute-start(bf16[128,2048]{1,0:T(8,128)(2,1)S(1)} %get-tuple-element.40), channel_id=1, source_target_pairs={{0,24},{8,16},{16,8},{24,0},{1,25},{9,17},{17,9},{25,1},{2,26},{10... | collective-permute-start | bytes 1572872 | tf_op jit(solution)/shard_map/ppermute | solution.py:407
  59.2 19.9 %collective-permute-start.13 = (bf16[160,1024]{1,0:T(8,128)(2,1)S(1)}, bf16[160,1024]{1,0:T(8,128)(2,1)S(1)}, u32[]{:S(2)}, u32[]{:S(2)}) collective-permute-start(bf16[160,1024]{1,0:T(8,128)(2,1)S(1)} %get-tuple-element.55), channel_id=1, source_target_pairs={{0,2},{2,0},{4,6},{6,4},{1,3},{3,1},{5,7},{7,5},{8,10},{10,8},{12,... | collective-permute-start | bytes 983048 | tf_op jit(solution)/shard_map/ppermute | solution.py:407
  60.8 7.3 %collective-permute-start.8 = (f32[4,3]{1,0:T(4,128)S(1)}, f32[4,3]{1,0:T(4,128)S(1)}, u32[]{:S(2)}, u32[]{:S(2)}) collective-permute-start(f32[4,3]{1,0:T(4,128)S(1)} %pad_maximum_fusion.1), channel_id=1, source_target_pairs={{0,4},{2,6},{4,0},{6,2},{1,5},{3,7},{5,1},{7,3},{8,12},{10,14},{12... | collective-permute-start | bytes 152 | tf_op jit(solution)/shard_map/ppermute | solution.py:407
  68.1 11.1 %collective-permute-start.14 = (bf16[160,1024]{1,0:T(8,128)(2,1)S(1)}, bf16[160,1024]{1,0:T(8,128)(2,1)S(1)}, u32[]{:S(2)}, u32[]{:S(2)}) collective-permute-start(bf16[160,1024]{1,0:T(8,128)(2,1)S(1)} %get-tuple-element.57), channel_id=1, source_target_pairs={{0,2},{2,0},{4,6},{6,4},{1,3},{3,1},{5,7},{7,5},{8,10},{10,8},{12,... | collective-permute-start | bytes 983048 | tf_op jit(solution)/shard_map/ppermute | solution.py:407
  79.4 4.2 %collective-permute-start.15 = (bf16[512,2048]{1,0:T(8,128)(2,1)S(1)}, bf16[512,2048]{1,0:T(8,128)(2,1)S(1)}, u32[]{:S(2)}, u32[]{:S(2)}) collective-permute-start(bf16[512,2048]{1,0:T(8,128)(2,1)S(1)} %join_blocks.3.mine), channel_id=1, source_target_pairs={{0,1},{1,0},{2,3},{3,2},{4,5},{5,4},{6,7},{7,6},{8,9},{9,8},{10,11... | collective-permute-start | bytes 6291464 | tf_op jit(solution)/shard_map/ppermute | solution.py:407
  85.1 17.5 %collective-permute-start.17 = (bf16[160,1024]{1,0:T(8,128)(2,1)S(1)}, bf16[160,1024]{1,0:T(8,128)(2,1)S(1)}, u32[]{:S(2)}, u32[]{:S(2)}) collective-permute-start(bf16[160,1024]{1,0:T(8,128)(2,1)S(1)} %get-tuple-element.64), channel_id=1, source_target_pairs={{0,2},{2,0},{4,6},{6,4},{1,3},{3,1},{5,7},{7,5},{8,10},{10,8},{12,... | collective-permute-start | bytes 983048 | tf_op jit(solution)/shard_map/ppermute | solution.py:407
  86.7 16.8 %collective-permute-start.19 = (bf16[160,1024]{1,0:T(8,128)(2,1)S(1)}, bf16[160,1024]{1,0:T(8,128)(2,1)S(1)}, u32[]{:S(2)}, u32[]{:S(2)}) collective-permute-start(bf16[160,1024]{1,0:T(8,128)(2,1)S(1)} %add_convert_fusion.1), channel_id=1, source_target_pairs={{0,4},{2,6},{4,0},{6,2},{1,5},{3,7},{5,1},{7,3},{8,12},{10,14},{12... | collective-permute-start | bytes 983048 | tf_op jit(solution)/shard_map/ppermute | solution.py:407
  89.3 25.9 %collective-permute-start.16 = (bf16[160,1024]{1,0:T(8,128)(2,1)S(1)}, bf16[160,1024]{1,0:T(8,128)(2,1)S(1)}, u32[]{:S(2)}, u32[]{:S(2)}) collective-permute-start(bf16[160,1024]{1,0:T(8,128)(2,1)S(1)} %get-tuple-element.62), channel_id=1, source_target_pairs={{0,2},{2,0},{4,6},{6,4},{1,3},{3,1},{5,7},{7,5},{8,10},{10,8},{12,... | collective-permute-start | bytes 983048 | tf_op jit(solution)/shard_map/ppermute | solution.py:407
  102.7 16.2 %collective-permute-start.18 = (bf16[160,1024]{1,0:T(8,128)(2,1)S(1)}, bf16[160,1024]{1,0:T(8,128)(2,1)S(1)}, u32[]{:S(2)}, u32[]{:S(2)}) collective-permute-start(bf16[160,1024]{1,0:T(8,128)(2,1)S(1)} %add_convert_fusion), channel_id=1, source_target_pairs={{0,4},{2,6},{4,0},{6,2},{1,5},{3,7},{5,1},{7,3},{8,12},{10,14},{12... | collective-permute-start | bytes 983048 | tf_op jit(solution)/shard_map/ppermute | solution.py:407

commit v6 on v5

--- a/solution.py
+++ b/solution.py
@@ -18,7 +18,8 @@
 SIDE = 128
 TILE = 256
 STRIP = 128
-PARTS = (2, 2)
+PARTS = (3, 3, 2)
+WHOLE = 8
 VMEM = 48 * 1024 * 1024
 COST = pl.CostEstimate(flops=1, bytes_accessed=1, transcendentals=0)
 
@@ -143,32 +144,32 @@
     )(place, coef, phases, shift)
 
 
-def filter_kernel(
-    weight, low_l, low_c, low_r, mid_l, mid_c, mid_r, high_l, high_c, high_r, rows_m, cols_m, *rest,
-    first_chunk, last_chunk, segments,
-):
-    *outs, ext_high, ext_low, mat_high, mat_low = rest
+def filter_kernel(weight, place, *rest, first_chunk, last_chunk, segments, pieces):
+    sources, (rows_m, cols_m), refs = rest[: 3 * pieces], rest[3 * pieces : 3 * pieces + 2], rest[3 * pieces + 2 :]
+    image, even, odd = sources[:pieces], sources[pieces : 2 * pieces], sources[2 * pieces :]
+    *outs, ext_high, ext_low, mat_high, mat_low = refs
     half = pl.program_id(0)
     halves = pl.num_programs(0)
-    rows, chunk = mid_c.shape
+    rows = image[0].shape[0]
+    chunk = (pieces - 2) * TILE
     at_left = first_chunk & (half == 0)
     at_right = last_chunk & (half == halves - 1)
     span = STRIP + 2 * HALO
-
-    for row, parts in (
-        (0, (low_l, low_c, low_r)),
-        (HALO, (mid_l, mid_c, mid_r)),
-        (HALO + rows, (high_l, high_c, high_r)),
-    ):
-        count = parts[0].shape[0]
-        for part, column, outside in zip(parts, (0, SIDE, SIDE + chunk), (at_left, False, at_right)):
-            value = part[...]
-            if outside is not False:
-                value = jnp.where(outside, 0.0, value)
-            high, low = split(value)
-            place = (pl.ds(row, count), pl.ds(column, value.shape[1]))
-            ext_high[place] = high
-            ext_low[place] = low
+    is_odd = (place[0] & 1) == 1
+
+    column = 0
+    for index in range(pieces):
+        wide = image[index].shape[1]
+        low = jnp.where(is_odd, even[index][...], odd[index][...])
+        high = jnp.where(is_odd, odd[index][...], even[index][...])
+        for row, value in ((0, low), (HALO, image[index][...]), (HALO + rows, high)):
+            if index == 0:
+                value = jnp.where(at_left, 0.0, value)
+            if index == pieces - 1:
+                value = jnp.where(at_right, 0.0, value)
+            target = (pl.ds(row, value.shape[0]), pl.ds(column, wide))
+            ext_high[target], ext_low[target] = split(value)
+        column += wide
 
     strips = rows // STRIP
     for tile in range((chunk + 2 * SIDE) // TILE):
@@ -205,33 +206,33 @@
                 out[pl.ds(strip * piece, piece), pl.ds(tile * TILE, TILE)] = sent[owner * piece : (owner + 1) * piece]
 
 
-def filter_chunk(weight, low, image, high, rows_m, cols_m, start, chunk, segments):
+def filter_chunk(weight, place, image, even, odd, rows_m, cols_m, start, chunk, segments):
     rows, width = image.shape
     halves = 2
-    half_blocks = width // halves // SIDE
-    first = start // SIDE
-    blocks = chunk // SIDE
+    half_cols = width // halves
     last = width // SIDE - 1
 
     def left(h):
-        return 0, jnp.maximum(h * half_blocks + first - 1, 0)
-
-    def centre(h):
-        return 0, h * (half_blocks // blocks) + start // chunk
+        return 0, jnp.maximum((h * half_cols + start) // SIDE - 1, 0)
 
     def right(h):
-        return 0, jnp.minimum(h * half_blocks + first + blocks, last)
+        return 0, jnp.minimum((h * half_cols + start + chunk) // SIDE, last)
+
+    def inner(index):
+        return lambda h: (0, (h * half_cols + start) // TILE + index)
 
     def whole(array):
         return pl.BlockSpec(array.shape, lambda h: (0,) * array.ndim)
 
-    specs = [pl.BlockSpec(memory_space=pltpu.SMEM)]
-    for source in (low, image, high):
-        specs += [
-            pl.BlockSpec((source.shape[0], SIDE), left),
-            pl.BlockSpec((source.shape[0], chunk), centre),
-            pl.BlockSpec((source.shape[0], SIDE), right),
-        ]
+    pieces = chunk // TILE + 2
+    specs = [pl.BlockSpec(memory_space=pltpu.SMEM)] * 2
+    operands = [weight, place]
+    for source in (image, even, odd):
+        count = source.shape[0]
+        specs.append(pl.BlockSpec((count, SIDE), left))
+        specs += [pl.BlockSpec((count, TILE), inner(index)) for index in range(pieces - 2)]
+        specs.append(pl.BlockSpec((count, SIDE), right))
+        operands += [source] * pieces
     wide = chunk + 2 * SIDE
     return pl.pallas_call(
         functools.partial(
@@ -239,6 +240,7 @@
             first_chunk=start == 0,
             last_chunk=start + chunk == width // halves,
             segments=segments,
+            pieces=pieces,
         ),
         out_shape=[jax.ShapeDtypeStruct((rows // segments, halves * chunk), jnp.bfloat16)] * segments,
         grid=(halves,),
@@ -253,7 +255,7 @@
         compiler_params=pltpu.CompilerParams(vmem_limit_bytes=VMEM),
         cost_estimate=COST,
         name="warp_filter",
-    )(weight, *([low] * 3), *([image] * 3), *([high] * 3), rows_m, cols_m)
+    )(*operands, rows_m, cols_m)
 
 
 def join_kernel(*refs):
@@ -435,18 +437,22 @@
     bands = segments * rows // BAND_ROWS
     place = jnp.stack([lax.axis_index(axis) for axis in ("seg", "line", "core")]).astype(jnp.int32)
 
-    forward = [(i, i + 1) for i in range(segments - 1)]
-    backward = [(i + 1, i) for i in range(segments - 1)]
-    low = lax.ppermute(image[rows - HALO :], "seg", forward)
-    high = lax.ppermute(image[:HALO], "seg", backward)
+    def pairs_from(first):
+        pairs = [(i, i + 1) for i in range(first, segments - 1, 2)]
+        return pairs + [(j, i) for i, j in pairs]
+
+    is_odd = (place[0] & 1) == 1
+    top, bottom = image[:HALO], image[rows - HALO :]
+    even = lax.ppermute(jnp.where(is_odd, top, bottom), "seg", pairs_from(0))
+    odd = lax.ppermute(jnp.where(is_odd, bottom, top), "seg", pairs_from(1))
     rows_m, cols_m = build_matrices(place, psf_coef, phases, col_shift, rows, width, segments)
     weight = exposure_weight.astype(jnp.float32)
 
     chunks = []
     start = 0
     for part in PARTS:
-        chunks.append((start, half_cols // part))
-        start += half_cols // part
+        chunks.append((start, half_cols * part // WHOLE))
+        start += half_cols * part // WHOLE
     other_offset = swapped(band_offset, "core", 1)
     sites = lax.dynamic_index_in_dim(patch_site.reshape(lines, cores, slots), place[2], 1, keepdims=False).reshape(-1)
     here = rows // BAND_ROWS
@@ -459,10 +465,8 @@
     table = jnp.concatenate([sites % 2, rows_from(band_offset), rows_from(other_offset)])
     facts = jnp.stack([col_shift.astype(jnp.float32), band_offset.astype(jnp.float32), weight], axis=1)
     facts = jnp.concatenate([facts, swapped(facts, "core", 1)], axis=0)
-    early = facts
     step = 1
     while step < lines:
-        early = facts
         facts = jnp.concatenate([facts, swapped(facts, "line", step)], axis=0)
         step *= 2
     scale = patch_weights(place, patch_site, facts, slots, quarter, cores, width, bands)
@@ -477,7 +481,7 @@
     def filtered(index):
         start, chunk = chunks[index]
         held = tied(weight, sums[index - 2]) if index >= 2 else weight
-        sent[index] = filter_chunk(held, low, image, high, rows_m, cols_m, start, chunk, segments)
+        sent[index] = filter_chunk(held, place, image, even, odd, rows_m, cols_m, start, chunk, segments)
 
     filtered(0)
     for index, (start, chunk) in enumerate(chunks):
@@ -487,11 +491,13 @@
             filtered(index + 1)
             received = tied(received, sent[index + 1])
         if index == 0:
-            received = tied(received, early)
-        if index == 1:
             received = tied(received, scale)
         if index >= 1:
-            received = tied(received, (added[index - 1], kept[index - 1][:-1]))
+            received = tied(received, added[index - 1])
+        if index == 1:
+            received = tied(received, kept[0][:-1])
+        if index >= 2:
+            received = tied(received, kept[index - 2])
         mine = joined([outgoing[0]] + received)
         other = swapped(mine, "core", 1)
         sums[index] = pair_sum(place, table, mine, other, slots, lines, quarter)

time: 120 us -> 124 us (1.033)
  waiting for transfers between devices: 60.8 us -> 49.9 us
  Pallas kernels: 24.5 us -> 30.9 us
  starting transfers between devices: 28.5 us -> 33.9 us
  local copies, waits for them, and re-layouts: 2.61 us -> 4.52 us
    ppermute x18 -> x25, waiting for transfers between devices: 53.9 us -> 43.9 us  [swapped(): return lax.ppermute(value, axis, [(i, i ^ distance) for i in range(count)])]
    ppermute x18 -> x25, starting transfers between devices: 22.3 us -> 27.5 us  [swapped(): return lax.ppermute(value, axis, [(i, i ^ distance) for i in range(count)])]
    pallas_call x2 -> x3, Pallas kernels: 14.3 us -> 17.7 us  [filter_chunk(): pl.pallas_call(functools.partial(filter_kernel, first_chunk=start == 0, l...]
    unnamed x10 -> x20, local copies, waits for them, and re-layouts: 1.35 us -> 4.33 us
    pallas_call x2 -> x3, Pallas kernels: 3.91 us -> 5.11 us  [pair_sum(): pl.pallas_call(functools.partial(pair_kernel, slots=slots, distances=dist...]
    pallas_call x2 -> x3, Pallas kernels: 1.99 us -> 2.63 us  [finish_chunk(): pl.pallas_call(functools.partial(finish_kernel, count=len(pieces)), out_s...]
  transfers between devices with their start and end apart: 20 -> 27, of which waited for: 12 -> 14; matrix products, arithmetic and copies ran while one was open for 1% -> 1% of each run, Pallas kernels for 12% -> 16%
where the time goes in v6:
time: 124 us
  waiting for transfers between devices  49.9 us (40%)
  starting transfers between devices  33.9 us (27%)
  Pallas kernels  30.9 us (25%)
  local copies, waits for them, and re-layouts  4.52 us (4%)
  other arithmetic  2.27 us (2%)
  between operations  2.23 us (2%)
    ppermute x25, waiting for transfers between devices, swapped(): return lax.ppermute(value, axis, [(i, i ^ distance) for i in range(count)])  43.9 us
    ppermute x25, starting transfers between devices, swapped(): return lax.ppermute(value, axis, [(i, i ^ distance) for i in range(count)])  27.5 us
    pallas_call x3, Pallas kernels, filter_chunk(): pl.pallas_call(functools.partial(filter_kernel, first_chunk=start == 0, l...  17.7 us
    ppermute x1, waiting for transfers between devices, per_device(): even = lax.ppermute(jnp.where(is_odd, top, bottom), 'seg', pairs_from(0))  5.98 us
    ppermute x1, starting transfers between devices, per_device(): even = lax.ppermute(jnp.where(is_odd, top, bottom), 'seg', pairs_from(0))  5.73 us
    pallas_call x3, Pallas kernels, pair_sum(): pl.pallas_call(functools.partial(pair_kernel, slots=slots, distances=dist...  5.11 us
    unnamed x20, local copies, waits for them, and re-layouts  4.33 us
    pallas_call x3, Pallas kernels, finish_chunk(): pl.pallas_call(functools.partial(finish_kernel, count=len(pieces)), out_s...  2.63 us
  transfers between devices with their start and end apart: 27, of which 14 were waited for; matrix products, arithmetic and copies ran while one was open for 1% of the time, Pallas kernels for 16%

profile of v6, /device:TPU:0, one launch (start us, length us, event | category | flops | bytes accessed | tf_op | source)
XLA Modules:
  0.0 123.7 jit_solution(8114405183614572606)
XLA Ops:
  0.0 1.1 select_bitcast_fusion
  1.1 0.7 collective-permute-start.2
  1.8 5.7 %collective-permute-start.1 = (f32[16,4096]{1,0:T(8,128)S(1)}, f32[16,4096]{1,0:T(8,128)S(1)}, u32[]{:S(2)}, u32[]{:S(2)}) collective-permute-start(f32[16,4096]{1,0:T(8,128)S(1)} %get-tuple-element.104), channel_id=1, source_target_pairs={{0,8},{16,24},{8,0},{24,16},{1,9},{17,25},{9,1},{25,17},{2,10},{18... | collective-permute-start | bytes 786440 | tf_op jit(solution)/shard_map/ppermute | solution.py:446
  8.2 0.7 copy-done.5
  9.5 2.1 %band_matrices.1 = (bf16[3,128,480]{2,1,0:T(8,128)(2,1)S(1)}, bf16[3,2,512,256]{3,2,1,0:T(8,128)(2,1)S(1)}) custom-call(s32[3]{0:T(128)S(1)} %pad_add_fusion.1.place, f32[1,2,3]{2,1,0:T(2,128)S(1)} %copy-done.5, s32[1,2]{1,0:T(1,128)S(1)} %copy-done.6, s32[1]{0:T(128)S(6)} %copy.12.shift), custom_call_target="tpu_custom_call" | custom-call | flops 1 | bytes 1 | tf_op jit(solution)/shard_map/band_matrices/pallas_call | solution.py:133
  13.1 6.0 %collective-permute-done.1.rest_5_.rest_6_.rest_7_.rest_8_.rest_9_.rest_4_ = f32[16,4096]{1,0:T(8,128)S(1)} collective-permute-done((f32[16,4096]{1,0:T(8,128)S(1)}, f32[16,4096]{1,0:T(8,128)S(1)}, u32[]{:S(2)}, u32[]{:S(2)}) %collective-permute-start.1) | collective-permute-done | bytes 262176 | tf_op jit(solution)/shard_map/ppermute | solution.py:446
  19.0 6.5 %warp_filter.3 = (bf16[128,1536]{1,0:T(8,128)(2,1)S(1)}, bf16[128,1536]{1,0:T(8,128)(2,1)S(1)}, bf16[128,1536]{1,0:T(8,128)(2,1)S(1)}, bf16[128,1536]{1,0:T(8,128)(2,1)S(1)}) custom-call(f32[1]{0:T(128)} %convert_element_type.36.weight, s32[3]{0:T(128)S(1)} %pad_add_fusion.1.place, f32[512,4096]{1,0:T(8,128)} %bitcast.15, f32[512,4096]{1,0:T(8,128)} %bitcast.16, ...), custom_call_target="tpu_custom_call" | custom-call | flops 1 | bytes 1 | tf_op jit(solution)/shard_map/warp_filter/pallas_call | solution.py:237
  25.6 2.0 %collective-permute-start.4 = (bf16[128,1536]{1,0:T(8,128)(2,1)S(1)}, bf16[128,1536]{1,0:T(8,128)(2,1)S(1)}, u32[]{:S(2)}, u32[]{:S(2)}) collective-permute-start(bf16[128,1536]{1,0:T(8,128)(2,1)S(1)} %get-tuple-element.57), channel_id=1, source_target_pairs={{0,16},{8,24},{16,0},{24,8},{1,17},{9,25},{17,1},{25,9},{2,18},{10... | collective-permute-start | bytes 1179656 | tf_op jit(solution)/shard_map/ppermute | solution.py:409
  27.6 1.5 %collective-permute-start.5 = (bf16[128,1536]{1,0:T(8,128)(2,1)S(1)}, bf16[128,1536]{1,0:T(8,128)(2,1)S(1)}, u32[]{:S(2)}, u32[]{:S(2)}) collective-permute-start(bf16[128,1536]{1,0:T(8,128)(2,1)S(1)} %get-tuple-element.58), channel_id=1, source_target_pairs={{0,24},{8,16},{16,8},{24,0},{1,25},{9,17},{17,9},{25,1},{2,26},{10... | collective-permute-start | bytes 1179656 | tf_op jit(solution)/shard_map/ppermute | solution.py:409
  29.2 1.1 collective-permute-done.6
  30.4 1.6 %collective-permute-start.7 = (f32[2,3]{1,0:T(2,128)S(1)}, f32[2,3]{1,0:T(2,128)S(1)}, u32[]{:S(2)}, u32[]{:S(2)}) collective-permute-start(f32[2,3]{1,0:T(2,128)S(1)} %pad_maximum_fusion.2), channel_id=1, source_target_pairs={{0,2},{2,0},{4,6},{6,4},{1,3},{3,1},{5,7},{7,5},{8,10},{10,8},{12,... | collective-permute-start | bytes 80 | tf_op jit(solution)/shard_map/ppermute | solution.py:409
  32.0 2.0 %collective-permute-done.7 = f32[2,3]{1,0:T(2,128)S(1)} collective-permute-done((f32[2,3]{1,0:T(2,128)S(1)}, f32[2,3]{1,0:T(2,128)S(1)}, u32[]{:S(2)}, u32[]{:S(2)}) %collective-permute-start.7) | collective-permute-done | bytes 56 | tf_op jit(solution)/shard_map/ppermute | solution.py:409
  34.0 2.6 %collective-permute-start.8 = (f32[4,3]{1,0:T(4,128)S(1)}, f32[4,3]{1,0:T(4,128)S(1)}, u32[]{:S(2)}, u32[]{:S(2)}) collective-permute-start(f32[4,3]{1,0:T(4,128)S(1)} %pad_maximum_fusion.1), channel_id=1, source_target_pairs={{0,4},{2,6},{4,0},{6,2},{1,5},{3,7},{5,1},{7,3},{8,12},{10,14},{12... | collective-permute-start | bytes 152 | tf_op jit(solution)/shard_map/ppermute | solution.py:409
  36.6 1.9 %collective-permute-done.8 = f32[4,3]{1,0:T(4,128)S(1)} collective-permute-done((f32[4,3]{1,0:T(4,128)S(1)}, f32[4,3]{1,0:T(4,128)S(1)}, u32[]{:S(2)}, u32[]{:S(2)}) %collective-permute-start.8) | collective-permute-done | bytes 80 | tf_op jit(solution)/shard_map/ppermute | solution.py:409
  38.6 1.8 %patch_weights.1.refs_3_ = f32[160,2048]{1,0:T(8,128)S(1)} custom-call(s32[3]{0:T(128)S(1)} %pad_add_fusion.1.place, s32[160]{0:T(256)S(1)} %copy-done.4, f32[8,3]{1,0:T(8,128)S(1)} %pad_maximum_fusion.facts), custom_call_target="tpu_custom_call" | custom-call | flops 1 | bytes 1 | tf_op jit(solution)/shard_map/patch_weights/pallas_call | solution.py:362
  40.4 6.6 %warp_filter.4 = (bf16[128,1536]{1,0:T(8,128)(2,1)S(1)}, bf16[128,1536]{1,0:T(8,128)(2,1)S(1)}, bf16[128,1536]{1,0:T(8,128)(2,1)S(1)}, bf16[128,1536]{1,0:T(8,128)(2,1)S(1)}) custom-call(f32[1]{0:T(128)} %convert_element_type.36.weight, s32[3]{0:T(128)S(1)} %pad_add_fusion.1.place, f32[512,4096]{1,0:T(8,128)} %bitcast.20, f32[512,4096]{1,0:T(8,128)} %bitcast.21, ...), custom_call_target="tpu_custom_call" | custom-call | flops 1 | bytes 1 | tf_op jit(solution)/shard_map/warp_filter/pallas_call | solution.py:237
  47.0 0.7 copy-done.2
  47.8 0.7 copy-done.7
  48.5 0.7 copy-done.8
  49.3 0.7 copy-done.9
  50.0 1.3 %join_blocks.3.mine = bf16[512,1536]{1,0:T(8,128)(2,1)} custom-call(bf16[128,1536]{1,0:T(8,128)(2,1)S(1)} %get-tuple-element.55.refs_0_, bf16[128,1536]{1,0:T(8,128)(2,1)S(1)} %collective-permute-done.3.refs_1_, bf16[128,1536]{1,0:T(8,128)(2,1)S(1)} %collective-permute-done.4.refs_2_, bf16[128,1536]{1,0:T(8,128)(2,1)S(1)} %collective-permute-done.5.refs_3_), custom_call_target="tpu_custom_call" | custom-call | flops 1 | bytes 1 | tf_op jit(solution)/shard_map/join_blocks/pallas_call | solution.py:270
  52.2 1.9 %collective-permute-start.14 = (bf16[128,1536]{1,0:T(8,128)(2,1)}, bf16[128,1536]{1,0:T(8,128)(2,1)S(1)}, u32[]{:S(2)}, u32[]{:S(2)}) collective-permute-start(bf16[128,1536]{1,0:T(8,128)(2,1)} %copy-done.8), channel_id=1, source_target_pairs={{0,16},{8,24},{16,0},{24,8},{1,17},{9,25},{17,1},{25,9},{2,18},{10... | collective-permute-start | bytes 1179656 | tf_op jit(solution)/shard_map/ppermute | solution.py:409
  54.1 1.5 %collective-permute-start.15 = (bf16[128,1536]{1,0:T(8,128)(2,1)}, bf16[128,1536]{1,0:T(8,128)(2,1)S(1)}, u32[]{:S(2)}, u32[]{:S(2)}) collective-permute-start(bf16[128,1536]{1,0:T(8,128)(2,1)} %copy-done.7), channel_id=1, source_target_pairs={{0,24},{8,16},{16,8},{24,0},{1,25},{9,17},{17,9},{25,1},{2,26},{10... | collective-permute-start | bytes 1179656 | tf_op jit(solution)/shard_map/ppermute | solution.py:409
  56.3 2.7 %pair_sum.3 = (bf16[160,768]{1,0:T(8,128)(2,1)S(1)}, bf16[160,768]{1,0:T(8,128)(2,1)S(1)}, bf16[160,768]{1,0:T(8,128)(2,1)S(1)}, bf16[160,768]{1,0:T(8,128)(2,1)S(1)}) custom-call(s32[3]{0:T(128)S(1)} %pad_add_fusion.1.place, s32[240]{0:T(256)S(1)} %pad_add_fusion.table, bf16[512,1536]{1,0:T(8,128)(2,1)} %join_blocks.3.mine, ...), custom_call_target="tpu_custom_call" | custom-call | flops 1 | bytes 1 | tf_op jit(solution)/shard_map/pair_sum/pallas_call | solution.py:322
  58.9 1.6 %collective-permute-start.16 = (bf16[160,768]{1,0:T(8,128)(2,1)S(1)}, bf16[160,768]{1,0:T(8,128)(2,1)S(1)}, u32[]{:S(2)}, u32[]{:S(2)}) collective-permute-start(bf16[160,768]{1,0:T(8,128)(2,1)S(1)} %get-tuple-element.72), channel_id=1, source_target_pairs={{0,2},{2,0},{4,6},{6,4},{1,3},{3,1},{5,7},{7,5},{8,10},{10,8},{12,... | collective-permute-start | bytes 737288 | tf_op jit(solution)/shard_map/ppermute | solution.py:409
  61.0 4.6 %warp_filter.5 = (bf16[128,1024]{1,0:T(8,128)(2,1)S(1)}, bf16[128,1024]{1,0:T(8,128)(2,1)S(1)}, bf16[128,1024]{1,0:T(8,128)(2,1)S(1)}, bf16[128,1024]{1,0:T(8,128)(2,1)S(1)}) custom-call(f32[1]{0:T(128)} %convert_element_type.36.weight, s32[3]{0:T(128)S(1)} %pad_add_fusion.1.place, f32[512,4096]{1,0:T(8,128)} %bitcast.25, f32[512,4096]{1,0:T(8,128)} %bitcast.26, ...), custom_call_target="tpu_custom_call" | custom-call | flops 1 | bytes 1 | tf_op jit(solution)/shard_map/warp_filter/pallas_call | solution.py:237
  65.7 6.1 %collective-permute-done.14.refs_2_ = bf16[128,1536]{1,0:T(8,128)(2,1)S(1)} collective-permute-done((bf16[128,1536]{1,0:T(8,128)(2,1)}, bf16[128,1536]{1,0:T(8,128)(2,1)S(1)}, u32[]{:S(2)}, u32[]{:S(2)}) %collective-permute-start.14) | collective-permute-done | bytes 393248 | tf_op jit(solution)/shard_map/ppermute | solution.py:409
  72.1 3.4 %collective-permute-done.18.other = bf16[512,1536]{1,0:T(8,128)(2,1)S(1)} collective-permute-done((bf16[512,1536]{1,0:T(8,128)(2,1)S(1)}, bf16[512,1536]{1,0:T(8,128)(2,1)S(1)}, u32[]{:S(2)}, u32[]{:S(2)}) %collective-permute-start.18) | collective-permute-done | bytes 1572896 | tf_op jit(solution)/shard_map/ppermute | solution.py:409
  75.5 1.3 %pair_sum.4 = (bf16[160,768]{1,0:T(8,128)(2,1)S(1)}, bf16[160,768]{1,0:T(8,128)(2,1)S(1)}, bf16[160,768]{1,0:T(8,128)(2,1)S(1)}, bf16[160,768]{1,0:T(8,128)(2,1)S(1)}) custom-call(s32[3]{0:T(128)S(1)} %pad_add_fusion.1.place, s32[240]{0:T(256)S(1)} %pad_add_fusion.table, bf16[512,1536]{1,0:T(8,128)(2,1)S(1)} %join_blocks.4.mine, ...), custom_call_target="tpu_custom_call" | custom-call | flops 1 | bytes 1 | tf_op jit(solution)/shard_map/pair_sum/pallas_call | solution.py:322
  76.8 1.6 %collective-permute-start.19 = (bf16[160,768]{1,0:T(8,128)(2,1)S(1)}, bf16[160,768]{1,0:T(8,128)(2,1)S(1)}, u32[]{:S(2)}, u32[]{:S(2)}) collective-permute-start(bf16[160,768]{1,0:T(8,128)(2,1)S(1)} %get-tuple-element.88), channel_id=1, source_target_pairs={{0,2},{2,0},{4,6},{6,4},{1,3},{3,1},{5,7},{7,5},{8,10},{10,8},{12,... | collective-permute-start | bytes 737288 | tf_op jit(solution)/shard_map/ppermute | solution.py:409
  78.5 1.7 %collective-permute-start.10 = (bf16[128,1024]{1,0:T(8,128)(2,1)S(1)}, bf16[128,1024]{1,0:T(8,128)(2,1)S(1)}, u32[]{:S(2)}, u32[]{:S(2)}) collective-permute-start(bf16[128,1024]{1,0:T(8,128)(2,1)S(1)} %get-tuple-element.75), channel_id=1, source_target_pairs={{0,8},{8,0},{16,24},{24,16},{1,9},{9,1},{17,25},{25,17},{2,10},{10... | collective-permute-start | bytes 786440 | tf_op jit(solution)/shard_map/ppermute | solution.py:409
  80.5 1.5 %collective-permute-start.12 = (bf16[128,1024]{1,0:T(8,128)(2,1)S(1)}, bf16[128,1024]{1,0:T(8,128)(2,1)S(1)}, u32[]{:S(2)}, u32[]{:S(2)}) collective-permute-start(bf16[128,1024]{1,0:T(8,128)(2,1)S(1)} %get-tuple-element.77), channel_id=1, source_target_pairs={{0,24},{8,16},{16,8},{24,0},{1,25},{9,17},{17,9},{25,1},{2,26},{10... | collective-permute-start | bytes 786440 | tf_op jit(solution)/shard_map/ppermute | solution.py:409
  82.0 2.6 %collective-permute-start.20 = (bf16[160,768]{1,0:T(8,128)(2,1)S(1)}, bf16[160,768]{1,0:T(8,128)(2,1)S(1)}, u32[]{:S(2)}, u32[]{:S(2)}) collective-permute-start(bf16[160,768]{1,0:T(8,128)(2,1)S(1)} %add_convert_fusion.1), channel_id=1, source_target_pairs={{0,4},{2,6},{4,0},{6,2},{1,5},{3,7},{5,1},{7,3},{8,12},{10,14},{12... | collective-permute-start | bytes 737288 | tf_op jit(solution)/shard_map/ppermute | solution.py:409
  84.6 2.3 %collective-permute-done.19 = bf16[160,768]{1,0:T(8,128)(2,1)S(1)} collective-permute-done((bf16[160,768]{1,0:T(8,128)(2,1)S(1)}, bf16[160,768]{1,0:T(8,128)(2,1)S(1)}, u32[]{:S(2)}, u32[]{:S(2)}) %collective-permute-start.19) | collective-permute-done | bytes 245792 | tf_op jit(solution)/shard_map/ppermute | solution.py:409
  86.9 0.7 collective-permute-done.10.refs_1_
  87.7 5.9 %collective-permute-done.11.refs_2_ = bf16[128,1024]{1,0:T(8,128)(2,1)S(1)} collective-permute-done((bf16[128,1024]{1,0:T(8,128)(2,1)S(1)}, bf16[128,1024]{1,0:T(8,128)(2,1)S(1)}, u32[]{:S(2)}, u32[]{:S(2)}) %collective-permute-start.11) | collective-permute-done | bytes 262176 | tf_op jit(solution)/shard_map/ppermute | solution.py:409
  93.6 1.5 %collective-permute-done.20.refs_2_ = bf16[160,768]{1,0:T(8,128)(2,1)S(1)} collective-permute-done((bf16[160,768]{1,0:T(8,128)(2,1)S(1)}, bf16[160,768]{1,0:T(8,128)(2,1)S(1)}, u32[]{:S(2)}, u32[]{:S(2)}) %collective-permute-start.20) | collective-permute-done | bytes 245792 | tf_op jit(solution)/shard_map/ppermute | solution.py:409
  95.2 2.6 %collective-permute-done.21.other = bf16[512,1024]{1,0:T(8,128)(2,1)S(1)} collective-permute-done((bf16[512,1024]{1,0:T(8,128)(2,1)S(1)}, bf16[512,1024]{1,0:T(8,128)(2,1)S(1)}, u32[]{:S(2)}, u32[]{:S(2)}) %collective-permute-start.21) | collective-permute-done | bytes 1048608 | tf_op jit(solution)/shard_map/ppermute | solution.py:409
  97.9 1.1 pair_sum.5
  99.1 2.0 %collective-permute-start.25 = (bf16[160,768]{1,0:T(8,128)(2,1)S(1)}, bf16[160,768]{1,0:T(8,128)(2,1)S(1)}, u32[]{:S(2)}, u32[]{:S(2)}) collective-permute-start(bf16[160,768]{1,0:T(8,128)(2,1)S(1)} %get-tuple-element.100), channel_id=1, source_target_pairs={{0,2},{2,0},{4,6},{6,4},{1,3},{3,1},{5,7},{7,5},{8,10},{10,8},{12,... | collective-permute-start | bytes 737288 | tf_op jit(solution)/shard_map/ppermute | solution.py:409
  101.1 1.1 collective-permute-start.26
  102.2 1.9 %collective-permute-start.22 = (bf16[160,512]{1,0:T(8,128)(2,1)S(1)}, bf16[160,512]{1,0:T(8,128)(2,1)S(1)}, u32[]{:S(2)}, u32[]{:S(2)}) collective-permute-start(bf16[160,512]{1,0:T(8,128)(2,1)S(1)} %get-tuple-element.96), channel_id=1, source_target_pairs={{0,2},{2,0},{4,6},{6,4},{1,3},{3,1},{5,7},{7,5},{8,10},{10,8},{12,... | collective-permute-start | bytes 491528 | tf_op jit(solution)/shard_map/ppermute | solution.py:409
  104.1 7.2 %collective-permute-done.23 = bf16[160,512]{1,0:T(8,128)(2,1)S(1)} collective-permute-done((bf16[160,512]{1,0:T(8,128)(2,1)S(1)}, bf16[160,512]{1,0:T(8,128)(2,1)S(1)}, u32[]{:S(2)}, u32[]{:S(2)}) %collective-permute-start.23) | collective-permute-done | bytes 163872 | tf_op jit(solution)/shard_map/ppermute | solution.py:409
  112.0 0.9 patch_mean.3.refs_4_
  113.0 4.3 %collective-permute-done.25.refs_1_ = bf16[160,768]{1,0:T(8,128)(2,1)S(1)} collective-permute-done((bf16[160,768]{1,0:T(8,128)(2,1)S(1)}, bf16[160,768]{1,0:T(8,128)(2,1)S(1)}, u32[]{:S(2)}, u32[]{:S(2)}) %collective-permute-start.25) | collective-permute-done | bytes 245792 | tf_op jit(solution)/shard_map/ppermute | solution.py:409
  117.3 0.9 patch_mean.4.refs_4_
  118.2 4.7 %collective-permute-done.22.refs_1_ = bf16[160,512]{1,0:T(8,128)(2,1)S(1)} collective-permute-done((bf16[160,512]{1,0:T(8,128)(2,1)S(1)}, bf16[160,512]{1,0:T(8,128)(2,1)S(1)}, u32[]{:S(2)}, u32[]{:S(2)}) %collective-permute-start.22) | collective-permute-done | bytes 163872 | tf_op jit(solution)/shard_map/ppermute | solution.py:409
  122.9 0.8 patch_mean.5
  (55 shorter events, 4.6 us)
Async XLA Ops:
  1.1 12.0 %collective-permute-start.2 = (f32[16,4096]{1,0:T(8,128)S(1)}, f32[16,4096]{1,0:T(8,128)S(1)}, u32[]{:S(2)}, u32[]{:S(2)}) collective-permute-start(f32[16,4096]{1,0:T(8,128)S(1)} %get-tuple-element.103), channel_id=1, source_target_pairs={{8,16},{16,8},{9,17},{17,9},{10,18},{18,10},{11,19},{19,11},{12,20... | collective-permute-start | bytes 786440 | tf_op jit(solution)/shard_map/ppermute | solution.py:447
  1.8 17.3 %collective-permute-start.1 = (f32[16,4096]{1,0:T(8,128)S(1)}, f32[16,4096]{1,0:T(8,128)S(1)}, u32[]{:S(2)}, u32[]{:S(2)}) collective-permute-start(f32[16,4096]{1,0:T(8,128)S(1)} %get-tuple-element.104), channel_id=1, source_target_pairs={{0,8},{16,24},{8,0},{24,16},{1,9},{17,25},{9,1},{25,17},{2,10},{18... | collective-permute-start | bytes 786440 | tf_op jit(solution)/shard_map/ppermute | solution.py:446
  8.2 0.7 copy-start.5
  8.9 0.7 copy-start.6
  11.7 28.7 %copy-start = (bf16[3,128,480]{2,1,0:T(8,128)(2,1)}, bf16[3,128,480]{2,1,0:T(8,128)(2,1)S(1)}, u32[]{:S(2)}) copy-start(bf16[3,128,480]{2,1,0:T(8,128)(2,1)S(1)} %get-tuple-element.53.rest_15_.rest_12_) | copy-start | bytes 1105924
  19.0 19.6 %copy-start.4 = (s32[160]{0:T(256)S(1)}, s32[160]{0:T(256)}, u32[]{:S(2)}) copy-start(s32[160]{0:T(256)} %sites.1) | copy-start | bytes 1924
  25.5 24.5 %collective-permute-start.3 = (bf16[128,1536]{1,0:T(8,128)(2,1)S(1)}, bf16[128,1536]{1,0:T(8,128)(2,1)S(1)}, u32[]{:S(2)}, u32[]{:S(2)}) collective-permute-start(bf16[128,1536]{1,0:T(8,128)(2,1)S(1)} %get-tuple-element.56), channel_id=1, source_target_pairs={{0,8},{8,0},{16,24},{24,16},{1,9},{9,1},{17,25},{25,17},{2,10},{10... | collective-permute-start | bytes 1179656 | tf_op jit(solution)/shard_map/ppermute | solution.py:409
  25.6 24.4 %collective-permute-start.4 = (bf16[128,1536]{1,0:T(8,128)(2,1)S(1)}, bf16[128,1536]{1,0:T(8,128)(2,1)S(1)}, u32[]{:S(2)}, u32[]{:S(2)}) collective-permute-start(bf16[128,1536]{1,0:T(8,128)(2,1)S(1)} %get-tuple-element.57), channel_id=1, source_target_pairs={{0,16},{8,24},{16,0},{24,8},{1,17},{9,25},{17,1},{25,9},{2,18},{10... | collective-permute-start | bytes 1179656 | tf_op jit(solution)/shard_map/ppermute | solution.py:409
  27.6 22.4 %collective-permute-start.5 = (bf16[128,1536]{1,0:T(8,128)(2,1)S(1)}, bf16[128,1536]{1,0:T(8,128)(2,1)S(1)}, u32[]{:S(2)}, u32[]{:S(2)}) collective-permute-start(bf16[128,1536]{1,0:T(8,128)(2,1)S(1)} %get-tuple-element.58), channel_id=1, source_target_pairs={{0,24},{8,16},{16,8},{24,0},{1,25},{9,17},{17,9},{25,1},{2,26},{10... | collective-permute-start | bytes 1179656 | tf_op jit(solution)/shard_map/ppermute | solution.py:409
  29.2 1.1 collective-permute-start.6
  30.4 3.6 %collective-permute-start.7 = (f32[2,3]{1,0:T(2,128)S(1)}, f32[2,3]{1,0:T(2,128)S(1)}, u32[]{:S(2)}, u32[]{:S(2)}) collective-permute-start(f32[2,3]{1,0:T(2,128)S(1)} %pad_maximum_fusion.2), channel_id=1, source_target_pairs={{0,2},{2,0},{4,6},{6,4},{1,3},{3,1},{5,7},{7,5},{8,10},{10,8},{12,... | collective-permute-start | bytes 80 | tf_op jit(solution)/shard_map/ppermute | solution.py:409
  34.0 4.5 %collective-permute-start.8 = (f32[4,3]{1,0:T(4,128)S(1)}, f32[4,3]{1,0:T(4,128)S(1)}, u32[]{:S(2)}, u32[]{:S(2)}) collective-permute-start(f32[4,3]{1,0:T(4,128)S(1)} %pad_maximum_fusion.1), channel_id=1, source_target_pairs={{0,4},{2,6},{4,0},{6,2},{1,5},{3,7},{5,1},{7,3},{8,12},{10,14},{12... | collective-permute-start | bytes 152 | tf_op jit(solution)/shard_map/ppermute | solution.py:409
  47.0 0.7 copy-start.2
  47.8 0.7 copy-start.7
  48.5 0.7 copy-start.8
  49.3 0.7 copy-start.9
  51.3 4.9 %collective-permute-start.9 = (bf16[512,1536]{1,0:T(8,128)(2,1)}, bf16[512,1536]{1,0:T(8,128)(2,1)}, u32[]{:S(2)}, u32[]{:S(2)}) collective-permute-start(bf16[512,1536]{1,0:T(8,128)(2,1)} %join_blocks.3.mine), channel_id=1, source_target_pairs={{0,1},{1,0},{2,3},{3,2},{4,5},{5,4},{6,7},{7,6},{8,9},{9,8},{10,11... | collective-permute-start | bytes 4718600 | tf_op jit(solution)/shard_map/ppermute | solution.py:409
  51.3 4.3 %collective-permute-start = (s32[1]{0:T(128)}, s32[1]{0:T(128)}, u32[]{:S(2)}, u32[]{:S(2)}) collective-permute-start(s32[1]{0:T(128)} %param.11), channel_id=1, source_target_pairs={{0,1},{1,0},{2,3},{3,2},{4,5},{5,4},{6,7},{7,6},{8,9},{9,8},{10,11... | collective-permute-start | bytes 20 | tf_op jit(solution)/shard_map/ppermute | solution.py:409
  52.1 13.6 %collective-permute-start.13 = (bf16[128,1536]{1,0:T(8,128)(2,1)}, bf16[128,1536]{1,0:T(8,128)(2,1)S(1)}, u32[]{:S(2)}, u32[]{:S(2)}) collective-permute-start(bf16[128,1536]{1,0:T(8,128)(2,1)} %copy-done.9), channel_id=1, source_target_pairs={{0,8},{8,0},{16,24},{24,16},{1,9},{9,1},{17,25},{25,17},{2,10},{10... | collective-permute-start | bytes 1179656 | tf_op jit(solution)/shard_map/ppermute | solution.py:409
  52.2 19.7 %collective-permute-start.14 = (bf16[128,1536]{1,0:T(8,128)(2,1)}, bf16[128,1536]{1,0:T(8,128)(2,1)S(1)}, u32[]{:S(2)}, u32[]{:S(2)}) collective-permute-start(bf16[128,1536]{1,0:T(8,128)(2,1)} %copy-done.8), channel_id=1, source_target_pairs={{0,16},{8,24},{16,0},{24,8},{1,17},{9,25},{17,1},{25,9},{2,18},{10... | collective-permute-start | bytes 1179656 | tf_op jit(solution)/shard_map/ppermute | solution.py:409
  54.1 17.7 %collective-permute-start.15 = (bf16[128,1536]{1,0:T(8,128)(2,1)}, bf16[128,1536]{1,0:T(8,128)(2,1)S(1)}, u32[]{:S(2)}, u32[]{:S(2)}) collective-permute-start(bf16[128,1536]{1,0:T(8,128)(2,1)} %copy-done.7), channel_id=1, source_target_pairs={{0,24},{8,16},{16,8},{24,0},{1,25},{9,17},{17,9},{25,1},{2,26},{10... | collective-permute-start | bytes 1179656 | tf_op jit(solution)/shard_map/ppermute | solution.py:409
  56.3 4.8 %copy-start.1 = (bf16[3,128,480]{2,1,0:T(8,128)(2,1)S(1)}, bf16[3,128,480]{2,1,0:T(8,128)(2,1)}, u32[]{:S(2)}) copy-start(bf16[3,128,480]{2,1,0:T(8,128)(2,1)} %copy-done) | copy-start | bytes 1105924
  58.9 12.9 %collective-permute-start.16 = (bf16[160,768]{1,0:T(8,128)(2,1)S(1)}, bf16[160,768]{1,0:T(8,128)(2,1)S(1)}, u32[]{:S(2)}, u32[]{:S(2)}) collective-permute-start(bf16[160,768]{1,0:T(8,128)(2,1)S(1)} %get-tuple-element.72), channel_id=1, source_target_pairs={{0,2},{2,0},{4,6},{6,4},{1,3},{3,1},{5,7},{7,5},{8,10},{10,8},{12,... | collective-permute-start | bytes 737288 | tf_op jit(solution)/shard_map/ppermute | solution.py:409
  60.6 11.3 %collective-permute-start.17 = (bf16[160,768]{1,0:T(8,128)(2,1)S(1)}, bf16[160,768]{1,0:T(8,128)(2,1)S(1)}, u32[]{:S(2)}, u32[]{:S(2)}) collective-permute-start(bf16[160,768]{1,0:T(8,128)(2,1)S(1)} %get-tuple-element.70), channel_id=1, source_target_pairs={{0,2},{2,0},{4,6},{6,4},{1,3},{3,1},{5,7},{7,5},{8,10},{10,8},{12,... | collective-permute-start | bytes 737288 | tf_op jit(solution)/shard_map/ppermute | solution.py:409
  61.0 10.9 %copy-start.3 = (bf16[128,1536]{1,0:T(8,128)(2,1)S(1)}, bf16[128,1536]{1,0:T(8,128)(2,1)}, u32[]{:S(2)}) copy-start(bf16[128,1536]{1,0:T(8,128)(2,1)} %copy-done.2) | copy-start | bytes 1179652
  72.1 3.5 %collective-permute-start.18 = (bf16[512,1536]{1,0:T(8,128)(2,1)S(1)}, bf16[512,1536]{1,0:T(8,128)(2,1)S(1)}, u32[]{:S(2)}, u32[]{:S(2)}) collective-permute-start(bf16[512,1536]{1,0:T(8,128)(2,1)S(1)} %join_blocks.4.mine), channel_id=1, source_target_pairs={{0,1},{1,0},{2,3},{3,2},{4,5},{5,4},{6,7},{7,6},{8,9},{9,8},{10,11... | collective-permute-start | bytes 4718600 | tf_op jit(solution)/shard_map/ppermute | solution.py:409
  76.8 10.0 %collective-permute-start.19 = (bf16[160,768]{1,0:T(8,128)(2,1)S(1)}, bf16[160,768]{1,0:T(8,128)(2,1)S(1)}, u32[]{:S(2)}, u32[]{:S(2)}) collective-permute-start(bf16[160,768]{1,0:T(8,128)(2,1)S(1)} %get-tuple-element.88), channel_id=1, source_target_pairs={{0,2},{2,0},{4,6},{6,4},{1,3},{3,1},{5,7},{7,5},{8,10},{10,8},{12,... | collective-permute-start | bytes 737288 | tf_op jit(solution)/shard_map/ppermute | solution.py:409
  78.5 9.2 %collective-permute-start.10 = (bf16[128,1024]{1,0:T(8,128)(2,1)S(1)}, bf16[128,1024]{1,0:T(8,128)(2,1)S(1)}, u32[]{:S(2)}, u32[]{:S(2)}) collective-permute-start(bf16[128,1024]{1,0:T(8,128)(2,1)S(1)} %get-tuple-element.75), channel_id=1, source_target_pairs={{0,8},{8,0},{16,24},{24,16},{1,9},{9,1},{17,25},{25,17},{2,10},{10... | collective-permute-start | bytes 786440 | tf_op jit(solution)/shard_map/ppermute | solution.py:409
  80.1 13.4 %collective-permute-start.11 = (bf16[128,1024]{1,0:T(8,128)(2,1)S(1)}, bf16[128,1024]{1,0:T(8,128)(2,1)S(1)}, u32[]{:S(2)}, u32[]{:S(2)}) collective-permute-start(bf16[128,1024]{1,0:T(8,128)(2,1)S(1)} %get-tuple-element.76), channel_id=1, source_target_pairs={{0,16},{8,24},{16,0},{24,8},{1,17},{9,25},{17,1},{25,9},{2,18},{10... | collective-permute-start | bytes 786440 | tf_op jit(solution)/shard_map/ppermute | solution.py:409
  80.5 13.1 %collective-permute-start.12 = (bf16[128,1024]{1,0:T(8,128)(2,1)S(1)}, bf16[128,1024]{1,0:T(8,128)(2,1)S(1)}, u32[]{:S(2)}, u32[]{:S(2)}) collective-permute-start(bf16[128,1024]{1,0:T(8,128)(2,1)S(1)} %get-tuple-element.77), channel_id=1, source_target_pairs={{0,24},{8,16},{16,8},{24,0},{1,25},{9,17},{17,9},{25,1},{2,26},{10... | collective-permute-start | bytes 786440 | tf_op jit(solution)/shard_map/ppermute | solution.py:409
  82.0 13.1 %collective-permute-start.20 = (bf16[160,768]{1,0:T(8,128)(2,1)S(1)}, bf16[160,768]{1,0:T(8,128)(2,1)S(1)}, u32[]{:S(2)}, u32[]{:S(2)}) collective-permute-start(bf16[160,768]{1,0:T(8,128)(2,1)S(1)} %add_convert_fusion.1), channel_id=1, source_target_pairs={{0,4},{2,6},{4,0},{6,2},{1,5},{3,7},{5,1},{7,3},{8,12},{10,14},{12... | collective-permute-start | bytes 737288 | tf_op jit(solution)/shard_map/ppermute | solution.py:409
  95.1 2.7 %collective-permute-start.21 = (bf16[512,1024]{1,0:T(8,128)(2,1)S(1)}, bf16[512,1024]{1,0:T(8,128)(2,1)S(1)}, u32[]{:S(2)}, u32[]{:S(2)}) collective-permute-start(bf16[512,1024]{1,0:T(8,128)(2,1)S(1)} %join_blocks.5.mine), channel_id=1, source_target_pairs={{0,1},{1,0},{2,3},{3,2},{4,5},{5,4},{6,7},{7,6},{8,9},{9,8},{10,11... | collective-permute-start | bytes 3145736 | tf_op jit(solution)/shard_map/ppermute | solution.py:409
  99.0 12.4 %collective-permute-start.23 = (bf16[160,512]{1,0:T(8,128)(2,1)S(1)}, bf16[160,512]{1,0:T(8,128)(2,1)S(1)}, u32[]{:S(2)}, u32[]{:S(2)}) collective-permute-start(bf16[160,512]{1,0:T(8,128)(2,1)S(1)} %get-tuple-element.98), channel_id=1, source_target_pairs={{0,2},{2,0},{4,6},{6,4},{1,3},{3,1},{5,7},{7,5},{8,10},{10,8},{12,... | collective-permute-start | bytes 491528 | tf_op jit(solution)/shard_map/ppermute | solution.py:409
  99.1 18.2 %collective-permute-start.25 = (bf16[160,768]{1,0:T(8,128)(2,1)S(1)}, bf16[160,768]{1,0:T(8,128)(2,1)S(1)}, u32[]{:S(2)}, u32[]{:S(2)}) collective-permute-start(bf16[160,768]{1,0:T(8,128)(2,1)S(1)} %get-tuple-element.100), channel_id=1, source_target_pairs={{0,2},{2,0},{4,6},{6,4},{1,3},{3,1},{5,7},{7,5},{8,10},{10,8},{12,... | collective-permute-start | bytes 737288 | tf_op jit(solution)/shard_map/ppermute | solution.py:409
  101.1 16.2 %collective-permute-start.26 = (bf16[160,768]{1,0:T(8,128)(2,1)S(1)}, bf16[160,768]{1,0:T(8,128)(2,1)S(1)}, u32[]{:S(2)}, u32[]{:S(2)}) collective-permute-start(bf16[160,768]{1,0:T(8,128)(2,1)S(1)} %add_convert_fusion), channel_id=1, source_target_pairs={{0,4},{2,6},{4,0},{6,2},{1,5},{3,7},{5,1},{7,3},{8,12},{10,14},{12... | collective-permute-start | bytes 737288 | tf_op jit(solution)/shard_map/ppermute | solution.py:409
  102.2 20.7 %collective-permute-start.22 = (bf16[160,512]{1,0:T(8,128)(2,1)S(1)}, bf16[160,512]{1,0:T(8,128)(2,1)S(1)}, u32[]{:S(2)}, u32[]{:S(2)}) collective-permute-start(bf16[160,512]{1,0:T(8,128)(2,1)S(1)} %get-tuple-element.96), channel_id=1, source_target_pairs={{0,2},{2,0},{4,6},{6,4},{1,3},{3,1},{5,7},{7,5},{8,10},{10,8},{12,... | collective-permute-start | bytes 491528 | tf_op jit(solution)/shard_map/ppermute | solution.py:409
  111.4 11.4 %collective-permute-start.24 = (bf16[160,512]{1,0:T(8,128)(2,1)S(1)}, bf16[160,512]{1,0:T(8,128)(2,1)S(1)}, u32[]{:S(2)}, u32[]{:S(2)}) collective-permute-start(bf16[160,512]{1,0:T(8,128)(2,1)S(1)} %add_convert_fusion.2), channel_id=1, source_target_pairs={{0,4},{2,6},{4,0},{6,2},{1,5},{3,7},{5,1},{7,3},{8,12},{10,14},{12... | collective-permute-start | bytes 491528 | tf_op jit(solution)/shard_map/ppermute | solution.py:409

commit v7 on v6

--- a/solution.py
+++ b/solution.py
@@ -18,9 +18,9 @@
 SIDE = 128
 TILE = 256
 STRIP = 128
-PARTS = (3, 3, 2)
+PARTS = (4, 4)
 WHOLE = 8
-VMEM = 48 * 1024 * 1024
+VMEM = 24 * 1024 * 1024
 COST = pl.CostEstimate(flops=1, bytes_accessed=1, transcendentals=0)
 
 sigmas = (1.0, 2.0, 3.5)
@@ -493,11 +493,7 @@
         if index == 0:
             received = tied(received, scale)
         if index >= 1:
-            received = tied(received, added[index - 1])
-        if index == 1:
-            received = tied(received, kept[0][:-1])
-        if index >= 2:
-            received = tied(received, kept[index - 2])
+            received = tied(received, kept[index - 1])
         mine = joined([outgoing[0]] + received)
         other = swapped(mine, "core", 1)
         sums[index] = pair_sum(place, table, mine, other, slots, lines, quarter)

time: 124 us -> 125 us (level)
  waiting for transfers between devices: 49.9 us -> 61.5 us
  starting transfers between devices: 33.9 us -> 27.7 us
  Pallas kernels: 30.9 us -> 25.2 us
    ppermute x25 -> x18, waiting for transfers between devices: 43.9 us -> 54.8 us  [swapped(): return lax.ppermute(value, axis, [(i, i ^ distance) for i in range(count)])]
    ppermute x25 -> x18, starting transfers between devices: 27.5 us -> 21.3 us  [swapped(): return lax.ppermute(value, axis, [(i, i ^ distance) for i in range(count)])]
    pallas_call x3 -> x2, Pallas kernels: 17.7 us -> 13 us  [filter_chunk(): pl.pallas_call(functools.partial(filter_kernel, first_chunk=start == 0, l...]
    unnamed x20 -> x14, local copies, waits for them, and re-layouts: 4.33 us -> 5.52 us
    pallas_call x3 -> x2, Pallas kernels: 2.63 us -> 1.98 us  [finish_chunk(): pl.pallas_call(functools.partial(finish_kernel, count=len(pieces)), out_s...]
    pallas_call x3 -> x2, Pallas kernels: 5.11 us -> 4.6 us  [pair_sum(): pl.pallas_call(functools.partial(pair_kernel, slots=slots, distances=dist...]
  transfers between devices with their start and end apart: 27 -> 20, of which waited for: 14 -> 13; matrix products, arithmetic and copies ran while one was open for 1% -> 1% of each run, Pallas kernels for 16% -> 9%
where the time goes in v7:
time: 125 us
  waiting for transfers between devices  61.5 us (49%)
  starting transfers between devices  27.7 us (22%)
  Pallas kernels  25.2 us (20%)
  local copies, waits for them, and re-layouts  5.71 us (5%)
  other arithmetic  2.32 us (2%)
  between operations  2.13 us (2%)
    ppermute x18, waiting for transfers between devices, swapped(): return lax.ppermute(value, axis, [(i, i ^ distance) for i in range(count)])  54.8 us
    ppermute x18, starting transfers between devices, swapped(): return lax.ppermute(value, axis, [(i, i ^ distance) for i in range(count)])  21.3 us
    pallas_call x2, Pallas kernels, filter_chunk(): pl.pallas_call(functools.partial(filter_kernel, first_chunk=start == 0, l...  13 us
    ppermute x1, waiting for transfers between devices, per_device(): even = lax.ppermute(jnp.where(is_odd, top, bottom), 'seg', pairs_from(0))  6.66 us
    ppermute x1, starting transfers between devices, per_device(): even = lax.ppermute(jnp.where(is_odd, top, bottom), 'seg', pairs_from(0))  5.73 us
    unnamed x14, local copies, waits for them, and re-layouts  5.52 us
    pallas_call x2, Pallas kernels, pair_sum(): pl.pallas_call(functools.partial(pair_kernel, slots=slots, distances=dist...  4.6 us
  transfers between devices with their start and end apart: 20, of which 13 were waited for; matrix products, arithmetic and copies ran while one was open for 1% of the time, Pallas kernels for 9%

profile of v7, /device:TPU:0, one launch (start us, length us, event | category | flops | bytes accessed | tf_op | source)
XLA Modules:
  0.0 124.5 jit_solution(2141268335880606788)
XLA Ops:
  0.0 1.1 select_bitcast_fusion
  1.1 0.7 collective-permute-start.2
  1.8 5.7 %collective-permute-start.1 = (f32[16,4096]{1,0:T(8,128)S(1)}, f32[16,4096]{1,0:T(8,128)S(1)}, u32[]{:S(2)}, u32[]{:S(2)}) collective-permute-start(f32[16,4096]{1,0:T(8,128)S(1)} %get-tuple-element.62), channel_id=1, source_target_pairs={{0,8},{16,24},{8,0},{24,16},{1,9},{17,25},{9,1},{25,17},{2,10},{18... | collective-permute-start | bytes 786440 | tf_op jit(solution)/shard_map/ppermute | solution.py:446
  8.2 0.7 copy-done.3
  8.9 0.7 copy-done.4
  9.5 2.1 %band_matrices.1 = (bf16[3,128,480]{2,1,0:T(8,128)(2,1)S(1)}, bf16[3,2,512,256]{3,2,1,0:T(8,128)(2,1)S(1)}) custom-call(s32[3]{0:T(128)S(1)} %pad_add_fusion.1.place, f32[1,2,3]{2,1,0:T(2,128)S(1)} %copy-done.3, s32[1,2]{1,0:T(1,128)S(1)} %copy-done.4, s32[1]{0:T(128)S(6)} %copy.10.shift), custom_call_target="tpu_custom_call" | custom-call | flops 1 | bytes 1 | tf_op jit(solution)/shard_map/band_matrices/pallas_call | solution.py:133
  12.4 6.7 %collective-permute-done.1.rest_6_.rest_7_.rest_8_.rest_9_.rest_10_.rest_11_ = f32[16,4096]{1,0:T(8,128)S(1)} collective-permute-done((f32[16,4096]{1,0:T(8,128)S(1)}, f32[16,4096]{1,0:T(8,128)S(1)}, u32[]{:S(2)}, u32[]{:S(2)}) %collective-permute-start.1) | collective-permute-done | bytes 262176 | tf_op jit(solution)/shard_map/ppermute | solution.py:446
  19.0 3.4 %copy-done = f32[1,512,4096]{2,1,0:T(8,128)S(1)} copy-done((f32[1,512,4096]{2,1,0:T(8,128)S(1)}, f32[1,512,4096]{2,1,0:T(8,128)}, u32[]{:S(2)}) %copy-start) | copy-done | bytes 8388632
  22.4 6.5 %warp_filter.3 = (bf16[128,2048]{1,0:T(8,128)(2,1)S(1)}, bf16[128,2048]{1,0:T(8,128)(2,1)S(1)}, bf16[128,2048]{1,0:T(8,128)(2,1)S(1)}, bf16[128,2048]{1,0:T(8,128)(2,1)S(1)}) custom-call(f32[1]{0:T(128)} %convert_element_type.27.weight, s32[3]{0:T(128)S(1)} %pad_add_fusion.1.place, f32[512,4096]{1,0:T(8,128)S(1)} %bitcast.15, f32[512,4096]{1,0:T(8,128)S(1)} %bitcast.16, ...), custom_call_target="tpu_custom_call" | custom-call | flops 1 | bytes 1 | tf_op jit(solution)/shard_map/warp_filter/pallas_call | solution.py:237
  29.0 2.0 %collective-permute-start.7 = (bf16[128,2048]{1,0:T(8,128)(2,1)S(1)}, bf16[128,2048]{1,0:T(8,128)(2,1)S(1)}, u32[]{:S(2)}, u32[]{:S(2)}) collective-permute-start(bf16[128,2048]{1,0:T(8,128)(2,1)S(1)} %get-tuple-element.40), channel_id=1, source_target_pairs={{0,16},{8,24},{16,0},{24,8},{1,17},{9,25},{17,1},{25,9},{2,18},{10... | collective-permute-start | bytes 1572872 | tf_op jit(solution)/shard_map/ppermute | solution.py:409
  30.9 1.5 %collective-permute-start.8 = (bf16[128,2048]{1,0:T(8,128)(2,1)S(1)}, bf16[128,2048]{1,0:T(8,128)(2,1)S(1)}, u32[]{:S(2)}, u32[]{:S(2)}) collective-permute-start(bf16[128,2048]{1,0:T(8,128)(2,1)S(1)} %get-tuple-element.41), channel_id=1, source_target_pairs={{0,24},{8,16},{16,8},{24,0},{1,25},{9,17},{17,9},{25,1},{2,26},{10... | collective-permute-start | bytes 1572872 | tf_op jit(solution)/shard_map/ppermute | solution.py:409
  33.2 1.1 collective-permute-done.9
  34.4 1.6 %collective-permute-start.10 = (f32[2,3]{1,0:T(2,128)S(1)}, f32[2,3]{1,0:T(2,128)S(1)}, u32[]{:S(2)}, u32[]{:S(2)}) collective-permute-start(f32[2,3]{1,0:T(2,128)S(1)} %pad_maximum_fusion.2), channel_id=1, source_target_pairs={{0,2},{2,0},{4,6},{6,4},{1,3},{3,1},{5,7},{7,5},{8,10},{10,8},{12,... | collective-permute-start | bytes 80 | tf_op jit(solution)/shard_map/ppermute | solution.py:409
  36.0 2.0 %collective-permute-done.10 = f32[2,3]{1,0:T(2,128)S(1)} collective-permute-done((f32[2,3]{1,0:T(2,128)S(1)}, f32[2,3]{1,0:T(2,128)S(1)}, u32[]{:S(2)}, u32[]{:S(2)}) %collective-permute-start.10) | collective-permute-done | bytes 56 | tf_op jit(solution)/shard_map/ppermute | solution.py:409
  38.0 2.6 %collective-permute-start.11 = (f32[4,3]{1,0:T(4,128)S(1)}, f32[4,3]{1,0:T(4,128)S(1)}, u32[]{:S(2)}, u32[]{:S(2)}) collective-permute-start(f32[4,3]{1,0:T(4,128)S(1)} %pad_maximum_fusion.1), channel_id=1, source_target_pairs={{0,4},{2,6},{4,0},{6,2},{1,5},{3,7},{5,1},{7,3},{8,12},{10,14},{12... | collective-permute-start | bytes 152 | tf_op jit(solution)/shard_map/ppermute | solution.py:409
  40.6 1.9 %collective-permute-done.11 = f32[4,3]{1,0:T(4,128)S(1)} collective-permute-done((f32[4,3]{1,0:T(4,128)S(1)}, f32[4,3]{1,0:T(4,128)S(1)}, u32[]{:S(2)}, u32[]{:S(2)}) %collective-permute-start.11) | collective-permute-done | bytes 80 | tf_op jit(solution)/shard_map/ppermute | solution.py:409
  42.6 1.8 %patch_weights.1.refs_3_ = f32[160,2048]{1,0:T(8,128)S(1)} custom-call(s32[3]{0:T(128)S(1)} %pad_add_fusion.1.place, s32[160]{0:T(256)S(1)} %copy-done.2, f32[8,3]{1,0:T(8,128)S(1)} %pad_maximum_fusion.facts), custom_call_target="tpu_custom_call" | custom-call | flops 1 | bytes 1 | tf_op jit(solution)/shard_map/patch_weights/pallas_call | solution.py:362
  44.5 6.5 %warp_filter.2 = (bf16[128,2048]{1,0:T(8,128)(2,1)S(1)}, bf16[128,2048]{1,0:T(8,128)(2,1)S(1)}, bf16[128,2048]{1,0:T(8,128)(2,1)S(1)}, bf16[128,2048]{1,0:T(8,128)(2,1)S(1)}) custom-call(f32[1]{0:T(128)} %convert_element_type.27.weight, s32[3]{0:T(128)S(1)} %pad_add_fusion.1.place, f32[512,4096]{1,0:T(8,128)S(1)} %bitcast.21, f32[512,4096]{1,0:T(8,128)S(1)} %bitcast.22, ...), custom_call_target="tpu_custom_call" | custom-call | flops 1 | bytes 1 | tf_op jit(solution)/shard_map/warp_filter/pallas_call | solution.py:237
  51.0 0.8 copy-done.5
  51.8 1.3 %collective-permute-done.7.refs_2_ = bf16[128,2048]{1,0:T(8,128)(2,1)S(1)} collective-permute-done((bf16[128,2048]{1,0:T(8,128)(2,1)S(1)}, bf16[128,2048]{1,0:T(8,128)(2,1)S(1)}, u32[]{:S(2)}, u32[]{:S(2)}) %collective-permute-start.7) | collective-permute-done | bytes 524320 | tf_op jit(solution)/shard_map/ppermute | solution.py:409
  53.1 1.5 %join_blocks.2.mine = bf16[512,2048]{1,0:T(8,128)(2,1)} custom-call(bf16[128,2048]{1,0:T(8,128)(2,1)S(1)} %get-tuple-element.38.refs_0_, bf16[128,2048]{1,0:T(8,128)(2,1)S(1)} %collective-permute-done.6.refs_1_, bf16[128,2048]{1,0:T(8,128)(2,1)S(1)} %collective-permute-done.7.refs_2_, bf16[128,2048]{1,0:T(8,128)(2,1)S(1)} %collective-permute-done.8.refs_3_), custom_call_target="tpu_custom_call" | custom-call | flops 1 | bytes 1 | tf_op jit(solution)/shard_map/join_blocks/pallas_call | solution.py:270
  54.5 0.5 collective-permute-start
  55.2 0.1 reshape.17
  55.3 3.8 %collective-permute-done = s32[1]{0:T(128)} collective-permute-done((s32[1]{0:T(128)}, s32[1]{0:T(128)}, u32[]{:S(2)}, u32[]{:S(2)}) %collective-permute-start) | collective-permute-done | bytes 36 | tf_op jit(solution)/shard_map/ppermute | solution.py:409
  59.0 0.6 fusion.2
  59.7 3.2 %pair_sum.2 = (bf16[160,1024]{1,0:T(8,128)(2,1)S(1)}, bf16[160,1024]{1,0:T(8,128)(2,1)S(1)}, bf16[160,1024]{1,0:T(8,128)(2,1)S(1)}, bf16[160,1024]{1,0:T(8,128)(2,1)S(1)}) custom-call(s32[3]{0:T(128)S(1)} %pad_add_fusion.1.place, s32[240]{0:T(256)S(1)} %pad_add_fusion.table, bf16[512,2048]{1,0:T(8,128)(2,1)} %join_blocks.2.mine, ...), custom_call_target="tpu_custom_call" | custom-call | flops 1 | bytes 1 | tf_op jit(solution)/shard_map/pair_sum/pallas_call | solution.py:322
  62.9 1.6 %collective-permute-start.14 = (bf16[160,1024]{1,0:T(8,128)(2,1)S(1)}, bf16[160,1024]{1,0:T(8,128)(2,1)S(1)}, u32[]{:S(2)}, u32[]{:S(2)}) collective-permute-start(bf16[160,1024]{1,0:T(8,128)(2,1)S(1)} %get-tuple-element.51), channel_id=1, source_target_pairs={{0,2},{2,0},{4,6},{6,4},{1,3},{3,1},{5,7},{7,5},{8,10},{10,8},{12,... | collective-permute-start | bytes 983048 | tf_op jit(solution)/shard_map/ppermute | solution.py:409
  64.5 1.7 %collective-permute-start.3 = (bf16[128,2048]{1,0:T(8,128)(2,1)S(1)}, bf16[128,2048]{1,0:T(8,128)(2,1)S(1)}, u32[]{:S(2)}, u32[]{:S(2)}) collective-permute-start(bf16[128,2048]{1,0:T(8,128)(2,1)S(1)} %copy-done.6), channel_id=1, source_target_pairs={{0,8},{8,0},{16,24},{24,16},{1,9},{9,1},{17,25},{25,17},{2,10},{10... | collective-permute-start | bytes 1572872 | tf_op jit(solution)/shard_map/ppermute | solution.py:409
  66.2 0.3 collective-permute-start.4
  66.5 1.5 %collective-permute-start.5 = (bf16[128,2048]{1,0:T(8,128)(2,1)S(1)}, bf16[128,2048]{1,0:T(8,128)(2,1)S(1)}, u32[]{:S(2)}, u32[]{:S(2)}) collective-permute-start(bf16[128,2048]{1,0:T(8,128)(2,1)S(1)} %get-tuple-element.37), channel_id=1, source_target_pairs={{0,24},{8,16},{16,8},{24,0},{1,25},{9,17},{17,9},{25,1},{2,26},{10... | collective-permute-start | bytes 1572872 | tf_op jit(solution)/shard_map/ppermute | solution.py:409
  68.0 0.4 collective-permute-start.13
  68.5 5.0 %collective-permute-done.14 = bf16[160,1024]{1,0:T(8,128)(2,1)S(1)} collective-permute-done((bf16[160,1024]{1,0:T(8,128)(2,1)S(1)}, bf16[160,1024]{1,0:T(8,128)(2,1)S(1)}, u32[]{:S(2)}, u32[]{:S(2)}) %collective-permute-start.14) | collective-permute-done | bytes 327712 | tf_op jit(solution)/shard_map/ppermute | solution.py:409
  73.5 0.1 add_convert_fusion.1
  73.6 2.7 %collective-permute-start.15 = (bf16[160,1024]{1,0:T(8,128)(2,1)S(1)}, bf16[160,1024]{1,0:T(8,128)(2,1)S(1)}, u32[]{:S(2)}, u32[]{:S(2)}) collective-permute-start(bf16[160,1024]{1,0:T(8,128)(2,1)S(1)} %add_convert_fusion.1), channel_id=1, source_target_pairs={{0,4},{2,6},{4,0},{6,2},{1,5},{3,7},{5,1},{7,3},{8,12},{10,14},{12... | collective-permute-start | bytes 983048 | tf_op jit(solution)/shard_map/ppermute | solution.py:409
  76.3 3.1 %collective-permute-done.3.refs_1_ = bf16[128,2048]{1,0:T(8,128)(2,1)S(1)} collective-permute-done((bf16[128,2048]{1,0:T(8,128)(2,1)S(1)}, bf16[128,2048]{1,0:T(8,128)(2,1)S(1)}, u32[]{:S(2)}, u32[]{:S(2)}) %collective-permute-start.3) | collective-permute-done | bytes 524320 | tf_op jit(solution)/shard_map/ppermute | solution.py:409
  79.3 11.5 %collective-permute-done.4.refs_2_ = bf16[128,2048]{1,0:T(8,128)(2,1)S(1)} collective-permute-done((bf16[128,2048]{1,0:T(8,128)(2,1)S(1)}, bf16[128,2048]{1,0:T(8,128)(2,1)S(1)}, u32[]{:S(2)}, u32[]{:S(2)}) %collective-permute-start.4) | collective-permute-done | bytes 524320 | tf_op jit(solution)/shard_map/ppermute | solution.py:409
  90.9 0.1 join_blocks.3.mine
  91.1 4.1 %collective-permute-done.16.other = bf16[512,2048]{1,0:T(8,128)(2,1)S(1)} collective-permute-done((bf16[512,2048]{1,0:T(8,128)(2,1)S(1)}, bf16[512,2048]{1,0:T(8,128)(2,1)S(1)}, u32[]{:S(2)}, u32[]{:S(2)}) %collective-permute-start.16) | collective-permute-done | bytes 2097184 | tf_op jit(solution)/shard_map/ppermute | solution.py:409
  95.2 1.4 %pair_sum.3 = (bf16[160,1024]{1,0:T(8,128)(2,1)S(1)}, bf16[160,1024]{1,0:T(8,128)(2,1)S(1)}, bf16[160,1024]{1,0:T(8,128)(2,1)S(1)}, bf16[160,1024]{1,0:T(8,128)(2,1)S(1)}) custom-call(s32[3]{0:T(128)S(1)} %pad_add_fusion.1.place, s32[240]{0:T(256)S(1)} %pad_add_fusion.table, bf16[512,2048]{1,0:T(8,128)(2,1)S(1)} %join_blocks.3.mine, ...), custom_call_target="tpu_custom_call" | custom-call | flops 1 | bytes 1 | tf_op jit(solution)/shard_map/pair_sum/pallas_call | solution.py:322
  96.7 0.5 collective-permute-start.18
  97.2 1.6 %collective-permute-start.17 = (bf16[160,1024]{1,0:T(8,128)(2,1)S(1)}, bf16[160,1024]{1,0:T(8,128)(2,1)S(1)}, u32[]{:S(2)}, u32[]{:S(2)}) collective-permute-start(bf16[160,1024]{1,0:T(8,128)(2,1)S(1)} %get-tuple-element.56), channel_id=1, source_target_pairs={{0,2},{2,0},{4,6},{6,4},{1,3},{3,1},{5,7},{7,5},{8,10},{10,8},{12,... | collective-permute-start | bytes 983048 | tf_op jit(solution)/shard_map/ppermute | solution.py:409
  98.8 8.5 %collective-permute-done.18 = bf16[160,1024]{1,0:T(8,128)(2,1)S(1)} collective-permute-done((bf16[160,1024]{1,0:T(8,128)(2,1)S(1)}, bf16[160,1024]{1,0:T(8,128)(2,1)S(1)}, u32[]{:S(2)}, u32[]{:S(2)}) %collective-permute-start.18) | collective-permute-done | bytes 327712 | tf_op jit(solution)/shard_map/ppermute | solution.py:409
  107.3 0.1 add_convert_fusion
  107.4 2.7 %collective-permute-start.19 = (bf16[160,1024]{1,0:T(8,128)(2,1)S(1)}, bf16[160,1024]{1,0:T(8,128)(2,1)S(1)}, u32[]{:S(2)}, u32[]{:S(2)}) collective-permute-start(bf16[160,1024]{1,0:T(8,128)(2,1)S(1)} %add_convert_fusion), channel_id=1, source_target_pairs={{0,4},{2,6},{4,0},{6,2},{1,5},{3,7},{5,1},{7,3},{8,12},{10,14},{12... | collective-permute-start | bytes 983048 | tf_op jit(solution)/shard_map/ppermute | solution.py:409
  110.0 1.0 patch_mean.2.refs_4_
  111.0 8.6 %collective-permute-done.17.refs_1_ = bf16[160,1024]{1,0:T(8,128)(2,1)S(1)} collective-permute-done((bf16[160,1024]{1,0:T(8,128)(2,1)S(1)}, bf16[160,1024]{1,0:T(8,128)(2,1)S(1)}, u32[]{:S(2)}, u32[]{:S(2)}) %collective-permute-start.17) | collective-permute-done | bytes 327712 | tf_op jit(solution)/shard_map/ppermute | solution.py:409
  119.6 3.9 %collective-permute-done.19.refs_2_ = bf16[160,1024]{1,0:T(8,128)(2,1)S(1)} collective-permute-done((bf16[160,1024]{1,0:T(8,128)(2,1)S(1)}, bf16[160,1024]{1,0:T(8,128)(2,1)S(1)}, u32[]{:S(2)}, u32[]{:S(2)}) %collective-permute-start.19) | collective-permute-done | bytes 327712 | tf_op jit(solution)/shard_map/ppermute | solution.py:409
  123.5 1.0 patch_mean.3
  (30 shorter events, 0.8 us)
Async XLA Ops:
  1.1 11.3 %collective-permute-start.2 = (f32[16,4096]{1,0:T(8,128)S(1)}, f32[16,4096]{1,0:T(8,128)S(1)}, u32[]{:S(2)}, u32[]{:S(2)}) collective-permute-start(f32[16,4096]{1,0:T(8,128)S(1)} %get-tuple-element.61), channel_id=1, source_target_pairs={{8,16},{16,8},{9,17},{17,9},{10,18},{18,10},{11,19},{19,11},{12,20... | collective-permute-start | bytes 786440 | tf_op jit(solution)/shard_map/ppermute | solution.py:447
  1.8 17.3 %collective-permute-start.1 = (f32[16,4096]{1,0:T(8,128)S(1)}, f32[16,4096]{1,0:T(8,128)S(1)}, u32[]{:S(2)}, u32[]{:S(2)}) collective-permute-start(f32[16,4096]{1,0:T(8,128)S(1)} %get-tuple-element.62), channel_id=1, source_target_pairs={{0,8},{16,24},{8,0},{24,16},{1,9},{17,25},{9,1},{25,17},{2,10},{18... | collective-permute-start | bytes 786440 | tf_op jit(solution)/shard_map/ppermute | solution.py:446
  8.2 0.7 copy-start.3
  8.9 0.7 copy-start.4
  19.0 3.4 %copy-start = (f32[1,512,4096]{2,1,0:T(8,128)S(1)}, f32[1,512,4096]{2,1,0:T(8,128)}, u32[]{:S(2)}) copy-start(f32[1,512,4096]{2,1,0:T(8,128)} %param.7) | copy-start | bytes 25165828
  22.4 20.2 %copy-start.2 = (s32[160]{0:T(256)S(1)}, s32[160]{0:T(256)}, u32[]{:S(2)}) copy-start(s32[160]{0:T(256)} %sites.1) | copy-start | bytes 1924
  22.4 22.0 %copy-start.1 = (f32[1,512,4096]{2,1,0:T(8,128)S(1)}, f32[1,512,4096]{2,1,0:T(8,128)}, u32[]{:S(2)}) copy-start(f32[1,512,4096]{2,1,0:T(8,128)} %param.7) | copy-start | bytes 25165828
  28.9 22.9 %collective-permute-start.6 = (bf16[128,2048]{1,0:T(8,128)(2,1)S(1)}, bf16[128,2048]{1,0:T(8,128)(2,1)S(1)}, u32[]{:S(2)}, u32[]{:S(2)}) collective-permute-start(bf16[128,2048]{1,0:T(8,128)(2,1)S(1)} %get-tuple-element.39), channel_id=1, source_target_pairs={{0,8},{8,0},{16,24},{24,16},{1,9},{9,1},{17,25},{25,17},{2,10},{10... | collective-permute-start | bytes 1572872 | tf_op jit(solution)/shard_map/ppermute | solution.py:409
  29.0 24.1 %collective-permute-start.7 = (bf16[128,2048]{1,0:T(8,128)(2,1)S(1)}, bf16[128,2048]{1,0:T(8,128)(2,1)S(1)}, u32[]{:S(2)}, u32[]{:S(2)}) collective-permute-start(bf16[128,2048]{1,0:T(8,128)(2,1)S(1)} %get-tuple-element.40), channel_id=1, source_target_pairs={{0,16},{8,24},{16,0},{24,8},{1,17},{9,25},{17,1},{25,9},{2,18},{10... | collective-permute-start | bytes 1572872 | tf_op jit(solution)/shard_map/ppermute | solution.py:409
  30.9 22.1 %collective-permute-start.8 = (bf16[128,2048]{1,0:T(8,128)(2,1)S(1)}, bf16[128,2048]{1,0:T(8,128)(2,1)S(1)}, u32[]{:S(2)}, u32[]{:S(2)}) collective-permute-start(bf16[128,2048]{1,0:T(8,128)(2,1)S(1)} %get-tuple-element.41), channel_id=1, source_target_pairs={{0,24},{8,16},{16,8},{24,0},{1,25},{9,17},{17,9},{25,1},{2,26},{10... | collective-permute-start | bytes 1572872 | tf_op jit(solution)/shard_map/ppermute | solution.py:409
  33.2 1.1 collective-permute-start.9
  34.4 3.6 %collective-permute-start.10 = (f32[2,3]{1,0:T(2,128)S(1)}, f32[2,3]{1,0:T(2,128)S(1)}, u32[]{:S(2)}, u32[]{:S(2)}) collective-permute-start(f32[2,3]{1,0:T(2,128)S(1)} %pad_maximum_fusion.2), channel_id=1, source_target_pairs={{0,2},{2,0},{4,6},{6,4},{1,3},{3,1},{5,7},{7,5},{8,10},{10,8},{12,... | collective-permute-start | bytes 80 | tf_op jit(solution)/shard_map/ppermute | solution.py:409
  38.0 4.5 %collective-permute-start.11 = (f32[4,3]{1,0:T(4,128)S(1)}, f32[4,3]{1,0:T(4,128)S(1)}, u32[]{:S(2)}, u32[]{:S(2)}) collective-permute-start(f32[4,3]{1,0:T(4,128)S(1)} %pad_maximum_fusion.1), channel_id=1, source_target_pairs={{0,4},{2,6},{4,0},{6,2},{1,5},{3,7},{5,1},{7,3},{8,12},{10,14},{12... | collective-permute-start | bytes 152 | tf_op jit(solution)/shard_map/ppermute | solution.py:409
  51.0 0.8 copy-start.5
  54.5 5.2 %collective-permute-start.12 = (bf16[512,2048]{1,0:T(8,128)(2,1)}, bf16[512,2048]{1,0:T(8,128)(2,1)}, u32[]{:S(2)}, u32[]{:S(2)}) collective-permute-start(bf16[512,2048]{1,0:T(8,128)(2,1)} %join_blocks.2.mine), channel_id=1, source_target_pairs={{0,1},{1,0},{2,3},{3,2},{4,5},{5,4},{6,7},{7,6},{8,9},{9,8},{10,11... | collective-permute-start | bytes 6291464 | tf_op jit(solution)/shard_map/ppermute | solution.py:409
  54.5 4.5 %collective-permute-start = (s32[1]{0:T(128)}, s32[1]{0:T(128)}, u32[]{:S(2)}, u32[]{:S(2)}) collective-permute-start(s32[1]{0:T(128)} %param.11), channel_id=1, source_target_pairs={{0,1},{1,0},{2,3},{3,2},{4,5},{5,4},{6,7},{7,6},{8,9},{9,8},{10,11... | collective-permute-start | bytes 20 | tf_op jit(solution)/shard_map/ppermute | solution.py:409
  59.7 4.8 %copy-start.6 = (bf16[128,2048]{1,0:T(8,128)(2,1)S(1)}, bf16[128,2048]{1,0:T(8,128)(2,1)}, u32[]{:S(2)}) copy-start(bf16[128,2048]{1,0:T(8,128)(2,1)} %copy-done.5) | copy-start | bytes 1572868
  62.9 10.6 %collective-permute-start.14 = (bf16[160,1024]{1,0:T(8,128)(2,1)S(1)}, bf16[160,1024]{1,0:T(8,128)(2,1)S(1)}, u32[]{:S(2)}, u32[]{:S(2)}) collective-permute-start(bf16[160,1024]{1,0:T(8,128)(2,1)S(1)} %get-tuple-element.51), channel_id=1, source_target_pairs={{0,2},{2,0},{4,6},{6,4},{1,3},{3,1},{5,7},{7,5},{8,10},{10,8},{12,... | collective-permute-start | bytes 983048 | tf_op jit(solution)/shard_map/ppermute | solution.py:409
  64.5 14.8 %collective-permute-start.3 = (bf16[128,2048]{1,0:T(8,128)(2,1)S(1)}, bf16[128,2048]{1,0:T(8,128)(2,1)S(1)}, u32[]{:S(2)}, u32[]{:S(2)}) collective-permute-start(bf16[128,2048]{1,0:T(8,128)(2,1)S(1)} %copy-done.6), channel_id=1, source_target_pairs={{0,8},{8,0},{16,24},{24,16},{1,9},{9,1},{17,25},{25,17},{2,10},{10... | collective-permute-start | bytes 1572872 | tf_op jit(solution)/shard_map/ppermute | solution.py:409
  66.2 24.6 %collective-permute-start.4 = (bf16[128,2048]{1,0:T(8,128)(2,1)S(1)}, bf16[128,2048]{1,0:T(8,128)(2,1)S(1)}, u32[]{:S(2)}, u32[]{:S(2)}) collective-permute-start(bf16[128,2048]{1,0:T(8,128)(2,1)S(1)} %get-tuple-element.36), channel_id=1, source_target_pairs={{0,16},{8,24},{16,0},{24,8},{1,17},{9,25},{17,1},{25,9},{2,18},{10... | collective-permute-start | bytes 1572872 | tf_op jit(solution)/shard_map/ppermute | solution.py:409
  66.5 24.3 %collective-permute-start.5 = (bf16[128,2048]{1,0:T(8,128)(2,1)S(1)}, bf16[128,2048]{1,0:T(8,128)(2,1)S(1)}, u32[]{:S(2)}, u32[]{:S(2)}) collective-permute-start(bf16[128,2048]{1,0:T(8,128)(2,1)S(1)} %get-tuple-element.37), channel_id=1, source_target_pairs={{0,24},{8,16},{16,8},{24,0},{1,25},{9,17},{17,9},{25,1},{2,26},{10... | collective-permute-start | bytes 1572872 | tf_op jit(solution)/shard_map/ppermute | solution.py:409
  68.0 22.8 %collective-permute-start.13 = (bf16[160,1024]{1,0:T(8,128)(2,1)S(1)}, bf16[160,1024]{1,0:T(8,128)(2,1)S(1)}, u32[]{:S(2)}, u32[]{:S(2)}) collective-permute-start(bf16[160,1024]{1,0:T(8,128)(2,1)S(1)} %get-tuple-element.49), channel_id=1, source_target_pairs={{0,2},{2,0},{4,6},{6,4},{1,3},{3,1},{5,7},{7,5},{8,10},{10,8},{12,... | collective-permute-start | bytes 983048 | tf_op jit(solution)/shard_map/ppermute | solution.py:409
  73.6 17.2 %collective-permute-start.15 = (bf16[160,1024]{1,0:T(8,128)(2,1)S(1)}, bf16[160,1024]{1,0:T(8,128)(2,1)S(1)}, u32[]{:S(2)}, u32[]{:S(2)}) collective-permute-start(bf16[160,1024]{1,0:T(8,128)(2,1)S(1)} %add_convert_fusion.1), channel_id=1, source_target_pairs={{0,4},{2,6},{4,0},{6,2},{1,5},{3,7},{5,1},{7,3},{8,12},{10,14},{12... | collective-permute-start | bytes 983048 | tf_op jit(solution)/shard_map/ppermute | solution.py:409
  91.0 4.2 %collective-permute-start.16 = (bf16[512,2048]{1,0:T(8,128)(2,1)S(1)}, bf16[512,2048]{1,0:T(8,128)(2,1)S(1)}, u32[]{:S(2)}, u32[]{:S(2)}) collective-permute-start(bf16[512,2048]{1,0:T(8,128)(2,1)S(1)} %join_blocks.3.mine), channel_id=1, source_target_pairs={{0,1},{1,0},{2,3},{3,2},{4,5},{5,4},{6,7},{7,6},{8,9},{9,8},{10,11... | collective-permute-start | bytes 6291464 | tf_op jit(solution)/shard_map/ppermute | solution.py:409
  96.7 10.6 %collective-permute-start.18 = (bf16[160,1024]{1,0:T(8,128)(2,1)S(1)}, bf16[160,1024]{1,0:T(8,128)(2,1)S(1)}, u32[]{:S(2)}, u32[]{:S(2)}) collective-permute-start(bf16[160,1024]{1,0:T(8,128)(2,1)S(1)} %get-tuple-element.58), channel_id=1, source_target_pairs={{0,2},{2,0},{4,6},{6,4},{1,3},{3,1},{5,7},{7,5},{8,10},{10,8},{12,... | collective-permute-start | bytes 983048 | tf_op jit(solution)/shard_map/ppermute | solution.py:409
  97.2 22.5 %collective-permute-start.17 = (bf16[160,1024]{1,0:T(8,128)(2,1)S(1)}, bf16[160,1024]{1,0:T(8,128)(2,1)S(1)}, u32[]{:S(2)}, u32[]{:S(2)}) collective-permute-start(bf16[160,1024]{1,0:T(8,128)(2,1)S(1)} %get-tuple-element.56), channel_id=1, source_target_pairs={{0,2},{2,0},{4,6},{6,4},{1,3},{3,1},{5,7},{7,5},{8,10},{10,8},{12,... | collective-permute-start | bytes 983048 | tf_op jit(solution)/shard_map/ppermute | solution.py:409
  107.4 16.2 %collective-permute-start.19 = (bf16[160,1024]{1,0:T(8,128)(2,1)S(1)}, bf16[160,1024]{1,0:T(8,128)(2,1)S(1)}, u32[]{:S(2)}, u32[]{:S(2)}) collective-permute-start(bf16[160,1024]{1,0:T(8,128)(2,1)S(1)} %add_convert_fusion), channel_id=1, source_target_pairs={{0,4},{2,6},{4,0},{6,2},{1,5},{3,7},{5,1},{7,3},{8,12},{10,14},{12... | collective-permute-start | bytes 983048 | tf_op jit(solution)/shard_map/ppermute | solution.py:409

commit v8 on v5

--- a/solution.py
+++ b/solution.py
@@ -162,7 +162,7 @@
     ):
         count = parts[0].shape[0]
         for part, column, outside in zip(parts, (0, SIDE, SIDE + chunk), (at_left, False, at_right)):
-            value = part[...]
+            value = part[...].astype(jnp.float32)
             if outside is not False:
                 value = jnp.where(outside, 0.0, value)
             high, low = split(value)
@@ -437,8 +437,8 @@
 
     forward = [(i, i + 1) for i in range(segments - 1)]
     backward = [(i + 1, i) for i in range(segments - 1)]
-    low = lax.ppermute(image[rows - HALO :], "seg", forward)
-    high = lax.ppermute(image[:HALO], "seg", backward)
+    low = lax.ppermute(image[rows - HALO :].astype(jnp.bfloat16), "seg", forward)
+    high = lax.ppermute(image[:HALO].astype(jnp.bfloat16), "seg", backward)
     rows_m, cols_m = build_matrices(place, psf_coef, phases, col_shift, rows, width, segments)
     weight = exposure_weight.astype(jnp.float32)
 

time: 120 us -> 117 us (0.975)
  waiting for transfers between devices: 60.8 us -> 56.1 us
  other arithmetic: 1.25 us -> 5.27 us
  local copies, waits for them, and re-layouts: 2.61 us -> 0.23 us
    ppermute x2, waiting for transfers between devices: 6.91 us -> 2.63 us  [the longest x1 2.62 us: per_device(): high = lax.ppermute(image[:HALO].astype(jnp.bfloat16), 'seg', backward)]
    another operation x0 -> x1, other arithmetic: none -> 4.02 us
    unnamed x10, local copies, waits for them, and re-layouts: 1.35 us -> 0.02 us
  transfers between devices with their start and end apart: 20 -> 20, of which waited for: 12 -> 13; matrix products, arithmetic and copies ran while one was open for 1% -> 1% of each run, Pallas kernels for 12% -> 12%
where the time goes in v8:
time: 117 us
  waiting for transfers between devices  56.1 us (48%)
  starting transfers between devices  28.8 us (25%)
  Pallas kernels  24.2 us (21%)
  other arithmetic  5.27 us (5%)
  between operations  2.17 us (2%)
    ppermute x18, waiting for transfers between devices, swapped(): return lax.ppermute(value, axis, [(i, i ^ distance) for i in range(count)])  53.4 us
    ppermute x18, starting transfers between devices, swapped(): return lax.ppermute(value, axis, [(i, i ^ distance) for i in range(count)])  22.6 us
    pallas_call x2, Pallas kernels, filter_chunk(): pl.pallas_call(functools.partial(filter_kernel, first_chunk=start == 0, l...  14 us
    ppermute x1, starting transfers between devices, per_device(): low = lax.ppermute(image[rows - HALO:].astype(jnp.bfloat16), 'seg', forward)  4.85 us
    another operation x1, other arithmetic  4.02 us
    pallas_call x2, Pallas kernels, pair_sum(): pl.pallas_call(functools.partial(pair_kernel, slots=slots, distances=dist...  3.91 us
    ppermute x1, waiting for transfers between devices, per_device(): high = lax.ppermute(image[:HALO].astype(jnp.bfloat16), 'seg', backward)  2.62 us
  transfers between devices with their start and end apart: 20, of which 13 were waited for; matrix products, arithmetic and copies ran while one was open for 1% of the time, Pallas kernels for 12%

profile of v8, /device:TPU:0, one launch (start us, length us, event | category | flops | bytes accessed | tf_op | source)
XLA Modules:
  0.0 116.7 jit_solution(4676278004328781428)
XLA Ops:
  0.0 4.0 %convert.4 = bf16[1,512,4096]{2,1,0:T(8,128)(2,1)S(1)} convert(f32[1,512,4096]{2,1,0:T(8,128)} %param.7) | non-fusion elementwise | flops 2097152 | bytes 12582912 | tf_op jit(solution)/shard_map/convert.1
  4.1 4.8 %collective-permute-start.1 = (bf16[16,4096]{1,0:T(8,128)(2,1)S(1)}, bf16[16,4096]{1,0:T(8,128)(2,1)S(1)}, u32[]{:S(2)}, u32[]{:S(2)}) collective-permute-start(bf16[16,4096]{1,0:T(8,128)(2,1)S(1)} %get-tuple-element.68), channel_id=1, source_target_pairs={{0,8},{8,16},{16,24},{1,9},{9,17},{17,25},{2,10},{10,18},{18,26},{... | collective-permute-start | bytes 393224 | tf_op jit(solution)/shard_map/ppermute | solution.py:440
  8.9 1.3 %collective-permute-start.2 = (bf16[16,4096]{1,0:T(8,128)(2,1)S(1)}, bf16[16,4096]{1,0:T(8,128)(2,1)S(1)}, u32[]{:S(2)}, u32[]{:S(2)}) collective-permute-start(bf16[16,4096]{1,0:T(8,128)(2,1)S(1)} %get-tuple-element.67), channel_id=1, source_target_pairs={{8,0},{16,8},{24,16},{9,1},{17,9},{25,17},{10,2},{18,10},{26,18},{... | collective-permute-start | bytes 393224 | tf_op jit(solution)/shard_map/ppermute | solution.py:441
  11.0 2.1 %band_matrices.1 = (bf16[3,128,480]{2,1,0:T(8,128)(2,1)S(1)}, bf16[3,2,512,256]{3,2,1,0:T(8,128)(2,1)S(1)}) custom-call(s32[3]{0:T(128)S(1)} %pad_add_fusion.1.place, f32[1,2,3]{2,1,0:T(2,128)S(1)} %copy-done.1, s32[1,2]{1,0:T(1,128)S(1)} %copy-done.2, s32[1]{0:T(128)S(6)} %copy.10.shift), custom_call_target="tpu_custom_call" | custom-call | flops 1 | bytes 1 | tf_op jit(solution)/shard_map/band_matrices/pallas_call | solution.py:132
  13.8 2.6 %collective-permute-done.2.high_l.high_c.high_r = bf16[16,4096]{1,0:T(8,128)(2,1)S(1)} collective-permute-done((bf16[16,4096]{1,0:T(8,128)(2,1)S(1)}, bf16[16,4096]{1,0:T(8,128)(2,1)S(1)}, u32[]{:S(2)}, u32[]{:S(2)}) %collective-permute-start.2) | collective-permute-done | bytes 131104 | tf_op jit(solution)/shard_map/ppermute | solution.py:441
  16.4 7.0 %warp_filter.3 = (bf16[128,2048]{1,0:T(8,128)(2,1)S(1)}, bf16[128,2048]{1,0:T(8,128)(2,1)S(1)}, bf16[128,2048]{1,0:T(8,128)(2,1)S(1)}, bf16[128,2048]{1,0:T(8,128)(2,1)S(1)}) custom-call(f32[1]{0:T(128)} %convert_element_type.35.weight, bf16[16,4096]{1,0:T(8,128)(2,1)S(1)} %collective-permute-done.1.low_l.low_c.low_r, ...), custom_call_target="tpu_custom_call" | custom-call | flops 1 | bytes 1 | tf_op jit(solution)/shard_map/warp_filter/pallas_call | solution.py:236
  23.4 1.1 collective-permute-start.10
  24.5 2.2 %collective-permute-start.11 = (bf16[128,2048]{1,0:T(8,128)(2,1)S(1)}, bf16[128,2048]{1,0:T(8,128)(2,1)S(1)}, u32[]{:S(2)}, u32[]{:S(2)}) collective-permute-start(bf16[128,2048]{1,0:T(8,128)(2,1)S(1)} %get-tuple-element.47), channel_id=1, source_target_pairs={{0,24},{8,16},{16,8},{24,0},{1,25},{9,17},{17,9},{25,1},{2,26},{10... | collective-permute-start | bytes 1572872 | tf_op jit(solution)/shard_map/ppermute | solution.py:407
  26.7 0.3 collective-permute-start.9
  27.7 1.1 collective-permute-done.6
  28.9 1.6 %collective-permute-start.7 = (f32[2,3]{1,0:T(2,128)S(1)}, f32[2,3]{1,0:T(2,128)S(1)}, u32[]{:S(2)}, u32[]{:S(2)}) collective-permute-start(f32[2,3]{1,0:T(2,128)S(1)} %pad_maximum_fusion.2), channel_id=1, source_target_pairs={{0,2},{2,0},{4,6},{6,4},{1,3},{3,1},{5,7},{7,5},{8,10},{10,8},{12,... | collective-permute-start | bytes 80 | tf_op jit(solution)/shard_map/ppermute | solution.py:407
  30.5 2.0 %collective-permute-done.7 = f32[2,3]{1,0:T(2,128)S(1)} collective-permute-done((f32[2,3]{1,0:T(2,128)S(1)}, f32[2,3]{1,0:T(2,128)S(1)}, u32[]{:S(2)}, u32[]{:S(2)}) %collective-permute-start.7) | collective-permute-done | bytes 56 | tf_op jit(solution)/shard_map/ppermute | solution.py:407
  32.5 0.1 pad_maximum_fusion.1
  32.6 7.0 %warp_filter.2 = (bf16[128,2048]{1,0:T(8,128)(2,1)S(1)}, bf16[128,2048]{1,0:T(8,128)(2,1)S(1)}, bf16[128,2048]{1,0:T(8,128)(2,1)S(1)}, bf16[128,2048]{1,0:T(8,128)(2,1)S(1)}) custom-call(f32[1]{0:T(128)} %convert_element_type.35.weight, bf16[16,4096]{1,0:T(8,128)(2,1)S(1)} %collective-permute-done.1.low_l.low_c.low_r, ...), custom_call_target="tpu_custom_call" | custom-call | flops 1 | bytes 1 | tf_op jit(solution)/shard_map/warp_filter/pallas_call | solution.py:236
  39.6 8.2 %collective-permute-done.10.refs_2_ = bf16[128,2048]{1,0:T(8,128)(2,1)S(1)} collective-permute-done((bf16[128,2048]{1,0:T(8,128)(2,1)S(1)}, bf16[128,2048]{1,0:T(8,128)(2,1)S(1)}, u32[]{:S(2)}, u32[]{:S(2)}) %collective-permute-start.10) | collective-permute-done | bytes 524320 | tf_op jit(solution)/shard_map/ppermute | solution.py:407
  47.8 1.2 %collective-permute-done.9.refs_1_ = bf16[128,2048]{1,0:T(8,128)(2,1)S(1)} collective-permute-done((bf16[128,2048]{1,0:T(8,128)(2,1)S(1)}, bf16[128,2048]{1,0:T(8,128)(2,1)S(1)}, u32[]{:S(2)}, u32[]{:S(2)}) %collective-permute-start.9) | collective-permute-done | bytes 524320 | tf_op jit(solution)/shard_map/ppermute | solution.py:407
  49.1 0.1 join_blocks.2.mine
  49.3 0.5 collective-permute-start
  49.8 0.1 reshape.14
  49.9 0.1 reshape.15
  50.0 1.0 collective-permute-start.3
  51.0 0.7 collective-permute-start.4
  51.7 1.9 %collective-permute-start.5 = (bf16[128,2048]{1,0:T(8,128)(2,1)S(1)}, bf16[128,2048]{1,0:T(8,128)(2,1)S(1)}, u32[]{:S(2)}, u32[]{:S(2)}) collective-permute-start(bf16[128,2048]{1,0:T(8,128)(2,1)S(1)} %get-tuple-element.40), channel_id=1, source_target_pairs={{0,24},{8,16},{16,8},{24,0},{1,25},{9,17},{17,9},{25,1},{2,26},{10... | collective-permute-start | bytes 1572872 | tf_op jit(solution)/shard_map/ppermute | solution.py:407
  53.6 0.6 fusion.2
  54.2 2.5 %pair_sum.2 = (bf16[160,1024]{1,0:T(8,128)(2,1)S(1)}, bf16[160,1024]{1,0:T(8,128)(2,1)S(1)}, bf16[160,1024]{1,0:T(8,128)(2,1)S(1)}, bf16[160,1024]{1,0:T(8,128)(2,1)S(1)}) custom-call(s32[3]{0:T(128)S(1)} %pad_add_fusion.1.place, s32[240]{0:T(256)S(1)} %pad_add_fusion.table, bf16[512,2048]{1,0:T(8,128)(2,1)S(1)} %join_blocks.2.mine, ...), custom_call_target="tpu_custom_call" | custom-call | flops 1 | bytes 1 | tf_op jit(solution)/shard_map/pair_sum/pallas_call | solution.py:320
  56.7 1.6 %collective-permute-start.13 = (bf16[160,1024]{1,0:T(8,128)(2,1)S(1)}, bf16[160,1024]{1,0:T(8,128)(2,1)S(1)}, u32[]{:S(2)}, u32[]{:S(2)}) collective-permute-start(bf16[160,1024]{1,0:T(8,128)(2,1)S(1)} %get-tuple-element.55), channel_id=1, source_target_pairs={{0,2},{2,0},{4,6},{6,4},{1,3},{3,1},{5,7},{7,5},{8,10},{10,8},{12,... | collective-permute-start | bytes 983048 | tf_op jit(solution)/shard_map/ppermute | solution.py:407
  58.4 2.6 %collective-permute-start.8 = (f32[4,3]{1,0:T(4,128)S(1)}, f32[4,3]{1,0:T(4,128)S(1)}, u32[]{:S(2)}, u32[]{:S(2)}) collective-permute-start(f32[4,3]{1,0:T(4,128)S(1)} %pad_maximum_fusion.1), channel_id=1, source_target_pairs={{0,4},{2,6},{4,0},{6,2},{1,5},{3,7},{5,1},{7,3},{8,12},{10,14},{12... | collective-permute-start | bytes 152 | tf_op jit(solution)/shard_map/ppermute | solution.py:407
  61.0 4.7 %collective-permute-done.8 = f32[4,3]{1,0:T(4,128)S(1)} collective-permute-done((f32[4,3]{1,0:T(4,128)S(1)}, f32[4,3]{1,0:T(4,128)S(1)}, u32[]{:S(2)}, u32[]{:S(2)}) %collective-permute-start.8) | collective-permute-done | bytes 80 | tf_op jit(solution)/shard_map/ppermute | solution.py:407
  65.6 3.5 %collective-permute-start.14 = (bf16[160,1024]{1,0:T(8,128)(2,1)S(1)}, bf16[160,1024]{1,0:T(8,128)(2,1)S(1)}, u32[]{:S(2)}, u32[]{:S(2)}) collective-permute-start(bf16[160,1024]{1,0:T(8,128)(2,1)S(1)} %get-tuple-element.57), channel_id=1, source_target_pairs={{0,2},{2,0},{4,6},{6,4},{1,3},{3,1},{5,7},{7,5},{8,10},{10,8},{12,... | collective-permute-start | bytes 983048 | tf_op jit(solution)/shard_map/ppermute | solution.py:407
  69.1 0.1 pad_maximum_fusion.facts
  69.2 1.8 %patch_weights.1.refs_3_ = f32[160,2048]{1,0:T(8,128)S(1)} custom-call(s32[3]{0:T(128)S(1)} %pad_add_fusion.1.place, s32[160]{0:T(256)S(1)} %copy-done, f32[8,3]{1,0:T(8,128)S(1)} %pad_maximum_fusion.facts), custom_call_target="tpu_custom_call" | custom-call | flops 1 | bytes 1 | tf_op jit(solution)/shard_map/patch_weights/pallas_call | solution.py:360
  71.1 5.0 %collective-permute-done.4.refs_2_ = bf16[128,2048]{1,0:T(8,128)(2,1)S(1)} collective-permute-done((bf16[128,2048]{1,0:T(8,128)(2,1)}, bf16[128,2048]{1,0:T(8,128)(2,1)S(1)}, u32[]{:S(2)}, u32[]{:S(2)}) %collective-permute-start.4) | collective-permute-done | bytes 524320 | tf_op jit(solution)/shard_map/ppermute | solution.py:407
  76.1 0.1 add_convert_fusion.1
  76.2 0.1 collective-permute-done.14.refs_1_
  76.3 0.1 join_blocks.3.mine
  76.5 4.1 %collective-permute-done.15.other = bf16[512,2048]{1,0:T(8,128)(2,1)S(1)} collective-permute-done((bf16[512,2048]{1,0:T(8,128)(2,1)S(1)}, bf16[512,2048]{1,0:T(8,128)(2,1)S(1)}, u32[]{:S(2)}, u32[]{:S(2)}) %collective-permute-start.15) | collective-permute-done | bytes 2097184 | tf_op jit(solution)/shard_map/ppermute | solution.py:407
  80.6 1.4 %pair_sum.3 = (bf16[160,1024]{1,0:T(8,128)(2,1)S(1)}, bf16[160,1024]{1,0:T(8,128)(2,1)S(1)}, bf16[160,1024]{1,0:T(8,128)(2,1)S(1)}, bf16[160,1024]{1,0:T(8,128)(2,1)S(1)}) custom-call(s32[3]{0:T(128)S(1)} %pad_add_fusion.1.place, s32[240]{0:T(256)S(1)} %pad_add_fusion.table, bf16[512,2048]{1,0:T(8,128)(2,1)S(1)} %join_blocks.3.mine, ...), custom_call_target="tpu_custom_call" | custom-call | flops 1 | bytes 1 | tf_op jit(solution)/shard_map/pair_sum/pallas_call | solution.py:320
  82.1 1.8 %collective-permute-start.17 = (bf16[160,1024]{1,0:T(8,128)(2,1)S(1)}, bf16[160,1024]{1,0:T(8,128)(2,1)S(1)}, u32[]{:S(2)}, u32[]{:S(2)}) collective-permute-start(bf16[160,1024]{1,0:T(8,128)(2,1)S(1)} %get-tuple-element.64), channel_id=1, source_target_pairs={{0,2},{2,0},{4,6},{6,4},{1,3},{3,1},{5,7},{7,5},{8,10},{10,8},{12,... | collective-permute-start | bytes 983048 | tf_op jit(solution)/shard_map/ppermute | solution.py:407
  83.9 2.3 %collective-permute-start.19 = (bf16[160,1024]{1,0:T(8,128)(2,1)S(1)}, bf16[160,1024]{1,0:T(8,128)(2,1)S(1)}, u32[]{:S(2)}, u32[]{:S(2)}) collective-permute-start(bf16[160,1024]{1,0:T(8,128)(2,1)S(1)} %add_convert_fusion.1), channel_id=1, source_target_pairs={{0,4},{2,6},{4,0},{6,2},{1,5},{3,7},{5,1},{7,3},{8,12},{10,14},{12... | collective-permute-start | bytes 983048 | tf_op jit(solution)/shard_map/ppermute | solution.py:407
  86.2 0.4 collective-permute-start.16
  86.7 12.7 %collective-permute-done.17 = bf16[160,1024]{1,0:T(8,128)(2,1)S(1)} collective-permute-done((bf16[160,1024]{1,0:T(8,128)(2,1)S(1)}, bf16[160,1024]{1,0:T(8,128)(2,1)S(1)}, u32[]{:S(2)}, u32[]{:S(2)}) %collective-permute-start.17) | collective-permute-done | bytes 327712 | tf_op jit(solution)/shard_map/ppermute | solution.py:407
  99.4 0.1 add_convert_fusion
  99.5 1.0 collective-permute-start.18
  100.4 0.5 collective-permute-done.19.refs_2_
  100.9 1.0 patch_mean.2.refs_4_
  101.9 10.4 %collective-permute-done.16.refs_1_ = bf16[160,1024]{1,0:T(8,128)(2,1)S(1)} collective-permute-done((bf16[160,1024]{1,0:T(8,128)(2,1)S(1)}, bf16[160,1024]{1,0:T(8,128)(2,1)S(1)}, u32[]{:S(2)}, u32[]{:S(2)}) %collective-permute-start.16) | collective-permute-done | bytes 327712 | tf_op jit(solution)/shard_map/ppermute | solution.py:407
  112.3 3.4 %collective-permute-done.18.refs_2_ = bf16[160,1024]{1,0:T(8,128)(2,1)S(1)} collective-permute-done((bf16[160,1024]{1,0:T(8,128)(2,1)S(1)}, bf16[160,1024]{1,0:T(8,128)(2,1)S(1)}, u32[]{:S(2)}, u32[]{:S(2)}) %collective-permute-start.18) | collective-permute-done | bytes 327712 | tf_op jit(solution)/shard_map/ppermute | solution.py:407
  115.7 1.0 patch_mean.3
  (27 shorter events, 0.6 us)
Async XLA Ops:
  0.0 11.0 %copy-start.1 = (f32[1,2,3]{2,1,0:T(2,128)S(1)}, f32[1,2,3]{2,1,0:T(2,128)}, u32[]{:S(2)}) copy-start(f32[1,2,3]{2,1,0:T(2,128)} %coef.1) | copy-start | bytes 76
  0.0 11.0 %copy-start.2 = (s32[1,2]{1,0:T(1,128)S(1)}, s32[1,2]{1,0:T(1,128)}, u32[]{:S(2)}) copy-start(s32[1,2]{1,0:T(1,128)} %phases.1) | copy-start | bytes 28
  4.1 9.7 %collective-permute-start.1 = (bf16[16,4096]{1,0:T(8,128)(2,1)S(1)}, bf16[16,4096]{1,0:T(8,128)(2,1)S(1)}, u32[]{:S(2)}, u32[]{:S(2)}) collective-permute-start(bf16[16,4096]{1,0:T(8,128)(2,1)S(1)} %get-tuple-element.68), channel_id=1, source_target_pairs={{0,8},{8,16},{16,24},{1,9},{9,17},{17,25},{2,10},{10,18},{18,26},{... | collective-permute-start | bytes 393224 | tf_op jit(solution)/shard_map/ppermute | solution.py:440
  8.9 7.5 %collective-permute-start.2 = (bf16[16,4096]{1,0:T(8,128)(2,1)S(1)}, bf16[16,4096]{1,0:T(8,128)(2,1)S(1)}, u32[]{:S(2)}, u32[]{:S(2)}) collective-permute-start(bf16[16,4096]{1,0:T(8,128)(2,1)S(1)} %get-tuple-element.67), channel_id=1, source_target_pairs={{8,0},{16,8},{24,16},{9,1},{17,9},{25,17},{10,2},{18,10},{26,18},{... | collective-permute-start | bytes 393224 | tf_op jit(solution)/shard_map/ppermute | solution.py:441
  23.4 24.4 %collective-permute-start.10 = (bf16[128,2048]{1,0:T(8,128)(2,1)S(1)}, bf16[128,2048]{1,0:T(8,128)(2,1)S(1)}, u32[]{:S(2)}, u32[]{:S(2)}) collective-permute-start(bf16[128,2048]{1,0:T(8,128)(2,1)S(1)} %get-tuple-element.46), channel_id=1, source_target_pairs={{0,16},{8,24},{16,0},{24,8},{1,17},{9,25},{17,1},{25,9},{2,18},{10... | collective-permute-start | bytes 1572872 | tf_op jit(solution)/shard_map/ppermute | solution.py:407
  24.5 23.3 %collective-permute-start.11 = (bf16[128,2048]{1,0:T(8,128)(2,1)S(1)}, bf16[128,2048]{1,0:T(8,128)(2,1)S(1)}, u32[]{:S(2)}, u32[]{:S(2)}) collective-permute-start(bf16[128,2048]{1,0:T(8,128)(2,1)S(1)} %get-tuple-element.47), channel_id=1, source_target_pairs={{0,24},{8,16},{16,8},{24,0},{1,25},{9,17},{17,9},{25,1},{2,26},{10... | collective-permute-start | bytes 1572872 | tf_op jit(solution)/shard_map/ppermute | solution.py:407
  26.7 22.3 %collective-permute-start.9 = (bf16[128,2048]{1,0:T(8,128)(2,1)S(1)}, bf16[128,2048]{1,0:T(8,128)(2,1)S(1)}, u32[]{:S(2)}, u32[]{:S(2)}) collective-permute-start(bf16[128,2048]{1,0:T(8,128)(2,1)S(1)} %get-tuple-element.45), channel_id=1, source_target_pairs={{0,8},{8,0},{16,24},{24,16},{1,9},{9,1},{17,25},{25,17},{2,10},{10... | collective-permute-start | bytes 1572872 | tf_op jit(solution)/shard_map/ppermute | solution.py:407
  27.7 1.1 collective-permute-start.6
  28.9 3.6 %collective-permute-start.7 = (f32[2,3]{1,0:T(2,128)S(1)}, f32[2,3]{1,0:T(2,128)S(1)}, u32[]{:S(2)}, u32[]{:S(2)}) collective-permute-start(f32[2,3]{1,0:T(2,128)S(1)} %pad_maximum_fusion.2), channel_id=1, source_target_pairs={{0,2},{2,0},{4,6},{6,4},{1,3},{3,1},{5,7},{7,5},{8,10},{10,8},{12,... | collective-permute-start | bytes 80 | tf_op jit(solution)/shard_map/ppermute | solution.py:407
  39.6 9.6 %copy-start.3 = (bf16[128,2048]{1,0:T(8,128)(2,1)}, bf16[128,2048]{1,0:T(8,128)(2,1)S(1)}, u32[]{:S(2)}) copy-start(bf16[128,2048]{1,0:T(8,128)(2,1)S(1)} %get-tuple-element.39) | copy-start | bytes 1572868
  39.6 9.6 %copy-start.4 = (bf16[128,2048]{1,0:T(8,128)(2,1)}, bf16[128,2048]{1,0:T(8,128)(2,1)S(1)}, u32[]{:S(2)}) copy-start(bf16[128,2048]{1,0:T(8,128)(2,1)S(1)} %get-tuple-element.38) | copy-start | bytes 1572868
  49.1 0.7 copy-start
  49.2 5.0 %collective-permute-start.12 = (bf16[512,2048]{1,0:T(8,128)(2,1)S(1)}, bf16[512,2048]{1,0:T(8,128)(2,1)}, u32[]{:S(2)}, u32[]{:S(2)}) collective-permute-start(bf16[512,2048]{1,0:T(8,128)(2,1)S(1)} %join_blocks.2.mine), channel_id=1, source_target_pairs={{0,1},{1,0},{2,3},{3,2},{4,5},{5,4},{6,7},{7,6},{8,9},{9,8},{10,11... | collective-permute-start | bytes 6291464 | tf_op jit(solution)/shard_map/ppermute | solution.py:407
  49.3 4.3 %collective-permute-start = (s32[1]{0:T(128)}, s32[1]{0:T(128)}, u32[]{:S(2)}, u32[]{:S(2)}) collective-permute-start(s32[1]{0:T(128)} %param.11), channel_id=1, source_target_pairs={{0,1},{1,0},{2,3},{3,2},{4,5},{5,4},{6,7},{7,6},{8,9},{9,8},{10,11... | collective-permute-start | bytes 20 | tf_op jit(solution)/shard_map/ppermute | solution.py:407
  50.0 21.0 %collective-permute-start.3 = (bf16[128,2048]{1,0:T(8,128)(2,1)}, bf16[128,2048]{1,0:T(8,128)(2,1)S(1)}, u32[]{:S(2)}, u32[]{:S(2)}) collective-permute-start(bf16[128,2048]{1,0:T(8,128)(2,1)} %copy-done.4), channel_id=1, source_target_pairs={{0,8},{8,0},{16,24},{24,16},{1,9},{9,1},{17,25},{25,17},{2,10},{10... | collective-permute-start | bytes 1572872 | tf_op jit(solution)/shard_map/ppermute | solution.py:407
  51.0 25.1 %collective-permute-start.4 = (bf16[128,2048]{1,0:T(8,128)(2,1)}, bf16[128,2048]{1,0:T(8,128)(2,1)S(1)}, u32[]{:S(2)}, u32[]{:S(2)}) collective-permute-start(bf16[128,2048]{1,0:T(8,128)(2,1)} %copy-done.3), channel_id=1, source_target_pairs={{0,16},{8,24},{16,0},{24,8},{1,17},{9,25},{17,1},{25,9},{2,18},{10... | collective-permute-start | bytes 1572872 | tf_op jit(solution)/shard_map/ppermute | solution.py:407
  51.7 24.4 %collective-permute-start.5 = (bf16[128,2048]{1,0:T(8,128)(2,1)S(1)}, bf16[128,2048]{1,0:T(8,128)(2,1)S(1)}, u32[]{:S(2)}, u32[]{:S(2)}) collective-permute-start(bf16[128,2048]{1,0:T(8,128)(2,1)S(1)} %get-tuple-element.40), channel_id=1, source_target_pairs={{0,24},{8,16},{16,8},{24,0},{1,25},{9,17},{17,9},{25,1},{2,26},{10... | collective-permute-start | bytes 1572872 | tf_op jit(solution)/shard_map/ppermute | solution.py:407
  56.7 19.3 %collective-permute-start.13 = (bf16[160,1024]{1,0:T(8,128)(2,1)S(1)}, bf16[160,1024]{1,0:T(8,128)(2,1)S(1)}, u32[]{:S(2)}, u32[]{:S(2)}) collective-permute-start(bf16[160,1024]{1,0:T(8,128)(2,1)S(1)} %get-tuple-element.55), channel_id=1, source_target_pairs={{0,2},{2,0},{4,6},{6,4},{1,3},{3,1},{5,7},{7,5},{8,10},{10,8},{12,... | collective-permute-start | bytes 983048 | tf_op jit(solution)/shard_map/ppermute | solution.py:407
  58.4 7.3 %collective-permute-start.8 = (f32[4,3]{1,0:T(4,128)S(1)}, f32[4,3]{1,0:T(4,128)S(1)}, u32[]{:S(2)}, u32[]{:S(2)}) collective-permute-start(f32[4,3]{1,0:T(4,128)S(1)} %pad_maximum_fusion.1), channel_id=1, source_target_pairs={{0,4},{2,6},{4,0},{6,2},{1,5},{3,7},{5,1},{7,3},{8,12},{10,14},{12... | collective-permute-start | bytes 152 | tf_op jit(solution)/shard_map/ppermute | solution.py:407
  65.6 10.6 %collective-permute-start.14 = (bf16[160,1024]{1,0:T(8,128)(2,1)S(1)}, bf16[160,1024]{1,0:T(8,128)(2,1)S(1)}, u32[]{:S(2)}, u32[]{:S(2)}) collective-permute-start(bf16[160,1024]{1,0:T(8,128)(2,1)S(1)} %get-tuple-element.57), channel_id=1, source_target_pairs={{0,2},{2,0},{4,6},{6,4},{1,3},{3,1},{5,7},{7,5},{8,10},{10,8},{12,... | collective-permute-start | bytes 983048 | tf_op jit(solution)/shard_map/ppermute | solution.py:407
  76.4 4.2 %collective-permute-start.15 = (bf16[512,2048]{1,0:T(8,128)(2,1)S(1)}, bf16[512,2048]{1,0:T(8,128)(2,1)S(1)}, u32[]{:S(2)}, u32[]{:S(2)}) collective-permute-start(bf16[512,2048]{1,0:T(8,128)(2,1)S(1)} %join_blocks.3.mine), channel_id=1, source_target_pairs={{0,1},{1,0},{2,3},{3,2},{4,5},{5,4},{6,7},{7,6},{8,9},{9,8},{10,11... | collective-permute-start | bytes 6291464 | tf_op jit(solution)/shard_map/ppermute | solution.py:407
  82.1 17.3 %collective-permute-start.17 = (bf16[160,1024]{1,0:T(8,128)(2,1)S(1)}, bf16[160,1024]{1,0:T(8,128)(2,1)S(1)}, u32[]{:S(2)}, u32[]{:S(2)}) collective-permute-start(bf16[160,1024]{1,0:T(8,128)(2,1)S(1)} %get-tuple-element.64), channel_id=1, source_target_pairs={{0,2},{2,0},{4,6},{6,4},{1,3},{3,1},{5,7},{7,5},{8,10},{10,8},{12,... | collective-permute-start | bytes 983048 | tf_op jit(solution)/shard_map/ppermute | solution.py:407
  83.9 17.0 %collective-permute-start.19 = (bf16[160,1024]{1,0:T(8,128)(2,1)S(1)}, bf16[160,1024]{1,0:T(8,128)(2,1)S(1)}, u32[]{:S(2)}, u32[]{:S(2)}) collective-permute-start(bf16[160,1024]{1,0:T(8,128)(2,1)S(1)} %add_convert_fusion.1), channel_id=1, source_target_pairs={{0,4},{2,6},{4,0},{6,2},{1,5},{3,7},{5,1},{7,3},{8,12},{10,14},{12... | collective-permute-start | bytes 983048 | tf_op jit(solution)/shard_map/ppermute | solution.py:407
  86.2 26.1 %collective-permute-start.16 = (bf16[160,1024]{1,0:T(8,128)(2,1)S(1)}, bf16[160,1024]{1,0:T(8,128)(2,1)S(1)}, u32[]{:S(2)}, u32[]{:S(2)}) collective-permute-start(bf16[160,1024]{1,0:T(8,128)(2,1)S(1)} %get-tuple-element.62), channel_id=1, source_target_pairs={{0,2},{2,0},{4,6},{6,4},{1,3},{3,1},{5,7},{7,5},{8,10},{10,8},{12,... | collective-permute-start | bytes 983048 | tf_op jit(solution)/shard_map/ppermute | solution.py:407
  99.5 16.2 %collective-permute-start.18 = (bf16[160,1024]{1,0:T(8,128)(2,1)S(1)}, bf16[160,1024]{1,0:T(8,128)(2,1)S(1)}, u32[]{:S(2)}, u32[]{:S(2)}) collective-permute-start(bf16[160,1024]{1,0:T(8,128)(2,1)S(1)} %add_convert_fusion), channel_id=1, source_target_pairs={{0,4},{2,6},{4,0},{6,2},{1,5},{3,7},{5,1},{7,3},{8,12},{10,14},{12... | collective-permute-start | bytes 983048 | tf_op jit(solution)/shard_map/ppermute | solution.py:407

commit v9 on v8

--- a/solution.py
+++ b/solution.py
@@ -141,6 +141,26 @@
         cost_estimate=COST,
         name="band_matrices",
     )(place, coef, phases, shift)
+
+
+def edge_kernel(first, last, top, bottom):
+    top[...] = first[...].astype(jnp.bfloat16)
+    bottom[...] = last[...].astype(jnp.bfloat16)
+
+
+def edge_rows(image):
+    rows, width = image.shape
+    block = (HALO, width)
+    shape = jax.ShapeDtypeStruct(block, jnp.bfloat16)
+    return pl.pallas_call(
+        edge_kernel,
+        out_shape=(shape, shape),
+        grid=(1,),
+        in_specs=[pl.BlockSpec(block, lambda i: (0, 0)), pl.BlockSpec(block, lambda i: (rows // HALO - 1, 0))],
+        out_specs=(pl.BlockSpec(block, lambda i: (0, 0)), pl.BlockSpec(block, lambda i: (0, 0))),
+        cost_estimate=COST,
+        name="edge_rows",
+    )(image, image)
 
 
 def filter_kernel(
@@ -407,11 +427,13 @@
     return lax.ppermute(value, axis, [(i, i ^ distance) for i in range(count)])
 
 
-def scatter_sum(pieces):
+def scatter_sum(pieces, in_turn):
     pieces = dict(pieces)
     kept, added = [pieces[0]], []
     for stage, distances in enumerate(stage_distances(len(pieces))):
         for distance in distances:
+            if in_turn and distance != distances[0]:
+                pieces[distance], _ = lax.optimization_barrier((pieces[distance], added))
             received = swapped(pieces[distance], "line", 1 << stage)
             target = distance ^ (1 << stage)
             if target:
@@ -437,8 +459,9 @@
 
     forward = [(i, i + 1) for i in range(segments - 1)]
     backward = [(i + 1, i) for i in range(segments - 1)]
-    low = lax.ppermute(image[rows - HALO :].astype(jnp.bfloat16), "seg", forward)
-    high = lax.ppermute(image[:HALO].astype(jnp.bfloat16), "seg", backward)
+    top, bottom = edge_rows(image)
+    low = lax.ppermute(bottom, "seg", forward)
+    high = lax.ppermute(top, "seg", backward)
     rows_m, cols_m = build_matrices(place, psf_coef, phases, col_shift, rows, width, segments)
     weight = exposure_weight.astype(jnp.float32)
 
@@ -495,7 +518,7 @@
         mine = joined([outgoing[0]] + received)
         other = swapped(mine, "core", 1)
         sums[index] = pair_sum(place, table, mine, other, slots, lines, quarter)
-        kept[index], added[index] = scatter_sum(sums[index])
+        kept[index], added[index] = scatter_sum(sums[index], index + 1 == count)
         result = finish_chunk(kept[index], scale, result, start)
     return result.reshape(slots, quarter, half_cols)
 

time: 117 us -> 115 us (0.983)
  other arithmetic: 5.27 us -> 1.25 us
  starting transfers between devices: 28.8 us -> 30.9 us
  Pallas kernels: 24.2 us -> 25.9 us
  waiting for transfers between devices: 56.1 us -> 54.6 us
    another operation x1 -> x0, other arithmetic: 4.02 us -> none
    ppermute x18, starting transfers between devices: 22.6 us -> 24.7 us  [swapped(): return lax.ppermute(value, axis, [(i, i ^ distance) for i in range(count)])]
    pallas_call x0 -> x1, Pallas kernels: none -> 1.76 us  [edge_rows(): pl.pallas_call(edge_kernel, out_shape=(shape, shape), grid=(1,), in_specs...]
    ppermute x18, waiting for transfers between devices: 53.4 us -> 51.8 us  [swapped(): return lax.ppermute(value, axis, [(i, i ^ distance) for i in range(count)])]
  transfers between devices with their start and end apart: 20 -> 20, of which waited for: 13 -> 12; matrix products, arithmetic and copies ran while one was open for 1% -> 1% of each run, Pallas kernels for 12% -> 13%
where the time goes in v9:
time: 115 us
  waiting for transfers between devices  54.6 us (47%)
  starting transfers between devices  30.9 us (27%)
  Pallas kernels  25.9 us (23%)
  between operations  2.17 us (2%)
  other arithmetic  1.25 us (1%)
    ppermute x18, waiting for transfers between devices, swapped(): return lax.ppermute(value, axis, [(i, i ^ distance) for i in range(count)])  51.8 us
    ppermute x18, starting transfers between devices, swapped(): return lax.ppermute(value, axis, [(i, i ^ distance) for i in range(count)])  24.7 us
    pallas_call x2, Pallas kernels, filter_chunk(): pl.pallas_call(functools.partial(filter_kernel, first_chunk=start == 0, l...  14 us
    ppermute x1, starting transfers between devices, per_device(): low = lax.ppermute(bottom, 'seg', forward)  4.84 us
    pallas_call x2, Pallas kernels, pair_sum(): pl.pallas_call(functools.partial(pair_kernel, slots=slots, distances=dist...  3.91 us
    ppermute x1, waiting for transfers between devices, per_device(): high = lax.ppermute(top, 'seg', backward)  2.84 us
  transfers between devices with their start and end apart: 20, of which 12 were waited for; matrix products, arithmetic and copies ran while one was open for 1% of the time, Pallas kernels for 13%

profile of v9, /device:TPU:0, one launch (start us, length us, event | category | flops | bytes accessed | tf_op | source)
XLA Modules:
  0.0 115.0 jit_solution(157255075196128578)
XLA Ops:
  0.0 1.8 %edge_rows.1 = (bf16[16,4096]{1,0:T(8,128)(2,1)}, bf16[16,4096]{1,0:T(8,128)(2,1)}) custom-call(f32[512,4096]{1,0:T(8,128)} %bitcast.11, f32[512,4096]{1,0:T(8,128)} %bitcast.12), custom_call_target="tpu_custom_call" | custom-call | flops 1 | bytes 1 | tf_op jit(solution)/shard_map/edge_rows/pallas_call | solution.py:155
  1.8 4.8 %collective-permute-start.1 = (bf16[16,4096]{1,0:T(8,128)(2,1)}, bf16[16,4096]{1,0:T(8,128)(2,1)S(1)}, u32[]{:S(2)}, u32[]{:S(2)}) collective-permute-start(bf16[16,4096]{1,0:T(8,128)(2,1)} %get-tuple-element.38), channel_id=1, source_target_pairs={{0,8},{8,16},{16,24},{1,9},{9,17},{17,25},{2,10},{10,18},{18,26},{... | collective-permute-start | bytes 393224 | tf_op jit(solution)/shard_map/ppermute | solution.py:463
  6.6 1.3 %collective-permute-start.2 = (bf16[16,4096]{1,0:T(8,128)(2,1)}, bf16[16,4096]{1,0:T(8,128)(2,1)S(1)}, u32[]{:S(2)}, u32[]{:S(2)}) collective-permute-start(bf16[16,4096]{1,0:T(8,128)(2,1)} %get-tuple-element.39), channel_id=1, source_target_pairs={{8,0},{16,8},{24,16},{9,1},{17,9},{25,17},{10,2},{18,10},{26,18},{... | collective-permute-start | bytes 393224 | tf_op jit(solution)/shard_map/ppermute | solution.py:464
  8.6 2.1 %band_matrices.1 = (bf16[3,128,480]{2,1,0:T(8,128)(2,1)S(1)}, bf16[3,2,512,256]{3,2,1,0:T(8,128)(2,1)S(1)}) custom-call(s32[3]{0:T(128)S(1)} %pad_add_fusion.1.place, f32[1,2,3]{2,1,0:T(2,128)S(1)} %copy-done.1, s32[1,2]{1,0:T(1,128)S(1)} %copy-done.2, s32[1]{0:T(128)S(6)} %copy.10.shift), custom_call_target="tpu_custom_call" | custom-call | flops 1 | bytes 1 | tf_op jit(solution)/shard_map/band_matrices/pallas_call | solution.py:132
  11.5 2.8 %collective-permute-done.2.high_l.high_c.high_r = bf16[16,4096]{1,0:T(8,128)(2,1)S(1)} collective-permute-done((bf16[16,4096]{1,0:T(8,128)(2,1)}, bf16[16,4096]{1,0:T(8,128)(2,1)S(1)}, u32[]{:S(2)}, u32[]{:S(2)}) %collective-permute-start.2) | collective-permute-done | bytes 131104 | tf_op jit(solution)/shard_map/ppermute | solution.py:464
  14.3 7.0 %warp_filter.3 = (bf16[128,2048]{1,0:T(8,128)(2,1)S(1)}, bf16[128,2048]{1,0:T(8,128)(2,1)S(1)}, bf16[128,2048]{1,0:T(8,128)(2,1)S(1)}, bf16[128,2048]{1,0:T(8,128)(2,1)S(1)}) custom-call(f32[1]{0:T(128)} %convert_element_type.27.weight, bf16[16,4096]{1,0:T(8,128)(2,1)S(1)} %collective-permute-done.1.low_l.low_c.low_r, ...), custom_call_target="tpu_custom_call" | custom-call | flops 1 | bytes 1 | tf_op jit(solution)/shard_map/warp_filter/pallas_call | solution.py:256
  21.3 1.0 collective-permute-start.10
  22.3 2.3 %collective-permute-start.11 = (bf16[128,2048]{1,0:T(8,128)(2,1)S(1)}, bf16[128,2048]{1,0:T(8,128)(2,1)S(1)}, u32[]{:S(2)}, u32[]{:S(2)}) collective-permute-start(bf16[128,2048]{1,0:T(8,128)(2,1)S(1)} %get-tuple-element.52), channel_id=1, source_target_pairs={{0,24},{8,16},{16,8},{24,0},{1,25},{9,17},{17,9},{25,1},{2,26},{10... | collective-permute-start | bytes 1572872 | tf_op jit(solution)/shard_map/ppermute | solution.py:427
  24.6 0.3 collective-permute-start.9
  25.6 1.1 collective-permute-done.6
  26.7 0.1 pad_maximum_fusion.2
  26.8 1.6 %collective-permute-start.7 = (f32[2,3]{1,0:T(2,128)S(1)}, f32[2,3]{1,0:T(2,128)S(1)}, u32[]{:S(2)}, u32[]{:S(2)}) collective-permute-start(f32[2,3]{1,0:T(2,128)S(1)} %pad_maximum_fusion.2), channel_id=1, source_target_pairs={{0,2},{2,0},{4,6},{6,4},{1,3},{3,1},{5,7},{7,5},{8,10},{10,8},{12,... | collective-permute-start | bytes 80 | tf_op jit(solution)/shard_map/ppermute | solution.py:427
  28.4 2.0 %collective-permute-done.7 = f32[2,3]{1,0:T(2,128)S(1)} collective-permute-done((f32[2,3]{1,0:T(2,128)S(1)}, f32[2,3]{1,0:T(2,128)S(1)}, u32[]{:S(2)}, u32[]{:S(2)}) %collective-permute-start.7) | collective-permute-done | bytes 56 | tf_op jit(solution)/shard_map/ppermute | solution.py:427
  30.4 0.1 pad_maximum_fusion.1
  30.5 7.0 %warp_filter.2 = (bf16[128,2048]{1,0:T(8,128)(2,1)S(1)}, bf16[128,2048]{1,0:T(8,128)(2,1)S(1)}, bf16[128,2048]{1,0:T(8,128)(2,1)S(1)}, bf16[128,2048]{1,0:T(8,128)(2,1)S(1)}) custom-call(f32[1]{0:T(128)} %convert_element_type.27.weight, bf16[16,4096]{1,0:T(8,128)(2,1)S(1)} %collective-permute-done.1.low_l.low_c.low_r, ...), custom_call_target="tpu_custom_call" | custom-call | flops 1 | bytes 1 | tf_op jit(solution)/shard_map/warp_filter/pallas_call | solution.py:256
  37.5 8.2 %collective-permute-done.10.refs_2_ = bf16[128,2048]{1,0:T(8,128)(2,1)S(1)} collective-permute-done((bf16[128,2048]{1,0:T(8,128)(2,1)S(1)}, bf16[128,2048]{1,0:T(8,128)(2,1)S(1)}, u32[]{:S(2)}, u32[]{:S(2)}) %collective-permute-start.10) | collective-permute-done | bytes 524320 | tf_op jit(solution)/shard_map/ppermute | solution.py:427
  45.7 1.2 %collective-permute-done.9.refs_1_ = bf16[128,2048]{1,0:T(8,128)(2,1)S(1)} collective-permute-done((bf16[128,2048]{1,0:T(8,128)(2,1)S(1)}, bf16[128,2048]{1,0:T(8,128)(2,1)S(1)}, u32[]{:S(2)}, u32[]{:S(2)}) %collective-permute-start.9) | collective-permute-done | bytes 524320 | tf_op jit(solution)/shard_map/ppermute | solution.py:427
  47.0 0.1 join_blocks.2.mine
  47.2 0.5 collective-permute-start
  47.7 0.1 reshape.10
  47.8 0.1 reshape.11
  47.9 1.0 collective-permute-start.3
  48.9 0.5 collective-permute-start.4
  49.4 2.1 %collective-permute-start.5 = (bf16[128,2048]{1,0:T(8,128)(2,1)S(1)}, bf16[128,2048]{1,0:T(8,128)(2,1)S(1)}, u32[]{:S(2)}, u32[]{:S(2)}) collective-permute-start(bf16[128,2048]{1,0:T(8,128)(2,1)S(1)} %get-tuple-element.45), channel_id=1, source_target_pairs={{0,24},{8,16},{16,8},{24,0},{1,25},{9,17},{17,9},{25,1},{2,26},{10... | collective-permute-start | bytes 1572872 | tf_op jit(solution)/shard_map/ppermute | solution.py:427
  51.5 0.6 fusion.2
  52.1 0.1 pad_add_fusion.table
  52.1 2.5 %pair_sum.2 = (bf16[160,1024]{1,0:T(8,128)(2,1)S(1)}, bf16[160,1024]{1,0:T(8,128)(2,1)S(1)}, bf16[160,1024]{1,0:T(8,128)(2,1)S(1)}, bf16[160,1024]{1,0:T(8,128)(2,1)S(1)}) custom-call(s32[3]{0:T(128)S(1)} %pad_add_fusion.1.place, s32[240]{0:T(256)S(1)} %pad_add_fusion.table, bf16[512,2048]{1,0:T(8,128)(2,1)S(1)} %join_blocks.2.mine, ...), custom_call_target="tpu_custom_call" | custom-call | flops 1 | bytes 1 | tf_op jit(solution)/shard_map/pair_sum/pallas_call | solution.py:340
  54.6 1.6 %collective-permute-start.13 = (bf16[160,1024]{1,0:T(8,128)(2,1)S(1)}, bf16[160,1024]{1,0:T(8,128)(2,1)S(1)}, u32[]{:S(2)}, u32[]{:S(2)}) collective-permute-start(bf16[160,1024]{1,0:T(8,128)(2,1)S(1)} %get-tuple-element.60), channel_id=1, source_target_pairs={{0,2},{2,0},{4,6},{6,4},{1,3},{3,1},{5,7},{7,5},{8,10},{10,8},{12,... | collective-permute-start | bytes 983048 | tf_op jit(solution)/shard_map/ppermute | solution.py:427
  56.3 2.6 %collective-permute-start.8 = (f32[4,3]{1,0:T(4,128)S(1)}, f32[4,3]{1,0:T(4,128)S(1)}, u32[]{:S(2)}, u32[]{:S(2)}) collective-permute-start(f32[4,3]{1,0:T(4,128)S(1)} %pad_maximum_fusion.1), channel_id=1, source_target_pairs={{0,4},{2,6},{4,0},{6,2},{1,5},{3,7},{5,1},{7,3},{8,12},{10,14},{12... | collective-permute-start | bytes 152 | tf_op jit(solution)/shard_map/ppermute | solution.py:427
  58.9 4.7 %collective-permute-done.8 = f32[4,3]{1,0:T(4,128)S(1)} collective-permute-done((f32[4,3]{1,0:T(4,128)S(1)}, f32[4,3]{1,0:T(4,128)S(1)}, u32[]{:S(2)}, u32[]{:S(2)}) %collective-permute-start.8) | collective-permute-done | bytes 80 | tf_op jit(solution)/shard_map/ppermute | solution.py:427
  63.5 3.5 %collective-permute-start.14 = (bf16[160,1024]{1,0:T(8,128)(2,1)S(1)}, bf16[160,1024]{1,0:T(8,128)(2,1)S(1)}, u32[]{:S(2)}, u32[]{:S(2)}) collective-permute-start(bf16[160,1024]{1,0:T(8,128)(2,1)S(1)} %get-tuple-element.62), channel_id=1, source_target_pairs={{0,2},{2,0},{4,6},{6,4},{1,3},{3,1},{5,7},{7,5},{8,10},{10,8},{12,... | collective-permute-start | bytes 983048 | tf_op jit(solution)/shard_map/ppermute | solution.py:427
  67.0 0.1 pad_maximum_fusion.facts
  67.1 1.8 %patch_weights.1.refs_3_ = f32[160,2048]{1,0:T(8,128)S(1)} custom-call(s32[3]{0:T(128)S(1)} %pad_add_fusion.1.place, s32[160]{0:T(256)S(1)} %copy-done, f32[8,3]{1,0:T(8,128)S(1)} %pad_maximum_fusion.facts), custom_call_target="tpu_custom_call" | custom-call | flops 1 | bytes 1 | tf_op jit(solution)/shard_map/patch_weights/pallas_call | solution.py:380
  69.0 5.0 %collective-permute-done.4.refs_2_ = bf16[128,2048]{1,0:T(8,128)(2,1)S(1)} collective-permute-done((bf16[128,2048]{1,0:T(8,128)(2,1)}, bf16[128,2048]{1,0:T(8,128)(2,1)S(1)}, u32[]{:S(2)}, u32[]{:S(2)}) %collective-permute-start.4) | collective-permute-done | bytes 524320 | tf_op jit(solution)/shard_map/ppermute | solution.py:427
  74.0 0.1 add_convert_fusion.1
  74.1 0.1 collective-permute-done.14.refs_1_
  74.2 0.1 join_blocks.3.mine
  74.4 4.1 %collective-permute-done.15.other = bf16[512,2048]{1,0:T(8,128)(2,1)S(1)} collective-permute-done((bf16[512,2048]{1,0:T(8,128)(2,1)S(1)}, bf16[512,2048]{1,0:T(8,128)(2,1)S(1)}, u32[]{:S(2)}, u32[]{:S(2)}) %collective-permute-start.15) | collective-permute-done | bytes 2097184 | tf_op jit(solution)/shard_map/ppermute | solution.py:427
  78.5 1.4 %pair_sum.3 = (bf16[160,1024]{1,0:T(8,128)(2,1)S(1)}, bf16[160,1024]{1,0:T(8,128)(2,1)S(1)}, bf16[160,1024]{1,0:T(8,128)(2,1)S(1)}, bf16[160,1024]{1,0:T(8,128)(2,1)S(1)}) custom-call(s32[3]{0:T(128)S(1)} %pad_add_fusion.1.place, s32[240]{0:T(256)S(1)} %pad_add_fusion.table, bf16[512,2048]{1,0:T(8,128)(2,1)S(1)} %join_blocks.3.mine, ...), custom_call_target="tpu_custom_call" | custom-call | flops 1 | bytes 1 | tf_op jit(solution)/shard_map/pair_sum/pallas_call | solution.py:340
  80.0 1.8 %collective-permute-start.16 = (bf16[160,1024]{1,0:T(8,128)(2,1)S(1)}, bf16[160,1024]{1,0:T(8,128)(2,1)S(1)}, u32[]{:S(2)}, u32[]{:S(2)}) collective-permute-start(bf16[160,1024]{1,0:T(8,128)(2,1)S(1)} %get-tuple-element.69), channel_id=1, source_target_pairs={{0,2},{2,0},{4,6},{6,4},{1,3},{3,1},{5,7},{7,5},{8,10},{10,8},{12,... | collective-permute-start | bytes 983048 | tf_op jit(solution)/shard_map/ppermute | solution.py:427
  81.8 2.3 %collective-permute-start.19 = (bf16[160,1024]{1,0:T(8,128)(2,1)S(1)}, bf16[160,1024]{1,0:T(8,128)(2,1)S(1)}, u32[]{:S(2)}, u32[]{:S(2)}) collective-permute-start(bf16[160,1024]{1,0:T(8,128)(2,1)S(1)} %add_convert_fusion.1), channel_id=1, source_target_pairs={{0,4},{2,6},{4,0},{6,2},{1,5},{3,7},{5,1},{7,3},{8,12},{10,14},{12... | collective-permute-start | bytes 983048 | tf_op jit(solution)/shard_map/ppermute | solution.py:427
  84.1 12.3 %collective-permute-done.16 = bf16[160,1024]{1,0:T(8,128)(2,1)S(1)} collective-permute-done((bf16[160,1024]{1,0:T(8,128)(2,1)S(1)}, bf16[160,1024]{1,0:T(8,128)(2,1)S(1)}, u32[]{:S(2)}, u32[]{:S(2)}) %collective-permute-start.16) | collective-permute-done | bytes 327712 | tf_op jit(solution)/shard_map/ppermute | solution.py:427
  96.5 0.1 add_convert_fusion
  96.6 3.4 %collective-permute-start.18 = (bf16[160,1024]{1,0:T(8,128)(2,1)S(1)}, bf16[160,1024]{1,0:T(8,128)(2,1)S(1)}, u32[]{:S(2)}, u32[]{:S(2)}) collective-permute-start(bf16[160,1024]{1,0:T(8,128)(2,1)S(1)} %add_convert_fusion), channel_id=1, source_target_pairs={{0,4},{2,6},{4,0},{6,2},{1,5},{3,7},{5,1},{7,3},{8,12},{10,14},{12... | collective-permute-start | bytes 983048 | tf_op jit(solution)/shard_map/ppermute | solution.py:427
  100.1 1.0 patch_mean.2.refs_4_
  101.1 11.6 %collective-permute-done.17.refs_1_ = bf16[160,1024]{1,0:T(8,128)(2,1)S(1)} collective-permute-done((bf16[160,1024]{1,0:T(8,128)(2,1)S(1)}, bf16[160,1024]{1,0:T(8,128)(2,1)S(1)}, u32[]{:S(2)}, u32[]{:S(2)}) %collective-permute-start.17) | collective-permute-done | bytes 327712 | tf_op jit(solution)/shard_map/ppermute | solution.py:427
  112.7 1.3 %collective-permute-done.18.refs_2_ = bf16[160,1024]{1,0:T(8,128)(2,1)S(1)} collective-permute-done((bf16[160,1024]{1,0:T(8,128)(2,1)S(1)}, bf16[160,1024]{1,0:T(8,128)(2,1)S(1)}, u32[]{:S(2)}, u32[]{:S(2)}) %collective-permute-start.18) | collective-permute-done | bytes 327712 | tf_op jit(solution)/shard_map/ppermute | solution.py:427
  114.0 1.0 patch_mean.3
  (26 shorter events, 0.5 us)
Async XLA Ops:
  0.0 8.6 %copy-start.1 = (f32[1,2,3]{2,1,0:T(2,128)S(1)}, f32[1,2,3]{2,1,0:T(2,128)}, u32[]{:S(2)}) copy-start(f32[1,2,3]{2,1,0:T(2,128)} %coef.1) | copy-start | bytes 76
  0.0 8.6 %copy-start.2 = (s32[1,2]{1,0:T(1,128)S(1)}, s32[1,2]{1,0:T(1,128)}, u32[]{:S(2)}) copy-start(s32[1,2]{1,0:T(1,128)} %phases.1) | copy-start | bytes 28
  1.8 9.7 %collective-permute-start.1 = (bf16[16,4096]{1,0:T(8,128)(2,1)}, bf16[16,4096]{1,0:T(8,128)(2,1)S(1)}, u32[]{:S(2)}, u32[]{:S(2)}) collective-permute-start(bf16[16,4096]{1,0:T(8,128)(2,1)} %get-tuple-element.38), channel_id=1, source_target_pairs={{0,8},{8,16},{16,24},{1,9},{9,17},{17,25},{2,10},{10,18},{18,26},{... | collective-permute-start | bytes 393224 | tf_op jit(solution)/shard_map/ppermute | solution.py:463
  6.6 7.7 %collective-permute-start.2 = (bf16[16,4096]{1,0:T(8,128)(2,1)}, bf16[16,4096]{1,0:T(8,128)(2,1)S(1)}, u32[]{:S(2)}, u32[]{:S(2)}) collective-permute-start(bf16[16,4096]{1,0:T(8,128)(2,1)} %get-tuple-element.39), channel_id=1, source_target_pairs={{8,0},{16,8},{24,16},{9,1},{17,9},{25,17},{10,2},{18,10},{26,18},{... | collective-permute-start | bytes 393224 | tf_op jit(solution)/shard_map/ppermute | solution.py:464
  21.3 24.4 %collective-permute-start.10 = (bf16[128,2048]{1,0:T(8,128)(2,1)S(1)}, bf16[128,2048]{1,0:T(8,128)(2,1)S(1)}, u32[]{:S(2)}, u32[]{:S(2)}) collective-permute-start(bf16[128,2048]{1,0:T(8,128)(2,1)S(1)} %get-tuple-element.51), channel_id=1, source_target_pairs={{0,16},{8,24},{16,0},{24,8},{1,17},{9,25},{17,1},{25,9},{2,18},{10... | collective-permute-start | bytes 1572872 | tf_op jit(solution)/shard_map/ppermute | solution.py:427
  22.3 23.5 %collective-permute-start.11 = (bf16[128,2048]{1,0:T(8,128)(2,1)S(1)}, bf16[128,2048]{1,0:T(8,128)(2,1)S(1)}, u32[]{:S(2)}, u32[]{:S(2)}) collective-permute-start(bf16[128,2048]{1,0:T(8,128)(2,1)S(1)} %get-tuple-element.52), channel_id=1, source_target_pairs={{0,24},{8,16},{16,8},{24,0},{1,25},{9,17},{17,9},{25,1},{2,26},{10... | collective-permute-start | bytes 1572872 | tf_op jit(solution)/shard_map/ppermute | solution.py:427
  24.6 22.3 %collective-permute-start.9 = (bf16[128,2048]{1,0:T(8,128)(2,1)S(1)}, bf16[128,2048]{1,0:T(8,128)(2,1)S(1)}, u32[]{:S(2)}, u32[]{:S(2)}) collective-permute-start(bf16[128,2048]{1,0:T(8,128)(2,1)S(1)} %get-tuple-element.50), channel_id=1, source_target_pairs={{0,8},{8,0},{16,24},{24,16},{1,9},{9,1},{17,25},{25,17},{2,10},{10... | collective-permute-start | bytes 1572872 | tf_op jit(solution)/shard_map/ppermute | solution.py:427
  25.6 1.1 collective-permute-start.6
  26.8 3.6 %collective-permute-start.7 = (f32[2,3]{1,0:T(2,128)S(1)}, f32[2,3]{1,0:T(2,128)S(1)}, u32[]{:S(2)}, u32[]{:S(2)}) collective-permute-start(f32[2,3]{1,0:T(2,128)S(1)} %pad_maximum_fusion.2), channel_id=1, source_target_pairs={{0,2},{2,0},{4,6},{6,4},{1,3},{3,1},{5,7},{7,5},{8,10},{10,8},{12,... | collective-permute-start | bytes 80 | tf_op jit(solution)/shard_map/ppermute | solution.py:427
  37.5 9.6 %copy-start.3 = (bf16[128,2048]{1,0:T(8,128)(2,1)}, bf16[128,2048]{1,0:T(8,128)(2,1)S(1)}, u32[]{:S(2)}) copy-start(bf16[128,2048]{1,0:T(8,128)(2,1)S(1)} %get-tuple-element.44) | copy-start | bytes 1572868
  37.5 9.6 %copy-start.4 = (bf16[128,2048]{1,0:T(8,128)(2,1)}, bf16[128,2048]{1,0:T(8,128)(2,1)S(1)}, u32[]{:S(2)}) copy-start(bf16[128,2048]{1,0:T(8,128)(2,1)S(1)} %get-tuple-element.43) | copy-start | bytes 1572868
  47.0 0.7 copy-start
  47.1 5.0 %collective-permute-start.12 = (bf16[512,2048]{1,0:T(8,128)(2,1)S(1)}, bf16[512,2048]{1,0:T(8,128)(2,1)}, u32[]{:S(2)}, u32[]{:S(2)}) collective-permute-start(bf16[512,2048]{1,0:T(8,128)(2,1)S(1)} %join_blocks.2.mine), channel_id=1, source_target_pairs={{0,1},{1,0},{2,3},{3,2},{4,5},{5,4},{6,7},{7,6},{8,9},{9,8},{10,11... | collective-permute-start | bytes 6291464 | tf_op jit(solution)/shard_map/ppermute | solution.py:427
  47.2 4.3 %collective-permute-start = (s32[1]{0:T(128)}, s32[1]{0:T(128)}, u32[]{:S(2)}, u32[]{:S(2)}) collective-permute-start(s32[1]{0:T(128)} %param.11), channel_id=1, source_target_pairs={{0,1},{1,0},{2,3},{3,2},{4,5},{5,4},{6,7},{7,6},{8,9},{9,8},{10,11... | collective-permute-start | bytes 20 | tf_op jit(solution)/shard_map/ppermute | solution.py:427
  47.9 21.0 %collective-permute-start.3 = (bf16[128,2048]{1,0:T(8,128)(2,1)}, bf16[128,2048]{1,0:T(8,128)(2,1)S(1)}, u32[]{:S(2)}, u32[]{:S(2)}) collective-permute-start(bf16[128,2048]{1,0:T(8,128)(2,1)} %copy-done.4), channel_id=1, source_target_pairs={{0,8},{8,0},{16,24},{24,16},{1,9},{9,1},{17,25},{25,17},{2,10},{10... | collective-permute-start | bytes 1572872 | tf_op jit(solution)/shard_map/ppermute | solution.py:427
  48.9 25.1 %collective-permute-start.4 = (bf16[128,2048]{1,0:T(8,128)(2,1)}, bf16[128,2048]{1,0:T(8,128)(2,1)S(1)}, u32[]{:S(2)}, u32[]{:S(2)}) collective-permute-start(bf16[128,2048]{1,0:T(8,128)(2,1)} %copy-done.3), channel_id=1, source_target_pairs={{0,16},{8,24},{16,0},{24,8},{1,17},{9,25},{17,1},{25,9},{2,18},{10... | collective-permute-start | bytes 1572872 | tf_op jit(solution)/shard_map/ppermute | solution.py:427
  49.4 24.6 %collective-permute-start.5 = (bf16[128,2048]{1,0:T(8,128)(2,1)S(1)}, bf16[128,2048]{1,0:T(8,128)(2,1)S(1)}, u32[]{:S(2)}, u32[]{:S(2)}) collective-permute-start(bf16[128,2048]{1,0:T(8,128)(2,1)S(1)} %get-tuple-element.45), channel_id=1, source_target_pairs={{0,24},{8,16},{16,8},{24,0},{1,25},{9,17},{17,9},{25,1},{2,26},{10... | collective-permute-start | bytes 1572872 | tf_op jit(solution)/shard_map/ppermute | solution.py:427
  54.6 19.3 %collective-permute-start.13 = (bf16[160,1024]{1,0:T(8,128)(2,1)S(1)}, bf16[160,1024]{1,0:T(8,128)(2,1)S(1)}, u32[]{:S(2)}, u32[]{:S(2)}) collective-permute-start(bf16[160,1024]{1,0:T(8,128)(2,1)S(1)} %get-tuple-element.60), channel_id=1, source_target_pairs={{0,2},{2,0},{4,6},{6,4},{1,3},{3,1},{5,7},{7,5},{8,10},{10,8},{12,... | collective-permute-start | bytes 983048 | tf_op jit(solution)/shard_map/ppermute | solution.py:427
  56.3 7.3 %collective-permute-start.8 = (f32[4,3]{1,0:T(4,128)S(1)}, f32[4,3]{1,0:T(4,128)S(1)}, u32[]{:S(2)}, u32[]{:S(2)}) collective-permute-start(f32[4,3]{1,0:T(4,128)S(1)} %pad_maximum_fusion.1), channel_id=1, source_target_pairs={{0,4},{2,6},{4,0},{6,2},{1,5},{3,7},{5,1},{7,3},{8,12},{10,14},{12... | collective-permute-start | bytes 152 | tf_op jit(solution)/shard_map/ppermute | solution.py:427
  63.5 10.6 %collective-permute-start.14 = (bf16[160,1024]{1,0:T(8,128)(2,1)S(1)}, bf16[160,1024]{1,0:T(8,128)(2,1)S(1)}, u32[]{:S(2)}, u32[]{:S(2)}) collective-permute-start(bf16[160,1024]{1,0:T(8,128)(2,1)S(1)} %get-tuple-element.62), channel_id=1, source_target_pairs={{0,2},{2,0},{4,6},{6,4},{1,3},{3,1},{5,7},{7,5},{8,10},{10,8},{12,... | collective-permute-start | bytes 983048 | tf_op jit(solution)/shard_map/ppermute | solution.py:427
  74.3 4.2 %collective-permute-start.15 = (bf16[512,2048]{1,0:T(8,128)(2,1)S(1)}, bf16[512,2048]{1,0:T(8,128)(2,1)S(1)}, u32[]{:S(2)}, u32[]{:S(2)}) collective-permute-start(bf16[512,2048]{1,0:T(8,128)(2,1)S(1)} %join_blocks.3.mine), channel_id=1, source_target_pairs={{0,1},{1,0},{2,3},{3,2},{4,5},{5,4},{6,7},{7,6},{8,9},{9,8},{10,11... | collective-permute-start | bytes 6291464 | tf_op jit(solution)/shard_map/ppermute | solution.py:427
  80.0 16.5 %collective-permute-start.16 = (bf16[160,1024]{1,0:T(8,128)(2,1)S(1)}, bf16[160,1024]{1,0:T(8,128)(2,1)S(1)}, u32[]{:S(2)}, u32[]{:S(2)}) collective-permute-start(bf16[160,1024]{1,0:T(8,128)(2,1)S(1)} %get-tuple-element.69), channel_id=1, source_target_pairs={{0,2},{2,0},{4,6},{6,4},{1,3},{3,1},{5,7},{7,5},{8,10},{10,8},{12,... | collective-permute-start | bytes 983048 | tf_op jit(solution)/shard_map/ppermute | solution.py:427
  81.8 18.3 %collective-permute-start.19 = (bf16[160,1024]{1,0:T(8,128)(2,1)S(1)}, bf16[160,1024]{1,0:T(8,128)(2,1)S(1)}, u32[]{:S(2)}, u32[]{:S(2)}) collective-permute-start(bf16[160,1024]{1,0:T(8,128)(2,1)S(1)} %add_convert_fusion.1), channel_id=1, source_target_pairs={{0,4},{2,6},{4,0},{6,2},{1,5},{3,7},{5,1},{7,3},{8,12},{10,14},{12... | collective-permute-start | bytes 983048 | tf_op jit(solution)/shard_map/ppermute | solution.py:427
  96.6 16.1 %collective-permute-start.17 = (bf16[160,1024]{1,0:T(8,128)(2,1)S(1)}, bf16[160,1024]{1,0:T(8,128)(2,1)S(1)}, u32[]{:S(2)}, u32[]{:S(2)}) collective-permute-start(bf16[160,1024]{1,0:T(8,128)(2,1)S(1)} %get-tuple-element.70), channel_id=1, source_target_pairs={{0,2},{2,0},{4,6},{6,4},{1,3},{3,1},{5,7},{7,5},{8,10},{10,8},{12,... | collective-permute-start | bytes 983048 | tf_op jit(solution)/shard_map/ppermute | solution.py:427
  96.6 17.4 %collective-permute-start.18 = (bf16[160,1024]{1,0:T(8,128)(2,1)S(1)}, bf16[160,1024]{1,0:T(8,128)(2,1)S(1)}, u32[]{:S(2)}, u32[]{:S(2)}) collective-permute-start(bf16[160,1024]{1,0:T(8,128)(2,1)S(1)} %add_convert_fusion), channel_id=1, source_target_pairs={{0,4},{2,6},{4,0},{6,2},{1,5},{3,7},{5,1},{7,3},{8,12},{10,14},{12... | collective-permute-start | bytes 983048 | tf_op jit(solution)/shard_map/ppermute | solution.py:427

commit v10 on v9

--- a/solution.py
+++ b/solution.py
@@ -427,22 +427,28 @@
     return lax.ppermute(value, axis, [(i, i ^ distance) for i in range(count)])
 
 
-def scatter_sum(pieces, in_turn):
+def scatter_sum(pieces, in_turn, halved, after):
     pieces = dict(pieces)
-    kept, added = [pieces[0]], []
+    kept, added, early = [pieces[0]], [], []
     for stage, distances in enumerate(stage_distances(len(pieces))):
         for distance in distances:
             if in_turn and distance != distances[0]:
                 pieces[distance], _ = lax.optimization_barrier((pieces[distance], added))
+            if halved and 2 * distance == len(pieces):
+                width = pieces[distance].shape[1] // 2
+                parts = [swapped(pieces[distance][:, first : first + width], "line", 1 << stage) for first in (0, width)]
+                early = parts
+                kept.append(jnp.concatenate(parts, axis=1))
+                continue
             received = swapped(pieces[distance], "line", 1 << stage)
             target = distance ^ (1 << stage)
             if target:
                 both = pieces[target].astype(jnp.float32) + received.astype(jnp.float32)
-                pieces[target] = both.astype(jnp.bfloat16)
+                pieces[target], _ = lax.optimization_barrier((both.astype(jnp.bfloat16), after))
                 added = [pieces[target]]
             else:
                 kept.append(received)
-    return kept, added
+    return kept, added, early
 
 
 def per_device(images, psf_coef, phases, col_shift, band_offset, exposure_weight, patch_site):
@@ -495,7 +501,7 @@
 
     result = None
     count = len(chunks)
-    sent, sums, kept, added = [None] * count, [None] * count, [None] * count, [None] * count
+    sent, sums, kept, added, parts = ([None] * count for _ in range(5))
 
     def filtered(index):
         start, chunk = chunks[index]
@@ -517,8 +523,12 @@
             received = tied(received, (added[index - 1], kept[index - 1][:-1]))
         mine = joined([outgoing[0]] + received)
         other = swapped(mine, "core", 1)
+        if index >= 1:
+            other = tied(other, parts[index - 1][:1])
         sums[index] = pair_sum(place, table, mine, other, slots, lines, quarter)
-        kept[index], added[index] = scatter_sum(sums[index], index + 1 == count)
+        kept[index], added[index], parts[index] = scatter_sum(
+            sums[index], index + 1 == count, index + 1 < count, parts[index - 1][1:] if index else []
+        )
         result = finish_chunk(kept[index], scale, result, start)
     return result.reshape(slots, quarter, half_cols)
 

time: 115 us -> 121 us (1.052)
  starting transfers between devices: 30.9 us -> 34.4 us
  waiting for transfers between devices: 54.6 us -> 56.1 us
    ppermute x18 -> x19, starting transfers between devices: 24.7 us -> 28.3 us  [swapped(): return lax.ppermute(value, axis, [(i, i ^ distance) for i in range(count)])]
    ppermute x18 -> x19, waiting for transfers between devices: 51.8 us -> 53.2 us  [swapped(): return lax.ppermute(value, axis, [(i, i ^ distance) for i in range(count)])]
  transfers between devices with their start and end apart: 20 -> 21, of which waited for: 12 -> 11; matrix products, arithmetic and copies ran while one was open for 1% -> 1% of each run, Pallas kernels for 13% -> 12%
where the time goes in v10:
time: 121 us; the launch traced here: 120 us
  waiting for transfers between devices  56.1 us (46%)
  starting transfers between devices  34.4 us (28%)
  Pallas kernels  25.9 us (21%)
  between operations  2.19 us (2%)
  other arithmetic  1.4 us (1%)
    ppermute x19, waiting for transfers between devices, swapped(): return lax.ppermute(value, axis, [(i, i ^ distance) for i in range(count)])  53.2 us
    ppermute x19, starting transfers between devices, swapped(): return lax.ppermute(value, axis, [(i, i ^ distance) for i in range(count)])  28.3 us
    pallas_call x2, Pallas kernels, filter_chunk(): pl.pallas_call(functools.partial(filter_kernel, first_chunk=start == 0, l...  14 us
    ppermute x1, starting transfers between devices, per_device(): low = lax.ppermute(bottom, 'seg', forward)  4.84 us
    pallas_call x2, Pallas kernels, pair_sum(): pl.pallas_call(functools.partial(pair_kernel, slots=slots, distances=dist...  3.91 us
    ppermute x1, waiting for transfers between devices, per_device(): high = lax.ppermute(top, 'seg', backward)  2.84 us
  transfers between devices with their start and end apart: 21, of which 11 were waited for; matrix products, arithmetic and copies ran while one was open for 1% of the time, Pallas kernels for 12%

profile of v10, /device:TPU:0, one launch (start us, length us, event | category | flops | bytes accessed | tf_op | source)
XLA Modules:
  0.0 120.3 jit_solution(4173878592890754033)
XLA Ops:
  0.0 1.8 %edge_rows.1 = (bf16[16,4096]{1,0:T(8,128)(2,1)}, bf16[16,4096]{1,0:T(8,128)(2,1)}) custom-call(f32[512,4096]{1,0:T(8,128)} %bitcast.11, f32[512,4096]{1,0:T(8,128)} %bitcast.12), custom_call_target="tpu_custom_call" | custom-call | flops 1 | bytes 1 | tf_op jit(solution)/shard_map/edge_rows/pallas_call | solution.py:155
  1.8 4.8 %collective-permute-start.1 = (bf16[16,4096]{1,0:T(8,128)(2,1)}, bf16[16,4096]{1,0:T(8,128)(2,1)S(1)}, u32[]{:S(2)}, u32[]{:S(2)}) collective-permute-start(bf16[16,4096]{1,0:T(8,128)(2,1)} %get-tuple-element.40), channel_id=1, source_target_pairs={{0,8},{8,16},{16,24},{1,9},{9,17},{17,25},{2,10},{10,18},{18,26},{... | collective-permute-start | bytes 393224 | tf_op jit(solution)/shard_map/ppermute | solution.py:469
  6.6 1.3 %collective-permute-start.2 = (bf16[16,4096]{1,0:T(8,128)(2,1)}, bf16[16,4096]{1,0:T(8,128)(2,1)S(1)}, u32[]{:S(2)}, u32[]{:S(2)}) collective-permute-start(bf16[16,4096]{1,0:T(8,128)(2,1)} %get-tuple-element.41), channel_id=1, source_target_pairs={{8,0},{16,8},{24,16},{9,1},{17,9},{25,17},{10,2},{18,10},{26,18},{... | collective-permute-start | bytes 393224 | tf_op jit(solution)/shard_map/ppermute | solution.py:470
  8.6 2.1 %band_matrices.1 = (bf16[3,128,480]{2,1,0:T(8,128)(2,1)S(1)}, bf16[3,2,512,256]{3,2,1,0:T(8,128)(2,1)S(1)}) custom-call(s32[3]{0:T(128)S(1)} %pad_add_fusion.1.place, f32[1,2,3]{2,1,0:T(2,128)S(1)} %copy-done.1, s32[1,2]{1,0:T(1,128)S(1)} %copy-done.2, s32[1]{0:T(128)S(6)} %copy.10.shift), custom_call_target="tpu_custom_call" | custom-call | flops 1 | bytes 1 | tf_op jit(solution)/shard_map/band_matrices/pallas_call | solution.py:132
  11.5 2.8 %collective-permute-done.2.high_l.high_c.high_r = bf16[16,4096]{1,0:T(8,128)(2,1)S(1)} collective-permute-done((bf16[16,4096]{1,0:T(8,128)(2,1)}, bf16[16,4096]{1,0:T(8,128)(2,1)S(1)}, u32[]{:S(2)}, u32[]{:S(2)}) %collective-permute-start.2) | collective-permute-done | bytes 131104 | tf_op jit(solution)/shard_map/ppermute | solution.py:470
  14.3 7.0 %warp_filter.3 = (bf16[128,2048]{1,0:T(8,128)(2,1)S(1)}, bf16[128,2048]{1,0:T(8,128)(2,1)S(1)}, bf16[128,2048]{1,0:T(8,128)(2,1)S(1)}, bf16[128,2048]{1,0:T(8,128)(2,1)S(1)}) custom-call(f32[1]{0:T(128)} %convert_element_type.27.weight, bf16[16,4096]{1,0:T(8,128)(2,1)S(1)} %collective-permute-done.1.low_l.low_c.low_r, ...), custom_call_target="tpu_custom_call" | custom-call | flops 1 | bytes 1 | tf_op jit(solution)/shard_map/warp_filter/pallas_call | solution.py:256
  21.3 1.0 collective-permute-start.10
  22.3 2.3 %collective-permute-start.11 = (bf16[128,2048]{1,0:T(8,128)(2,1)S(1)}, bf16[128,2048]{1,0:T(8,128)(2,1)S(1)}, u32[]{:S(2)}, u32[]{:S(2)}) collective-permute-start(bf16[128,2048]{1,0:T(8,128)(2,1)S(1)} %get-tuple-element.54), channel_id=1, source_target_pairs={{0,24},{8,16},{16,8},{24,0},{1,25},{9,17},{17,9},{25,1},{2,26},{10... | collective-permute-start | bytes 1572872 | tf_op jit(solution)/shard_map/ppermute | solution.py:427
  24.6 0.3 collective-permute-start.9
  25.6 1.1 collective-permute-done.6
  26.7 0.1 pad_maximum_fusion.3
  26.8 1.6 %collective-permute-start.7 = (f32[2,3]{1,0:T(2,128)S(1)}, f32[2,3]{1,0:T(2,128)S(1)}, u32[]{:S(2)}, u32[]{:S(2)}) collective-permute-start(f32[2,3]{1,0:T(2,128)S(1)} %pad_maximum_fusion.3), channel_id=1, source_target_pairs={{0,2},{2,0},{4,6},{6,4},{1,3},{3,1},{5,7},{7,5},{8,10},{10,8},{12,... | collective-permute-start | bytes 80 | tf_op jit(solution)/shard_map/ppermute | solution.py:427
  28.4 2.0 %collective-permute-done.7 = f32[2,3]{1,0:T(2,128)S(1)} collective-permute-done((f32[2,3]{1,0:T(2,128)S(1)}, f32[2,3]{1,0:T(2,128)S(1)}, u32[]{:S(2)}, u32[]{:S(2)}) %collective-permute-start.7) | collective-permute-done | bytes 56 | tf_op jit(solution)/shard_map/ppermute | solution.py:427
  30.4 0.1 pad_maximum_fusion.2
  30.5 7.0 %warp_filter.2 = (bf16[128,2048]{1,0:T(8,128)(2,1)S(1)}, bf16[128,2048]{1,0:T(8,128)(2,1)S(1)}, bf16[128,2048]{1,0:T(8,128)(2,1)S(1)}, bf16[128,2048]{1,0:T(8,128)(2,1)S(1)}) custom-call(f32[1]{0:T(128)} %convert_element_type.27.weight, bf16[16,4096]{1,0:T(8,128)(2,1)S(1)} %collective-permute-done.1.low_l.low_c.low_r, ...), custom_call_target="tpu_custom_call" | custom-call | flops 1 | bytes 1 | tf_op jit(solution)/shard_map/warp_filter/pallas_call | solution.py:256
  37.5 8.2 %collective-permute-done.10.refs_2_ = bf16[128,2048]{1,0:T(8,128)(2,1)S(1)} collective-permute-done((bf16[128,2048]{1,0:T(8,128)(2,1)S(1)}, bf16[128,2048]{1,0:T(8,128)(2,1)S(1)}, u32[]{:S(2)}, u32[]{:S(2)}) %collective-permute-start.10) | collective-permute-done | bytes 524320 | tf_op jit(solution)/shard_map/ppermute | solution.py:427
  45.7 1.2 %collective-permute-done.9.refs_1_ = bf16[128,2048]{1,0:T(8,128)(2,1)S(1)} collective-permute-done((bf16[128,2048]{1,0:T(8,128)(2,1)S(1)}, bf16[128,2048]{1,0:T(8,128)(2,1)S(1)}, u32[]{:S(2)}, u32[]{:S(2)}) %collective-permute-start.9) | collective-permute-done | bytes 524320 | tf_op jit(solution)/shard_map/ppermute | solution.py:427
  47.0 0.1 join_blocks.2.mine
  47.2 0.5 collective-permute-start
  47.7 0.1 reshape.10
  47.8 0.1 reshape.11
  47.9 1.0 collective-permute-start.3
  48.9 0.5 collective-permute-start.4
  49.4 2.1 %collective-permute-start.5 = (bf16[128,2048]{1,0:T(8,128)(2,1)S(1)}, bf16[128,2048]{1,0:T(8,128)(2,1)S(1)}, u32[]{:S(2)}, u32[]{:S(2)}) collective-permute-start(bf16[128,2048]{1,0:T(8,128)(2,1)S(1)} %get-tuple-element.47), channel_id=1, source_target_pairs={{0,24},{8,16},{16,8},{24,0},{1,25},{9,17},{17,9},{25,1},{2,26},{10... | collective-permute-start | bytes 1572872 | tf_op jit(solution)/shard_map/ppermute | solution.py:427
  51.5 0.7 fusion.2
  52.3 2.5 %pair_sum.2 = (bf16[160,1024]{1,0:T(8,128)(2,1)S(1)}, bf16[160,1024]{1,0:T(8,128)(2,1)S(1)}, bf16[160,1024]{1,0:T(8,128)(2,1)S(1)}, bf16[160,1024]{1,0:T(8,128)(2,1)S(1)}) custom-call(s32[3]{0:T(128)S(1)} %pad_add_fusion.1.place, s32[240]{0:T(256)S(1)} %pad_add_fusion.table, bf16[512,2048]{1,0:T(8,128)(2,1)S(1)} %join_blocks.2.mine, ...), custom_call_target="tpu_custom_call" | custom-call | flops 1 | bytes 1 | tf_op jit(solution)/shard_map/pair_sum/pallas_call | solution.py:340
  54.8 1.6 %collective-permute-start.13 = (bf16[160,1024]{1,0:T(8,128)(2,1)S(1)}, bf16[160,1024]{1,0:T(8,128)(2,1)S(1)}, u32[]{:S(2)}, u32[]{:S(2)}) collective-permute-start(bf16[160,1024]{1,0:T(8,128)(2,1)S(1)} %get-tuple-element.62), channel_id=1, source_target_pairs={{0,2},{2,0},{4,6},{6,4},{1,3},{3,1},{5,7},{7,5},{8,10},{10,8},{12,... | collective-permute-start | bytes 983048 | tf_op jit(solution)/shard_map/ppermute | solution.py:427
  56.4 2.6 %collective-permute-start.8 = (f32[4,3]{1,0:T(4,128)S(1)}, f32[4,3]{1,0:T(4,128)S(1)}, u32[]{:S(2)}, u32[]{:S(2)}) collective-permute-start(f32[4,3]{1,0:T(4,128)S(1)} %pad_maximum_fusion.2), channel_id=1, source_target_pairs={{0,4},{2,6},{4,0},{6,2},{1,5},{3,7},{5,1},{7,3},{8,12},{10,14},{12... | collective-permute-start | bytes 152 | tf_op jit(solution)/shard_map/ppermute | solution.py:427
  59.0 4.5 %collective-permute-done.8 = f32[4,3]{1,0:T(4,128)S(1)} collective-permute-done((f32[4,3]{1,0:T(4,128)S(1)}, f32[4,3]{1,0:T(4,128)S(1)}, u32[]{:S(2)}, u32[]{:S(2)}) %collective-permute-start.8) | collective-permute-done | bytes 80 | tf_op jit(solution)/shard_map/ppermute | solution.py:427
  63.5 3.5 %collective-permute-start.14 = (bf16[160,1024]{1,0:T(8,128)(2,1)S(1)}, bf16[160,1024]{1,0:T(8,128)(2,1)S(1)}, u32[]{:S(2)}, u32[]{:S(2)}) collective-permute-start(bf16[160,1024]{1,0:T(8,128)(2,1)S(1)} %get-tuple-element.64), channel_id=1, source_target_pairs={{0,2},{2,0},{4,6},{6,4},{1,3},{3,1},{5,7},{7,5},{8,10},{10,8},{12,... | collective-permute-start | bytes 983048 | tf_op jit(solution)/shard_map/ppermute | solution.py:427
  67.0 0.1 pad_maximum_fusion.1.facts
  67.1 1.8 %patch_weights.1.refs_3_ = f32[160,2048]{1,0:T(8,128)S(1)} custom-call(s32[3]{0:T(128)S(1)} %pad_add_fusion.1.place, s32[160]{0:T(256)S(1)} %copy-done, f32[8,3]{1,0:T(8,128)S(1)} %pad_maximum_fusion.1.facts), custom_call_target="tpu_custom_call" | custom-call | flops 1 | bytes 1 | tf_op jit(solution)/shard_map/patch_weights/pallas_call | solution.py:380
  68.9 5.0 %collective-permute-done.4.refs_2_ = bf16[128,2048]{1,0:T(8,128)(2,1)S(1)} collective-permute-done((bf16[128,2048]{1,0:T(8,128)(2,1)}, bf16[128,2048]{1,0:T(8,128)(2,1)S(1)}, u32[]{:S(2)}, u32[]{:S(2)}) %collective-permute-start.4) | collective-permute-done | bytes 524320 | tf_op jit(solution)/shard_map/ppermute | solution.py:427
  74.0 0.1 add_convert_fusion.1
  74.1 0.1 join_blocks.3.mine
  74.3 2.7 %collective-permute-start.16 = (bf16[160,512]{1,0:T(8,128)(2,1)S(1)}, bf16[160,512]{1,0:T(8,128)(2,1)S(1)}, u32[]{:S(2)}, u32[]{:S(2)}) collective-permute-start(bf16[160,512]{1,0:T(8,128)(2,1)S(1)} %get-tuple-element.78), channel_id=1, source_target_pairs={{0,4},{2,6},{4,0},{6,2},{1,5},{3,7},{5,1},{7,3},{8,12},{10,14},{12... | collective-permute-start | bytes 491528 | tf_op jit(solution)/shard_map/ppermute | solution.py:427
  77.0 8.4 %collective-permute-done.16 = bf16[160,512]{1,0:T(8,128)(2,1)S(1)} collective-permute-done((bf16[160,512]{1,0:T(8,128)(2,1)S(1)}, bf16[160,512]{1,0:T(8,128)(2,1)S(1)}, u32[]{:S(2)}, u32[]{:S(2)}) %collective-permute-start.16) | collective-permute-done | bytes 163872 | tf_op jit(solution)/shard_map/ppermute | solution.py:427
  85.4 1.4 %pair_sum.3 = (bf16[160,1024]{1,0:T(8,128)(2,1)S(1)}, bf16[160,1024]{1,0:T(8,128)(2,1)S(1)}, bf16[160,1024]{1,0:T(8,128)(2,1)S(1)}, bf16[160,1024]{1,0:T(8,128)(2,1)S(1)}) custom-call(s32[3]{0:T(128)S(1)} %pad_add_fusion.1.place, s32[240]{0:T(256)S(1)} %pad_add_fusion.table, bf16[512,2048]{1,0:T(8,128)(2,1)S(1)} %join_blocks.3.mine, ...), custom_call_target="tpu_custom_call" | custom-call | flops 1 | bytes 1 | tf_op jit(solution)/shard_map/pair_sum/pallas_call | solution.py:340
  86.9 0.8 collective-permute-start.17
  87.6 3.4 %collective-permute-start.18 = (bf16[160,512]{1,0:T(8,128)(2,1)S(1)}, bf16[160,512]{1,0:T(8,128)(2,1)S(1)}, u32[]{:S(2)}, u32[]{:S(2)}) collective-permute-start(bf16[160,512]{1,0:T(8,128)(2,1)S(1)} %get-tuple-element.77), channel_id=1, source_target_pairs={{0,4},{2,6},{4,0},{6,2},{1,5},{3,7},{5,1},{7,3},{8,12},{10,14},{12... | collective-permute-start | bytes 491528 | tf_op jit(solution)/shard_map/ppermute | solution.py:427
  91.0 8.8 %collective-permute-done.17 = bf16[160,1024]{1,0:T(8,128)(2,1)S(1)} collective-permute-done((bf16[160,1024]{1,0:T(8,128)(2,1)S(1)}, bf16[160,1024]{1,0:T(8,128)(2,1)S(1)}, u32[]{:S(2)}, u32[]{:S(2)}) %collective-permute-start.17) | collective-permute-done | bytes 327712 | tf_op jit(solution)/shard_map/ppermute | solution.py:427
  99.8 0.1 add_convert_fusion
  99.9 2.6 %collective-permute-start.19 = (bf16[160,1024]{1,0:T(8,128)(2,1)S(1)}, bf16[160,1024]{1,0:T(8,128)(2,1)S(1)}, u32[]{:S(2)}, u32[]{:S(2)}) collective-permute-start(bf16[160,1024]{1,0:T(8,128)(2,1)S(1)} %get-tuple-element.74), channel_id=1, source_target_pairs={{0,2},{2,0},{4,6},{6,4},{1,3},{3,1},{5,7},{7,5},{8,10},{10,8},{12,... | collective-permute-start | bytes 983048 | tf_op jit(solution)/shard_map/ppermute | solution.py:427
  102.4 1.9 %collective-permute-start.20 = (bf16[160,1024]{1,0:T(8,128)(2,1)S(1)}, bf16[160,1024]{1,0:T(8,128)(2,1)S(1)}, u32[]{:S(2)}, u32[]{:S(2)}) collective-permute-start(bf16[160,1024]{1,0:T(8,128)(2,1)S(1)} %add_convert_fusion), channel_id=1, source_target_pairs={{0,4},{2,6},{4,0},{6,2},{1,5},{3,7},{5,1},{7,3},{8,12},{10,14},{12... | collective-permute-start | bytes 983048 | tf_op jit(solution)/shard_map/ppermute | solution.py:427
  104.4 1.0 patch_mean.2.refs_4_
  105.4 10.2 %collective-permute-done.19.refs_1_ = bf16[160,1024]{1,0:T(8,128)(2,1)S(1)} collective-permute-done((bf16[160,1024]{1,0:T(8,128)(2,1)S(1)}, bf16[160,1024]{1,0:T(8,128)(2,1)S(1)}, u32[]{:S(2)}, u32[]{:S(2)}) %collective-permute-start.19) | collective-permute-done | bytes 327712 | tf_op jit(solution)/shard_map/ppermute | solution.py:427
  115.6 3.7 %collective-permute-done.20.refs_2_ = bf16[160,1024]{1,0:T(8,128)(2,1)S(1)} collective-permute-done((bf16[160,1024]{1,0:T(8,128)(2,1)S(1)}, bf16[160,1024]{1,0:T(8,128)(2,1)S(1)}, u32[]{:S(2)}, u32[]{:S(2)}) %collective-permute-start.20) | collective-permute-done | bytes 327712 | tf_op jit(solution)/shard_map/ppermute | solution.py:427
  119.3 1.0 patch_mean.3
  (30 shorter events, 0.5 us)
Async XLA Ops:
  0.0 8.6 %copy-start.1 = (f32[1,2,3]{2,1,0:T(2,128)S(1)}, f32[1,2,3]{2,1,0:T(2,128)}, u32[]{:S(2)}) copy-start(f32[1,2,3]{2,1,0:T(2,128)} %coef.1) | copy-start | bytes 76
  0.0 8.6 %copy-start.2 = (s32[1,2]{1,0:T(1,128)S(1)}, s32[1,2]{1,0:T(1,128)}, u32[]{:S(2)}) copy-start(s32[1,2]{1,0:T(1,128)} %phases.1) | copy-start | bytes 28
  1.8 9.7 %collective-permute-start.1 = (bf16[16,4096]{1,0:T(8,128)(2,1)}, bf16[16,4096]{1,0:T(8,128)(2,1)S(1)}, u32[]{:S(2)}, u32[]{:S(2)}) collective-permute-start(bf16[16,4096]{1,0:T(8,128)(2,1)} %get-tuple-element.40), channel_id=1, source_target_pairs={{0,8},{8,16},{16,24},{1,9},{9,17},{17,25},{2,10},{10,18},{18,26},{... | collective-permute-start | bytes 393224 | tf_op jit(solution)/shard_map/ppermute | solution.py:469
  6.6 7.7 %collective-permute-start.2 = (bf16[16,4096]{1,0:T(8,128)(2,1)}, bf16[16,4096]{1,0:T(8,128)(2,1)S(1)}, u32[]{:S(2)}, u32[]{:S(2)}) collective-permute-start(bf16[16,4096]{1,0:T(8,128)(2,1)} %get-tuple-element.41), channel_id=1, source_target_pairs={{8,0},{16,8},{24,16},{9,1},{17,9},{25,17},{10,2},{18,10},{26,18},{... | collective-permute-start | bytes 393224 | tf_op jit(solution)/shard_map/ppermute | solution.py:470
  21.3 24.4 %collective-permute-start.10 = (bf16[128,2048]{1,0:T(8,128)(2,1)S(1)}, bf16[128,2048]{1,0:T(8,128)(2,1)S(1)}, u32[]{:S(2)}, u32[]{:S(2)}) collective-permute-start(bf16[128,2048]{1,0:T(8,128)(2,1)S(1)} %get-tuple-element.53), channel_id=1, source_target_pairs={{0,16},{8,24},{16,0},{24,8},{1,17},{9,25},{17,1},{25,9},{2,18},{10... | collective-permute-start | bytes 1572872 | tf_op jit(solution)/shard_map/ppermute | solution.py:427
  22.3 23.5 %collective-permute-start.11 = (bf16[128,2048]{1,0:T(8,128)(2,1)S(1)}, bf16[128,2048]{1,0:T(8,128)(2,1)S(1)}, u32[]{:S(2)}, u32[]{:S(2)}) collective-permute-start(bf16[128,2048]{1,0:T(8,128)(2,1)S(1)} %get-tuple-element.54), channel_id=1, source_target_pairs={{0,24},{8,16},{16,8},{24,0},{1,25},{9,17},{17,9},{25,1},{2,26},{10... | collective-permute-start | bytes 1572872 | tf_op jit(solution)/shard_map/ppermute | solution.py:427
  24.6 22.3 %collective-permute-start.9 = (bf16[128,2048]{1,0:T(8,128)(2,1)S(1)}, bf16[128,2048]{1,0:T(8,128)(2,1)S(1)}, u32[]{:S(2)}, u32[]{:S(2)}) collective-permute-start(bf16[128,2048]{1,0:T(8,128)(2,1)S(1)} %get-tuple-element.52), channel_id=1, source_target_pairs={{0,8},{8,0},{16,24},{24,16},{1,9},{9,1},{17,25},{25,17},{2,10},{10... | collective-permute-start | bytes 1572872 | tf_op jit(solution)/shard_map/ppermute | solution.py:427
  25.6 1.1 collective-permute-start.6
  26.8 3.6 %collective-permute-start.7 = (f32[2,3]{1,0:T(2,128)S(1)}, f32[2,3]{1,0:T(2,128)S(1)}, u32[]{:S(2)}, u32[]{:S(2)}) collective-permute-start(f32[2,3]{1,0:T(2,128)S(1)} %pad_maximum_fusion.3), channel_id=1, source_target_pairs={{0,2},{2,0},{4,6},{6,4},{1,3},{3,1},{5,7},{7,5},{8,10},{10,8},{12,... | collective-permute-start | bytes 80 | tf_op jit(solution)/shard_map/ppermute | solution.py:427
  37.5 9.6 %copy-start.3 = (bf16[128,2048]{1,0:T(8,128)(2,1)}, bf16[128,2048]{1,0:T(8,128)(2,1)S(1)}, u32[]{:S(2)}) copy-start(bf16[128,2048]{1,0:T(8,128)(2,1)S(1)} %get-tuple-element.46) | copy-start | bytes 1572868
  37.5 9.6 %copy-start.4 = (bf16[128,2048]{1,0:T(8,128)(2,1)}, bf16[128,2048]{1,0:T(8,128)(2,1)S(1)}, u32[]{:S(2)}) copy-start(bf16[128,2048]{1,0:T(8,128)(2,1)S(1)} %get-tuple-element.45) | copy-start | bytes 1572868
  47.0 0.7 copy-start
  47.1 5.1 %collective-permute-start.12 = (bf16[512,2048]{1,0:T(8,128)(2,1)S(1)}, bf16[512,2048]{1,0:T(8,128)(2,1)}, u32[]{:S(2)}, u32[]{:S(2)}) collective-permute-start(bf16[512,2048]{1,0:T(8,128)(2,1)S(1)} %join_blocks.2.mine), channel_id=1, source_target_pairs={{0,1},{1,0},{2,3},{3,2},{4,5},{5,4},{6,7},{7,6},{8,9},{9,8},{10,11... | collective-permute-start | bytes 6291464 | tf_op jit(solution)/shard_map/ppermute | solution.py:427
  47.2 4.3 %collective-permute-start = (s32[1]{0:T(128)}, s32[1]{0:T(128)}, u32[]{:S(2)}, u32[]{:S(2)}) collective-permute-start(s32[1]{0:T(128)} %param.11), channel_id=1, source_target_pairs={{0,1},{1,0},{2,3},{3,2},{4,5},{5,4},{6,7},{7,6},{8,9},{9,8},{10,11... | collective-permute-start | bytes 20 | tf_op jit(solution)/shard_map/ppermute | solution.py:427
  47.9 21.0 %collective-permute-start.3 = (bf16[128,2048]{1,0:T(8,128)(2,1)}, bf16[128,2048]{1,0:T(8,128)(2,1)S(1)}, u32[]{:S(2)}, u32[]{:S(2)}) collective-permute-start(bf16[128,2048]{1,0:T(8,128)(2,1)} %copy-done.4), channel_id=1, source_target_pairs={{0,8},{8,0},{16,24},{24,16},{1,9},{9,1},{17,25},{25,17},{2,10},{10... | collective-permute-start | bytes 1572872 | tf_op jit(solution)/shard_map/ppermute | solution.py:427
  48.9 25.1 %collective-permute-start.4 = (bf16[128,2048]{1,0:T(8,128)(2,1)}, bf16[128,2048]{1,0:T(8,128)(2,1)S(1)}, u32[]{:S(2)}, u32[]{:S(2)}) collective-permute-start(bf16[128,2048]{1,0:T(8,128)(2,1)} %copy-done.3), channel_id=1, source_target_pairs={{0,16},{8,24},{16,0},{24,8},{1,17},{9,25},{17,1},{25,9},{2,18},{10... | collective-permute-start | bytes 1572872 | tf_op jit(solution)/shard_map/ppermute | solution.py:427
  49.4 24.6 %collective-permute-start.5 = (bf16[128,2048]{1,0:T(8,128)(2,1)S(1)}, bf16[128,2048]{1,0:T(8,128)(2,1)S(1)}, u32[]{:S(2)}, u32[]{:S(2)}) collective-permute-start(bf16[128,2048]{1,0:T(8,128)(2,1)S(1)} %get-tuple-element.47), channel_id=1, source_target_pairs={{0,24},{8,16},{16,8},{24,0},{1,25},{9,17},{17,9},{25,1},{2,26},{10... | collective-permute-start | bytes 1572872 | tf_op jit(solution)/shard_map/ppermute | solution.py:427
  54.8 19.2 %collective-permute-start.13 = (bf16[160,1024]{1,0:T(8,128)(2,1)S(1)}, bf16[160,1024]{1,0:T(8,128)(2,1)S(1)}, u32[]{:S(2)}, u32[]{:S(2)}) collective-permute-start(bf16[160,1024]{1,0:T(8,128)(2,1)S(1)} %get-tuple-element.62), channel_id=1, source_target_pairs={{0,2},{2,0},{4,6},{6,4},{1,3},{3,1},{5,7},{7,5},{8,10},{10,8},{12,... | collective-permute-start | bytes 983048 | tf_op jit(solution)/shard_map/ppermute | solution.py:427
  56.4 7.1 %collective-permute-start.8 = (f32[4,3]{1,0:T(4,128)S(1)}, f32[4,3]{1,0:T(4,128)S(1)}, u32[]{:S(2)}, u32[]{:S(2)}) collective-permute-start(f32[4,3]{1,0:T(4,128)S(1)} %pad_maximum_fusion.2), channel_id=1, source_target_pairs={{0,4},{2,6},{4,0},{6,2},{1,5},{3,7},{5,1},{7,3},{8,12},{10,14},{12... | collective-permute-start | bytes 152 | tf_op jit(solution)/shard_map/ppermute | solution.py:427
  63.5 10.6 %collective-permute-start.14 = (bf16[160,1024]{1,0:T(8,128)(2,1)S(1)}, bf16[160,1024]{1,0:T(8,128)(2,1)S(1)}, u32[]{:S(2)}, u32[]{:S(2)}) collective-permute-start(bf16[160,1024]{1,0:T(8,128)(2,1)S(1)} %get-tuple-element.64), channel_id=1, source_target_pairs={{0,2},{2,0},{4,6},{6,4},{1,3},{3,1},{5,7},{7,5},{8,10},{10,8},{12,... | collective-permute-start | bytes 983048 | tf_op jit(solution)/shard_map/ppermute | solution.py:427
  74.2 11.2 %collective-permute-start.15 = (bf16[512,2048]{1,0:T(8,128)(2,1)S(1)}, bf16[512,2048]{1,0:T(8,128)(2,1)S(1)}, u32[]{:S(2)}, u32[]{:S(2)}) collective-permute-start(bf16[512,2048]{1,0:T(8,128)(2,1)S(1)} %join_blocks.3.mine), channel_id=1, source_target_pairs={{0,1},{1,0},{2,3},{3,2},{4,5},{5,4},{6,7},{7,6},{8,9},{9,8},{10,11... | collective-permute-start | bytes 6291464 | tf_op jit(solution)/shard_map/ppermute | solution.py:427
  74.3 11.1 %collective-permute-start.16 = (bf16[160,512]{1,0:T(8,128)(2,1)S(1)}, bf16[160,512]{1,0:T(8,128)(2,1)S(1)}, u32[]{:S(2)}, u32[]{:S(2)}) collective-permute-start(bf16[160,512]{1,0:T(8,128)(2,1)S(1)} %get-tuple-element.78), channel_id=1, source_target_pairs={{0,4},{2,6},{4,0},{6,2},{1,5},{3,7},{5,1},{7,3},{8,12},{10,14},{12... | collective-permute-start | bytes 491528 | tf_op jit(solution)/shard_map/ppermute | solution.py:427
  86.9 12.9 %collective-permute-start.17 = (bf16[160,1024]{1,0:T(8,128)(2,1)S(1)}, bf16[160,1024]{1,0:T(8,128)(2,1)S(1)}, u32[]{:S(2)}, u32[]{:S(2)}) collective-permute-start(bf16[160,1024]{1,0:T(8,128)(2,1)S(1)} %get-tuple-element.72), channel_id=1, source_target_pairs={{0,2},{2,0},{4,6},{6,4},{1,3},{3,1},{5,7},{7,5},{8,10},{10,8},{12,... | collective-permute-start | bytes 983048 | tf_op jit(solution)/shard_map/ppermute | solution.py:427
  87.6 12.2 %collective-permute-start.18 = (bf16[160,512]{1,0:T(8,128)(2,1)S(1)}, bf16[160,512]{1,0:T(8,128)(2,1)S(1)}, u32[]{:S(2)}, u32[]{:S(2)}) collective-permute-start(bf16[160,512]{1,0:T(8,128)(2,1)S(1)} %get-tuple-element.77), channel_id=1, source_target_pairs={{0,4},{2,6},{4,0},{6,2},{1,5},{3,7},{5,1},{7,3},{8,12},{10,14},{12... | collective-permute-start | bytes 491528 | tf_op jit(solution)/shard_map/ppermute | solution.py:427
  99.9 15.7 %collective-permute-start.19 = (bf16[160,1024]{1,0:T(8,128)(2,1)S(1)}, bf16[160,1024]{1,0:T(8,128)(2,1)S(1)}, u32[]{:S(2)}, u32[]{:S(2)}) collective-permute-start(bf16[160,1024]{1,0:T(8,128)(2,1)S(1)} %get-tuple-element.74), channel_id=1, source_target_pairs={{0,2},{2,0},{4,6},{6,4},{1,3},{3,1},{5,7},{7,5},{8,10},{10,8},{12,... | collective-permute-start | bytes 983048 | tf_op jit(solution)/shard_map/ppermute | solution.py:427
  102.4 16.9 %collective-permute-start.20 = (bf16[160,1024]{1,0:T(8,128)(2,1)S(1)}, bf16[160,1024]{1,0:T(8,128)(2,1)S(1)}, u32[]{:S(2)}, u32[]{:S(2)}) collective-permute-start(bf16[160,1024]{1,0:T(8,128)(2,1)S(1)} %add_convert_fusion), channel_id=1, source_target_pairs={{0,4},{2,6},{4,0},{6,2},{1,5},{3,7},{5,1},{7,3},{8,12},{10,14},{12... | collective-permute-start | bytes 983048 | tf_op jit(solution)/shard_map/ppermute | solution.py:427

commit v11 on v9

--- a/solution.py
+++ b/solution.py
@@ -510,7 +510,7 @@
             filtered(index + 1)
             received = tied(received, sent[index + 1])
         if index == 0:
-            received = tied(received, early)
+            received = tied(received, scale)
         if index == 1:
             received = tied(received, scale)
         if index >= 1:

time: 115 us -> 115 us (level)
  starting transfers between devices: 30.9 us -> 27.5 us
  waiting for transfers between devices: 54.6 us -> 56.4 us
    ppermute x18, starting transfers between devices: 24.7 us -> 21.3 us  [swapped(): return lax.ppermute(value, axis, [(i, i ^ distance) for i in range(count)])]
    ppermute x18, waiting for transfers between devices: 51.8 us -> 53.6 us  [swapped(): return lax.ppermute(value, axis, [(i, i ^ distance) for i in range(count)])]
  transfers between devices with their start and end apart: 20 -> 20, of which waited for: 12 -> 11; matrix products, arithmetic and copies ran while one was open for 1% -> 1% of each run, Pallas kernels for 13% -> 13%
where the time goes in v11:
time: 115 us
  waiting for transfers between devices  56.4 us (49%)
  starting transfers between devices  27.5 us (24%)
  Pallas kernels  26.2 us (23%)
  between operations  2.18 us (2%)
  other arithmetic  1.26 us (1%)
    ppermute x18, waiting for transfers between devices, swapped(): return lax.ppermute(value, axis, [(i, i ^ distance) for i in range(count)])  53.6 us
    ppermute x18, starting transfers between devices, swapped(): return lax.ppermute(value, axis, [(i, i ^ distance) for i in range(count)])  21.3 us
    pallas_call x2, Pallas kernels, filter_chunk(): pl.pallas_call(functools.partial(filter_kernel, first_chunk=start == 0, l...  14.2 us
    ppermute x1, starting transfers between devices, per_device(): low = lax.ppermute(bottom, 'seg', forward)  4.84 us
    pallas_call x2, Pallas kernels, pair_sum(): pl.pallas_call(functools.partial(pair_kernel, slots=slots, distances=dist...  3.97 us
    ppermute x1, waiting for transfers between devices, per_device(): high = lax.ppermute(top, 'seg', backward)  2.84 us
  transfers between devices with their start and end apart: 20, of which 11 were waited for; matrix products, arithmetic and copies ran while one was open for 1% of the time, Pallas kernels for 13%

profile of v11, /device:TPU:0, one launch (start us, length us, event | category | flops | bytes accessed | tf_op | source)
XLA Modules:
  0.0 114.5 jit_solution(18028679316456331832)
XLA Ops:
  0.0 1.8 %edge_rows.1 = (bf16[16,4096]{1,0:T(8,128)(2,1)}, bf16[16,4096]{1,0:T(8,128)(2,1)}) custom-call(f32[512,4096]{1,0:T(8,128)} %bitcast.11, f32[512,4096]{1,0:T(8,128)} %bitcast.12), custom_call_target="tpu_custom_call" | custom-call | flops 1 | bytes 1 | tf_op jit(solution)/shard_map/edge_rows/pallas_call | solution.py:155
  1.8 4.8 %collective-permute-start.1 = (bf16[16,4096]{1,0:T(8,128)(2,1)}, bf16[16,4096]{1,0:T(8,128)(2,1)S(1)}, u32[]{:S(2)}, u32[]{:S(2)}) collective-permute-start(bf16[16,4096]{1,0:T(8,128)(2,1)} %get-tuple-element.38), channel_id=1, source_target_pairs={{0,8},{8,16},{16,24},{1,9},{9,17},{17,25},{2,10},{10,18},{18,26},{... | collective-permute-start | bytes 393224 | tf_op jit(solution)/shard_map/ppermute | solution.py:463
  6.6 1.3 %collective-permute-start.2 = (bf16[16,4096]{1,0:T(8,128)(2,1)}, bf16[16,4096]{1,0:T(8,128)(2,1)S(1)}, u32[]{:S(2)}, u32[]{:S(2)}) collective-permute-start(bf16[16,4096]{1,0:T(8,128)(2,1)} %get-tuple-element.39), channel_id=1, source_target_pairs={{8,0},{16,8},{24,16},{9,1},{17,9},{25,17},{10,2},{18,10},{26,18},{... | collective-permute-start | bytes 393224 | tf_op jit(solution)/shard_map/ppermute | solution.py:464
  8.6 0.1 pad_add_fusion.1.place
  8.7 2.1 %band_matrices.1 = (bf16[3,128,480]{2,1,0:T(8,128)(2,1)S(1)}, bf16[3,2,512,256]{3,2,1,0:T(8,128)(2,1)S(1)}) custom-call(s32[3]{0:T(128)S(1)} %pad_add_fusion.1.place, f32[1,2,3]{2,1,0:T(2,128)S(1)} %copy-done.3, s32[1,2]{1,0:T(1,128)S(1)} %copy-done.4, s32[1]{0:T(128)S(6)} %copy.10.shift), custom_call_target="tpu_custom_call" | custom-call | flops 1 | bytes 1 | tf_op jit(solution)/shard_map/band_matrices/pallas_call | solution.py:132
  11.5 2.8 %collective-permute-done.2.high_l.high_c.high_r = bf16[16,4096]{1,0:T(8,128)(2,1)S(1)} collective-permute-done((bf16[16,4096]{1,0:T(8,128)(2,1)}, bf16[16,4096]{1,0:T(8,128)(2,1)S(1)}, u32[]{:S(2)}, u32[]{:S(2)}) %collective-permute-start.2) | collective-permute-done | bytes 131104 | tf_op jit(solution)/shard_map/ppermute | solution.py:464
  14.3 7.1 %warp_filter.3 = (bf16[128,2048]{1,0:T(8,128)(2,1)S(1)}, bf16[128,2048]{1,0:T(8,128)(2,1)S(1)}, bf16[128,2048]{1,0:T(8,128)(2,1)S(1)}, bf16[128,2048]{1,0:T(8,128)(2,1)S(1)}) custom-call(f32[1]{0:T(128)} %convert_element_type.27.weight, bf16[16,4096]{1,0:T(8,128)(2,1)S(1)} %collective-permute-done.1.low_l.low_c.low_r, ...), custom_call_target="tpu_custom_call" | custom-call | flops 1 | bytes 1 | tf_op jit(solution)/shard_map/warp_filter/pallas_call | solution.py:256
  21.4 1.8 %collective-permute-start.9 = (bf16[128,2048]{1,0:T(8,128)(2,1)S(1)}, bf16[128,2048]{1,0:T(8,128)(2,1)S(1)}, u32[]{:S(2)}, u32[]{:S(2)}) collective-permute-start(bf16[128,2048]{1,0:T(8,128)(2,1)S(1)} %get-tuple-element.50), channel_id=1, source_target_pairs={{0,8},{8,0},{16,24},{24,16},{1,9},{9,1},{17,25},{25,17},{2,10},{10... | collective-permute-start | bytes 1572872 | tf_op jit(solution)/shard_map/ppermute | solution.py:427
  23.2 1.7 %collective-permute-start.11 = (bf16[128,2048]{1,0:T(8,128)(2,1)S(1)}, bf16[128,2048]{1,0:T(8,128)(2,1)S(1)}, u32[]{:S(2)}, u32[]{:S(2)}) collective-permute-start(bf16[128,2048]{1,0:T(8,128)(2,1)S(1)} %get-tuple-element.52), channel_id=1, source_target_pairs={{0,24},{8,16},{16,8},{24,0},{1,25},{9,17},{17,9},{25,1},{2,26},{10... | collective-permute-start | bytes 1572872 | tf_op jit(solution)/shard_map/ppermute | solution.py:427
  25.7 1.1 collective-permute-done.6
  26.8 0.1 pad_maximum_fusion.2
  26.9 1.6 %collective-permute-start.7 = (f32[2,3]{1,0:T(2,128)S(1)}, f32[2,3]{1,0:T(2,128)S(1)}, u32[]{:S(2)}, u32[]{:S(2)}) collective-permute-start(f32[2,3]{1,0:T(2,128)S(1)} %pad_maximum_fusion.2), channel_id=1, source_target_pairs={{0,2},{2,0},{4,6},{6,4},{1,3},{3,1},{5,7},{7,5},{8,10},{10,8},{12,... | collective-permute-start | bytes 80 | tf_op jit(solution)/shard_map/ppermute | solution.py:427
  28.5 2.0 %collective-permute-done.7 = f32[2,3]{1,0:T(2,128)S(1)} collective-permute-done((f32[2,3]{1,0:T(2,128)S(1)}, f32[2,3]{1,0:T(2,128)S(1)}, u32[]{:S(2)}, u32[]{:S(2)}) %collective-permute-start.7) | collective-permute-done | bytes 56 | tf_op jit(solution)/shard_map/ppermute | solution.py:427
  30.5 0.1 pad_maximum_fusion.1
  30.5 2.6 %collective-permute-start.8 = (f32[4,3]{1,0:T(4,128)S(1)}, f32[4,3]{1,0:T(4,128)S(1)}, u32[]{:S(2)}, u32[]{:S(2)}) collective-permute-start(f32[4,3]{1,0:T(4,128)S(1)} %pad_maximum_fusion.1), channel_id=1, source_target_pairs={{0,4},{2,6},{4,0},{6,2},{1,5},{3,7},{5,1},{7,3},{8,12},{10,14},{12... | collective-permute-start | bytes 152 | tf_op jit(solution)/shard_map/ppermute | solution.py:427
  33.1 1.9 %collective-permute-done.8 = f32[4,3]{1,0:T(4,128)S(1)} collective-permute-done((f32[4,3]{1,0:T(4,128)S(1)}, f32[4,3]{1,0:T(4,128)S(1)}, u32[]{:S(2)}, u32[]{:S(2)}) %collective-permute-start.8) | collective-permute-done | bytes 80 | tf_op jit(solution)/shard_map/ppermute | solution.py:427
  35.0 0.1 pad_maximum_fusion.facts
  35.1 1.8 %patch_weights.1.refs_3_ = f32[160,2048]{1,0:T(8,128)S(1)} custom-call(s32[3]{0:T(128)S(1)} %pad_add_fusion.1.place, s32[160]{0:T(256)S(1)} %copy-done.2, f32[8,3]{1,0:T(8,128)S(1)} %pad_maximum_fusion.facts), custom_call_target="tpu_custom_call" | custom-call | flops 1 | bytes 1 | tf_op jit(solution)/shard_map/patch_weights/pallas_call | solution.py:380
  36.9 7.1 %warp_filter.2 = (bf16[128,2048]{1,0:T(8,128)(2,1)S(1)}, bf16[128,2048]{1,0:T(8,128)(2,1)S(1)}, bf16[128,2048]{1,0:T(8,128)(2,1)S(1)}, bf16[128,2048]{1,0:T(8,128)(2,1)S(1)}) custom-call(f32[1]{0:T(128)} %convert_element_type.27.weight, bf16[16,4096]{1,0:T(8,128)(2,1)S(1)} %collective-permute-done.1.low_l.low_c.low_r, ...), custom_call_target="tpu_custom_call" | custom-call | flops 1 | bytes 1 | tf_op jit(solution)/shard_map/warp_filter/pallas_call | solution.py:256
  44.1 0.8 copy-done
  44.9 1.5 %collective-permute-done.10.refs_2_ = bf16[128,2048]{1,0:T(8,128)(2,1)S(1)} collective-permute-done((bf16[128,2048]{1,0:T(8,128)(2,1)S(1)}, bf16[128,2048]{1,0:T(8,128)(2,1)S(1)}, u32[]{:S(2)}, u32[]{:S(2)}) %collective-permute-start.10) | collective-permute-done | bytes 524320 | tf_op jit(solution)/shard_map/ppermute | solution.py:427
  46.4 0.1 join_blocks.2.mine
  46.7 0.5 collective-permute-start
  47.1 0.1 reshape.10
  47.3 0.1 reshape.11
  47.4 1.2 %collective-permute-start.3 = (bf16[128,2048]{1,0:T(8,128)(2,1)}, bf16[128,2048]{1,0:T(8,128)(2,1)S(1)}, u32[]{:S(2)}, u32[]{:S(2)}) collective-permute-start(bf16[128,2048]{1,0:T(8,128)(2,1)} %copy-done.7), channel_id=1, source_target_pairs={{0,8},{8,0},{16,24},{24,16},{1,9},{9,1},{17,25},{25,17},{2,10},{10... | collective-permute-start | bytes 1572872 | tf_op jit(solution)/shard_map/ppermute | solution.py:427
  48.6 0.8 collective-permute-start.4
  49.4 1.6 %collective-permute-start.5 = (bf16[128,2048]{1,0:T(8,128)(2,1)}, bf16[128,2048]{1,0:T(8,128)(2,1)S(1)}, u32[]{:S(2)}, u32[]{:S(2)}) collective-permute-start(bf16[128,2048]{1,0:T(8,128)(2,1)} %copy-done.5), channel_id=1, source_target_pairs={{0,24},{8,16},{16,8},{24,0},{1,25},{9,17},{17,9},{25,1},{2,26},{10... | collective-permute-start | bytes 1572872 | tf_op jit(solution)/shard_map/ppermute | solution.py:427
  50.9 0.6 fusion.2
  51.5 0.1 pad_add_fusion.table
  51.6 2.5 %pair_sum.2 = (bf16[160,1024]{1,0:T(8,128)(2,1)S(1)}, bf16[160,1024]{1,0:T(8,128)(2,1)S(1)}, bf16[160,1024]{1,0:T(8,128)(2,1)S(1)}, bf16[160,1024]{1,0:T(8,128)(2,1)S(1)}) custom-call(s32[3]{0:T(128)S(1)} %pad_add_fusion.1.place, s32[240]{0:T(256)S(1)} %pad_add_fusion.table, bf16[512,2048]{1,0:T(8,128)(2,1)S(1)} %join_blocks.2.mine, ...), custom_call_target="tpu_custom_call" | custom-call | flops 1 | bytes 1 | tf_op jit(solution)/shard_map/pair_sum/pallas_call | solution.py:340
  54.1 1.6 %collective-permute-start.13 = (bf16[160,1024]{1,0:T(8,128)(2,1)S(1)}, bf16[160,1024]{1,0:T(8,128)(2,1)S(1)}, u32[]{:S(2)}, u32[]{:S(2)}) collective-permute-start(bf16[160,1024]{1,0:T(8,128)(2,1)S(1)} %get-tuple-element.60), channel_id=1, source_target_pairs={{0,2},{2,0},{4,6},{6,4},{1,3},{3,1},{5,7},{7,5},{8,10},{10,8},{12,... | collective-permute-start | bytes 983048 | tf_op jit(solution)/shard_map/ppermute | solution.py:427
  55.8 0.5 collective-permute-start.14
  56.2 6.2 %collective-permute-done.3.refs_1_ = bf16[128,2048]{1,0:T(8,128)(2,1)S(1)} collective-permute-done((bf16[128,2048]{1,0:T(8,128)(2,1)}, bf16[128,2048]{1,0:T(8,128)(2,1)S(1)}, u32[]{:S(2)}, u32[]{:S(2)}) %collective-permute-start.3) | collective-permute-done | bytes 524320 | tf_op jit(solution)/shard_map/ppermute | solution.py:427
  62.4 11.2 %collective-permute-done.4.refs_2_ = bf16[128,2048]{1,0:T(8,128)(2,1)S(1)} collective-permute-done((bf16[128,2048]{1,0:T(8,128)(2,1)}, bf16[128,2048]{1,0:T(8,128)(2,1)S(1)}, u32[]{:S(2)}, u32[]{:S(2)}) %collective-permute-start.4) | collective-permute-done | bytes 524320 | tf_op jit(solution)/shard_map/ppermute | solution.py:427
  73.7 0.1 add_convert_fusion.1
  73.8 0.1 join_blocks.3.mine
  74.0 4.1 %collective-permute-done.15.other = bf16[512,2048]{1,0:T(8,128)(2,1)S(1)} collective-permute-done((bf16[512,2048]{1,0:T(8,128)(2,1)S(1)}, bf16[512,2048]{1,0:T(8,128)(2,1)S(1)}, u32[]{:S(2)}, u32[]{:S(2)}) %collective-permute-start.15) | collective-permute-done | bytes 2097184 | tf_op jit(solution)/shard_map/ppermute | solution.py:427
  78.2 1.4 %pair_sum.3 = (bf16[160,1024]{1,0:T(8,128)(2,1)S(1)}, bf16[160,1024]{1,0:T(8,128)(2,1)S(1)}, bf16[160,1024]{1,0:T(8,128)(2,1)S(1)}, bf16[160,1024]{1,0:T(8,128)(2,1)S(1)}) custom-call(s32[3]{0:T(128)S(1)} %pad_add_fusion.1.place, s32[240]{0:T(256)S(1)} %pad_add_fusion.table, bf16[512,2048]{1,0:T(8,128)(2,1)S(1)} %join_blocks.3.mine, ...), custom_call_target="tpu_custom_call" | custom-call | flops 1 | bytes 1 | tf_op jit(solution)/shard_map/pair_sum/pallas_call | solution.py:340
  79.6 1.6 %collective-permute-start.16 = (bf16[160,1024]{1,0:T(8,128)(2,1)S(1)}, bf16[160,1024]{1,0:T(8,128)(2,1)S(1)}, u32[]{:S(2)}, u32[]{:S(2)}) collective-permute-start(bf16[160,1024]{1,0:T(8,128)(2,1)S(1)} %get-tuple-element.69), channel_id=1, source_target_pairs={{0,2},{2,0},{4,6},{6,4},{1,3},{3,1},{5,7},{7,5},{8,10},{10,8},{12,... | collective-permute-start | bytes 983048 | tf_op jit(solution)/shard_map/ppermute | solution.py:427
  81.2 2.6 %collective-permute-start.19 = (bf16[160,1024]{1,0:T(8,128)(2,1)S(1)}, bf16[160,1024]{1,0:T(8,128)(2,1)S(1)}, u32[]{:S(2)}, u32[]{:S(2)}) collective-permute-start(bf16[160,1024]{1,0:T(8,128)(2,1)S(1)} %add_convert_fusion.1), channel_id=1, source_target_pairs={{0,4},{2,6},{4,0},{6,2},{1,5},{3,7},{5,1},{7,3},{8,12},{10,14},{12... | collective-permute-start | bytes 983048 | tf_op jit(solution)/shard_map/ppermute | solution.py:427
  83.8 12.5 %collective-permute-done.16 = bf16[160,1024]{1,0:T(8,128)(2,1)S(1)} collective-permute-done((bf16[160,1024]{1,0:T(8,128)(2,1)S(1)}, bf16[160,1024]{1,0:T(8,128)(2,1)S(1)}, u32[]{:S(2)}, u32[]{:S(2)}) %collective-permute-start.16) | collective-permute-done | bytes 327712 | tf_op jit(solution)/shard_map/ppermute | solution.py:427
  96.3 0.1 add_convert_fusion
  96.5 3.0 %collective-permute-start.18 = (bf16[160,1024]{1,0:T(8,128)(2,1)S(1)}, bf16[160,1024]{1,0:T(8,128)(2,1)S(1)}, u32[]{:S(2)}, u32[]{:S(2)}) collective-permute-start(bf16[160,1024]{1,0:T(8,128)(2,1)S(1)} %add_convert_fusion), channel_id=1, source_target_pairs={{0,4},{2,6},{4,0},{6,2},{1,5},{3,7},{5,1},{7,3},{8,12},{10,14},{12... | collective-permute-start | bytes 983048 | tf_op jit(solution)/shard_map/ppermute | solution.py:427
  99.5 1.0 patch_mean.2.refs_4_
  100.5 11.8 %collective-permute-done.17.refs_1_ = bf16[160,1024]{1,0:T(8,128)(2,1)S(1)} collective-permute-done((bf16[160,1024]{1,0:T(8,128)(2,1)S(1)}, bf16[160,1024]{1,0:T(8,128)(2,1)S(1)}, u32[]{:S(2)}, u32[]{:S(2)}) %collective-permute-start.17) | collective-permute-done | bytes 327712 | tf_op jit(solution)/shard_map/ppermute | solution.py:427
  112.3 1.2 %collective-permute-done.18.refs_2_ = bf16[160,1024]{1,0:T(8,128)(2,1)S(1)} collective-permute-done((bf16[160,1024]{1,0:T(8,128)(2,1)S(1)}, bf16[160,1024]{1,0:T(8,128)(2,1)S(1)}, u32[]{:S(2)}, u32[]{:S(2)}) %collective-permute-start.18) | collective-permute-done | bytes 327712 | tf_op jit(solution)/shard_map/ppermute | solution.py:427
  113.5 1.0 patch_mean.3
  (32 shorter events, 0.4 us)
Async XLA Ops:
  0.0 8.6 %copy-start.3 = (f32[1,2,3]{2,1,0:T(2,128)S(1)}, f32[1,2,3]{2,1,0:T(2,128)}, u32[]{:S(2)}) copy-start(f32[1,2,3]{2,1,0:T(2,128)} %coef.1) | copy-start | bytes 76
  0.0 8.6 %copy-start.4 = (s32[1,2]{1,0:T(1,128)S(1)}, s32[1,2]{1,0:T(1,128)}, u32[]{:S(2)}) copy-start(s32[1,2]{1,0:T(1,128)} %phases.1) | copy-start | bytes 28
  1.8 9.7 %collective-permute-start.1 = (bf16[16,4096]{1,0:T(8,128)(2,1)}, bf16[16,4096]{1,0:T(8,128)(2,1)S(1)}, u32[]{:S(2)}, u32[]{:S(2)}) collective-permute-start(bf16[16,4096]{1,0:T(8,128)(2,1)} %get-tuple-element.38), channel_id=1, source_target_pairs={{0,8},{8,16},{16,24},{1,9},{9,17},{17,25},{2,10},{10,18},{18,26},{... | collective-permute-start | bytes 393224 | tf_op jit(solution)/shard_map/ppermute | solution.py:463
  6.6 7.7 %collective-permute-start.2 = (bf16[16,4096]{1,0:T(8,128)(2,1)}, bf16[16,4096]{1,0:T(8,128)(2,1)S(1)}, u32[]{:S(2)}, u32[]{:S(2)}) collective-permute-start(bf16[16,4096]{1,0:T(8,128)(2,1)} %get-tuple-element.39), channel_id=1, source_target_pairs={{8,0},{16,8},{24,16},{9,1},{17,9},{25,17},{10,2},{18,10},{26,18},{... | collective-permute-start | bytes 393224 | tf_op jit(solution)/shard_map/ppermute | solution.py:464
  14.3 20.8 %copy-start.2 = (s32[160]{0:T(256)S(1)}, s32[160]{0:T(256)}, u32[]{:S(2)}) copy-start(s32[160]{0:T(256)} %sites.1) | copy-start | bytes 1924
  21.4 23.5 %collective-permute-start.9 = (bf16[128,2048]{1,0:T(8,128)(2,1)S(1)}, bf16[128,2048]{1,0:T(8,128)(2,1)S(1)}, u32[]{:S(2)}, u32[]{:S(2)}) collective-permute-start(bf16[128,2048]{1,0:T(8,128)(2,1)S(1)} %get-tuple-element.50), channel_id=1, source_target_pairs={{0,8},{8,0},{16,24},{24,16},{1,9},{9,1},{17,25},{25,17},{2,10},{10... | collective-permute-start | bytes 1572872 | tf_op jit(solution)/shard_map/ppermute | solution.py:427
  23.2 23.2 %collective-permute-start.10 = (bf16[128,2048]{1,0:T(8,128)(2,1)S(1)}, bf16[128,2048]{1,0:T(8,128)(2,1)S(1)}, u32[]{:S(2)}, u32[]{:S(2)}) collective-permute-start(bf16[128,2048]{1,0:T(8,128)(2,1)S(1)} %get-tuple-element.51), channel_id=1, source_target_pairs={{0,16},{8,24},{16,0},{24,8},{1,17},{9,25},{17,1},{25,9},{2,18},{10... | collective-permute-start | bytes 1572872 | tf_op jit(solution)/shard_map/ppermute | solution.py:427
  23.2 23.2 %collective-permute-start.11 = (bf16[128,2048]{1,0:T(8,128)(2,1)S(1)}, bf16[128,2048]{1,0:T(8,128)(2,1)S(1)}, u32[]{:S(2)}, u32[]{:S(2)}) collective-permute-start(bf16[128,2048]{1,0:T(8,128)(2,1)S(1)} %get-tuple-element.52), channel_id=1, source_target_pairs={{0,24},{8,16},{16,8},{24,0},{1,25},{9,17},{17,9},{25,1},{2,26},{10... | collective-permute-start | bytes 1572872 | tf_op jit(solution)/shard_map/ppermute | solution.py:427
  25.7 1.1 collective-permute-start.6
  26.9 3.6 %collective-permute-start.7 = (f32[2,3]{1,0:T(2,128)S(1)}, f32[2,3]{1,0:T(2,128)S(1)}, u32[]{:S(2)}, u32[]{:S(2)}) collective-permute-start(f32[2,3]{1,0:T(2,128)S(1)} %pad_maximum_fusion.2), channel_id=1, source_target_pairs={{0,2},{2,0},{4,6},{6,4},{1,3},{3,1},{5,7},{7,5},{8,10},{10,8},{12,... | collective-permute-start | bytes 80 | tf_op jit(solution)/shard_map/ppermute | solution.py:427
  30.5 4.5 %collective-permute-start.8 = (f32[4,3]{1,0:T(4,128)S(1)}, f32[4,3]{1,0:T(4,128)S(1)}, u32[]{:S(2)}, u32[]{:S(2)}) collective-permute-start(f32[4,3]{1,0:T(4,128)S(1)} %pad_maximum_fusion.1), channel_id=1, source_target_pairs={{0,4},{2,6},{4,0},{6,2},{1,5},{3,7},{5,1},{7,3},{8,12},{10,14},{12... | collective-permute-start | bytes 152 | tf_op jit(solution)/shard_map/ppermute | solution.py:427
  44.1 0.8 copy-start
  44.9 1.7 %copy-start.5 = (bf16[128,2048]{1,0:T(8,128)(2,1)}, bf16[128,2048]{1,0:T(8,128)(2,1)S(1)}, u32[]{:S(2)}) copy-start(bf16[128,2048]{1,0:T(8,128)(2,1)S(1)} %get-tuple-element.45) | copy-start | bytes 1572868
  44.9 1.8 %copy-start.6 = (bf16[128,2048]{1,0:T(8,128)(2,1)}, bf16[128,2048]{1,0:T(8,128)(2,1)S(1)}, u32[]{:S(2)}) copy-start(bf16[128,2048]{1,0:T(8,128)(2,1)S(1)} %get-tuple-element.44) | copy-start | bytes 1572868
  44.9 1.8 %copy-start.7 = (bf16[128,2048]{1,0:T(8,128)(2,1)}, bf16[128,2048]{1,0:T(8,128)(2,1)S(1)}, u32[]{:S(2)}) copy-start(bf16[128,2048]{1,0:T(8,128)(2,1)S(1)} %get-tuple-element.43) | copy-start | bytes 1572868
  46.6 5.0 %collective-permute-start.12 = (bf16[512,2048]{1,0:T(8,128)(2,1)S(1)}, bf16[512,2048]{1,0:T(8,128)(2,1)}, u32[]{:S(2)}, u32[]{:S(2)}) collective-permute-start(bf16[512,2048]{1,0:T(8,128)(2,1)S(1)} %join_blocks.2.mine), channel_id=1, source_target_pairs={{0,1},{1,0},{2,3},{3,2},{4,5},{5,4},{6,7},{7,6},{8,9},{9,8},{10,11... | collective-permute-start | bytes 6291464 | tf_op jit(solution)/shard_map/ppermute | solution.py:427
  46.7 4.3 %collective-permute-start = (s32[1]{0:T(128)}, s32[1]{0:T(128)}, u32[]{:S(2)}, u32[]{:S(2)}) collective-permute-start(s32[1]{0:T(128)} %param.11), channel_id=1, source_target_pairs={{0,1},{1,0},{2,3},{3,2},{4,5},{5,4},{6,7},{7,6},{8,9},{9,8},{10,11... | collective-permute-start | bytes 20 | tf_op jit(solution)/shard_map/ppermute | solution.py:427
  47.4 15.0 %collective-permute-start.3 = (bf16[128,2048]{1,0:T(8,128)(2,1)}, bf16[128,2048]{1,0:T(8,128)(2,1)S(1)}, u32[]{:S(2)}, u32[]{:S(2)}) collective-permute-start(bf16[128,2048]{1,0:T(8,128)(2,1)} %copy-done.7), channel_id=1, source_target_pairs={{0,8},{8,0},{16,24},{24,16},{1,9},{9,1},{17,25},{25,17},{2,10},{10... | collective-permute-start | bytes 1572872 | tf_op jit(solution)/shard_map/ppermute | solution.py:427
  48.6 25.1 %collective-permute-start.4 = (bf16[128,2048]{1,0:T(8,128)(2,1)}, bf16[128,2048]{1,0:T(8,128)(2,1)S(1)}, u32[]{:S(2)}, u32[]{:S(2)}) collective-permute-start(bf16[128,2048]{1,0:T(8,128)(2,1)} %copy-done.6), channel_id=1, source_target_pairs={{0,16},{8,24},{16,0},{24,8},{1,17},{9,25},{17,1},{25,9},{2,18},{10... | collective-permute-start | bytes 1572872 | tf_op jit(solution)/shard_map/ppermute | solution.py:427
  49.4 24.3 %collective-permute-start.5 = (bf16[128,2048]{1,0:T(8,128)(2,1)}, bf16[128,2048]{1,0:T(8,128)(2,1)S(1)}, u32[]{:S(2)}, u32[]{:S(2)}) collective-permute-start(bf16[128,2048]{1,0:T(8,128)(2,1)} %copy-done.5), channel_id=1, source_target_pairs={{0,24},{8,16},{16,8},{24,0},{1,25},{9,17},{17,9},{25,1},{2,26},{10... | collective-permute-start | bytes 1572872 | tf_op jit(solution)/shard_map/ppermute | solution.py:427
  51.6 22.2 %copy-start.1 = (bf16[128,2048]{1,0:T(8,128)(2,1)S(1)}, bf16[128,2048]{1,0:T(8,128)(2,1)}, u32[]{:S(2)}) copy-start(bf16[128,2048]{1,0:T(8,128)(2,1)} %copy-done) | copy-start | bytes 1572868
  54.1 19.5 %collective-permute-start.13 = (bf16[160,1024]{1,0:T(8,128)(2,1)S(1)}, bf16[160,1024]{1,0:T(8,128)(2,1)S(1)}, u32[]{:S(2)}, u32[]{:S(2)}) collective-permute-start(bf16[160,1024]{1,0:T(8,128)(2,1)S(1)} %get-tuple-element.60), channel_id=1, source_target_pairs={{0,2},{2,0},{4,6},{6,4},{1,3},{3,1},{5,7},{7,5},{8,10},{10,8},{12,... | collective-permute-start | bytes 983048 | tf_op jit(solution)/shard_map/ppermute | solution.py:427
  55.8 18.0 %collective-permute-start.14 = (bf16[160,1024]{1,0:T(8,128)(2,1)S(1)}, bf16[160,1024]{1,0:T(8,128)(2,1)S(1)}, u32[]{:S(2)}, u32[]{:S(2)}) collective-permute-start(bf16[160,1024]{1,0:T(8,128)(2,1)S(1)} %get-tuple-element.62), channel_id=1, source_target_pairs={{0,2},{2,0},{4,6},{6,4},{1,3},{3,1},{5,7},{7,5},{8,10},{10,8},{12,... | collective-permute-start | bytes 983048 | tf_op jit(solution)/shard_map/ppermute | solution.py:427
  73.9 4.2 %collective-permute-start.15 = (bf16[512,2048]{1,0:T(8,128)(2,1)S(1)}, bf16[512,2048]{1,0:T(8,128)(2,1)S(1)}, u32[]{:S(2)}, u32[]{:S(2)}) collective-permute-start(bf16[512,2048]{1,0:T(8,128)(2,1)S(1)} %join_blocks.3.mine), channel_id=1, source_target_pairs={{0,1},{1,0},{2,3},{3,2},{4,5},{5,4},{6,7},{7,6},{8,9},{9,8},{10,11... | collective-permute-start | bytes 6291464 | tf_op jit(solution)/shard_map/ppermute | solution.py:427
  79.6 16.7 %collective-permute-start.16 = (bf16[160,1024]{1,0:T(8,128)(2,1)S(1)}, bf16[160,1024]{1,0:T(8,128)(2,1)S(1)}, u32[]{:S(2)}, u32[]{:S(2)}) collective-permute-start(bf16[160,1024]{1,0:T(8,128)(2,1)S(1)} %get-tuple-element.69), channel_id=1, source_target_pairs={{0,2},{2,0},{4,6},{6,4},{1,3},{3,1},{5,7},{7,5},{8,10},{10,8},{12,... | collective-permute-start | bytes 983048 | tf_op jit(solution)/shard_map/ppermute | solution.py:427
  81.2 18.3 %collective-permute-start.19 = (bf16[160,1024]{1,0:T(8,128)(2,1)S(1)}, bf16[160,1024]{1,0:T(8,128)(2,1)S(1)}, u32[]{:S(2)}, u32[]{:S(2)}) collective-permute-start(bf16[160,1024]{1,0:T(8,128)(2,1)S(1)} %add_convert_fusion.1), channel_id=1, source_target_pairs={{0,4},{2,6},{4,0},{6,2},{1,5},{3,7},{5,1},{7,3},{8,12},{10,14},{12... | collective-permute-start | bytes 983048 | tf_op jit(solution)/shard_map/ppermute | solution.py:427
  96.4 15.9 %collective-permute-start.17 = (bf16[160,1024]{1,0:T(8,128)(2,1)S(1)}, bf16[160,1024]{1,0:T(8,128)(2,1)S(1)}, u32[]{:S(2)}, u32[]{:S(2)}) collective-permute-start(bf16[160,1024]{1,0:T(8,128)(2,1)S(1)} %get-tuple-element.70), channel_id=1, source_target_pairs={{0,2},{2,0},{4,6},{6,4},{1,3},{3,1},{5,7},{7,5},{8,10},{10,8},{12,... | collective-permute-start | bytes 983048 | tf_op jit(solution)/shard_map/ppermute | solution.py:427
  96.5 17.0 %collective-permute-start.18 = (bf16[160,1024]{1,0:T(8,128)(2,1)S(1)}, bf16[160,1024]{1,0:T(8,128)(2,1)S(1)}, u32[]{:S(2)}, u32[]{:S(2)}) collective-permute-start(bf16[160,1024]{1,0:T(8,128)(2,1)S(1)} %add_convert_fusion), channel_id=1, source_target_pairs={{0,4},{2,6},{4,0},{6,2},{1,5},{3,7},{5,1},{7,3},{8,12},{10,14},{12... | collective-permute-start | bytes 983048 | tf_op jit(solution)/shard_map/ppermute | solution.py:427
